TPU v7x, 32 devices: a whole 2x2x4 slice. The times are simulated.
32 devices in a mesh: groups: 2 (over x), tile: 16 (over z, y, core).
Axes of the slice: x: 2, y: 2, z: 4, core: 2. Of those that a mesh axis runs over, the one named last changes fastest.
Arguments:
- inputs: bfloat16 [64, 16, 16, 256], P(('groups', 'tile')), parts along dimension 0, may hold values from -6 to 6
- out_grad: bfloat16 [64, 16, 16, 256], P(('groups', 'tile')), parts along dimension 0, may hold values from -4 to 4
- kernel: float32 [2, 7, 7, 256], replicated, may hold values from -0.875 to 0.875
- norm_gain: float32 [2, 256], replicated, may hold values from 0.5 to 1.5
- up_weight: bfloat16 [2, 256, 1024], replicated, may hold values from -0.375 to 0.375
- down_weight: bfloat16 [2, 1024, 256], replicated, may hold values from -0.1875 to 0.1875
- layer_scale: float32 [2, 256], replicated, may hold values from 0.3 to 1
- seam_table: int32 [32, 4, 2], replicated, may hold values from 0 to 31, as said below
- corner_table: int32 [32, 4, 2], replicated, may hold values from 0 to 31, as said below
Outputs:
- output: bfloat16 [64, 16, 16, 256], P(('groups', 'tile')), parts along dimension 0
- in_grad: bfloat16 [64, 16, 16, 256], P(('groups', 'tile')), parts along dimension 0
- grad_kernel: float32 [4, 7, 7, 256], P('groups'), parts along dimension 0
- grad_gain: float32 [4, 256], P('groups'), parts along dimension 0
- grad_up: float32 [4, 256, 1024], P('groups'), parts along dimension 0
- grad_down: float32 [4, 1024, 256], P('groups'), parts along dimension 0
- grad_scale: float32 [4, 256], P('groups'), parts along dimension 0
There are 2 independent parts, one for each index of `groups`. A program takes and returns all parts, laid end to end along the dimension named above; an argument that names none is the same for every part. Nothing has to cross between parts.
Inputs may be any that keep to these rules, and one draw needn't show every extreme that they name: `seam_table`: tile q is held by device q // 2 of the tile axis. Entry [q, e] names a tile and one of its sides (0 to 3); every side of every tile is named exactly once. The named tile lies on the device of q or on one of the two devices beside it along the tile axis, counted cyclically. From one device beside it a device needs at most 4 strips, and some devices need exactly that many. `corner_table`: entry [q, e] names a tile and one of its corners (0 to 3), lying on the device of q or on one of the two devices beside it along the tile axis, counted cyclically. From one device beside it a device needs at most 6 corner blocks, and some devices need exactly that many.
All inputs are finite; a program needn't handle non-finite values.
Results may differ from a plain program's by a relative error of at most 0.0085.
Values may be sent and summed in bfloat16 or wider, within the bound.
No kernel may reach another device: no remote copies, remote signals or barrier semaphores. Data moves between devices by JAX's collectives and lax.ppermute only.
A program may use at most 192 MiB of HBM per device.

v0:
```python
import functools

import jax
import jax.numpy as jnp
from jax import lax
from jax.experimental import pallas as pl
from jax.experimental.pallas import tpu as pltpu
from jax.sharding import PartitionSpec as P

epsilon = 1e-06
inverse_root_two = 0.7071067811865476
inverse_root_tau = 0.3989422804014327

LANES = 128
TAPS = 7
REACH = 3
PITCH = 24
GRAD_PITCH = 32
SMALL_ROWS = 64
F32 = jnp.float32
BF16 = jnp.bfloat16


def flip_rows(value):
    rows = value.shape[0]
    order = 7 - lax.broadcasted_iota(jnp.int32, (8, LANES), 0)
    parts = [
        jnp.take_along_axis(value[at : at + 8], order, axis=0, mode="promise_in_bounds")
        for at in range(0, rows, 8)
    ]
    return jnp.concatenate(parts[::-1], axis=0)


def halves(value):
    return [value[:, at : at + LANES] for at in range(0, value.shape[1], LANES)]


class Sizes:
    def __init__(self, tiles, edge, channels, hidden):
        self.tiles = tiles
        self.edge = edge
        self.channels = channels
        self.hidden = hidden
        self.lanes = channels // LANES
        self.cells = edge * edge
        self.rows = tiles * edge * edge
        self.pieces = tiles * 4
        self.outer = edge + 2 * REACH
        self.slabs = tiles * self.lanes

    def key(self):
        return (self.tiles, self.edge, self.channels, self.hidden)


def strip_window(edge, side, row):
    if side == 0:
        return pl.ds(row * edge, edge), False
    if side == 1:
        return pl.ds(edge - 1 - row, edge, stride=edge), False
    if side == 2:
        return pl.ds((edge - 1 - row) * edge, edge), True
    return pl.ds(row, edge, stride=edge), True


def margin_window(edge, side, row):
    last = edge + 2 * REACH - 1
    if side == 0:
        return pl.ds((2 - row) * PITCH + REACH, edge), True
    if side == 1:
        return pl.ds(REACH * PITCH + last - 2 + row, edge, stride=PITCH), True
    if side == 2:
        return pl.ds((last - 2 + row) * PITCH + REACH, edge), False
    return pl.ds(REACH * PITCH + 2 - row, edge, stride=PITCH), False


def corner_cell(edge, corner, row, column):
    last = edge + 2 * REACH - 1
    r, x = 2 - row, 2 - column
    if corner == 0:
        at = (r, x)
    elif corner == 1:
        at = (x, last - r)
    elif corner == 2:
        at = (last - r, last - x)
    else:
        at = (last - x, r)
    return at[0] * PITCH + at[1]


def write_strips(sz, flat, strips_ref):
    for q in range(sz.tiles):
        for side in range(4):
            for row in range(REACH):
                window, turned = strip_window(sz.edge, side, row)
                parts = [flat[q * sz.lanes + h, window, :] for h in range(sz.lanes)]
                if turned:
                    parts = [flip_rows(part) for part in parts]
                strips_ref[q * 4 + side, row] = jnp.concatenate(parts, axis=1).astype(BF16)


def surround(sz, strip_at, corner_at, cur, own, below, above, pool, pad):
    pool[0 : sz.pieces] = own[...]
    pool[sz.pieces : 2 * sz.pieces] = below[...]
    pool[2 * sz.pieces : 3 * sz.pieces] = above[...]
    for q in range(sz.tiles):
        for i in range(sz.edge):
            for h, part in enumerate(halves(cur[q, i].astype(F32))):
                pad[q * sz.lanes + h, pl.ds((i + REACH) * PITCH + REACH, sz.edge), :] = part
    for q in range(sz.tiles):
        for side in range(4):
            piece = strip_at[q * 4 + side]
            for row in range(REACH):
                window, turned = margin_window(sz.edge, side, row)
                for h, part in enumerate(halves(pool[piece, row].astype(F32))):
                    pad[q * sz.lanes + h, window, :] = flip_rows(part) if turned else part
            piece = corner_at[q * 4 + side]
            for row in range(REACH):
                for h, part in enumerate(halves(pool[piece, row].astype(F32))):
                    for column in range(REACH):
                        at = corner_cell(sz.edge, side, row, column)
                        pad[q * sz.lanes + h, pl.ds(at, 1), :] = part[column : column + 1]


def hold_taps(sz, kern, layer, taps):
    for a in range(TAPS):
        for h, part in enumerate(halves(kern[layer, a])):
            taps[h, pl.ds(a * 8, TAPS), :] = part


def tap(taps, h, a, b):
    return jnp.broadcast_to(taps[h, pl.ds(a * 8 + b, 1), :], (8, LANES))


def convolve(sz, pad, taps, conv):
    @pl.loop(0, sz.slabs)
    def _(slab):
        h = lax.rem(slab, sz.lanes)
        for g in range(sz.edge // 8):
            acc = [None] * sz.edge
            for b in range(TAPS):
                weights = [tap(taps, h, a, b) for a in range(TAPS)]
                for r in range(sz.outer):
                    x = pad[slab, pl.ds(r * PITCH + b + 8 * g, 8), :]
                    for a in range(TAPS):
                        i = r - a
                        if 0 <= i < sz.edge:
                            term = x * weights[a]
                            acc[i] = term if acc[i] is None else acc[i] + term
            for i in range(sz.edge):
                conv[slab, pl.ds(i * sz.edge + 8 * g, 8), :] = acc[i]


def normalise(sz, conv, gain, layer, normal, inverse, normed):
    scale = 1.0 / sz.channels
    for q in range(sz.tiles):

        @pl.loop(0, sz.edge, unroll=2)
        def _(i):
            at = pl.ds(pl.multiple_of(i * sz.edge, sz.edge), sz.edge)
            parts = [conv[q * sz.lanes + h, at, :] for h in range(sz.lanes)]
            mean = jnp.sum(sum(parts[1:], parts[0]), axis=-1, keepdims=True) * scale
            parts = [part - mean for part in parts]
            squares = [part * part for part in parts]
            variance = jnp.sum(sum(squares[1:], squares[0]), axis=-1, keepdims=True) * scale
            root = lax.rsqrt(variance + epsilon)
            inverse[q, at, :] = jnp.broadcast_to(root, (sz.edge, LANES))
            flat_at = pl.ds(pl.multiple_of(q * sz.cells + i * sz.edge, sz.edge), sz.edge)
            for h, part in enumerate(parts):
                part = part * root
                normal[q * sz.lanes + h, at, :] = part
                gains = gain[layer : layer + 1, h * LANES : (h + 1) * LANES]
                normed[flat_at, h * LANES : (h + 1) * LANES] = (part * gains).astype(BF16)


def activate(sz, upward, active, slope):
    width = 512

    @pl.loop(0, sz.rows // 16)
    def _(t):
        at = pl.ds(pl.multiple_of(t * 16, 16), 16)
        for start in range(0, sz.hidden, width):
            u = upward[at, start : start + width]
            chance = 0.5 * (1.0 + lax.erf(u * inverse_root_two))
            active[at, start : start + width] = (u * chance).astype(BF16)
            slope[at, start : start + width] = (
                chance + u * jnp.exp(-0.5 * u * u) * inverse_root_tau
            ).astype(slope.dtype)


def multiply(a, b, ca=1, cb=0):
    return lax.dot_general(a, b, (((ca,), (cb,)), ((), ())), preferred_element_type=F32)


def finish_forward(sz, cur, branch, lscale, layer, out, flat):
    for q in range(sz.tiles):

        @pl.loop(0, sz.edge, unroll=2)
        def _(i):
            at = pl.ds(pl.multiple_of(q * sz.cells + i * sz.edge, sz.edge), sz.edge)
            value = cur[q, i].astype(F32) + branch[at, :] * lscale[layer : layer + 1, :]
            value = value.astype(BF16)
            out[q, i] = value
            if flat is not None:
                local = pl.ds(pl.multiple_of(i * sz.edge, sz.edge), sz.edge)
                for h, part in enumerate(halves(value.astype(F32))):
                    flat[q * sz.lanes + h, local, :] = part


def scale_rows(sz, grad_row, branch, lscale, layer, down_in, sums):
    sums[...] = jnp.zeros_like(sums)
    for q in range(sz.tiles):

        @pl.loop(0, sz.edge, unroll=2)
        def _(i):
            at = pl.ds(pl.multiple_of(q * sz.cells + i * sz.edge, sz.edge), sz.edge)
            g = grad_row(q, i)
            down_in[at, :] = (g * lscale[layer : layer + 1, :]).astype(BF16)
            sums[...] += g * branch[at, :]


def slope_rows(sz, grad_active, slope, up_in):
    @pl.loop(0, sz.rows // 16, unroll=2)
    def _(t):
        at = pl.ds(pl.multiple_of(t * 16, 16), 16)
        up_in[at, :] = (grad_active[at, :] * slope[at, :].astype(F32)).astype(BF16)


def weight_gradients(sz, active, down_in, normed, up_in, weights_out):
    weights_out[0 : sz.hidden, :] = multiply(active[...], down_in[...], 0, 0).astype(BF16)
    for k in range(sz.hidden // sz.channels):
        part = multiply(
            normed[...], up_in[:, k * sz.channels : (k + 1) * sz.channels], 0, 0
        ).astype(BF16)
        start = sz.hidden + k * sz.channels
        weights_out[start : start + sz.channels, :] = part


def norm_gradients(sz, grad_normed, normal, inverse, gain, layer, grad_conv, sums):
    scale = 1.0 / sz.channels
    sums[...] = jnp.zeros_like(sums)
    blank = jnp.zeros((8, LANES), F32)
    for q in range(sz.tiles):

        @pl.loop(0, sz.edge, unroll=2)
        def _(i):
            at = pl.ds(pl.multiple_of(q * sz.cells + i * sz.edge, sz.edge), sz.edge)
            local = pl.ds(pl.multiple_of(i * sz.edge, sz.edge), sz.edge)
            g = halves(grad_normed[at, :])
            n = [normal[q * sz.lanes + h, local, :] for h in range(sz.lanes)]
            sums[...] += jnp.concatenate([a * b for a, b in zip(g, n)], axis=1)
            s = [
                part * gain[layer : layer + 1, h * LANES : (h + 1) * LANES]
                for h, part in enumerate(g)
            ]
            products = [a * b for a, b in zip(s, n)]
            mean = jnp.sum(sum(s[1:], s[0]), axis=-1, keepdims=True) * scale
            slant = jnp.sum(sum(products[1:], products[0]), axis=-1, keepdims=True) * scale
            root = inverse[q, local, :]
            for h in range(sz.lanes):
                slab = q * sz.lanes + h
                base = pl.multiple_of(i * GRAD_PITCH, GRAD_PITCH)
                grad_conv[slab, pl.ds(base, 8), :] = blank
                grad_conv[slab, pl.ds(base + 8, sz.edge), :] = root * (s[h] - mean - n[h] * slant)
                grad_conv[slab, pl.ds(base + 8 + sz.edge, 8), :] = blank


def tap_gradients(sz, pad, grad_conv, tap_sums, small):
    tap_sums[...] = jnp.zeros_like(tap_sums)

    @pl.loop(0, sz.slabs)
    def _(slab):
        h = lax.rem(slab, sz.lanes)
        for b in range(TAPS):
            acc = [None] * TAPS
            for g in range(sz.edge // 8):
                grads = [
                    grad_conv[slab, pl.ds(i * GRAD_PITCH + 8 + 8 * g, 8), :]
                    for i in range(sz.edge)
                ]
                for r in range(sz.outer):
                    x = pad[slab, pl.ds(r * PITCH + b + 8 * g, 8), :]
                    for a in range(TAPS):
                        i = r - a
                        if 0 <= i < sz.edge:
                            term = x * grads[i]
                            acc[a] = term if acc[a] is None else acc[a] + term
            for a in range(TAPS):
                tap_sums[h, a * TAPS + b] += acc[a]

    for h in range(sz.lanes):
        for k in range(TAPS * TAPS):
            row = k // TAPS * 8 + k % TAPS
            small[row : row + 1, h * LANES : (h + 1) * LANES] = jnp.sum(
                tap_sums[h, k], axis=0, keepdims=True
            )


def spread_gradients(sz, grad_conv, taps, grad_pad):
    @pl.loop(0, sz.slabs)
    def _(slab):
        h = lax.rem(slab, sz.lanes)
        for g in range(PITCH // 8):
            acc = [None] * sz.outer
            for b in range(TAPS):
                start = 8 * g - b + 8
                if start >= 8 + sz.edge:
                    continue
                weights = [tap(taps, h, a, b) for a in range(TAPS)]
                for i in range(sz.edge):
                    x = grad_conv[slab, pl.ds(i * GRAD_PITCH + start, 8), :]
                    for a in range(TAPS):
                        term = x * weights[a]
                        acc[i + a] = term if acc[i + a] is None else acc[i + a] + term
            for p in range(sz.outer):
                grad_pad[slab, pl.ds(p * PITCH + 8 * g, 8), :] = acc[p]


def return_margins(sz, strip_at, corner_at, grad_pad, pool):
    pool[...] = jnp.zeros_like(pool)
    for q in range(sz.tiles):
        for side in range(4):
            piece = strip_at[q * 4 + side]
            for row in range(REACH):
                window, turned = margin_window(sz.edge, side, row)
                for h in range(sz.lanes):
                    part = grad_pad[q * sz.lanes + h, window, :]
                    pool[piece, row, h] = flip_rows(part) if turned else part
    for q in range(sz.tiles):
        for side in range(4):
            piece = corner_at[q * 4 + side]
            for row in range(REACH):
                for column in range(REACH):
                    at = corner_cell(sz.edge, side, row, column)
                    for h in range(sz.lanes):
                        pool[piece, row, h, pl.ds(column, 1), :] += grad_pad[
                            q * sz.lanes + h, pl.ds(at, 1), :
                        ]


def send_margins(sz, pool, own, below, above):
    own[...] = pool[0 : sz.pieces]
    for piece in range(sz.pieces):
        for row in range(REACH):
            for offset, ref in ((1, below), (2, above)):
                parts = [pool[offset * sz.pieces + piece, row, h] for h in range(sz.lanes)]
                ref[piece, row] = jnp.concatenate(parts, axis=1).astype(BF16)


def gather_inner(sz, grad_row, grad_pad, base):
    for q in range(sz.tiles):
        for i in range(sz.edge):
            for h, part in enumerate(halves(grad_row(q, i))):
                slab = q * sz.lanes + h
                base[slab, pl.ds(i * sz.edge, sz.edge), :] = (
                    part + grad_pad[slab, pl.ds((i + REACH) * PITCH + REACH, sz.edge), :]
                )


def add_strips(sz, base, own, first, second, flat):
    flat[...] = base[...]
    for q in range(sz.tiles):
        for side in range(4):
            piece = q * 4 + side
            for row in range(REACH):
                window, turned = strip_window(sz.edge, side, row)
                came = first[piece, row].astype(F32) + second[piece, row].astype(F32)
                for h, part in enumerate(halves(came)):
                    part = part + own[piece, row, h]
                    flat[q * sz.lanes + h, window, :] += flip_rows(part) if turned else part


def fill_small(sz, small, gain_sums, scale_sums, weights_out):
    small[TAPS * 8 : TAPS * 8 + 1, :] = jnp.sum(gain_sums[...], axis=0, keepdims=True)
    small[TAPS * 8 + 1 : TAPS * 8 + 2, :] = jnp.sum(scale_sums[...], axis=0, keepdims=True)
    weights_out[2 * sz.hidden : 2 * sz.hidden + SMALL_ROWS, :] = small[...].astype(BF16)


def flat_grad_row(sz, flat):
    def row(q, i):
        at = pl.ds(i * sz.edge, sz.edge)
        parts = [flat[q * sz.lanes + h, at, :] for h in range(sz.lanes)]
        return jnp.concatenate(parts, axis=1)

    return row


def strips_kernel(sz, cur, strips, flat):
    for q in range(sz.tiles):
        for i in range(sz.edge):
            for h, part in enumerate(halves(cur[q, i].astype(F32))):
                flat[q * sz.lanes + h, pl.ds(i * sz.edge, sz.edge), :] = part
    write_strips(sz, flat, strips)


def forward_kernel(
    sz, layer, strip_at, corner_at, cur, own, below, above, kern, gain, lscale, up, down,
    out, strips, pad, normal, inverse, normed, slope, active, branch,
    pool, taps, conv, upward, flat,
):
    hold_taps(sz, kern, layer, taps)
    surround(sz, strip_at, corner_at, cur, own, below, above, pool, pad)
    convolve(sz, pad, taps, conv)
    normalise(sz, conv, gain, layer, normal, inverse, normed)
    upward[...] = multiply(normed[...], up[...])
    activate(sz, upward, active, slope)
    branch[...] = multiply(active[...], down[...])
    finish_forward(sz, cur, branch, lscale, layer, out, flat)
    write_strips(sz, flat, strips)


def backward_steps(
    sz, layer, strip_at, corner_at, grad_row, kern, gain, lscale, up, down,
    pad, normal, inverse, normed, slope, active, branch,
    weights_out, base, grad_own, grad_below, grad_above,
    grad_pool, taps, hidden, up_in, down_in, grad_conv, grad_pad, tap_sums, small,
    gain_sums, scale_sums,
):
    small[...] = jnp.zeros_like(small)
    scale_rows(sz, grad_row, branch, lscale, layer, down_in, scale_sums)
    hidden[...] = multiply(down_in[...], down[...], 1, 1)
    slope_rows(sz, hidden, slope, up_in)
    branch_grad = hidden.at[:, 0 : sz.channels]
    branch_grad[...] = multiply(up_in[...], up[...], 1, 1)
    norm_gradients(sz, branch_grad, normal, inverse, gain, layer, grad_conv, gain_sums)
    weight_gradients(sz, active, down_in, normed, up_in, weights_out)
    spread_gradients(sz, grad_conv, taps, grad_pad)
    return_margins(sz, strip_at, corner_at, grad_pad, grad_pool)
    send_margins(sz, grad_pool, grad_own, grad_below, grad_above)
    gather_inner(sz, grad_row, grad_pad, base)
    tap_gradients(sz, pad, grad_conv, tap_sums, small)
    fill_small(sz, small, gain_sums, scale_sums, weights_out)


def turn_kernel(
    sz, layer, strip_at, corner_at, cur, own, below, above, kern, gain, lscale, up, down, out_grad,
    out, weights_out, base, grad_own, grad_below, grad_above,
    pool, taps, conv, upward, pad, normal, inverse, normed, slope, active, branch,
    *rest,
):
    hold_taps(sz, kern, layer, taps)
    surround(sz, strip_at, corner_at, cur, own, below, above, pool, pad)
    convolve(sz, pad, taps, conv)
    normalise(sz, conv, gain, layer, normal, inverse, normed)
    upward[...] = multiply(normed[...], up[...])
    activate(sz, upward, active, slope)
    branch[...] = multiply(active[...], down[...])
    finish_forward(sz, cur, branch, lscale, layer, out, None)

    def grad_row(q, i):
        return out_grad[q, i].astype(F32)

    backward_steps(
        sz, layer, strip_at, corner_at, grad_row, kern, gain, lscale, up, down,
        pad, normal, inverse, normed, slope, active, branch,
        weights_out, base, grad_own, grad_below, grad_above,
        rest[0], taps, upward, *rest[1:],
    )


def backward_kernel(
    sz, layer, strip_at, corner_at, base_in, own_in, first, second, kern, gain, lscale, up, down,
    pad, normal, inverse, normed, slope, active, branch,
    weights_out, base, grad_own, grad_below, grad_above,
    flat, taps, hidden, grad_pool, *rest,
):
    hold_taps(sz, kern, layer, taps)
    add_strips(sz, base_in, own_in, first, second, flat)
    for q in range(sz.slabs):
        flat[q] = flat[q].astype(BF16).astype(F32)
    grad_row = flat_grad_row(sz, flat)
    backward_steps(
        sz, layer, strip_at, corner_at, grad_row, kern, gain, lscale, up, down,
        pad, normal, inverse, normed, slope, active, branch,
        weights_out, base, grad_own, grad_below, grad_above,
        grad_pool, taps, hidden, *rest,
    )


def last_kernel(sz, base, own, first, second, out, flat):
    add_strips(sz, base, own, first, second, flat)
    row = flat_grad_row(sz, flat)
    for q in range(sz.tiles):
        for i in range(sz.edge):
            out[q, i] = row(q, i).astype(BF16)


def call(body, outs, scratch, scalars, arrays, name):
    specs = [pl.BlockSpec(memory_space=pltpu.SMEM) for _ in scalars]
    values = list(scalars)
    for array in arrays:
        if isinstance(array, tuple):
            array, layer = array
            specs.append(
                pl.BlockSpec((None,) + array.shape[1:], lambda _, layer=layer: (layer, 0, 0))
            )
        else:
            rank = len(array.shape)
            specs.append(pl.BlockSpec(array.shape, lambda _, rank=rank: (0,) * rank))
        values.append(array)
    out_specs = [
        pl.BlockSpec(out.shape, lambda _, rank=len(out.shape): (0,) * rank) for out in outs
    ]
    return pl.pallas_call(
        body,
        grid=(1,),
        in_specs=specs,
        out_specs=out_specs,
        out_shape=outs,
        scratch_shapes=scratch,
        compiler_params=pltpu.CompilerParams(vmem_limit_bytes=48 * 1024 * 1024),
        name=name,
    )(*values)


def pass_on(shard, by):
    length = lax.axis_size("tile")
    return lax.ppermute(shard, "tile", [(i, (i + by) % length) for i in range(length)])


def margin_plan(table, tile_count, columns, device):
    pieces = tile_count * 4
    entries = lax.dynamic_slice_in_dim(table, device * tile_count, tile_count, 0).reshape(
        (pieces, 2)
    )
    source = entries[:, 0]
    source_device = source // tile_count
    local_piece = (source - source_device * tile_count) * 4 + entries[:, 1]
    below_device = (device + columns - 1) % columns
    return jnp.where(
        source_device == device,
        local_piece,
        jnp.where(source_device == below_device, pieces + local_piece, 2 * pieces + local_piece),
    )


def on_device(
    inputs,
    out_grad,
    kernel,
    norm_gain,
    up_weight,
    down_weight,
    layer_scale,
    seam_table,
    corner_table,
):
    tiles, edge, _, channels = inputs.shape
    hidden = up_weight.shape[2]
    sz = Sizes(tiles, edge, channels, hidden)
    columns = lax.axis_size("tile")
    device = lax.axis_index("tile")
    strip_at = margin_plan(seam_table, tiles, columns, device)
    corner_at = margin_plan(corner_table, tiles, columns, device)
    scalars = (strip_at, corner_at)

    def shape(dims, dtype=F32):
        return jax.ShapeDtypeStruct(dims, dtype)

    image = shape(inputs.shape, BF16)
    strips_shape = shape((sz.pieces, REACH, edge, channels), BF16)
    slab_dims = (sz.slabs, sz.cells, LANES)
    pad_dims = (sz.slabs, sz.outer * PITCH, LANES)
    saved = [
        shape(pad_dims),
        shape(slab_dims),
        shape((tiles, sz.cells, LANES)),
        shape((sz.rows, channels), BF16),
        shape((sz.rows, hidden), BF16),
        shape((sz.rows, hidden), BF16),
        shape((sz.rows, channels)),
    ]
    returned = [
        shape((2 * hidden + SMALL_ROWS, channels), BF16),
        shape(slab_dims),
        shape((sz.pieces, REACH, sz.lanes, edge, LANES)),
        strips_shape,
        strips_shape,
    ]
    flat = pltpu.VMEM(slab_dims, F32)
    taps = pltpu.VMEM((sz.lanes, TAPS * 8, LANES), F32)
    pool = pltpu.VMEM((3 * sz.pieces, REACH, edge, channels), BF16)
    wide = pltpu.VMEM((sz.rows, hidden), F32)
    grad_pool = pltpu.VMEM((3 * sz.pieces, REACH, sz.lanes, edge, LANES), F32)
    backward_scratch = [
        grad_pool,
        pltpu.VMEM((sz.rows, hidden), BF16),
        pltpu.VMEM((sz.rows, channels), BF16),
        pltpu.VMEM((sz.slabs, edge * GRAD_PITCH, LANES), F32),
        pltpu.VMEM(pad_dims, F32),
        pltpu.VMEM((sz.lanes, TAPS * TAPS, 8, LANES), F32),
        pltpu.VMEM((SMALL_ROWS, channels), F32),
        pltpu.VMEM((edge, channels), F32),
        pltpu.VMEM((edge, channels), F32),
    ]
    common = (kernel, norm_gain, layer_scale)

    (strips,) = call(
        functools.partial(strips_kernel, sz), [strips_shape], [flat], (), (inputs,), "strips"
    )
    below, above = pass_on(strips, 1), pass_on(strips, -1)
    first = call(
        functools.partial(forward_kernel, sz, 0),
        [image, strips_shape] + saved,
        [pool, taps, flat, wide, flat],
        scalars,
        (inputs, strips, below, above) + common + ((up_weight, 0), (down_weight, 0)),
        "forward",
    )
    middle, strips = first[:2]
    kept = first[2:]
    below, above = pass_on(strips, 1), pass_on(strips, -1)
    result, weights_one, base, grad_own, grad_below, grad_above = call(
        functools.partial(turn_kernel, sz, 1),
        [image] + returned,
        [pool, taps, flat, wide] + [pltpu.VMEM(one.shape, one.dtype) for one in saved]
        + backward_scratch,
        scalars,
        (middle, strips, below, above) + common
        + ((up_weight, 1), (down_weight, 1), out_grad),
        "turn",
    )
    weights_one = lax.psum(weights_one, "tile")
    from_below, from_above = pass_on(grad_above, 1), pass_on(grad_below, -1)
    weights_zero, base, grad_own, grad_below, grad_above = call(
        functools.partial(backward_kernel, sz, 0),
        returned,
        [flat, taps, wide] + backward_scratch,
        scalars,
        (base, grad_own, from_below, from_above) + common
        + ((up_weight, 0), (down_weight, 0)) + tuple(kept),
        "backward",
    )
    weights_zero = lax.psum(weights_zero, "tile")
    from_below, from_above = pass_on(grad_above, 1), pass_on(grad_below, -1)
    (in_grad,) = call(
        functools.partial(last_kernel, sz),
        [image],
        [flat],
        (),
        (base, grad_own, from_below, from_above),
        "last",
    )

    both = [weights_zero, weights_one]
    grad_down = jnp.stack([one[:hidden] for one in both]).astype(F32)
    grad_up = jnp.stack(
        [
            one[hidden : 2 * hidden]
            .reshape((hidden // channels, channels, channels))
            .transpose((1, 0, 2))
            .reshape((channels, hidden))
            for one in both
        ]
    ).astype(F32)
    small = jnp.stack([one[2 * hidden :] for one in both]).astype(F32)
    grad_kernel = small[:, : TAPS * 8].reshape((-1, TAPS, 8, channels))[:, :, :TAPS]
    grad_gain = small[:, TAPS * 8]
    grad_scale = small[:, TAPS * 8 + 1]
    return (result, in_grad, grad_kernel, grad_gain, grad_up, grad_down, grad_scale)


def solution(mesh):
    placed = (
        P(("groups", "tile"), None, None, None),
        P(("groups", "tile"), None, None, None),
        P(),
        P(),
        P(),
        P(),
        P(),
        P(),
        P(),
    )
    return jax.shard_map(
        on_device,
        mesh=mesh,
        in_specs=placed,
        out_specs=(
            P(("groups", "tile"), None, None, None),
            P(("groups", "tile"), None, None, None),
            P("groups", None, None, None),
            P("groups", None),
            P("groups", None, None),
            P("groups", None, None),
            P("groups", None),
        ),
        check_vma=False,
    )
```

profile of v0, /device:TPU:0, one launch (start us, length us, event | category | flops | bytes accessed | tf_op | source)
XLA Modules:
  0.0 200.5 jit_solution(17134584322062213531)
XLA Ops:
  7.2 0.0 copy-start
  7.2 0.0 all-reduce.3.cloned.1.call-start
  7.2 0.0 copy-start.4
  7.2 0.9 copy-done.4
  8.2 0.1 strips.1.own
  8.3 5.5 %collective-permute-start.1 = (bf16[8,3,16,256]{3,2,1,0:T(8,128)(2,1)S(1)}, bf16[8,3,16,256]{3,2,1,0:T(8,128)(2,1)S(1)}, u32[]{:S(2)}, u32[]{:S(2)}) collective-permute-start(bf16[8,3,16,256]{3,2,1,0:T(8,128)(2,1)S(1)} %strips.1.own), channel_id=1, source_target_pairs={{0,15},{1,0},{2,1},{3,2},{4,3},{5,4},{6,5},{7,6},{8,7},{9,8},{10,9... | collective-permute-start | bytes 589832 | tf_op jit(solution)/shard_map/ppermute | solution.py:517
  13.8 0.0 collective-permute-start
  13.8 0.0 copy-done
  13.8 0.1 constant_dynamic-slice_fusion.1
  13.9 0.1 copy.16
  14.0 0.1 reshape.29
  14.0 0.8 constant_dynamic-slice_fusion
  14.8 0.1 copy.17
  14.9 0.1 reshape.30
  15.0 0.9 copy.18.kern
  15.9 1.0 collective-permute-done.1.above
  17.0 4.6 %collective-permute-done.below = bf16[8,3,16,256]{3,2,1,0:T(8,128)(2,1)S(1)} collective-permute-done((bf16[8,3,16,256]{3,2,1,0:T(8,128)(2,1)S(1)}, bf16[8,3,16,256]{3,2,1,0:T(8,128)(2,1)S(1)}, u32[]{:S(2)}, u32[]{:S(2)}) %collective-permute-start) | collective-permute-done | bytes 196640 | tf_op jit(solution)/shard_map/ppermute | solution.py:517
  21.6 0.0 copy-start.1
  21.6 1.2 copy-done.1
  22.8 0.9 copy-done.5
  23.7 0.0 copy-start.9
  23.8 0.7 copy-done.9
  24.4 0.0 copy-start.11
  24.4 0.7 copy-done.11
  25.1 0.0 copy-start.2
  25.1 0.0 copy-start.3
  25.1 0.0 copy-start.8
  25.1 9.9 %forward.1 = (bf16[2,16,16,256]{3,2,1,0:T(8,128)(2,1)S(1)}, bf16[8,3,16,256]{3,2,1,0:T(8,128)(2,1)S(1)}, f32[4,528,128]{2,1,0:T(8,128)}, f32[4,256,128]{2,1,0:T(...) custom-call(s32[8]{0:T(128)S(1)} %get-tuple-element.56.strip_at, ...), custom_call_target="tpu_custom_call" | custom-call | tf_op jit(solution)/shard_map/forward/pallas_call | solution.py:503
  35.1 1.0 copy-done.6
  36.1 1.0 copy-done.7
  37.0 0.0 collective-permute-start.3
  37.0 0.5 collective-permute-start.2
  37.5 2.7 %collective-permute-done.3.above = bf16[8,3,16,256]{3,2,1,0:T(8,128)(2,1)S(1)} collective-permute-done((bf16[8,3,16,256]{3,2,1,0:T(8,128)(2,1)S(1)}, bf16[8,3,16,256]{3,2,1,0:T(8,128)(2,1)S(1)}, u32[]{:S(2)}, u32[]{:S(2)}) %collective-permute-start.3) | collective-permute-done | bytes 196640 | tf_op jit(solution)/shard_map/ppermute | solution.py:517
  40.2 4.6 %collective-permute-done.2.below = bf16[8,3,16,256]{3,2,1,0:T(8,128)(2,1)S(1)} collective-permute-done((bf16[8,3,16,256]{3,2,1,0:T(8,128)(2,1)S(1)}, bf16[8,3,16,256]{3,2,1,0:T(8,128)(2,1)S(1)}, u32[]{:S(2)}, u32[]{:S(2)}) %collective-permute-start.2) | collective-permute-done | bytes 196640 | tf_op jit(solution)/shard_map/ppermute | solution.py:517
  44.8 0.0 copy-done.2
  44.8 0.0 copy-done.3
  44.8 0.0 copy-done.8
  44.8 0.0 copy-done.10
  44.9 19.2 %turn.1 = (bf16[2,16,16,256]{3,2,1,0:T(8,128)(2,1)}, bf16[2112,256]{1,0:T(8,128)(2,1)}, f32[4,256,128]{2,1,0:T(8,128)S(1)}, f32[8,3,2,16,128]{4,3,2,1,0:T(8,128)...) custom-call(s32[8]{0:T(128)S(1)} %get-tuple-element.56.strip_at, ...), custom_call_target="tpu_custom_call" | custom-call | tf_op jit(solution)/shard_map/turn/pallas_call | solution.py:503
  64.1 0.0 collective-permute-start.4
  64.1 4.4 %collective-permute-start.5 = (bf16[8,3,16,256]{3,2,1,0:T(8,128)(2,1)S(1)}, bf16[8,3,16,256]{3,2,1,0:T(8,128)(2,1)S(1)}, u32[]{:S(2)}, u32[]{:S(2)}) collective-permute-start(bf16[8,3,16,256]{3,2,1,0:T(8,128)(2,1)S(1)} %get-tuple-element.33), channel_id=1, source_target_pairs={{0,15},{1,0},{2,1},{3,2},{4,3},{5,4},{6,5},{7,6},{8,7},{9,8},{10,9... | collective-permute-start | bytes 589832 | tf_op jit(solution)/shard_map/ppermute | solution.py:517
  68.5 3.3 %collective-permute-done.4.first = bf16[8,3,16,256]{3,2,1,0:T(8,128)(2,1)S(1)} collective-permute-done((bf16[8,3,16,256]{3,2,1,0:T(8,128)(2,1)S(1)}, bf16[8,3,16,256]{3,2,1,0:T(8,128)(2,1)S(1)}, u32[]{:S(2)}, u32[]{:S(2)}) %collective-permute-start.4) | collective-permute-done | bytes 196640 | tf_op jit(solution)/shard_map/ppermute | solution.py:517
  71.9 0.0 collective-permute-done.5.second
  71.9 13.2 %backward.1 = (bf16[2112,256]{1,0:T(8,128)(2,1)}, f32[4,256,128]{2,1,0:T(8,128)S(1)}, f32[8,3,2,16,128]{4,3,2,1,0:T(8,128)S(1)}, bf16[8,3,16,256]{3,2,1,0:T(8,128)(2,1)S(1)}, bf16[8,3,16,256]{3,2,1,0:T(8,128)(2,1)S(1)}) custom-call(s32[8]{0:T(128)S(1)} %get-tuple-element.56.strip_at, s32[8]{0:T(128)S(1)} %get-tuple-element.55.corner_at, ...), custom_call_target="tpu_custom_call" | custom-call | tf_op jit(solution)/shard_map/backward/pallas_call | solution.py:503
  85.0 0.0 all-reduce.3.cloned.1.call-update
  85.1 0.1 collective-permute-start.6
  85.1 4.7 %collective-permute-start.7 = (bf16[8,3,16,256]{3,2,1,0:T(8,128)(2,1)S(1)}, bf16[8,3,16,256]{3,2,1,0:T(8,128)(2,1)S(1)}, u32[]{:S(2)}, u32[]{:S(2)}) collective-permute-start(bf16[8,3,16,256]{3,2,1,0:T(8,128)(2,1)S(1)} %get-tuple-element.44), channel_id=1, source_target_pairs={{0,15},{1,0},{2,1},{3,2},{4,3},{5,4},{6,5},{7,6},{8,7},{9,8},{10,9... | collective-permute-start | bytes 589832 | tf_op jit(solution)/shard_map/ppermute | solution.py:517
  89.8 3.1 %collective-permute-done.6.first = bf16[8,3,16,256]{3,2,1,0:T(8,128)(2,1)S(1)} collective-permute-done((bf16[8,3,16,256]{3,2,1,0:T(8,128)(2,1)S(1)}, bf16[8,3,16,256]{3,2,1,0:T(8,128)(2,1)S(1)}, u32[]{:S(2)}, u32[]{:S(2)}) %collective-permute-start.6) | collective-permute-done | bytes 196640 | tf_op jit(solution)/shard_map/ppermute | solution.py:517
  92.9 2.3 %collective-permute-done.7.second = bf16[8,3,16,256]{3,2,1,0:T(8,128)(2,1)S(1)} collective-permute-done((bf16[8,3,16,256]{3,2,1,0:T(8,128)(2,1)S(1)}, bf16[8,3,16,256]{3,2,1,0:T(8,128)(2,1)S(1)}, u32[]{:S(2)}, u32[]{:S(2)}) %collective-permute-start.7) | collective-permute-done | bytes 196640 | tf_op jit(solution)/shard_map/ppermute | solution.py:517
  95.2 0.9 last.1
  96.2 88.9 %all-reduce.3.cloned.1.call-done = (bf16[2112,256]{1,0:T(8,128)(2,1)}, bf16[2112,256]{1,0:T(8,128)(2,1)}) async-done(((bf16[2112,256]{1,0:T(8,128)(2,1)}, bf16[2112,256]{1,0:T(8,128)(2,1)}), (bf16[2112,256]{1,0:T(8,128)(2,1)}, bf16[2112,256]{1,0:T(8,128)(2,1)})) %all-reduce.3.cloned.1.call-update) | async-done | bytes 2162704 | tf_op jit(solution)/shard_map/psum | solution.py:622
  185.1 0.9 slice_bitcast_fusion.3
  185.9 1.3 slice_bitcast_fusion
  187.2 0.0 copy-done.12
  187.2 0.1 slice_bitcast_fusion.1
  187.3 0.4 copy.23
  187.7 0.4 stack_reshape.7
  188.1 0.4 copy.22
  188.5 0.4 stack_reshape.6
  188.9 0.6 copy.29
  189.5 0.6 copy.30
  190.1 0.7 copy.26
  190.8 1.5 maximum_convert_fusion
  192.2 1.5 maximum_convert_fusion.1
  (10 shorter events, 0.1 us)
Async XLA Ops:
  7.2 6.6 %copy-start = (s32[32,4,2]{0,2,1:T(2,128)S(1)}, s32[32,4,2]{0,2,1:T(2,128)}, u32[]{:S(2)}) copy-start(s32[32,4,2]{0,2,1:T(2,128)} %param.16) | copy-start | bytes 3076
  7.2 177.9 %all-reduce.3.cloned.1.call-start = ((), (), s32[]{:S(2)}) async-start(), calls=%async_computation | async-start | bytes 4325376 | tf_op jit(solution)/shard_map/psum | solution.py:622
  7.2 1.0 copy-start.4
  8.3 8.7 %collective-permute-start.1 = (bf16[8,3,16,256]{3,2,1,0:T(8,128)(2,1)S(1)}, bf16[8,3,16,256]{3,2,1,0:T(8,128)(2,1)S(1)}, u32[]{:S(2)}, u32[]{:S(2)}) collective-permute-start(bf16[8,3,16,256]{3,2,1,0:T(8,128)(2,1)S(1)} %strips.1.own), channel_id=1, source_target_pairs={{0,15},{1,0},{2,1},{3,2},{4,3},{5,4},{6,5},{7,6},{8,7},{9,8},{10,9... | collective-permute-start | bytes 589832 | tf_op jit(solution)/shard_map/ppermute | solution.py:517
  13.8 7.8 %collective-permute-start = (bf16[8,3,16,256]{3,2,1,0:T(8,128)(2,1)S(1)}, bf16[8,3,16,256]{3,2,1,0:T(8,128)(2,1)S(1)}, u32[]{:S(2)}, u32[]{:S(2)}) collective-permute-start(bf16[8,3,16,256]{3,2,1,0:T(8,128)(2,1)S(1)} %strips.1.own), channel_id=1, source_target_pairs={{0,1},{1,2},{2,3},{3,4},{4,5},{5,6},{6,7},{7,8},{8,9},{9,10},{10,1... | collective-permute-start | bytes 589832 | tf_op jit(solution)/shard_map/ppermute | solution.py:517
  21.6 1.2 copy-start.1
  22.8 0.9 copy-start.5
  23.7 0.7 copy-start.9
  24.4 0.7 copy-start.11
  25.1 19.7 %copy-start.2 = (bf16[2,256,1024]{2,1,0:T(8,128)(2,1)S(1)}, bf16[2,256,1024]{2,1,0:T(8,128)(2,1)}, u32[]{:S(2)}) copy-start(bf16[2,256,1024]{2,1,0:T(8,128)(2,1)} %up.5) | copy-start | bytes 3145732
  25.1 19.7 %copy-start.3 = (bf16[2,1024,256]{2,1,0:T(8,128)(2,1)S(1)}, bf16[2,1024,256]{2,1,0:T(8,128)(2,1)}, u32[]{:S(2)}) copy-start(bf16[2,1024,256]{2,1,0:T(8,128)(2,1)} %down.5) | copy-start | bytes 3145732
  25.1 19.7 %copy-start.8 = (bf16[2,16,16,256]{3,2,1,0:T(8,128)(2,1)S(1)}, bf16[2,16,16,256]{3,2,1,0:T(8,128)(2,1)}, u32[]{:S(2)}) copy-start(bf16[2,16,16,256]{3,2,1,0:T(8,128)(2,1)} %out_grad.1) | copy-start | bytes 786436
  25.1 19.7 %copy-start.10 = (f32[2,256]{1,0:T(2,128)S(1)}, f32[2,256]{1,0:T(2,128)}, u32[]{:S(2)}) copy-start(f32[2,256]{1,0:T(2,128)} %gain.5) | copy-start | bytes 6148
  35.1 1.0 copy-start.6
  36.0 1.0 copy-start.7
  37.0 3.2 %collective-permute-start.3 = (bf16[8,3,16,256]{3,2,1,0:T(8,128)(2,1)S(1)}, bf16[8,3,16,256]{3,2,1,0:T(8,128)(2,1)S(1)}, u32[]{:S(2)}, u32[]{:S(2)}) collective-permute-start(bf16[8,3,16,256]{3,2,1,0:T(8,128)(2,1)S(1)} %get-tuple-element.28.own), channel_id=1, source_target_pairs={{0,15},{1,0},{2,1},{3,2},{4,3},{5,4},{6,5},{7,6},{8,7},{9,8},{10,9... | collective-permute-start | bytes 589832 | tf_op jit(solution)/shard_map/ppermute | solution.py:517
  37.0 7.8 %collective-permute-start.2 = (bf16[8,3,16,256]{3,2,1,0:T(8,128)(2,1)S(1)}, bf16[8,3,16,256]{3,2,1,0:T(8,128)(2,1)S(1)}, u32[]{:S(2)}, u32[]{:S(2)}) collective-permute-start(bf16[8,3,16,256]{3,2,1,0:T(8,128)(2,1)S(1)} %get-tuple-element.28.own), channel_id=1, source_target_pairs={{0,1},{1,2},{2,3},{3,4},{4,5},{5,6},{6,7},{7,8},{8,9},{9,10},{10,1... | collective-permute-start | bytes 589832 | tf_op jit(solution)/shard_map/ppermute | solution.py:517
  64.1 7.8 %collective-permute-start.4 = (bf16[8,3,16,256]{3,2,1,0:T(8,128)(2,1)S(1)}, bf16[8,3,16,256]{3,2,1,0:T(8,128)(2,1)S(1)}, u32[]{:S(2)}, u32[]{:S(2)}) collective-permute-start(bf16[8,3,16,256]{3,2,1,0:T(8,128)(2,1)S(1)} %get-tuple-element.32), channel_id=1, source_target_pairs={{0,1},{1,2},{2,3},{3,4},{4,5},{5,6},{6,7},{7,8},{8,9},{9,10},{10,1... | collective-permute-start | bytes 589832 | tf_op jit(solution)/shard_map/ppermute | solution.py:517
  64.1 7.8 %collective-permute-start.5 = (bf16[8,3,16,256]{3,2,1,0:T(8,128)(2,1)S(1)}, bf16[8,3,16,256]{3,2,1,0:T(8,128)(2,1)S(1)}, u32[]{:S(2)}, u32[]{:S(2)}) collective-permute-start(bf16[8,3,16,256]{3,2,1,0:T(8,128)(2,1)S(1)} %get-tuple-element.33), channel_id=1, source_target_pairs={{0,15},{1,0},{2,1},{3,2},{4,3},{5,4},{6,5},{7,6},{8,7},{9,8},{10,9... | collective-permute-start | bytes 589832 | tf_op jit(solution)/shard_map/ppermute | solution.py:517
  85.1 7.8 %collective-permute-start.6 = (bf16[8,3,16,256]{3,2,1,0:T(8,128)(2,1)S(1)}, bf16[8,3,16,256]{3,2,1,0:T(8,128)(2,1)S(1)}, u32[]{:S(2)}, u32[]{:S(2)}) collective-permute-start(bf16[8,3,16,256]{3,2,1,0:T(8,128)(2,1)S(1)} %get-tuple-element.43), channel_id=1, source_target_pairs={{0,1},{1,2},{2,3},{3,4},{4,5},{5,6},{6,7},{7,8},{8,9},{9,10},{10,1... | collective-permute-start | bytes 589832 | tf_op jit(solution)/shard_map/ppermute | solution.py:517
  85.1 10.1 %collective-permute-start.7 = (bf16[8,3,16,256]{3,2,1,0:T(8,128)(2,1)S(1)}, bf16[8,3,16,256]{3,2,1,0:T(8,128)(2,1)S(1)}, u32[]{:S(2)}, u32[]{:S(2)}) collective-permute-start(bf16[8,3,16,256]{3,2,1,0:T(8,128)(2,1)S(1)} %get-tuple-element.44), channel_id=1, source_target_pairs={{0,15},{1,0},{2,1},{3,2},{4,3},{5,4},{6,5},{7,6},{8,7},{9,8},{10,9... | collective-permute-start | bytes 589832 | tf_op jit(solution)/shard_map/ppermute | solution.py:517
  185.1 2.1 %copy-start.12 = (bf16[2112,256]{1,0:T(8,128)(2,1)S(1)}, bf16[2112,256]{1,0:T(8,128)(2,1)}, u32[]{:S(2)}) copy-start(bf16[2112,256]{1,0:T(8,128)(2,1)} %get-tuple-element.48) | copy-start | bytes 3244036
Sparse Core Ops, SparseCore 0:
  85.2 99.8 all-reduce.2
where the time goes:
time: 201 us
  waiting for transfers between devices  111 us (55%)
  Pallas kernels  43.4 us (22%)
  starting transfers between devices  15.2 us (8%)
  local copies, waits for them, and re-layouts  14.2 us (7%)
  between operations  14.2 us (7%)
  other arithmetic  2.95 us (1%)
    psum x1, waiting for transfers between devices, on_device(): weights_one = lax.psum(weights_one, 'tile')  88.9 us
    pallas_call x5, Pallas kernels, call(): pl.pallas_call(body, grid=(1,), in_specs=specs, out_specs=out_specs, out_...  43.4 us
    ppermute x8, waiting for transfers between devices, pass_on(): lax.ppermute(shard, 'tile', [(i, (i + by) % length) for i in range(length)])  21.7 us
    ppermute x8, starting transfers between devices, pass_on(): lax.ppermute(shard, 'tile', [(i, (i + by) % length) for i in range(length)])  15.2 us
    unnamed x30, local copies, waits for them, and re-layouts  9.23 us
  transfers between devices with their start and end apart: 9, of which 8 were waited for; matrix products, arithmetic and copies ran while one was open for 1% of the time, Pallas kernels for 0%

commit v1 on v0

--- a/solution.py
+++ b/solution.py
@@ -123,8 +123,9 @@
 
 def hold_taps(sz, kern, layer, taps):
     for a in range(TAPS):
-        for h, part in enumerate(halves(kern[layer, a])):
-            taps[h, pl.ds(a * 8, TAPS), :] = part
+        for b in range(TAPS):
+            for h, part in enumerate(halves(kern[a, b, layer : layer + 1])):
+                taps[h, pl.ds(a * 8 + b, 1), :] = part
 
 
 def tap(taps, h, a, b):
@@ -369,10 +370,9 @@
                     flat[q * sz.lanes + h, window, :] += flip_rows(part) if turned else part
 
 
-def fill_small(sz, small, gain_sums, scale_sums, weights_out):
+def fill_small(small, gain_sums, scale_sums):
     small[TAPS * 8 : TAPS * 8 + 1, :] = jnp.sum(gain_sums[...], axis=0, keepdims=True)
     small[TAPS * 8 + 1 : TAPS * 8 + 2, :] = jnp.sum(scale_sums[...], axis=0, keepdims=True)
-    weights_out[2 * sz.hidden : 2 * sz.hidden + SMALL_ROWS, :] = small[...].astype(BF16)
 
 
 def flat_grad_row(sz, flat):
@@ -384,7 +384,23 @@
     return row
 
 
-def strips_kernel(sz, cur, strips, flat):
+class Loads:
+    def __init__(self, pairs, sems):
+        self.copies = [
+            pltpu.make_async_copy(source, target, sems.at[k])
+            for k, (source, target) in enumerate(pairs)
+        ]
+        for copy in self.copies:
+            copy.start()
+
+    def wait(self, *which):
+        for k in which:
+            self.copies[k].wait()
+
+
+def strips_kernel(sz, cur_hbm, strips, flat, cur, sems):
+    loads = Loads([(cur_hbm, cur)], sems)
+    loads.wait(0)
     for q in range(sz.tiles):
         for i in range(sz.edge):
             for h, part in enumerate(halves(cur[q, i].astype(F32))):
@@ -393,128 +409,243 @@
 
 
 def forward_kernel(
-    sz, layer, strip_at, corner_at, cur, own, below, above, kern, gain, lscale, up, down,
+    sz, layer, strip_at, corner_at, cur_hbm, own, below, above,
+    kern_hbm, gain_hbm, lscale_hbm, up_hbm, down_hbm,
     out, strips, pad, normal, inverse, normed, slope, active, branch,
-    pool, taps, conv, upward, flat,
+    pool, taps, conv, upward, flat, cur, kern, gain, lscale, up, down, sems,
 ):
+    loads = Loads(
+        [
+            (cur_hbm, cur), (kern_hbm, kern), (gain_hbm, gain), (lscale_hbm, lscale),
+            (up_hbm.at[layer], up), (down_hbm.at[layer], down),
+        ],
+        sems,
+    )
+    loads.wait(0)
+    surround(sz, strip_at, corner_at, cur, own, below, above, pool, pad)
+    loads.wait(1)
     hold_taps(sz, kern, layer, taps)
-    surround(sz, strip_at, corner_at, cur, own, below, above, pool, pad)
     convolve(sz, pad, taps, conv)
+    loads.wait(2)
     normalise(sz, conv, gain, layer, normal, inverse, normed)
+    loads.wait(4)
     upward[...] = multiply(normed[...], up[...])
     activate(sz, upward, active, slope)
+    loads.wait(5)
     branch[...] = multiply(active[...], down[...])
+    loads.wait(3)
     finish_forward(sz, cur, branch, lscale, layer, out, flat)
     write_strips(sz, flat, strips)
 
 
-def backward_steps(
-    sz, layer, strip_at, corner_at, grad_row, kern, gain, lscale, up, down,
-    pad, normal, inverse, normed, slope, active, branch,
-    weights_out, base, grad_own, grad_below, grad_above,
-    grad_pool, taps, hidden, up_in, down_in, grad_conv, grad_pad, tap_sums, small,
-    gain_sums, scale_sums,
+def turn_kernel(
+    sz, layer, strip_at, corner_at, cur, own, below, above,
+    kern_hbm, gain_hbm, lscale_hbm, up_hbm, down_hbm, out_grad_hbm,
+    out_hbm, base, grad_own, grad_below, grad_above,
+    pad, grad_conv, normed, active, down_in, up_in, gain_sums, scale_sums,
+    pool, taps, conv, upward, kern, gain, lscale, up, down, sems,
+    out_grad, out, normal, inverse, slope, branch, grad_pool, grad_pad, out_sem,
 ):
-    small[...] = jnp.zeros_like(small)
+    loads = Loads(
+        [
+            (kern_hbm, kern), (gain_hbm, gain), (lscale_hbm, lscale),
+            (up_hbm.at[layer], up), (down_hbm.at[layer], down), (out_grad_hbm, out_grad),
+        ],
+        sems,
+    )
+    surround(sz, strip_at, corner_at, cur, own, below, above, pool, pad)
+    loads.wait(0)
+    hold_taps(sz, kern, layer, taps)
+    convolve(sz, pad, taps, conv)
+    loads.wait(1)
+    normalise(sz, conv, gain, layer, normal, inverse, normed)
+    loads.wait(3)
+    upward[...] = multiply(normed[...], up[...])
+    activate(sz, upward, active, slope)
+    loads.wait(4)
+    branch[...] = multiply(active[...], down[...])
+    loads.wait(2, 5)
+    finish_forward(sz, cur, branch, lscale, layer, out, None)
+    store = pltpu.make_async_copy(out, out_hbm, out_sem.at[0])
+    store.start()
+
+    def grad_row(q, i):
+        return out_grad[q, i].astype(F32)
+
     scale_rows(sz, grad_row, branch, lscale, layer, down_in, scale_sums)
-    hidden[...] = multiply(down_in[...], down[...], 1, 1)
-    slope_rows(sz, hidden, slope, up_in)
-    branch_grad = hidden.at[:, 0 : sz.channels]
-    branch_grad[...] = multiply(up_in[...], up[...], 1, 1)
-    norm_gradients(sz, branch_grad, normal, inverse, gain, layer, grad_conv, gain_sums)
-    weight_gradients(sz, active, down_in, normed, up_in, weights_out)
+    upward[...] = multiply(down_in[...], down[...], 1, 1)
+    slope_rows(sz, upward, slope, up_in)
+    branch[...] = multiply(up_in[...], up[...], 1, 1)
+    norm_gradients(sz, branch, normal, inverse, gain, layer, grad_conv, gain_sums)
     spread_gradients(sz, grad_conv, taps, grad_pad)
     return_margins(sz, strip_at, corner_at, grad_pad, grad_pool)
     send_margins(sz, grad_pool, grad_own, grad_below, grad_above)
     gather_inner(sz, grad_row, grad_pad, base)
+    store.wait()
+
+
+def weights_kernel(
+    sz, pad, grad_conv, normed, active, down_in, up_in, gain_sums, scale_sums,
+    weights_out, small, tap_sums,
+):
+    small[...] = jnp.zeros_like(small)
+    weight_gradients(sz, active, down_in, normed, up_in, weights_out)
     tap_gradients(sz, pad, grad_conv, tap_sums, small)
-    fill_small(sz, small, gain_sums, scale_sums, weights_out)
-
-
-def turn_kernel(
-    sz, layer, strip_at, corner_at, cur, own, below, above, kern, gain, lscale, up, down, out_grad,
-    out, weights_out, base, grad_own, grad_below, grad_above,
-    pool, taps, conv, upward, pad, normal, inverse, normed, slope, active, branch,
-    *rest,
+    fill_small(small, gain_sums, scale_sums)
+
+
+def backward_kernel(
+    sz, layer, base, own, first, second, lscale_hbm, down_hbm, normed, slope, active, branch,
+    weights_out, flat, up_in, scale_sums,
+    hidden, down_in, lscale, down, sems,
 ):
+    loads = Loads([(lscale_hbm, lscale), (down_hbm.at[layer], down)], sems)
+    add_strips(sz, base, own, first, second, flat)
+    for slab in range(sz.slabs):
+        flat[slab] = flat[slab].astype(BF16).astype(F32)
+    loads.wait(0)
+    scale_rows(sz, flat_grad_row(sz, flat), branch, lscale, layer, down_in, scale_sums)
+    loads.wait(1)
+    hidden[...] = multiply(down_in[...], down[...], 1, 1)
+    slope_rows(sz, hidden, slope, up_in)
+    weight_gradients(sz, active, down_in, normed, up_in, weights_out)
+
+
+def spread_kernel(
+    sz, layer, strip_at, corner_at, kern_hbm, gain_hbm, up_hbm, flat, up_in, normal, inverse,
+    base, grad_own, grad_below, grad_above, grad_conv, gain_sums,
+    taps, branch, kern, gain, up, sems, grad_pool, grad_pad,
+):
+    loads = Loads([(up_hbm.at[layer], up), (gain_hbm, gain), (kern_hbm, kern)], sems)
+    loads.wait(0)
+    branch[...] = multiply(up_in[...], up[...], 1, 1)
+    loads.wait(1)
+    norm_gradients(sz, branch, normal, inverse, gain, layer, grad_conv, gain_sums)
+    loads.wait(2)
     hold_taps(sz, kern, layer, taps)
-    surround(sz, strip_at, corner_at, cur, own, below, above, pool, pad)
-    convolve(sz, pad, taps, conv)
-    normalise(sz, conv, gain, layer, normal, inverse, normed)
-    upward[...] = multiply(normed[...], up[...])
-    activate(sz, upward, active, slope)
-    branch[...] = multiply(active[...], down[...])
-    finish_forward(sz, cur, branch, lscale, layer, out, None)
-
-    def grad_row(q, i):
-        return out_grad[q, i].astype(F32)
-
-    backward_steps(
-        sz, layer, strip_at, corner_at, grad_row, kern, gain, lscale, up, down,
-        pad, normal, inverse, normed, slope, active, branch,
-        weights_out, base, grad_own, grad_below, grad_above,
-        rest[0], taps, upward, *rest[1:],
-    )
-
-
-def backward_kernel(
-    sz, layer, strip_at, corner_at, base_in, own_in, first, second, kern, gain, lscale, up, down,
-    pad, normal, inverse, normed, slope, active, branch,
-    weights_out, base, grad_own, grad_below, grad_above,
-    flat, taps, hidden, grad_pool, *rest,
-):
-    hold_taps(sz, kern, layer, taps)
-    add_strips(sz, base_in, own_in, first, second, flat)
-    for q in range(sz.slabs):
-        flat[q] = flat[q].astype(BF16).astype(F32)
-    grad_row = flat_grad_row(sz, flat)
-    backward_steps(
-        sz, layer, strip_at, corner_at, grad_row, kern, gain, lscale, up, down,
-        pad, normal, inverse, normed, slope, active, branch,
-        weights_out, base, grad_own, grad_below, grad_above,
-        grad_pool, taps, hidden, *rest,
-    )
-
-
-def last_kernel(sz, base, own, first, second, out, flat):
+    spread_gradients(sz, grad_conv, taps, grad_pad)
+    return_margins(sz, strip_at, corner_at, grad_pad, grad_pool)
+    send_margins(sz, grad_pool, grad_own, grad_below, grad_above)
+    gather_inner(sz, flat_grad_row(sz, flat), grad_pad, base)
+
+
+def taps_kernel(sz, pad, grad_conv, gain_sums, scale_sums, other, both, tap_sums, small):
+    small[...] = jnp.zeros_like(small)
+    tap_gradients(sz, pad, grad_conv, tap_sums, small)
+    fill_small(small, gain_sums, scale_sums)
+    both[0:SMALL_ROWS] = small[...]
+    both[SMALL_ROWS : 2 * SMALL_ROWS] = other[...]
+
+
+def last_kernel(sz, base, own, first, second, out_hbm, flat, out, sems):
     add_strips(sz, base, own, first, second, flat)
     row = flat_grad_row(sz, flat)
     for q in range(sz.tiles):
         for i in range(sz.edge):
             out[q, i] = row(q, i).astype(BF16)
-
-
-def call(body, outs, scratch, scalars, arrays, name):
-    specs = [pl.BlockSpec(memory_space=pltpu.SMEM) for _ in scalars]
-    values = list(scalars)
-    for array in arrays:
-        if isinstance(array, tuple):
-            array, layer = array
-            specs.append(
-                pl.BlockSpec((None,) + array.shape[1:], lambda _, layer=layer: (layer, 0, 0))
-            )
-        else:
-            rank = len(array.shape)
-            specs.append(pl.BlockSpec(array.shape, lambda _, rank=rank: (0,) * rank))
-        values.append(array)
-    out_specs = [
-        pl.BlockSpec(out.shape, lambda _, rank=len(out.shape): (0,) * rank) for out in outs
-    ]
+    store = pltpu.make_async_copy(out, out_hbm, sems.at[0])
+    store.start()
+    store.wait()
+
+
+def sum_rows(pieces, out):
+    devices, rows, _ = pieces.shape
+    for start in range(0, rows, 16):
+        total = pieces[0, start : start + 16].astype(F32)
+        for j in range(1, devices):
+            total = total + pieces[j, start : start + 16].astype(F32)
+        out[start : start + 16] = total.astype(BF16)
+
+
+def sum_kernel(pieces, out):
+    sum_rows(pieces, out)
+
+
+def sum_both_kernel(pieces, small, out, held):
+    rows = pieces.shape[1]
+    sum_rows(pieces, out)
+    total = small[0]
+    for j in range(1, small.shape[0]):
+        total = total + small[j]
+    held[...] = jnp.zeros_like(held)
+    held[0 : small.shape[1]] = total
+    out[rows : rows + 16] = held[...].astype(BF16)
+
+
+def unpack_kernel(
+    sz, small_rows, zero, one, up_hbm, down_hbm, kernel_out, gain_out, scale_out,
+    up, down, small, sems,
+):
+    devices, rows, channels = one.shape
+    copies = []
+    for layer, pieces in ((1, one), (0, zero)):
+        for j in range(devices):
+            value = pieces[j, 0:rows].astype(F32)
+            start = j * rows
+            if start < sz.hidden:
+                down[layer, start : start + rows] = value
+            else:
+                k, c = divmod(start - sz.hidden, channels)
+                up[layer, c : c + rows, k * channels : (k + 1) * channels] = value
+            if start + rows == sz.hidden:
+                copies.append((down.at[layer], down_hbm.at[layer]))
+            elif start + rows == 2 * sz.hidden:
+                copies.append((up.at[layer], up_hbm.at[layer]))
+            else:
+                continue
+            k = len(copies) - 1
+            copies[k] = pltpu.make_async_copy(*copies[k], sems.at[k])
+            copies[k].start()
+    for j in range(devices):
+        value = zero[j, rows : rows + 16].astype(F32)
+        small[j * small_rows : (j + 1) * small_rows] = value[0:small_rows]
+    for layer in range(2):
+        at = layer * SMALL_ROWS
+        for a in range(TAPS):
+            for b in range(TAPS):
+                row = at + a * 8 + b
+                kernel_out[a, b, layer : layer + 1] = small[row : row + 1]
+        at = at + TAPS * 8
+        gain_out[layer : layer + 1] = small[at : at + 1]
+        scale_out[layer : layer + 1] = small[at + 1 : at + 2]
+    for copy in copies:
+        copy.wait()
+
+
+IN_VMEM = pl.BlockSpec(memory_space=pltpu.VMEM)
+IN_SMEM = pl.BlockSpec(memory_space=pltpu.SMEM)
+IN_HBM = pl.BlockSpec(memory_space=pltpu.HBM)
+
+
+def call(body, name, ins, outs, scratch):
     return pl.pallas_call(
         body,
-        grid=(1,),
-        in_specs=specs,
-        out_specs=out_specs,
-        out_shape=outs,
+        in_specs=[spec for spec, _ in ins],
+        out_specs=[spec for spec, _ in outs],
+        out_shape=[out for _, out in outs],
         scratch_shapes=scratch,
-        compiler_params=pltpu.CompilerParams(vmem_limit_bytes=48 * 1024 * 1024),
+        compiler_params=pltpu.CompilerParams(vmem_limit_bytes=24 * 1024 * 1024),
         name=name,
-    )(*values)
+    )(*[array for _, array in ins])
+
+
+def near(*arrays):
+    return [(IN_VMEM, array) for array in arrays]
+
+
+def far(*arrays):
+    return [(IN_HBM, array) for array in arrays]
 
 
 def pass_on(shard, by):
     length = lax.axis_size("tile")
     return lax.ppermute(shard, "tile", [(i, (i + by) % length) for i in range(length)])
+
+
+def to_owners(rows):
+    devices = lax.axis_size("tile")
+    shared = rows.reshape((devices, rows.shape[0] // devices, rows.shape[1]))
+    return lax.all_to_all(shared, "tile", 0, 0)
 
 
 def margin_plan(table, tile_count, columns, device):
@@ -545,118 +676,157 @@
     corner_table,
 ):
     tiles, edge, _, channels = inputs.shape
-    hidden = up_weight.shape[2]
+    layers, _, hidden = up_weight.shape
     sz = Sizes(tiles, edge, channels, hidden)
     columns = lax.axis_size("tile")
     device = lax.axis_index("tile")
     strip_at = margin_plan(seam_table, tiles, columns, device)
     corner_at = margin_plan(corner_table, tiles, columns, device)
-    scalars = (strip_at, corner_at)
-
-    def shape(dims, dtype=F32):
-        return jax.ShapeDtypeStruct(dims, dtype)
-
+    plan = [(IN_SMEM, strip_at), (IN_SMEM, corner_at)]
+    kernel_turned = kernel.transpose((1, 2, 0, 3))
+
+    shape = jax.ShapeDtypeStruct
     image = shape(inputs.shape, BF16)
     strips_shape = shape((sz.pieces, REACH, edge, channels), BF16)
-    slab_dims = (sz.slabs, sz.cells, LANES)
-    pad_dims = (sz.slabs, sz.outer * PITCH, LANES)
-    saved = [
-        shape(pad_dims),
-        shape(slab_dims),
-        shape((tiles, sz.cells, LANES)),
-        shape((sz.rows, channels), BF16),
-        shape((sz.rows, hidden), BF16),
-        shape((sz.rows, hidden), BF16),
-        shape((sz.rows, channels)),
-    ]
-    returned = [
-        shape((2 * hidden + SMALL_ROWS, channels), BF16),
-        shape(slab_dims),
-        shape((sz.pieces, REACH, sz.lanes, edge, LANES)),
-        strips_shape,
-        strips_shape,
-    ]
-    flat = pltpu.VMEM(slab_dims, F32)
-    taps = pltpu.VMEM((sz.lanes, TAPS * 8, LANES), F32)
-    pool = pltpu.VMEM((3 * sz.pieces, REACH, edge, channels), BF16)
-    wide = pltpu.VMEM((sz.rows, hidden), F32)
-    grad_pool = pltpu.VMEM((3 * sz.pieces, REACH, sz.lanes, edge, LANES), F32)
-    backward_scratch = [
-        grad_pool,
-        pltpu.VMEM((sz.rows, hidden), BF16),
-        pltpu.VMEM((sz.rows, channels), BF16),
-        pltpu.VMEM((sz.slabs, edge * GRAD_PITCH, LANES), F32),
-        pltpu.VMEM(pad_dims, F32),
-        pltpu.VMEM((sz.lanes, TAPS * TAPS, 8, LANES), F32),
-        pltpu.VMEM((SMALL_ROWS, channels), F32),
-        pltpu.VMEM((edge, channels), F32),
-        pltpu.VMEM((edge, channels), F32),
-    ]
-    common = (kernel, norm_gain, layer_scale)
+    slabs = shape((sz.slabs, sz.cells, LANES), F32)
+    padded = shape((sz.slabs, sz.outer * PITCH, LANES), F32)
+    inverses = shape((tiles, sz.cells, LANES), F32)
+    narrow_short = shape((sz.rows, channels), BF16)
+    wide_short = shape((sz.rows, hidden), BF16)
+    narrow = shape((sz.rows, channels), F32)
+    wide = shape((sz.rows, hidden), F32)
+    sums = shape((edge, channels), F32)
+    grad_slabs = shape((sz.slabs, edge * GRAD_PITCH, LANES), F32)
+    own_shape = shape((sz.pieces, REACH, sz.lanes, edge, LANES), F32)
+    pool = shape((3 * sz.pieces, REACH, edge, channels), BF16)
+    grad_pool = shape((3 * sz.pieces, REACH, sz.lanes, edge, LANES), F32)
+    taps = shape((sz.lanes, TAPS * 8, LANES), F32)
+    tap_sums = shape((sz.lanes, TAPS * TAPS, 8, LANES), F32)
+    small = shape((SMALL_ROWS, channels), F32)
+    weights_shape = shape((2 * hidden, channels), BF16)
+    held_kernel = shape(kernel_turned.shape, F32)
+    vector = shape(norm_gain.shape, F32)
+    held_up = shape(up_weight.shape[1:], BF16)
+    held_down = shape(down_weight.shape[1:], BF16)
+    held_weights = [held_kernel, vector, vector, held_up, held_down]
+
+    def vmem(*shapes):
+        return [pltpu.VMEM(one.shape, one.dtype) for one in shapes]
+
+    def sems(count):
+        return [pltpu.SemaphoreType.DMA((count,))]
 
     (strips,) = call(
-        functools.partial(strips_kernel, sz), [strips_shape], [flat], (), (inputs,), "strips"
+        functools.partial(strips_kernel, sz),
+        "strips",
+        far(inputs),
+        near(strips_shape),
+        vmem(slabs, image) + sems(1),
     )
     below, above = pass_on(strips, 1), pass_on(strips, -1)
-    first = call(
+    middle, strips, pad_zero, normal, inverse, normed, slope, active, branch = call(
         functools.partial(forward_kernel, sz, 0),
-        [image, strips_shape] + saved,
-        [pool, taps, flat, wide, flat],
-        scalars,
-        (inputs, strips, below, above) + common + ((up_weight, 0), (down_weight, 0)),
         "forward",
-    )
-    middle, strips = first[:2]
-    kept = first[2:]
+        plan
+        + far(inputs)
+        + near(strips, below, above)
+        + far(kernel_turned, norm_gain, layer_scale, up_weight, down_weight),
+        near(
+            image, strips_shape, padded, slabs, inverses,
+            narrow_short, wide_short, wide_short, narrow,
+        ),
+        vmem(pool, taps, slabs, wide, slabs, image, *held_weights) + sems(6),
+    )
     below, above = pass_on(strips, 1), pass_on(strips, -1)
-    result, weights_one, base, grad_own, grad_below, grad_above = call(
+    result, base, grad_own, grad_below, grad_above, *for_weights = call(
         functools.partial(turn_kernel, sz, 1),
-        [image] + returned,
-        [pool, taps, flat, wide] + [pltpu.VMEM(one.shape, one.dtype) for one in saved]
-        + backward_scratch,
-        scalars,
-        (middle, strips, below, above) + common
-        + ((up_weight, 1), (down_weight, 1), out_grad),
         "turn",
-    )
-    weights_one = lax.psum(weights_one, "tile")
+        plan
+        + near(middle, strips, below, above)
+        + far(kernel_turned, norm_gain, layer_scale, up_weight, down_weight, out_grad),
+        far(image)
+        + near(
+            slabs, own_shape, strips_shape, strips_shape,
+            padded, grad_slabs, narrow_short, wide_short, narrow_short, wide_short, sums, sums,
+        ),
+        vmem(pool, taps, slabs, wide, *held_weights)
+        + sems(6)
+        + vmem(image, image, slabs, inverses, wide_short, narrow, grad_pool, padded)
+        + sems(1),
+    )
     from_below, from_above = pass_on(grad_above, 1), pass_on(grad_below, -1)
-    weights_zero, base, grad_own, grad_below, grad_above = call(
+    weights_one, small_one = call(
+        functools.partial(weights_kernel, sz),
+        "weights",
+        near(*for_weights),
+        near(weights_shape, small),
+        vmem(tap_sums),
+    )
+    pieces_one = to_owners(weights_one)
+    weights_zero, flat, up_in, scale_sums = call(
         functools.partial(backward_kernel, sz, 0),
-        returned,
-        [flat, taps, wide] + backward_scratch,
-        scalars,
-        (base, grad_own, from_below, from_above) + common
-        + ((up_weight, 0), (down_weight, 0)) + tuple(kept),
         "backward",
-    )
-    weights_zero = lax.psum(weights_zero, "tile")
+        near(base, grad_own, from_below, from_above)
+        + far(layer_scale, down_weight)
+        + near(normed, slope, active, branch),
+        near(weights_shape, slabs, wide_short, sums),
+        vmem(wide, narrow_short, vector, held_down) + sems(2),
+    )
+    pieces_zero = to_owners(weights_zero)
+    base, grad_own, grad_below, grad_above, grad_conv, gain_sums = call(
+        functools.partial(spread_kernel, sz, 0),
+        "spread",
+        plan + far(kernel_turned, norm_gain, up_weight) + near(flat, up_in, normal, inverse),
+        near(slabs, own_shape, strips_shape, strips_shape, grad_slabs, sums),
+        vmem(taps, narrow, held_kernel, vector, held_up) + sems(3) + vmem(grad_pool, padded),
+    )
     from_below, from_above = pass_on(grad_above, 1), pass_on(grad_below, -1)
+    both_rows = -(-2 * SMALL_ROWS // columns) * columns
+    (small_both,) = call(
+        functools.partial(taps_kernel, sz),
+        "taps",
+        near(pad_zero, grad_conv, gain_sums, scale_sums, small_one),
+        near(shape((both_rows, channels), F32)),
+        vmem(tap_sums, small),
+    )
+    pieces_small = to_owners(small_both)
     (in_grad,) = call(
         functools.partial(last_kernel, sz),
-        [image],
-        [flat],
-        (),
-        (base, grad_own, from_below, from_above),
         "last",
-    )
-
-    both = [weights_zero, weights_one]
-    grad_down = jnp.stack([one[:hidden] for one in both]).astype(F32)
-    grad_up = jnp.stack(
-        [
-            one[hidden : 2 * hidden]
-            .reshape((hidden // channels, channels, channels))
-            .transpose((1, 0, 2))
-            .reshape((channels, hidden))
-            for one in both
-        ]
-    ).astype(F32)
-    small = jnp.stack([one[2 * hidden :] for one in both]).astype(F32)
-    grad_kernel = small[:, : TAPS * 8].reshape((-1, TAPS, 8, channels))[:, :, :TAPS]
-    grad_gain = small[:, TAPS * 8]
-    grad_scale = small[:, TAPS * 8 + 1]
-    return (result, in_grad, grad_kernel, grad_gain, grad_up, grad_down, grad_scale)
+        near(base, grad_own, from_below, from_above),
+        far(image),
+        vmem(slabs, image) + sems(1),
+    )
+    share = 2 * hidden // columns
+    (sum_one,) = call(
+        sum_kernel, "sum_one", near(pieces_one), near(shape((share, channels), BF16)), []
+    )
+    all_one = lax.all_gather(sum_one, "tile")
+    (sum_zero,) = call(
+        sum_both_kernel,
+        "sum_zero",
+        near(pieces_zero, pieces_small),
+        near(shape((share + 16, channels), BF16)),
+        vmem(shape((16, channels), F32)),
+    )
+    all_zero = lax.all_gather(sum_zero, "tile")
+    grad_up, grad_down, grad_kernel, grad_gain, grad_scale = call(
+        functools.partial(unpack_kernel, sz, both_rows // columns),
+        "unpack",
+        near(all_zero, all_one),
+        far(shape(up_weight.shape, F32), shape(down_weight.shape, F32))
+        + near(held_kernel, vector, vector),
+        vmem(
+            shape(up_weight.shape, F32),
+            shape(down_weight.shape, F32),
+            shape((both_rows, channels), F32),
+        )
+        + sems(4),
+    )
+    return (
+        result, in_grad, grad_kernel.transpose((2, 0, 1, 3)),
+        grad_gain, grad_up, grad_down, grad_scale,
+    )
 
 
 def solution(mesh):

time: 201 us -> 221 us (1.100)
  blocking collectives: 0 us -> 40.9 us
  waiting for transfers between devices: 111 us -> 86.1 us
  starting transfers between devices: 15.2 us -> 26.1 us
  local copies, waits for them, and re-layouts: 14.2 us -> 10.3 us
  other arithmetic: 2.95 us -> 0.02 us
    psum x1 -> x0, waiting for transfers between devices: 88.9 us -> none  [on_device(): weights_one = lax.psum(weights_one, 'tile')]
    all_gather x0 -> x2, waiting for transfers between devices: none -> 52 us  [the longest x1 41.6 us: on_device(): all_zero = lax.all_gather(sum_zero, 'tile')]
    all_to_all x0 -> x2, blocking collectives: none -> 40.9 us  [to_owners(): return lax.all_to_all(shared, 'tile', 0, 0)]
    all_to_all x0 -> x1, waiting for transfers between devices: none -> 23.2 us  [to_owners(): return lax.all_to_all(shared, 'tile', 0, 0)]
    ppermute x8, waiting for transfers between devices: 21.7 us -> 10.9 us  [pass_on(): lax.ppermute(shard, 'tile', [(i, (i + by) % length) for i in range(length)])]
    ppermute x8, starting transfers between devices: 15.2 us -> 21.1 us  [pass_on(): lax.ppermute(shard, 'tile', [(i, (i + by) % length) for i in range(length)])]
    all_to_all x0 -> x1, starting transfers between devices: none -> 4.92 us  [to_owners(): return lax.all_to_all(shared, 'tile', 0, 0)]
    another operation x6 -> x0, local copies, waits for them, and re-layouts: 2.93 us -> none  [the longest x2 1.34 us: on_device(): grad_down = jnp.stack([one[:hidden] for one in both]).astype(F32)]
  transfers between devices with their start and end apart: 9 -> 11, of which waited for: 8 -> 8; matrix products, arithmetic and copies ran while one was open for 1% -> 1% of each run, Pallas kernels for 0% -> 2%
where the time goes in v1:
time: 221 us
  waiting for transfers between devices  86.1 us (39%)
  Pallas kernels  43.4 us (20%)
  blocking collectives  40.9 us (19%)
  starting transfers between devices  26.1 us (12%)
  between operations  14.2 us (6%)
  local copies, waits for them, and re-layouts  10.3 us (5%)
    pallas_call x11, Pallas kernels, call(): pl.pallas_call(body, in_specs=[spec for spec, _ in ins], out_specs=[spec...  43.4 us
    all_gather x1, waiting for transfers between devices, on_device(): all_zero = lax.all_gather(sum_zero, 'tile')  41.6 us
    all_to_all x2, blocking collectives, to_owners(): return lax.all_to_all(shared, 'tile', 0, 0)  40.9 us
    all_to_all x1, waiting for transfers between devices, to_owners(): return lax.all_to_all(shared, 'tile', 0, 0)  23.2 us
    ppermute x8, starting transfers between devices, pass_on(): lax.ppermute(shard, 'tile', [(i, (i + by) % length) for i in range(length)])  21.1 us
    ppermute x8, waiting for transfers between devices, pass_on(): lax.ppermute(shard, 'tile', [(i, (i + by) % length) for i in range(length)])  10.9 us
    all_gather x1, waiting for transfers between devices, on_device(): all_one = lax.all_gather(sum_one, 'tile')  10.4 us
    unnamed x26, local copies, waits for them, and re-layouts  9.12 us
  transfers between devices with their start and end apart: 11, of which 8 were waited for; matrix products, arithmetic and copies ran while one was open for 1% of the time, Pallas kernels for 2%

profile of v1, /device:TPU:0, one launch (start us, length us, event | category | flops | bytes accessed | tf_op | source)
XLA Modules:
  0.0 220.9 jit_solution(1141878962305021357)
XLA Ops:
  7.2 0.0 copy-start
  7.2 0.0 copy-start.6
  7.2 0.9 copy-done.6
  8.1 0.1 strips.1.own
  8.3 0.5 collective-permute-start
  8.8 5.1 %collective-permute-start.1 = (bf16[8,3,16,256]{3,2,1,0:T(8,128)(2,1)S(1)}, bf16[8,3,16,256]{3,2,1,0:T(8,128)(2,1)S(1)}, u32[]{:S(2)}, u32[]{:S(2)}) collective-permute-start(bf16[8,3,16,256]{3,2,1,0:T(8,128)(2,1)S(1)} %strips.1.own), channel_id=1, source_target_pairs={{0,15},{1,0},{2,1},{3,2},{4,3},{5,4},{6,5},{7,6},{8,7},{9,8},{10,9... | collective-permute-start | bytes 589832 | tf_op jit(solution)/shard_map/ppermute | solution.py:642
  13.8 0.0 copy-done
  13.8 0.1 constant_dynamic-slice_fusion.1
  13.9 0.1 copy.16
  14.0 0.1 reshape.29
  14.1 0.8 constant_dynamic-slice_fusion
  14.9 0.1 copy.17
  15.0 0.1 reshape.30
  15.1 2.2 collective-permute-done.below
  17.2 0.0 collective-permute-done.1.above
  17.2 0.0 copy-start.1
  17.2 1.2 copy-done.1
  18.5 0.0 copy-start.3
  18.5 1.2 copy-done.3
  19.7 0.0 copy-start.7
  19.7 0.9 copy-done.7
  20.6 0.0 copy-start.9
  20.6 0.9 copy-done.9
  21.5 0.0 copy-start.11
  21.5 0.7 copy-done.11
  22.2 0.0 copy-start.12
  22.2 0.7 copy-done.12
  22.9 8.8 %forward.1 = (bf16[2,16,16,256]{3,2,1,0:T(8,128)(2,1)S(1)}, bf16[8,3,16,256]{3,2,1,0:T(8,128)(2,1)S(1)}, f32[4,528,128]{2,1,0:T(8,128)S(1)}, f32[4,256,128]{2,1,...) custom-call(s32[8]{0:T(128)S(1)} %get-tuple-element.86.strip_at, ...), custom_call_target="tpu_custom_call" | custom-call | tf_op jit(solution)/shard_map/forward/pallas_call | solution.py:621
  31.7 1.4 collective-permute-start.2
  33.1 3.1 %collective-permute-start.3 = (bf16[8,3,16,256]{3,2,1,0:T(8,128)(2,1)S(1)}, bf16[8,3,16,256]{3,2,1,0:T(8,128)(2,1)S(1)}, u32[]{:S(2)}, u32[]{:S(2)}) collective-permute-start(bf16[8,3,16,256]{3,2,1,0:T(8,128)(2,1)S(1)} %get-tuple-element.47.own), channel_id=1, source_target_pairs={{0,15},{1,0},{2,1},{3,2},{4,3},{5,4},{6,5},{7,6},{8,7},{9,8},{10,9... | collective-permute-start | bytes 589832 | tf_op jit(solution)/shard_map/ppermute | solution.py:642
  36.2 3.4 %collective-permute-done.2.below = bf16[8,3,16,256]{3,2,1,0:T(8,128)(2,1)S(1)} collective-permute-done((bf16[8,3,16,256]{3,2,1,0:T(8,128)(2,1)S(1)}, bf16[8,3,16,256]{3,2,1,0:T(8,128)(2,1)S(1)}, u32[]{:S(2)}, u32[]{:S(2)}) %collective-permute-start.2) | collective-permute-done | bytes 196640 | tf_op jit(solution)/shard_map/ppermute | solution.py:642
  39.6 0.0 collective-permute-done.3.above
  39.6 0.0 copy-done.2
  39.6 0.0 copy-done.10
  39.6 15.4 %turn.1 = (bf16[2,16,16,256]{3,2,1,0:T(8,128)(2,1)}, f32[4,256,128]{2,1,0:T(8,128)S(1)}, f32[8,3,2,16,128]{4,3,2,1,0:T(8,128)S(1)}, bf16[8,3,16,256]{3,2,1,0:T(8...) custom-call(s32[8]{0:T(128)S(1)} %get-tuple-element.86.strip_at, ...), custom_call_target="tpu_custom_call" | custom-call | tf_op jit(solution)/shard_map/turn/pallas_call | solution.py:621
  55.0 0.8 collective-permute-start.4
  55.8 3.7 %collective-permute-start.5 = (bf16[8,3,16,256]{3,2,1,0:T(8,128)(2,1)S(1)}, bf16[8,3,16,256]{3,2,1,0:T(8,128)(2,1)S(1)}, u32[]{:S(2)}, u32[]{:S(2)}) collective-permute-start(bf16[8,3,16,256]{3,2,1,0:T(8,128)(2,1)S(1)} %get-tuple-element.52), channel_id=1, source_target_pairs={{0,15},{1,0},{2,1},{3,2},{4,3},{5,4},{6,5},{7,6},{8,7},{9,8},{10,9... | collective-permute-start | bytes 589832 | tf_op jit(solution)/shard_map/ppermute | solution.py:642
  59.5 2.8 %weights.1 = (bf16[2048,256]{1,0:T(8,128)(2,1)S(1)}, f32[64,256]{1,0:T(8,128)S(1)}) custom-call(f32[4,528,128]{2,1,0:T(8,128)S(1)} %get-tuple-element.70.pad, f32[4,512,128]{2,1,0:T(8,128)S(1)} %get-tuple-element.71.grad_conv, bf16[512,256]{1,0:T(8,128)(2,1)S(1)} %get-tuple-element.72.normed, bf16[512,1024]{1,0:T(8,128)(2,1)S(1)} %get-tuple-element.73.active, ...), custom_call_target="tpu_custom_call" | custom-call | tf_op jit(solution)/shard_map/weights/pallas_call | solution.py:621
  62.3 0.7 collective-permute-done.4.first
  63.0 0.0 collective-permute-done.5.second
  63.0 3.0 %backward.1 = (bf16[2048,256]{1,0:T(8,128)(2,1)}, f32[4,256,128]{2,1,0:T(8,128)S(1)}, bf16[512,1024]{1,0:T(8,128)(2,1)S(1)}, f32[16,256]{1,0:T(8,128)S(1)}) custom-call(f32[4,256,128]{2,1,0:T(8,128)S(1)} %get-tuple-element.49.base, f32[8,3,2,16,128]{4,3,2,1,0:T(8,128)S(1)} %get-tuple-element.50.own, ...), custom_call_target="tpu_custom_call" | custom-call | tf_op jit(solution)/shard_map/backward/pallas_call | solution.py:621
  66.0 0.0 copy-done.4
  66.0 6.0 %spread.1 = (f32[4,256,128]{2,1,0:T(8,128)S(1)}, f32[8,3,2,16,128]{4,3,2,1,0:T(8,128)S(1)}, bf16[8,3,16,256]{3,2,1,0:T(8,128)(2,1)S(1)}, bf16[8,3,16,256]{3,2,1,...) custom-call(s32[8]{0:T(128)S(1)} %get-tuple-element.86.strip_at, ...), custom_call_target="tpu_custom_call" | custom-call | tf_op jit(solution)/shard_map/spread/pallas_call | solution.py:621
  72.0 2.1 taps.1
  74.1 13.4 %all_to_all.15.small = f32[16,8,256]{2,1,0:T(8,128)S(1)} all-to-all(f32[16,8,256]{2,1,0:T(8,128)S(1)} %bitcast.59), channel_id=1, replica_groups=mesh['groups'=2,'tile'=16] {'tile'}, dimensions={0} | all-to-all | bytes 262144 | tf_op jit(solution)/shard_map/all_to_all | solution.py:648
  87.5 27.4 %all_to_all.16.pieces = bf16[16,128,256]{2,1,0:T(8,128)(2,1)S(1)} all-to-all(bf16[16,128,256]{2,1,0:T(8,128)(2,1)S(1)} %bitcast.55), channel_id=1, replica_groups=mesh['groups'=2,'tile'=16] {'tile'}, dimensions={0} | all-to-all | bytes 2097152 | tf_op jit(solution)/shard_map/all_to_all | solution.py:648
  114.9 4.9 %all-to-all-start = ((bf16[16,128,256]{2,1,0:T(8,128)(2,1)}), bf16[16,128,256]{2,1,0:T(8,128)(2,1)S(1)}, u32[]{:S(2)}, u32[]{:S(2)}) async-start(bf16[16,128,256]{2,1,0:T(8,128)(2,1)} %bitcast.5), calls=%async_computation | async-start | bytes 2097152 | tf_op jit(solution)/shard_map/all_to_all | solution.py:648
  119.9 0.0 all-gather.7.cloned.1.call-start
  119.9 0.8 sum_one.1
  120.7 0.0 all-gather.7.cloned.1.call-update
  120.7 0.0 all-gather.5.cloned.1.call-start
  120.8 23.2 %all-to-all-done.pieces = bf16[16,128,256]{2,1,0:T(8,128)(2,1)S(1)} async-done(((bf16[16,128,256]{2,1,0:T(8,128)(2,1)}), bf16[16,128,256]{2,1,0:T(8,128)(2,1)S(1)}, u32[]{:S(2)}, u32[]{:S(2)}) %all-to-all-start) | async-done | bytes 1048608 | tf_op jit(solution)/shard_map/all_to_all | solution.py:648
  143.9 0.8 sum_zero.1
  144.7 0.0 all-gather.5.cloned.1.call-update
  144.8 1.2 collective-permute-start.6
  145.9 5.3 %collective-permute-start.7 = (bf16[8,3,16,256]{3,2,1,0:T(8,128)(2,1)S(1)}, bf16[8,3,16,256]{3,2,1,0:T(8,128)(2,1)S(1)}, u32[]{:S(2)}, u32[]{:S(2)}) collective-permute-start(bf16[8,3,16,256]{3,2,1,0:T(8,128)(2,1)S(1)} %get-tuple-element.64), channel_id=1, source_target_pairs={{0,15},{1,0},{2,1},{3,2},{4,3},{5,4},{6,5},{7,6},{8,7},{9,8},{10,9... | collective-permute-start | bytes 589832 | tf_op jit(solution)/shard_map/ppermute | solution.py:642
  151.2 3.4 %collective-permute-done.6.first = bf16[8,3,16,256]{3,2,1,0:T(8,128)(2,1)S(1)} collective-permute-done((bf16[8,3,16,256]{3,2,1,0:T(8,128)(2,1)S(1)}, bf16[8,3,16,256]{3,2,1,0:T(8,128)(2,1)S(1)}, u32[]{:S(2)}, u32[]{:S(2)}) %collective-permute-start.6) | collective-permute-done | bytes 196640 | tf_op jit(solution)/shard_map/ppermute | solution.py:642
  154.6 1.2 collective-permute-done.7.second
  155.8 0.9 last.1
  156.8 10.4 %all-gather.7.cloned.1.call-done = bf16[2048,256]{1,0:T(8,128)(2,1)} async-done(((bf16[128,256]{1,0:T(8,128)(2,1)}), bf16[2048,256]{1,0:T(8,128)(2,1)}) %all-gather.7.cloned.1.call-update) | async-done | bytes 1048592 | tf_op jit(solution)/shard_map/all_gather | solution.py:804
  167.2 41.6 %all-gather.5.cloned.1.call-done = bf16[2304,256]{1,0:T(8,128)(2,1)} async-done(((bf16[144,256]{1,0:T(8,128)(2,1)}), bf16[2304,256]{1,0:T(8,128)(2,1)}) %all-gather.5.cloned.1.call-update) | async-done | bytes 1179664 | tf_op jit(solution)/shard_map/all_gather | solution.py:812
  208.8 1.3 copy-done.5
  210.0 1.2 copy-done.8
  211.3 2.8 %unpack.1 = (f32[2,256,1024]{2,1,0:T(8,128)}, f32[2,1024,256]{2,1,0:T(8,128)}, f32[7,7,2,256]{3,2,1,0:T(2,128)}, f32[2,256]{1,0:T(2,128)}, f32[2,256]{1,0:T(2,128)}) custom-call(bf16[16,144,256]{2,1,0:T(8,128)(2,1)S(1)} %bitcast.53, bf16[16,128,256]{2,1,0:T(8,128)(2,1)S(1)} %bitcast.54), custom_call_target="tpu_custom_call" | custom-call | tf_op jit(solution)/shard_map/unpack/pallas_call | solution.py:621
  (6 shorter events, 0.0 us)
Async XLA Ops:
  7.2 6.7 %copy-start = (s32[32,4,2]{0,2,1:T(2,128)S(1)}, s32[32,4,2]{0,2,1:T(2,128)}, u32[]{:S(2)}) copy-start(s32[32,4,2]{0,2,1:T(2,128)} %param.16) | copy-start | bytes 3076
  7.2 1.0 copy-start.6
  8.3 9.0 %collective-permute-start = (bf16[8,3,16,256]{3,2,1,0:T(8,128)(2,1)S(1)}, bf16[8,3,16,256]{3,2,1,0:T(8,128)(2,1)S(1)}, u32[]{:S(2)}, u32[]{:S(2)}) collective-permute-start(bf16[8,3,16,256]{3,2,1,0:T(8,128)(2,1)S(1)} %strips.1.own), channel_id=1, source_target_pairs={{0,1},{1,2},{2,3},{3,4},{4,5},{5,6},{6,7},{7,8},{8,9},{9,10},{10,1... | collective-permute-start | bytes 589832 | tf_op jit(solution)/shard_map/ppermute | solution.py:642
  8.8 8.5 %collective-permute-start.1 = (bf16[8,3,16,256]{3,2,1,0:T(8,128)(2,1)S(1)}, bf16[8,3,16,256]{3,2,1,0:T(8,128)(2,1)S(1)}, u32[]{:S(2)}, u32[]{:S(2)}) collective-permute-start(bf16[8,3,16,256]{3,2,1,0:T(8,128)(2,1)S(1)} %strips.1.own), channel_id=1, source_target_pairs={{0,15},{1,0},{2,1},{3,2},{4,3},{5,4},{6,5},{7,6},{8,7},{9,8},{10,9... | collective-permute-start | bytes 589832 | tf_op jit(solution)/shard_map/ppermute | solution.py:642
  17.2 1.2 copy-start.1
  18.5 1.2 copy-start.3
  19.7 0.9 copy-start.7
  20.6 0.9 copy-start.9
  21.5 0.7 copy-start.11
  22.2 0.7 copy-start.12
  22.9 16.7 %copy-start.2 = (bf16[2,1024,256]{2,1,0:T(8,128)(2,1)S(1)}, bf16[2,1024,256]{2,1,0:T(8,128)(2,1)}, u32[]{:S(2)}) copy-start(bf16[2,1024,256]{2,1,0:T(8,128)(2,1)} %down_hbm.5) | copy-start | bytes 3145732
  22.9 16.7 %copy-start.10 = (bf16[2,16,16,256]{3,2,1,0:T(8,128)(2,1)S(1)}, bf16[2,16,16,256]{3,2,1,0:T(8,128)(2,1)}, u32[]{:S(2)}) copy-start(bf16[2,16,16,256]{3,2,1,0:T(8,128)(2,1)} %out_grad_hbm.1) | copy-start | bytes 786436
  31.7 8.0 %collective-permute-start.2 = (bf16[8,3,16,256]{3,2,1,0:T(8,128)(2,1)S(1)}, bf16[8,3,16,256]{3,2,1,0:T(8,128)(2,1)S(1)}, u32[]{:S(2)}, u32[]{:S(2)}) collective-permute-start(bf16[8,3,16,256]{3,2,1,0:T(8,128)(2,1)S(1)} %get-tuple-element.47.own), channel_id=1, source_target_pairs={{0,1},{1,2},{2,3},{3,4},{4,5},{5,6},{6,7},{7,8},{8,9},{9,10},{10,1... | collective-permute-start | bytes 589832 | tf_op jit(solution)/shard_map/ppermute | solution.py:642
  33.1 6.5 %collective-permute-start.3 = (bf16[8,3,16,256]{3,2,1,0:T(8,128)(2,1)S(1)}, bf16[8,3,16,256]{3,2,1,0:T(8,128)(2,1)S(1)}, u32[]{:S(2)}, u32[]{:S(2)}) collective-permute-start(bf16[8,3,16,256]{3,2,1,0:T(8,128)(2,1)S(1)} %get-tuple-element.47.own), channel_id=1, source_target_pairs={{0,15},{1,0},{2,1},{3,2},{4,3},{5,4},{6,5},{7,6},{8,7},{9,8},{10,9... | collective-permute-start | bytes 589832 | tf_op jit(solution)/shard_map/ppermute | solution.py:642
  55.0 8.0 %collective-permute-start.4 = (bf16[8,3,16,256]{3,2,1,0:T(8,128)(2,1)S(1)}, bf16[8,3,16,256]{3,2,1,0:T(8,128)(2,1)S(1)}, u32[]{:S(2)}, u32[]{:S(2)}) collective-permute-start(bf16[8,3,16,256]{3,2,1,0:T(8,128)(2,1)S(1)} %get-tuple-element.51), channel_id=1, source_target_pairs={{0,1},{1,2},{2,3},{3,4},{4,5},{5,6},{6,7},{7,8},{8,9},{9,10},{10,1... | collective-permute-start | bytes 589832 | tf_op jit(solution)/shard_map/ppermute | solution.py:642
  55.8 7.2 %collective-permute-start.5 = (bf16[8,3,16,256]{3,2,1,0:T(8,128)(2,1)S(1)}, bf16[8,3,16,256]{3,2,1,0:T(8,128)(2,1)S(1)}, u32[]{:S(2)}, u32[]{:S(2)}) collective-permute-start(bf16[8,3,16,256]{3,2,1,0:T(8,128)(2,1)S(1)} %get-tuple-element.52), channel_id=1, source_target_pairs={{0,15},{1,0},{2,1},{3,2},{4,3},{5,4},{6,5},{7,6},{8,7},{9,8},{10,9... | collective-permute-start | bytes 589832 | tf_op jit(solution)/shard_map/ppermute | solution.py:642
  63.0 3.0 %copy-start.4 = (bf16[2,256,1024]{2,1,0:T(8,128)(2,1)S(1)}, bf16[2,256,1024]{2,1,0:T(8,128)(2,1)}, u32[]{:S(2)}) copy-start(bf16[2,256,1024]{2,1,0:T(8,128)(2,1)} %up_hbm.5) | copy-start | bytes 3145732
  114.9 29.0 %all-to-all-start = ((bf16[16,128,256]{2,1,0:T(8,128)(2,1)}), bf16[16,128,256]{2,1,0:T(8,128)(2,1)S(1)}, u32[]{:S(2)}, u32[]{:S(2)}) async-start(bf16[16,128,256]{2,1,0:T(8,128)(2,1)} %bitcast.5), calls=%async_computation | async-start | bytes 2097152 | tf_op jit(solution)/shard_map/all_to_all | solution.py:648
  119.9 47.3 %all-gather.7.cloned.1.call-start = ((), (), s32[]{:S(2)}) async-start(), calls=%async_computation.4 | async-start | bytes 1114112 | tf_op jit(solution)/shard_map/all_gather | solution.py:804
  120.7 88.0 %all-gather.5.cloned.1.call-start = ((), (), s32[]{:S(2)}) async-start(), calls=%async_computation.3 | async-start | bytes 1253376 | tf_op jit(solution)/shard_map/all_gather | solution.py:812
  144.8 9.9 %collective-permute-start.6 = (bf16[8,3,16,256]{3,2,1,0:T(8,128)(2,1)S(1)}, bf16[8,3,16,256]{3,2,1,0:T(8,128)(2,1)S(1)}, u32[]{:S(2)}, u32[]{:S(2)}) collective-permute-start(bf16[8,3,16,256]{3,2,1,0:T(8,128)(2,1)S(1)} %get-tuple-element.63), channel_id=1, source_target_pairs={{0,1},{1,2},{2,3},{3,4},{4,5},{5,6},{6,7},{7,8},{8,9},{9,10},{10,1... | collective-permute-start | bytes 589832 | tf_op jit(solution)/shard_map/ppermute | solution.py:642
  145.9 9.9 %collective-permute-start.7 = (bf16[8,3,16,256]{3,2,1,0:T(8,128)(2,1)S(1)}, bf16[8,3,16,256]{3,2,1,0:T(8,128)(2,1)S(1)}, u32[]{:S(2)}, u32[]{:S(2)}) collective-permute-start(bf16[8,3,16,256]{3,2,1,0:T(8,128)(2,1)S(1)} %get-tuple-element.64), channel_id=1, source_target_pairs={{0,15},{1,0},{2,1},{3,2},{4,3},{5,4},{6,5},{7,6},{8,7},{9,8},{10,9... | collective-permute-start | bytes 589832 | tf_op jit(solution)/shard_map/ppermute | solution.py:642
  208.8 1.3 copy-start.5
  210.0 1.2 copy-start.8
Sparse Core Ops, SparseCore 0:
  123.4 43.6 all-gather.6
  170.0 38.6 all-gather.4

commit v2 on v1

--- a/solution.py
+++ b/solution.py
@@ -226,14 +226,13 @@
         up_in[at, :] = (grad_active[at, :] * slope[at, :].astype(F32)).astype(BF16)
 
 
-def weight_gradients(sz, active, down_in, normed, up_in, weights_out):
-    weights_out[0 : sz.hidden, :] = multiply(active[...], down_in[...], 0, 0).astype(BF16)
+def weight_gradients(sz, core, active, down_in, normed, up_in, both, keep, send):
+    both[0] = multiply(active[...], down_in[...], 0, 0).astype(BF16)
     for k in range(sz.hidden // sz.channels):
-        part = multiply(
-            normed[...], up_in[:, k * sz.channels : (k + 1) * sz.channels], 0, 0
-        ).astype(BF16)
-        start = sz.hidden + k * sz.channels
-        weights_out[start : start + sz.channels, :] = part
+        part = multiply(normed[...], up_in[:, k * sz.channels : (k + 1) * sz.channels], 0, 0)
+        both[1, k * sz.channels : (k + 1) * sz.channels, :] = part.astype(BF16)
+    keep[...] = both[core]
+    send[...] = both[1 - core]
 
 
 def norm_gradients(sz, grad_normed, normal, inverse, gain, layer, grad_conv, sums):
@@ -384,23 +383,18 @@
     return row
 
 
-class Loads:
-    def __init__(self, pairs, sems):
-        self.copies = [
-            pltpu.make_async_copy(source, target, sems.at[k])
-            for k, (source, target) in enumerate(pairs)
-        ]
-        for copy in self.copies:
-            copy.start()
-
-    def wait(self, *which):
-        for k in which:
-            self.copies[k].wait()
-
-
-def strips_kernel(sz, cur_hbm, strips, flat, cur, sems):
-    loads = Loads([(cur_hbm, cur)], sems)
-    loads.wait(0)
+def fetch_kernel(*refs):
+    count = (len(refs) - 1) // 2
+    copies = [
+        pltpu.make_async_copy(refs[k], refs[count + k], refs[-1].at[k]) for k in range(count)
+    ]
+    for copy in copies:
+        copy.start()
+    for copy in copies:
+        copy.wait()
+
+
+def strips_kernel(sz, cur, strips, flat):
     for q in range(sz.tiles):
         for i in range(sz.edge):
             for h, part in enumerate(halves(cur[q, i].astype(F32))):
@@ -409,62 +403,34 @@
 
 
 def forward_kernel(
-    sz, layer, strip_at, corner_at, cur_hbm, own, below, above,
-    kern_hbm, gain_hbm, lscale_hbm, up_hbm, down_hbm,
+    sz, layer, strip_at, corner_at, cur, own, below, above, kern, gain, lscale, up, down,
     out, strips, pad, normal, inverse, normed, slope, active, branch,
-    pool, taps, conv, upward, flat, cur, kern, gain, lscale, up, down, sems,
+    pool, taps, conv, upward, flat,
 ):
-    loads = Loads(
-        [
-            (cur_hbm, cur), (kern_hbm, kern), (gain_hbm, gain), (lscale_hbm, lscale),
-            (up_hbm.at[layer], up), (down_hbm.at[layer], down),
-        ],
-        sems,
-    )
-    loads.wait(0)
     surround(sz, strip_at, corner_at, cur, own, below, above, pool, pad)
-    loads.wait(1)
     hold_taps(sz, kern, layer, taps)
     convolve(sz, pad, taps, conv)
-    loads.wait(2)
     normalise(sz, conv, gain, layer, normal, inverse, normed)
-    loads.wait(4)
-    upward[...] = multiply(normed[...], up[...])
+    upward[...] = multiply(normed[...], up[layer])
     activate(sz, upward, active, slope)
-    loads.wait(5)
-    branch[...] = multiply(active[...], down[...])
-    loads.wait(3)
+    branch[...] = multiply(active[...], down[layer])
     finish_forward(sz, cur, branch, lscale, layer, out, flat)
     write_strips(sz, flat, strips)
 
 
 def turn_kernel(
-    sz, layer, strip_at, corner_at, cur, own, below, above,
-    kern_hbm, gain_hbm, lscale_hbm, up_hbm, down_hbm, out_grad_hbm,
+    sz, layer, strip_at, corner_at, cur, own, below, above, kern, gain, lscale, up, down, out_grad,
     out_hbm, base, grad_own, grad_below, grad_above,
     pad, grad_conv, normed, active, down_in, up_in, gain_sums, scale_sums,
-    pool, taps, conv, upward, kern, gain, lscale, up, down, sems,
-    out_grad, out, normal, inverse, slope, branch, grad_pool, grad_pad, out_sem,
+    pool, taps, conv, upward, out, normal, inverse, slope, branch, grad_pool, grad_pad, out_sem,
 ):
-    loads = Loads(
-        [
-            (kern_hbm, kern), (gain_hbm, gain), (lscale_hbm, lscale),
-            (up_hbm.at[layer], up), (down_hbm.at[layer], down), (out_grad_hbm, out_grad),
-        ],
-        sems,
-    )
     surround(sz, strip_at, corner_at, cur, own, below, above, pool, pad)
-    loads.wait(0)
     hold_taps(sz, kern, layer, taps)
     convolve(sz, pad, taps, conv)
-    loads.wait(1)
     normalise(sz, conv, gain, layer, normal, inverse, normed)
-    loads.wait(3)
-    upward[...] = multiply(normed[...], up[...])
+    upward[...] = multiply(normed[...], up[layer])
     activate(sz, upward, active, slope)
-    loads.wait(4)
-    branch[...] = multiply(active[...], down[...])
-    loads.wait(2, 5)
+    branch[...] = multiply(active[...], down[layer])
     finish_forward(sz, cur, branch, lscale, layer, out, None)
     store = pltpu.make_async_copy(out, out_hbm, out_sem.at[0])
     store.start()
@@ -473,9 +439,9 @@
         return out_grad[q, i].astype(F32)
 
     scale_rows(sz, grad_row, branch, lscale, layer, down_in, scale_sums)
-    upward[...] = multiply(down_in[...], down[...], 1, 1)
+    upward[...] = multiply(down_in[...], down[layer], 1, 1)
     slope_rows(sz, upward, slope, up_in)
-    branch[...] = multiply(up_in[...], up[...], 1, 1)
+    branch[...] = multiply(up_in[...], up[layer], 1, 1)
     norm_gradients(sz, branch, normal, inverse, gain, layer, grad_conv, gain_sums)
     spread_gradients(sz, grad_conv, taps, grad_pad)
     return_margins(sz, strip_at, corner_at, grad_pad, grad_pool)
@@ -485,43 +451,36 @@
 
 
 def weights_kernel(
-    sz, pad, grad_conv, normed, active, down_in, up_in, gain_sums, scale_sums,
-    weights_out, small, tap_sums,
+    sz, place, pad, grad_conv, normed, active, down_in, up_in, gain_sums, scale_sums,
+    keep, send, small, tap_sums, both,
 ):
     small[...] = jnp.zeros_like(small)
-    weight_gradients(sz, active, down_in, normed, up_in, weights_out)
+    weight_gradients(sz, place[0], active, down_in, normed, up_in, both, keep, send)
     tap_gradients(sz, pad, grad_conv, tap_sums, small)
     fill_small(small, gain_sums, scale_sums)
 
 
 def backward_kernel(
-    sz, layer, base, own, first, second, lscale_hbm, down_hbm, normed, slope, active, branch,
-    weights_out, flat, up_in, scale_sums,
-    hidden, down_in, lscale, down, sems,
+    sz, layer, place, base, own, first, second, lscale, down, normed, slope, active, branch,
+    keep, send, flat, up_in, scale_sums,
+    hidden, down_in, both,
 ):
-    loads = Loads([(lscale_hbm, lscale), (down_hbm.at[layer], down)], sems)
     add_strips(sz, base, own, first, second, flat)
     for slab in range(sz.slabs):
         flat[slab] = flat[slab].astype(BF16).astype(F32)
-    loads.wait(0)
     scale_rows(sz, flat_grad_row(sz, flat), branch, lscale, layer, down_in, scale_sums)
-    loads.wait(1)
-    hidden[...] = multiply(down_in[...], down[...], 1, 1)
+    hidden[...] = multiply(down_in[...], down[layer], 1, 1)
     slope_rows(sz, hidden, slope, up_in)
-    weight_gradients(sz, active, down_in, normed, up_in, weights_out)
+    weight_gradients(sz, place[0], active, down_in, normed, up_in, both, keep, send)
 
 
 def spread_kernel(
-    sz, layer, strip_at, corner_at, kern_hbm, gain_hbm, up_hbm, flat, up_in, normal, inverse,
+    sz, layer, strip_at, corner_at, kern, gain, up, flat, up_in, normal, inverse,
     base, grad_own, grad_below, grad_above, grad_conv, gain_sums,
-    taps, branch, kern, gain, up, sems, grad_pool, grad_pad,
+    taps, branch, grad_pool, grad_pad,
 ):
-    loads = Loads([(up_hbm.at[layer], up), (gain_hbm, gain), (kern_hbm, kern)], sems)
-    loads.wait(0)
-    branch[...] = multiply(up_in[...], up[...], 1, 1)
-    loads.wait(1)
+    branch[...] = multiply(up_in[...], up[layer], 1, 1)
     norm_gradients(sz, branch, normal, inverse, gain, layer, grad_conv, gain_sums)
-    loads.wait(2)
     hold_taps(sz, kern, layer, taps)
     spread_gradients(sz, grad_conv, taps, grad_pad)
     return_margins(sz, strip_at, corner_at, grad_pad, grad_pool)
@@ -533,8 +492,8 @@
     small[...] = jnp.zeros_like(small)
     tap_gradients(sz, pad, grad_conv, tap_sums, small)
     fill_small(small, gain_sums, scale_sums)
-    both[0:SMALL_ROWS] = small[...]
-    both[SMALL_ROWS : 2 * SMALL_ROWS] = other[...]
+    both[0:SMALL_ROWS] = small[...].astype(BF16)
+    both[SMALL_ROWS : 2 * SMALL_ROWS] = other[...].astype(BF16)
 
 
 def last_kernel(sz, base, own, first, second, out_hbm, flat, out, sems):
@@ -548,66 +507,63 @@
     store.wait()
 
 
-def sum_rows(pieces, out):
-    devices, rows, _ = pieces.shape
-    for start in range(0, rows, 16):
-        total = pieces[0, start : start + 16].astype(F32)
-        for j in range(1, devices):
-            total = total + pieces[j, start : start + 16].astype(F32)
-        out[start : start + 16] = total.astype(BF16)
-
-
-def sum_kernel(pieces, out):
-    sum_rows(pieces, out)
-
-
-def sum_both_kernel(pieces, small, out, held):
-    rows = pieces.shape[1]
-    sum_rows(pieces, out)
-    total = small[0]
-    for j in range(1, small.shape[0]):
-        total = total + small[j]
-    held[...] = jnp.zeros_like(held)
-    held[0 : small.shape[1]] = total
-    out[rows : rows + 16] = held[...].astype(BF16)
+def add_rows(out, parts):
+    for start in range(0, out.shape[0], 16):
+        rows = slice(start, start + 16)
+        values = [part(rows).astype(F32) for part in parts]
+        out[rows] = sum(values[1:], values[0]).astype(BF16)
+
+
+def share_kernel(digit, *refs):
+    place, refs = refs[0], refs[1:]
+    count = refs[0].shape[0]
+    arrays, outs = refs[:-count], refs[-count:]
+    for k, out in enumerate(outs):
+        piece = place[digit] ^ k
+        add_rows(out, [lambda rows, array=array: array[piece, rows] for array in arrays])
+
+
+def total_kernel(*refs):
+    add_rows(refs[-1], [lambda rows, array=array: array[rows] for array in refs[:-1]])
+
+
+def order_kernel(digit, place, *refs):
+    for k, piece in enumerate(refs[:-1]):
+        refs[-1][place[digit] ^ k] = piece[...]
 
 
 def unpack_kernel(
-    sz, small_rows, zero, one, up_hbm, down_hbm, kernel_out, gain_out, scale_out,
-    up, down, small, sems,
+    sz, place, mine_zero, theirs_zero, mine_one, theirs_one, small,
+    up_hbm, down_hbm, kernel_out, gain_out, scale_out, up, down, sems,
 ):
-    devices, rows, channels = one.shape
+    even = place[0] == 0
     copies = []
-    for layer, pieces in ((1, one), (0, zero)):
-        for j in range(devices):
-            value = pieces[j, 0:rows].astype(F32)
-            start = j * rows
-            if start < sz.hidden:
-                down[layer, start : start + rows] = value
-            else:
-                k, c = divmod(start - sz.hidden, channels)
-                up[layer, c : c + rows, k * channels : (k + 1) * channels] = value
-            if start + rows == sz.hidden:
-                copies.append((down.at[layer], down_hbm.at[layer]))
-            elif start + rows == 2 * sz.hidden:
-                copies.append((up.at[layer], up_hbm.at[layer]))
-            else:
-                continue
-            k = len(copies) - 1
+    step = 32
+    for layer, mine, theirs in ((1, mine_one, theirs_one), (0, mine_zero, theirs_zero)):
+        for start in range(0, sz.hidden, step):
+            rows = slice(start, start + step)
+            down[layer, rows] = jnp.where(even, mine[rows], theirs[rows]).astype(F32)
+        copies.append((down.at[layer], down_hbm.at[layer]))
+        for start in range(0, sz.hidden, step):
+            rows = slice(start, start + step)
+            k, c = divmod(start, sz.channels)
+            up[layer, c : c + step, k * sz.channels : (k + 1) * sz.channels] = jnp.where(
+                even, theirs[rows], mine[rows]
+            ).astype(F32)
+        copies.append((up.at[layer], up_hbm.at[layer]))
+        for k in range(len(copies) - 2, len(copies)):
             copies[k] = pltpu.make_async_copy(*copies[k], sems.at[k])
             copies[k].start()
-    for j in range(devices):
-        value = zero[j, rows : rows + 16].astype(F32)
-        small[j * small_rows : (j + 1) * small_rows] = value[0:small_rows]
     for layer in range(2):
         at = layer * SMALL_ROWS
         for a in range(TAPS):
+            part = small[at + a * 8 - a % 2 * 8 : at + a * 8 - a % 2 * 8 + 16].astype(F32)
+            part = part[a % 2 * 8 : a % 2 * 8 + 8]
             for b in range(TAPS):
-                row = at + a * 8 + b
-                kernel_out[a, b, layer : layer + 1] = small[row : row + 1]
-        at = at + TAPS * 8
-        gain_out[layer : layer + 1] = small[at : at + 1]
-        scale_out[layer : layer + 1] = small[at + 1 : at + 2]
+                kernel_out[a, b, layer : layer + 1] = part[b : b + 1]
+        last = small[at + SMALL_ROWS - 16 : at + SMALL_ROWS].astype(F32)
+        gain_out[layer : layer + 1] = last[8:9]
+        scale_out[layer : layer + 1] = last[9:10]
     for copy in copies:
         copy.wait()
 
@@ -617,7 +573,7 @@
 IN_HBM = pl.BlockSpec(memory_space=pltpu.HBM)
 
 
-def call(body, name, ins, outs, scratch):
+def call(body, name, micros, ins, outs, scratch):
     return pl.pallas_call(
         body,
         in_specs=[spec for spec, _ in ins],
@@ -625,6 +581,9 @@
         out_shape=[out for _, out in outs],
         scratch_shapes=scratch,
         compiler_params=pltpu.CompilerParams(vmem_limit_bytes=24 * 1024 * 1024),
+        cost_estimate=pl.CostEstimate(
+            flops=0, bytes_accessed=int(micros * 3.5e6), transcendentals=0
+        ),
         name=name,
     )(*[array for _, array in ins])
 
@@ -642,10 +601,72 @@
     return lax.ppermute(shard, "tile", [(i, (i + by) % length) for i in range(length)])
 
 
-def to_owners(rows):
-    devices = lax.axis_size("tile")
-    shared = rows.reshape((devices, rows.shape[0] // devices, rows.shape[1]))
-    return lax.all_to_all(shared, "tile", 0, 0)
+def partners(array, masks):
+    length = lax.axis_size("tile")
+    return [
+        lax.ppermute(array, "tile", [(i, i ^ mask) for i in range(length)]) for mask in masks
+    ]
+
+
+def swap(arrays, masks):
+    length = lax.axis_size("tile")
+    return [
+        lax.ppermute(array, "tile", [(i, i ^ mask) for i in range(length)])
+        for array, mask in zip(arrays, masks)
+    ]
+
+
+class Reduction:
+    def __init__(self, place, devices):
+        self.place = [(IN_SMEM, place)]
+        self.rest = devices // 8
+        self.near_masks = [2 * k for k in range(1, 4)]
+        self.rest_masks = [8 * k for k in range(1, self.rest)]
+
+    def scatter(self, keep, send):
+        rows, channels = keep.shape
+        (came,) = swap([send], [1])
+        quarter = rows // 4
+        parts = (4, quarter, channels)
+        shape = jax.ShapeDtypeStruct((quarter, channels), BF16)
+        pieces = call(
+            functools.partial(share_kernel, 1), "share_near", 0.7,
+            self.place + near(keep.reshape(parts), came.reshape(parts)), near(*[shape] * 4), [],
+        )
+        arrived = swap(pieces[1:], self.near_masks)
+        parts = (self.rest, quarter // self.rest, channels)
+        shape = jax.ShapeDtypeStruct(parts[1:], BF16)
+        arrays = [piece.reshape(parts) for piece in [pieces[0]] + arrived]
+        pieces = call(
+            functools.partial(share_kernel, 2), "share_far", 0.5,
+            self.place + near(*arrays), near(*[shape] * self.rest), [],
+        )
+        arrived = swap(pieces[1:], self.rest_masks)
+        (total,) = call(
+            total_kernel, "total", 0.3, near(pieces[0], *arrived), near(shape), []
+        )
+        return total
+
+    def gather(self, total):
+        rows, channels = total.shape
+        for digit, masks, name in ((2, self.rest_masks, "order_far"), (1, self.near_masks, "order_near")):
+            pieces = [total] + partners(total, masks)
+            shape = jax.ShapeDtypeStruct((len(pieces),) + total.shape, BF16)
+            (total,) = call(
+                functools.partial(order_kernel, digit), name, 0.3,
+                self.place + near(*pieces), near(shape), [],
+            )
+            total = total.reshape((-1, channels))
+        return total, partners(total, [1])[0]
+
+    def whole(self, array):
+        for masks in ([1], self.near_masks, self.rest_masks):
+            shape = jax.ShapeDtypeStruct(array.shape, BF16)
+            (array,) = call(
+                total_kernel, "total_small", 0.3,
+                near(array, *partners(array, masks)), near(shape), [],
+            )
+        return array
 
 
 def margin_plan(table, tile_count, columns, device):
@@ -685,6 +706,10 @@
     plan = [(IN_SMEM, strip_at), (IN_SMEM, corner_at)]
     kernel_turned = kernel.transpose((1, 2, 0, 3))
 
+    place = jnp.stack([device % 2, device // 2 % 4, device // 8]).astype(jnp.int32)
+    where = [(IN_SMEM, place)]
+    reduction = Reduction(place, columns)
+
     shape = jax.ShapeDtypeStruct
     image = shape(inputs.shape, BF16)
     strips_shape = shape((sz.pieces, REACH, edge, channels), BF16)
@@ -703,12 +728,8 @@
     taps = shape((sz.lanes, TAPS * 8, LANES), F32)
     tap_sums = shape((sz.lanes, TAPS * TAPS, 8, LANES), F32)
     small = shape((SMALL_ROWS, channels), F32)
-    weights_shape = shape((2 * hidden, channels), BF16)
-    held_kernel = shape(kernel_turned.shape, F32)
-    vector = shape(norm_gain.shape, F32)
-    held_up = shape(up_weight.shape[1:], BF16)
-    held_down = shape(down_weight.shape[1:], BF16)
-    held_weights = [held_kernel, vector, vector, held_up, held_down]
+    half = shape((hidden, channels), BF16)
+    two_halves = shape((2, hidden, channels), BF16)
 
     def vmem(*shapes):
         return [pltpu.VMEM(one.shape, one.dtype) for one in shapes]
@@ -718,110 +739,100 @@
 
     (strips,) = call(
         functools.partial(strips_kernel, sz),
-        "strips",
-        far(inputs),
+        "strips", 0.3,
+        near(inputs),
         near(strips_shape),
-        vmem(slabs, image) + sems(1),
+        vmem(slabs),
     )
     below, above = pass_on(strips, 1), pass_on(strips, -1)
+    fetched = (inputs, out_grad, kernel_turned, norm_gain, layer_scale, up_weight, down_weight)
+    inputs, out_grad, kern, gain, lscale, up, down = call(
+        fetch_kernel,
+        "fetch", 2.0,
+        far(*fetched),
+        near(*[shape(one.shape, one.dtype) for one in fetched]),
+        sems(len(fetched)),
+    )
     middle, strips, pad_zero, normal, inverse, normed, slope, active, branch = call(
         functools.partial(forward_kernel, sz, 0),
-        "forward",
-        plan
-        + far(inputs)
-        + near(strips, below, above)
-        + far(kernel_turned, norm_gain, layer_scale, up_weight, down_weight),
+        "forward", 8.7,
+        plan + near(inputs, strips, below, above, kern, gain, lscale, up, down),
         near(
             image, strips_shape, padded, slabs, inverses,
             narrow_short, wide_short, wide_short, narrow,
         ),
-        vmem(pool, taps, slabs, wide, slabs, image, *held_weights) + sems(6),
+        vmem(pool, taps, slabs, wide, slabs),
     )
     below, above = pass_on(strips, 1), pass_on(strips, -1)
     result, base, grad_own, grad_below, grad_above, *for_weights = call(
         functools.partial(turn_kernel, sz, 1),
-        "turn",
-        plan
-        + near(middle, strips, below, above)
-        + far(kernel_turned, norm_gain, layer_scale, up_weight, down_weight, out_grad),
+        "turn", 15.4,
+        plan + near(middle, strips, below, above, kern, gain, lscale, up, down, out_grad),
         far(image)
         + near(
             slabs, own_shape, strips_shape, strips_shape,
             padded, grad_slabs, narrow_short, wide_short, narrow_short, wide_short, sums, sums,
         ),
-        vmem(pool, taps, slabs, wide, *held_weights)
-        + sems(6)
-        + vmem(image, image, slabs, inverses, wide_short, narrow, grad_pool, padded)
+        vmem(
+            pool, taps, slabs, wide, image, slabs, inverses, wide_short, narrow, grad_pool, padded
+        )
         + sems(1),
     )
     from_below, from_above = pass_on(grad_above, 1), pass_on(grad_below, -1)
-    weights_one, small_one = call(
+    keep_one, send_one, small_one = call(
         functools.partial(weights_kernel, sz),
-        "weights",
-        near(*for_weights),
-        near(weights_shape, small),
-        vmem(tap_sums),
-    )
-    pieces_one = to_owners(weights_one)
-    weights_zero, flat, up_in, scale_sums = call(
+        "weights", 2.8,
+        where + near(*for_weights),
+        near(half, half, small),
+        vmem(tap_sums, two_halves),
+    )
+    sum_one = reduction.scatter(keep_one, send_one)
+    keep_zero, send_zero, flat, up_in, scale_sums = call(
         functools.partial(backward_kernel, sz, 0),
-        "backward",
-        near(base, grad_own, from_below, from_above)
-        + far(layer_scale, down_weight)
-        + near(normed, slope, active, branch),
-        near(weights_shape, slabs, wide_short, sums),
-        vmem(wide, narrow_short, vector, held_down) + sems(2),
-    )
-    pieces_zero = to_owners(weights_zero)
+        "backward", 2.9,
+        where
+        + near(
+            base, grad_own, from_below, from_above, lscale, down, normed, slope, active, branch
+        ),
+        near(half, half, slabs, wide_short, sums),
+        vmem(wide, narrow_short, two_halves),
+    )
+    sum_zero = reduction.scatter(keep_zero, send_zero)
     base, grad_own, grad_below, grad_above, grad_conv, gain_sums = call(
         functools.partial(spread_kernel, sz, 0),
-        "spread",
-        plan + far(kernel_turned, norm_gain, up_weight) + near(flat, up_in, normal, inverse),
+        "spread", 6.0,
+        plan + near(kern, gain, up, flat, up_in, normal, inverse),
         near(slabs, own_shape, strips_shape, strips_shape, grad_slabs, sums),
-        vmem(taps, narrow, held_kernel, vector, held_up) + sems(3) + vmem(grad_pool, padded),
+        vmem(taps, narrow, grad_pool, padded),
     )
     from_below, from_above = pass_on(grad_above, 1), pass_on(grad_below, -1)
-    both_rows = -(-2 * SMALL_ROWS // columns) * columns
     (small_both,) = call(
         functools.partial(taps_kernel, sz),
-        "taps",
+        "taps", 2.1,
         near(pad_zero, grad_conv, gain_sums, scale_sums, small_one),
-        near(shape((both_rows, channels), F32)),
+        near(shape((2 * SMALL_ROWS, channels), BF16)),
         vmem(tap_sums, small),
     )
-    pieces_small = to_owners(small_both)
     (in_grad,) = call(
         functools.partial(last_kernel, sz),
-        "last",
+        "last", 1.0,
         near(base, grad_own, from_below, from_above),
         far(image),
         vmem(slabs, image) + sems(1),
     )
-    share = 2 * hidden // columns
-    (sum_one,) = call(
-        sum_kernel, "sum_one", near(pieces_one), near(shape((share, channels), BF16)), []
-    )
-    all_one = lax.all_gather(sum_one, "tile")
-    (sum_zero,) = call(
-        sum_both_kernel,
-        "sum_zero",
-        near(pieces_zero, pieces_small),
-        near(shape((share + 16, channels), BF16)),
-        vmem(shape((16, channels), F32)),
-    )
-    all_zero = lax.all_gather(sum_zero, "tile")
     grad_up, grad_down, grad_kernel, grad_gain, grad_scale = call(
-        functools.partial(unpack_kernel, sz, both_rows // columns),
-        "unpack",
-        near(all_zero, all_one),
+        functools.partial(unpack_kernel, sz),
+        "unpack", 2.7,
+        where
+        + near(
+            *reduction.gather(sum_zero), *reduction.gather(sum_one), reduction.whole(small_both)
+        ),
         far(shape(up_weight.shape, F32), shape(down_weight.shape, F32))
-        + near(held_kernel, vector, vector),
-        vmem(
-            shape(up_weight.shape, F32),
-            shape(down_weight.shape, F32),
-            shape((both_rows, channels), F32),
-        )
-        + sems(4),
+        + near(
+            shape(kernel_turned.shape, F32), shape(norm_gain.shape, F32),
+            shape(norm_gain.shape, F32),
+        ),
+        vmem(shape(up_weight.shape, F32), shape(down_weight.shape, F32)) + sems(4),
     )
     return (
         result, in_grad, grad_kernel.transpose((2, 0, 1, 3)),

time: 221 us -> 144 us (0.65)
  waiting for transfers between devices: 86.1 us -> 32.4 us
  blocking collectives: 40.9 us -> 0 us
  starting transfers between devices: 26.1 us -> 41.4 us
  between operations: 14.2 us -> 1.17 us
  local copies, waits for them, and re-layouts: 10.3 us -> 20.2 us
  Pallas kernels: 43.4 us -> 48.5 us
    all_gather x2 -> x0, waiting for transfers between devices: 52 us -> none  [the longest x1 41.6 us: on_device(): all_zero = lax.all_gather(sum_zero, 'tile')]
    all_to_all x2 -> x0, blocking collectives: 40.9 us -> none  [to_owners(): return lax.all_to_all(shared, 'tile', 0, 0)]
    ppermute x0 -> x25, waiting for transfers between devices: none -> 28.8 us  [the longest x15 21.1 us: partners(): lax.ppermute(array, 'tile', [(i, i ^ mask) for i in range(length)])]
    ppermute x0 -> x25, starting transfers between devices: none -> 24.5 us  [the longest x15 13.7 us: partners(): lax.ppermute(array, 'tile', [(i, i ^ mask) for i in range(length)])]
    all_to_all x1 -> x0, waiting for transfers between devices: 23.2 us -> none  [to_owners(): return lax.all_to_all(shared, 'tile', 0, 0)]
    unnamed x26 -> x58, local copies, waits for them, and re-layouts: 9.12 us -> 19 us
    ppermute x8, waiting for transfers between devices: 10.9 us -> 3.58 us  [pass_on(): lax.ppermute(shard, 'tile', [(i, (i + by) % length) for i in range(length)])]
    pallas_call x11 -> x23, Pallas kernels: 43.4 us -> 48.5 us  [call(): pl.pallas_call(body, in_specs=[spec for spec, _ in ins], out_specs=[spec...]
  transfers between devices with their start and end apart: 11 -> 33, of which waited for: 8 -> 13; matrix products, arithmetic and copies ran while one was open for 1% -> 1% of each run, Pallas kernels for 2% -> 14%
where the time goes in v2:
time: 144 us
  Pallas kernels  48.5 us (34%)
  starting transfers between devices  41.4 us (29%)
  waiting for transfers between devices  32.4 us (22%)
  local copies, waits for them, and re-layouts  20.2 us (14%)
    pallas_call x23, Pallas kernels, call(): pl.pallas_call(body, in_specs=[spec for spec, _ in ins], out_specs=[spec...  48.5 us
    ppermute x15, waiting for transfers between devices, partners(): lax.ppermute(array, 'tile', [(i, i ^ mask) for i in range(length)])  21.1 us
    unnamed x58, local copies, waits for them, and re-layouts  19 us
    ppermute x8, starting transfers between devices, pass_on(): lax.ppermute(shard, 'tile', [(i, (i + by) % length) for i in range(length)])  17 us
    ppermute x15, starting transfers between devices, partners(): lax.ppermute(array, 'tile', [(i, i ^ mask) for i in range(length)])  13.7 us
    ppermute x10, starting transfers between devices, swap(): lax.ppermute(array, 'tile', [(i, i ^ mask) for i in range(length)])  10.8 us
    ppermute x10, waiting for transfers between devices, swap(): lax.ppermute(array, 'tile', [(i, i ^ mask) for i in range(length)])  7.69 us
    ppermute x8, waiting for transfers between devices, pass_on(): lax.ppermute(shard, 'tile', [(i, (i + by) % length) for i in range(length)])  3.58 us
  transfers between devices with their start and end apart: 33, of which 13 were waited for; matrix products, arithmetic and copies ran while one was open for 1% of the time, Pallas kernels for 14%

profile of v2, /device:TPU:0, one launch (start us, length us, event | category | flops | bytes accessed | tf_op | source)
XLA Modules:
  0.0 143.8 jit_solution(6117375647470832775)
XLA Ops:
  0.7 0.9 copy-done.5
  2.2 5.1 %collective-permute-start.1 = (bf16[8,3,16,256]{3,2,1,0:T(8,128)(2,1)S(1)}, bf16[8,3,16,256]{3,2,1,0:T(8,128)(2,1)S(1)}, u32[]{:S(2)}, u32[]{:S(2)}) collective-permute-start(bf16[8,3,16,256]{3,2,1,0:T(8,128)(2,1)S(1)} %strips.1.own), channel_id=1, source_target_pairs={{0,15},{1,0},{2,1},{3,2},{4,3},{5,4},{6,5},{7,6},{8,7},{9,8},{10,9... | collective-permute-start | bytes 589832 | tf_op jit(solution)/shard_map/ppermute | solution.py:601
  7.5 0.8 constant_dynamic-slice_fusion
  8.5 0.9 copy-done.6
  9.4 1.2 copy-done.7
  10.7 1.2 copy-done.8
  11.9 0.9 copy-done.13
  12.8 0.9 copy-done.26
  13.7 0.7 copy-done.27
  14.4 0.7 copy-done.28
  15.5 0.7 copy-done.18
  16.2 0.7 copy-done.22
  16.9 0.7 copy-done.24
  17.6 0.9 copy-done.23
  18.5 0.9 copy-done.25
  19.4 9.2 %forward.1 = (bf16[2,16,16,256]{3,2,1,0:T(8,128)(2,1)S(1)}, bf16[8,3,16,256]{3,2,1,0:T(8,128)(2,1)}, f32[4,528,128]{2,1,0:T(8,128)S(1)}, f32[4,256,128]{2,1,0:T(...) custom-call(s32[8]{0:T(128)S(1)} %get-tuple-element.128.strip_at, ...), custom_call_target="tpu_custom_call" | custom-call | bytes 30450000 | tf_op jit(solution)/shard_map/forward/pallas_call | solution.py:577
  28.6 1.0 copy-done.1
  29.6 1.0 copy-done.3
  30.6 0.8 copy-done.9
  31.4 0.8 copy-done.11
  32.2 0.7 copy-done.14
  32.9 0.7 copy-done.16
  33.6 0.7 copy-done.20
  34.3 4.4 %collective-permute-start.3 = (bf16[8,3,16,256]{3,2,1,0:T(8,128)(2,1)}, bf16[8,3,16,256]{3,2,1,0:T(8,128)(2,1)}, u32[]{:S(2)}, u32[]{:S(2)}) collective-permute-start(bf16[8,3,16,256]{3,2,1,0:T(8,128)(2,1)} %get-tuple-element.74.own), channel_id=1, source_target_pairs={{0,15},{1,0},{2,1},{3,2},{4,3},{5,4},{6,5},{7,6},{8,7},{9,8},{10,9... | collective-permute-start | bytes 589832 | tf_op jit(solution)/shard_map/ppermute | solution.py:601
  38.7 3.6 %collective-permute-done.2.below = bf16[8,3,16,256]{3,2,1,0:T(8,128)(2,1)S(1)} collective-permute-done((bf16[8,3,16,256]{3,2,1,0:T(8,128)(2,1)}, bf16[8,3,16,256]{3,2,1,0:T(8,128)(2,1)S(1)}, u32[]{:S(2)}, u32[]{:S(2)}) %collective-permute-start.2) | collective-permute-done | bytes 196640 | tf_op jit(solution)/shard_map/ppermute | solution.py:601
  42.3 0.9 copy-done.19
  43.2 0.9 copy-done.21
  44.2 15.8 %turn.1 = (bf16[2,16,16,256]{3,2,1,0:T(8,128)(2,1)}, f32[4,256,128]{2,1,0:T(8,128)S(1)}, f32[8,3,2,16,128]{4,3,2,1,0:T(8,128)S(1)}, bf16[8,3,16,256]{3,2,1,0:T(8...) custom-call(s32[8]{0:T(128)S(1)} %get-tuple-element.128.strip_at, ...), custom_call_target="tpu_custom_call" | custom-call | bytes 53900000 | tf_op jit(solution)/shard_map/turn/pallas_call | solution.py:577
  60.0 4.8 %collective-permute-start.5 = (bf16[8,3,16,256]{3,2,1,0:T(8,128)(2,1)S(1)}, bf16[8,3,16,256]{3,2,1,0:T(8,128)(2,1)S(1)}, u32[]{:S(2)}, u32[]{:S(2)}) collective-permute-start(bf16[8,3,16,256]{3,2,1,0:T(8,128)(2,1)S(1)} %get-tuple-element.80), channel_id=1, source_target_pairs={{0,15},{1,0},{2,1},{3,2},{4,3},{5,4},{6,5},{7,6},{8,7},{9,8},{10,9... | collective-permute-start | bytes 589832 | tf_op jit(solution)/shard_map/ppermute | solution.py:601
  64.9 3.4 %weights.1 = (bf16[1024,256]{1,0:T(8,128)(2,1)S(1)}, bf16[1024,256]{1,0:T(8,128)(2,1)S(1)}, f32[64,256]{1,0:T(8,128)S(1)}) custom-call(s32[3]{0:T(128)S(1)} %pad_add_fusion.place.refs_0_, f32[4,528,128]{2,1,0:T(8,128)S(1)} %get-tuple-element.101.pad, f32[4,512,128]{2,1,0:T(8,128)S(1)} %get-tuple-element.102.grad_conv, ...), custom_call_target="tpu_custom_call" | custom-call | bytes 9800000 | tf_op jit(solution)/shard_map/weights/pallas_call | solution.py:577
  68.5 2.6 %backward.1 = (bf16[1024,256]{1,0:T(8,128)(2,1)S(1)}, bf16[1024,256]{1,0:T(8,128)(2,1)S(1)}, f32[4,256,128]{2,1,0:T(8,128)S(1)}, bf16[512,1024]{1,0:T(8,128)(2,1)S(1)}, f32[16,256]{1,0:T(8,128)S(1)}) custom-call(s32[3]{0:T(128)S(1)} %pad_add_fusion.place.refs_0_, f32[4,256,128]{2,1,0:T(8,128)S(1)} %get-tuple-element.77.base, ...), custom_call_target="tpu_custom_call" | custom-call | bytes 10150000 | tf_op jit(solution)/shard_map/backward/pallas_call | solution.py:577
  71.6 0.7 share_near.3
  72.4 3.4 %collective-permute-start.21 = (bf16[256,256]{1,0:T(8,128)(2,1)S(1)}, bf16[256,256]{1,0:T(8,128)(2,1)S(1)}, u32[]{:S(2)}, u32[]{:S(2)}) collective-permute-start(bf16[256,256]{1,0:T(8,128)(2,1)S(1)} %get-tuple-element.114), channel_id=1, source_target_pairs={{0,6},{1,7},{2,4},{3,5},{4,2},{5,3},{6,0},{7,1},{8,14},{9,15},{10,... | collective-permute-start | bytes 393224 | tf_op jit(solution)/shard_map/ppermute | solution.py:614
  75.8 0.7 share_near.2
  77.1 0.7 collective-permute-done.19
  77.8 2.2 %collective-permute-start.11 = (bf16[256,256]{1,0:T(8,128)(2,1)S(1)}, bf16[256,256]{1,0:T(8,128)(2,1)S(1)}, u32[]{:S(2)}, u32[]{:S(2)}) collective-permute-start(bf16[256,256]{1,0:T(8,128)(2,1)S(1)} %get-tuple-element.98), channel_id=1, source_target_pairs={{0,6},{1,7},{2,4},{3,5},{4,2},{5,3},{6,0},{7,1},{8,14},{9,15},{10,... | collective-permute-start | bytes 393224 | tf_op jit(solution)/shard_map/ppermute | solution.py:614
  80.1 2.9 %collective-permute-done.21 = bf16[256,256]{1,0:T(8,128)(2,1)S(1)} collective-permute-done((bf16[256,256]{1,0:T(8,128)(2,1)S(1)}, bf16[256,256]{1,0:T(8,128)(2,1)S(1)}, u32[]{:S(2)}, u32[]{:S(2)}) %collective-permute-start.21) | collective-permute-done | bytes 131104 | tf_op jit(solution)/shard_map/ppermute | solution.py:614
  83.0 0.6 share_far.3
  83.6 2.0 %collective-permute-start.22 = (bf16[128,256]{1,0:T(8,128)(2,1)S(1)}, bf16[128,256]{1,0:T(8,128)(2,1)S(1)}, u32[]{:S(2)}, u32[]{:S(2)}) collective-permute-start(bf16[128,256]{1,0:T(8,128)(2,1)S(1)} %get-tuple-element.116), channel_id=1, source_target_pairs={{0,8},{1,9},{2,10},{3,11},{4,12},{5,13},{6,14},{7,15},{8,0},{9,1},... | collective-permute-start | bytes 196616 | tf_op jit(solution)/shard_map/ppermute | solution.py:614
  85.6 4.1 %collective-permute-done.22.refs_1_ = bf16[128,256]{1,0:T(8,128)(2,1)S(1)} collective-permute-done((bf16[128,256]{1,0:T(8,128)(2,1)S(1)}, bf16[128,256]{1,0:T(8,128)(2,1)S(1)}, u32[]{:S(2)}, u32[]{:S(2)}) %collective-permute-start.22) | collective-permute-done | bytes 65568 | tf_op jit(solution)/shard_map/ppermute | solution.py:614
  89.7 1.3 collective-permute-start.23
  90.9 0.6 share_far.2
  91.5 1.8 %collective-permute-start.12 = (bf16[128,256]{1,0:T(8,128)(2,1)S(1)}, bf16[128,256]{1,0:T(8,128)(2,1)S(1)}, u32[]{:S(2)}, u32[]{:S(2)}) collective-permute-start(bf16[128,256]{1,0:T(8,128)(2,1)S(1)} %get-tuple-element.100), channel_id=1, source_target_pairs={{0,8},{1,9},{2,10},{3,11},{4,12},{5,13},{6,14},{7,15},{8,0},{9,1},... | collective-permute-start | bytes 196616 | tf_op jit(solution)/shard_map/ppermute | solution.py:614
  93.3 2.3 %collective-permute-done.23.refs_1_ = bf16[128,256]{1,0:T(8,128)(2,1)S(1)} collective-permute-done((bf16[128,256]{1,0:T(8,128)(2,1)S(1)}, bf16[128,256]{1,0:T(8,128)(2,1)S(1)}, u32[]{:S(2)}, u32[]{:S(2)}) %collective-permute-start.23) | collective-permute-done | bytes 65568 | tf_op jit(solution)/shard_map/ppermute | solution.py:607
  96.2 1.1 collective-permute-start.24
  97.4 1.6 %collective-permute-start.13 = (bf16[128,256]{1,0:T(8,128)(2,1)S(1)}, bf16[128,256]{1,0:T(8,128)(2,1)S(1)}, u32[]{:S(2)}, u32[]{:S(2)}) collective-permute-start(bf16[128,256]{1,0:T(8,128)(2,1)S(1)} %total.2.refs_0_), channel_id=1, source_target_pairs={{0,8},{1,9},{2,10},{3,11},{4,12},{5,13},{6,14},{7,15},{8,0},{9,1},... | collective-permute-start | bytes 196616 | tf_op jit(solution)/shard_map/ppermute | solution.py:607
  99.0 2.3 %collective-permute-start.25 = (bf16[256,256]{1,0:T(8,128)(2,1)S(1)}, bf16[256,256]{1,0:T(8,128)(2,1)S(1)}, u32[]{:S(2)}, u32[]{:S(2)}) collective-permute-start(bf16[256,256]{1,0:T(8,128)(2,1)S(1)} %bitcast.76), channel_id=1, source_target_pairs={{0,4},{1,5},{2,6},{3,7},{4,0},{5,1},{6,2},{7,3},{8,12},{9,13},{10,... | collective-permute-start | bytes 393224 | tf_op jit(solution)/shard_map/ppermute | solution.py:607
  101.3 1.4 collective-permute-done.13.refs_1_
  103.3 1.1 collective-permute-start.14
  104.3 2.1 %collective-permute-start.15 = (bf16[256,256]{1,0:T(8,128)(2,1)S(1)}, bf16[256,256]{1,0:T(8,128)(2,1)S(1)}, u32[]{:S(2)}, u32[]{:S(2)}) collective-permute-start(bf16[256,256]{1,0:T(8,128)(2,1)S(1)} %bitcast.80), channel_id=1, source_target_pairs={{0,4},{1,5},{2,6},{3,7},{4,0},{5,1},{6,2},{7,3},{8,12},{9,13},{10,... | collective-permute-start | bytes 393224 | tf_op jit(solution)/shard_map/ppermute | solution.py:607
  106.8 2.0 %collective-permute-done.26.refs_3_ = bf16[256,256]{1,0:T(8,128)(2,1)S(1)} collective-permute-done((bf16[256,256]{1,0:T(8,128)(2,1)S(1)}, bf16[256,256]{1,0:T(8,128)(2,1)S(1)}, u32[]{:S(2)}, u32[]{:S(2)}) %collective-permute-start.26) | collective-permute-done | bytes 131104 | tf_op jit(solution)/shard_map/ppermute | solution.py:607
  109.5 1.1 collective-permute-done.14.refs_1_
  110.6 1.6 %collective-permute-done.16.refs_3_ = bf16[256,256]{1,0:T(8,128)(2,1)S(1)} collective-permute-done((bf16[256,256]{1,0:T(8,128)(2,1)S(1)}, bf16[256,256]{1,0:T(8,128)(2,1)S(1)}, u32[]{:S(2)}, u32[]{:S(2)}) %collective-permute-start.16) | collective-permute-done | bytes 131104 | tf_op jit(solution)/shard_map/ppermute | solution.py:607
  112.9 5.8 %spread.1 = (f32[4,256,128]{2,1,0:T(8,128)S(1)}, f32[8,3,2,16,128]{4,3,2,1,0:T(8,128)S(1)}, bf16[8,3,16,256]{3,2,1,0:T(8,128)(2,1)S(1)}, bf16[8,3,16,256]{3,2,1,...) custom-call(s32[8]{0:T(128)S(1)} %get-tuple-element.128.strip_at, ...), custom_call_target="tpu_custom_call" | custom-call | bytes 21000000 | tf_op jit(solution)/shard_map/spread/pallas_call | solution.py:577
  118.8 2.1 %taps.1.refs_0_ = bf16[128,256]{1,0:T(8,128)(2,1)S(1)} custom-call(f32[4,528,128]{2,1,0:T(8,128)S(1)} %get-tuple-element.117.pad, f32[4,512,128]{2,1,0:T(8,128)S(1)} %get-tuple-element.118.grad_conv, f32[16,256]{1,0:T(8,128)S(1)} %get-tuple-element.119.gain_sums, f32[16,256]{1,0:T(8,128)S(1)} %get-tuple-element.120.scale_sums, ...), custom_call_target="tpu_custom_call" | custom-call | bytes 7350000 | tf_op jit(solution)/shard_map/taps/pallas_call | solution.py:577
  121.4 0.9 collective-permute-done.28.refs_1_
  122.8 1.6 %collective-permute-start.30 = (bf16[128,256]{1,0:T(8,128)(2,1)S(1)}, bf16[128,256]{1,0:T(8,128)(2,1)S(1)}, u32[]{:S(2)}, u32[]{:S(2)}) collective-permute-start(bf16[128,256]{1,0:T(8,128)(2,1)S(1)} %total_small.3.refs_0_), channel_id=1, source_target_pairs={{0,4},{1,5},{2,6},{3,7},{4,0},{5,1},{6,2},{7,3},{8,12},{9,13},{10,... | collective-permute-start | bytes 196616 | tf_op jit(solution)/shard_map/ppermute | solution.py:607
  124.4 2.3 %collective-permute-done.29.refs_1_ = bf16[128,256]{1,0:T(8,128)(2,1)S(1)} collective-permute-done((bf16[128,256]{1,0:T(8,128)(2,1)S(1)}, bf16[128,256]{1,0:T(8,128)(2,1)S(1)}, u32[]{:S(2)}, u32[]{:S(2)}) %collective-permute-start.29) | collective-permute-done | bytes 65568 | tf_op jit(solution)/shard_map/ppermute | solution.py:607
  126.7 2.1 %collective-permute-start.7 = (bf16[8,3,16,256]{3,2,1,0:T(8,128)(2,1)S(1)}, bf16[8,3,16,256]{3,2,1,0:T(8,128)(2,1)S(1)}, u32[]{:S(2)}, u32[]{:S(2)}) collective-permute-start(bf16[8,3,16,256]{3,2,1,0:T(8,128)(2,1)S(1)} %get-tuple-element.92), channel_id=1, source_target_pairs={{0,15},{1,0},{2,1},{3,2},{4,3},{5,4},{6,5},{7,6},{8,7},{9,8},{10,9... | collective-permute-start | bytes 589832 | tf_op jit(solution)/shard_map/ppermute | solution.py:601
  128.8 5.2 %collective-permute-done.31.refs_3_ = bf16[128,256]{1,0:T(8,128)(2,1)S(1)} collective-permute-done((bf16[128,256]{1,0:T(8,128)(2,1)S(1)}, bf16[128,256]{1,0:T(8,128)(2,1)S(1)}, u32[]{:S(2)}, u32[]{:S(2)}) %collective-permute-start.31) | collective-permute-done | bytes 65568 | tf_op jit(solution)/shard_map/ppermute | solution.py:607
  134.1 1.1 collective-permute-start.32
  135.2 4.2 %collective-permute-done.32.refs_1_ = bf16[128,256]{1,0:T(8,128)(2,1)S(1)} collective-permute-done((bf16[128,256]{1,0:T(8,128)(2,1)S(1)}, bf16[128,256]{1,0:T(8,128)(2,1)S(1)}, u32[]{:S(2)}, u32[]{:S(2)}) %collective-permute-start.32) | collective-permute-done | bytes 65568 | tf_op jit(solution)/shard_map/ppermute | solution.py:607
  139.4 0.9 last.1
  140.3 3.3 %unpack.1 = (f32[2,256,1024]{2,1,0:T(8,128)}, f32[2,1024,256]{2,1,0:T(8,128)}, f32[7,7,2,256]{3,2,1,0:T(2,128)}, f32[2,256]{1,0:T(2,128)}, f32[2,256]{1,0:T(2,128)}) custom-call(s32[3]{0:T(128)S(1)} %pad_add_fusion.place.refs_0_, bf16[1024,256]{1,0:T(8,128)(2,1)S(1)} %bitcast.70, bf16[1024,256]{1,0:T(8,128)(2,1)S(1)} %collective-permute-done.17.theirs_zero, ...), custom_call_target="tpu_custom_call" | custom-call | bytes 9450000 | tf_op jit(solution)/shard_map/unpack/pallas_call | solution.py:577
  (91 shorter events, 7.1 us)
Async XLA Ops:
  0.6 6.6 %copy-start = (s32[32,4,2]{0,2,1:T(2,128)S(1)}, s32[32,4,2]{0,2,1:T(2,128)}, u32[]{:S(2)}) copy-start(s32[32,4,2]{0,2,1:T(2,128)} %param.16) | copy-start | bytes 3076
  0.6 1.0 copy-start.5
  1.7 14.5 %collective-permute-start = (bf16[8,3,16,256]{3,2,1,0:T(8,128)(2,1)S(1)}, bf16[8,3,16,256]{3,2,1,0:T(8,128)(2,1)S(1)}, u32[]{:S(2)}, u32[]{:S(2)}) collective-permute-start(bf16[8,3,16,256]{3,2,1,0:T(8,128)(2,1)S(1)} %strips.1.own), channel_id=1, source_target_pairs={{0,1},{1,2},{2,3},{3,4},{4,5},{5,6},{6,7},{7,8},{8,9},{9,10},{10,1... | collective-permute-start | bytes 589832 | tf_op jit(solution)/shard_map/ppermute | solution.py:601
  2.2 14.7 %collective-permute-start.1 = (bf16[8,3,16,256]{3,2,1,0:T(8,128)(2,1)S(1)}, bf16[8,3,16,256]{3,2,1,0:T(8,128)(2,1)S(1)}, u32[]{:S(2)}, u32[]{:S(2)}) collective-permute-start(bf16[8,3,16,256]{3,2,1,0:T(8,128)(2,1)S(1)} %strips.1.own), channel_id=1, source_target_pairs={{0,15},{1,0},{2,1},{3,2},{4,3},{5,4},{6,5},{7,6},{8,7},{9,8},{10,9... | collective-permute-start | bytes 589832 | tf_op jit(solution)/shard_map/ppermute | solution.py:601
  8.5 1.0 copy-start.6
  9.4 1.2 copy-start.7
  10.7 1.2 copy-start.8
  11.9 0.9 copy-start.13
  12.8 0.9 copy-start.26
  13.7 0.7 copy-start.27
  14.4 0.7 copy-start.28
  15.5 0.7 copy-start.18
  16.2 0.7 copy-start.22
  16.9 0.7 copy-start.24
  17.6 0.9 copy-start.23
  18.5 0.9 copy-start.25
  28.6 1.0 copy-start.1
  29.6 1.0 copy-start.3
  30.6 0.8 copy-start.9
  31.4 0.8 copy-start.11
  32.2 0.7 copy-start.14
  32.9 0.7 copy-start.16
  33.6 0.7 copy-start.20
  34.3 8.0 %collective-permute-start.2 = (bf16[8,3,16,256]{3,2,1,0:T(8,128)(2,1)}, bf16[8,3,16,256]{3,2,1,0:T(8,128)(2,1)S(1)}, u32[]{:S(2)}, u32[]{:S(2)}) collective-permute-start(bf16[8,3,16,256]{3,2,1,0:T(8,128)(2,1)} %get-tuple-element.74.own), channel_id=1, source_target_pairs={{0,1},{1,2},{2,3},{3,4},{4,5},{5,6},{6,7},{7,8},{8,9},{9,10},{10,1... | collective-permute-start | bytes 589832 | tf_op jit(solution)/shard_map/ppermute | solution.py:601
  34.3 8.0 %collective-permute-start.3 = (bf16[8,3,16,256]{3,2,1,0:T(8,128)(2,1)}, bf16[8,3,16,256]{3,2,1,0:T(8,128)(2,1)}, u32[]{:S(2)}, u32[]{:S(2)}) collective-permute-start(bf16[8,3,16,256]{3,2,1,0:T(8,128)(2,1)} %get-tuple-element.74.own), channel_id=1, source_target_pairs={{0,15},{1,0},{2,1},{3,2},{4,3},{5,4},{6,5},{7,6},{8,7},{9,8},{10,9... | collective-permute-start | bytes 589832 | tf_op jit(solution)/shard_map/ppermute | solution.py:601
  42.3 1.0 copy-start.19
  43.2 0.9 copy-start.21
  60.0 8.4 %collective-permute-start.4 = (bf16[8,3,16,256]{3,2,1,0:T(8,128)(2,1)S(1)}, bf16[8,3,16,256]{3,2,1,0:T(8,128)(2,1)S(1)}, u32[]{:S(2)}, u32[]{:S(2)}) collective-permute-start(bf16[8,3,16,256]{3,2,1,0:T(8,128)(2,1)S(1)} %get-tuple-element.79), channel_id=1, source_target_pairs={{0,1},{1,2},{2,3},{3,4},{4,5},{5,6},{6,7},{7,8},{8,9},{9,10},{10,1... | collective-permute-start | bytes 589832 | tf_op jit(solution)/shard_map/ppermute | solution.py:601
  60.0 8.4 %collective-permute-start.5 = (bf16[8,3,16,256]{3,2,1,0:T(8,128)(2,1)S(1)}, bf16[8,3,16,256]{3,2,1,0:T(8,128)(2,1)S(1)}, u32[]{:S(2)}, u32[]{:S(2)}) collective-permute-start(bf16[8,3,16,256]{3,2,1,0:T(8,128)(2,1)S(1)} %get-tuple-element.80), channel_id=1, source_target_pairs={{0,15},{1,0},{2,1},{3,2},{4,3},{5,4},{6,5},{7,6},{8,7},{9,8},{10,9... | collective-permute-start | bytes 589832 | tf_op jit(solution)/shard_map/ppermute | solution.py:601
  64.9 3.5 %copy-start.2 = (bf16[512,1024]{1,0:T(8,128)(2,1)S(1)}, bf16[512,1024]{1,0:T(8,128)(2,1)}, u32[]{:S(2)}) copy-start(bf16[512,1024]{1,0:T(8,128)(2,1)} %copy-done.1) | copy-start | bytes 3145732
  64.9 3.5 %copy-start.4 = (bf16[512,1024]{1,0:T(8,128)(2,1)S(1)}, bf16[512,1024]{1,0:T(8,128)(2,1)}, u32[]{:S(2)}) copy-start(bf16[512,1024]{1,0:T(8,128)(2,1)} %copy-done.3) | copy-start | bytes 3145732
  64.9 3.5 %copy-start.12 = (f32[512,256]{1,0:T(8,128)S(1)}, f32[512,256]{1,0:T(8,128)}, u32[]{:S(2)}) copy-start(f32[512,256]{1,0:T(8,128)} %copy-done.11) | copy-start | bytes 1572868
  64.9 3.5 %copy-start.17 = (bf16[512,256]{1,0:T(8,128)(2,1)S(1)}, bf16[512,256]{1,0:T(8,128)(2,1)}, u32[]{:S(2)}) copy-start(bf16[512,256]{1,0:T(8,128)(2,1)} %copy-done.16) | copy-start | bytes 786436
  68.3 3.3 %collective-permute-start.18 = (bf16[1024,256]{1,0:T(8,128)(2,1)S(1)}, bf16[1024,256]{1,0:T(8,128)(2,1)S(1)}, u32[]{:S(2)}, u32[]{:S(2)}) collective-permute-start(bf16[1024,256]{1,0:T(8,128)(2,1)S(1)} %get-tuple-element.110), channel_id=1, source_target_pairs={{0,1},{1,0},{2,3},{3,2},{4,5},{5,4},{6,7},{7,6},{8,9},{9,8},{10,11... | collective-permute-start | bytes 1572872 | tf_op jit(solution)/shard_map/ppermute | solution.py:614
  71.0 4.8 %collective-permute-start.8 = (bf16[1024,256]{1,0:T(8,128)(2,1)S(1)}, bf16[1024,256]{1,0:T(8,128)(2,1)S(1)}, u32[]{:S(2)}, u32[]{:S(2)}) collective-permute-start(bf16[1024,256]{1,0:T(8,128)(2,1)S(1)} %get-tuple-element.94), channel_id=1, source_target_pairs={{0,1},{1,0},{2,3},{3,2},{4,5},{5,4},{6,7},{7,6},{8,9},{9,8},{10,11... | collective-permute-start | bytes 1572872 | tf_op jit(solution)/shard_map/ppermute | solution.py:614
  72.2 5.6 %collective-permute-start.19 = (bf16[256,256]{1,0:T(8,128)(2,1)S(1)}, bf16[256,256]{1,0:T(8,128)(2,1)S(1)}, u32[]{:S(2)}, u32[]{:S(2)}) collective-permute-start(bf16[256,256]{1,0:T(8,128)(2,1)S(1)} %get-tuple-element.112), channel_id=1, source_target_pairs={{0,2},{1,3},{2,0},{3,1},{4,6},{5,7},{6,4},{7,5},{8,10},{9,11},{10,... | collective-permute-start | bytes 393224 | tf_op jit(solution)/shard_map/ppermute | solution.py:614
  72.3 7.7 %collective-permute-start.20 = (bf16[256,256]{1,0:T(8,128)(2,1)S(1)}, bf16[256,256]{1,0:T(8,128)(2,1)S(1)}, u32[]{:S(2)}, u32[]{:S(2)}) collective-permute-start(bf16[256,256]{1,0:T(8,128)(2,1)S(1)} %get-tuple-element.113), channel_id=1, source_target_pairs={{0,4},{1,5},{2,6},{3,7},{4,0},{5,1},{6,2},{7,3},{8,12},{9,13},{10,... | collective-permute-start | bytes 393224 | tf_op jit(solution)/shard_map/ppermute | solution.py:614
  72.4 10.6 %collective-permute-start.21 = (bf16[256,256]{1,0:T(8,128)(2,1)S(1)}, bf16[256,256]{1,0:T(8,128)(2,1)S(1)}, u32[]{:S(2)}, u32[]{:S(2)}) collective-permute-start(bf16[256,256]{1,0:T(8,128)(2,1)S(1)} %get-tuple-element.114), channel_id=1, source_target_pairs={{0,6},{1,7},{2,4},{3,5},{4,2},{5,3},{6,0},{7,1},{8,14},{9,15},{10,... | collective-permute-start | bytes 393224 | tf_op jit(solution)/shard_map/ppermute | solution.py:614
  76.5 36.4 %copy-start.10 = (f32[4,256,128]{2,1,0:T(8,128)S(1)}, f32[4,256,128]{2,1,0:T(8,128)}, u32[]{:S(2)}) copy-start(f32[4,256,128]{2,1,0:T(8,128)} %copy-done.9) | copy-start | bytes 1572868
  76.5 36.4 %copy-start.15 = (f32[2,256,128]{2,1,0:T(8,128)S(1)}, f32[2,256,128]{2,1,0:T(8,128)}, u32[]{:S(2)}) copy-start(f32[2,256,128]{2,1,0:T(8,128)} %copy-done.14) | copy-start | bytes 786436
  76.5 14.4 %collective-permute-start.9 = (bf16[256,256]{1,0:T(8,128)(2,1)S(1)}, bf16[256,256]{1,0:T(8,128)(2,1)S(1)}, u32[]{:S(2)}, u32[]{:S(2)}) collective-permute-start(bf16[256,256]{1,0:T(8,128)(2,1)S(1)} %get-tuple-element.96), channel_id=1, source_target_pairs={{0,2},{1,3},{2,0},{3,1},{4,6},{5,7},{6,4},{7,5},{8,10},{9,11},{10,... | collective-permute-start | bytes 393224 | tf_op jit(solution)/shard_map/ppermute | solution.py:614
  76.6 14.3 %collective-permute-start.10 = (bf16[256,256]{1,0:T(8,128)(2,1)S(1)}, bf16[256,256]{1,0:T(8,128)(2,1)S(1)}, u32[]{:S(2)}, u32[]{:S(2)}) collective-permute-start(bf16[256,256]{1,0:T(8,128)(2,1)S(1)} %get-tuple-element.97), channel_id=1, source_target_pairs={{0,4},{1,5},{2,6},{3,7},{4,0},{5,1},{6,2},{7,3},{8,12},{9,13},{10,... | collective-permute-start | bytes 393224 | tf_op jit(solution)/shard_map/ppermute | solution.py:614
  77.8 13.1 %collective-permute-start.11 = (bf16[256,256]{1,0:T(8,128)(2,1)S(1)}, bf16[256,256]{1,0:T(8,128)(2,1)S(1)}, u32[]{:S(2)}, u32[]{:S(2)}) collective-permute-start(bf16[256,256]{1,0:T(8,128)(2,1)S(1)} %get-tuple-element.98), channel_id=1, source_target_pairs={{0,6},{1,7},{2,4},{3,5},{4,2},{5,3},{6,0},{7,1},{8,14},{9,15},{10,... | collective-permute-start | bytes 393224 | tf_op jit(solution)/shard_map/ppermute | solution.py:614
  83.6 6.0 %collective-permute-start.22 = (bf16[128,256]{1,0:T(8,128)(2,1)S(1)}, bf16[128,256]{1,0:T(8,128)(2,1)S(1)}, u32[]{:S(2)}, u32[]{:S(2)}) collective-permute-start(bf16[128,256]{1,0:T(8,128)(2,1)S(1)} %get-tuple-element.116), channel_id=1, source_target_pairs={{0,8},{1,9},{2,10},{3,11},{4,12},{5,13},{6,14},{7,15},{8,0},{9,1},... | collective-permute-start | bytes 196616 | tf_op jit(solution)/shard_map/ppermute | solution.py:614
  89.7 6.0 %collective-permute-start.23 = (bf16[128,256]{1,0:T(8,128)(2,1)S(1)}, bf16[128,256]{1,0:T(8,128)(2,1)S(1)}, u32[]{:S(2)}, u32[]{:S(2)}) collective-permute-start(bf16[128,256]{1,0:T(8,128)(2,1)S(1)} %total.3.refs_0_), channel_id=1, source_target_pairs={{0,8},{1,9},{2,10},{3,11},{4,12},{5,13},{6,14},{7,15},{8,0},{9,1},... | collective-permute-start | bytes 196616 | tf_op jit(solution)/shard_map/ppermute | solution.py:607
  91.5 5.8 %collective-permute-start.12 = (bf16[128,256]{1,0:T(8,128)(2,1)S(1)}, bf16[128,256]{1,0:T(8,128)(2,1)S(1)}, u32[]{:S(2)}, u32[]{:S(2)}) collective-permute-start(bf16[128,256]{1,0:T(8,128)(2,1)S(1)} %get-tuple-element.100), channel_id=1, source_target_pairs={{0,8},{1,9},{2,10},{3,11},{4,12},{5,13},{6,14},{7,15},{8,0},{9,1},... | collective-permute-start | bytes 196616 | tf_op jit(solution)/shard_map/ppermute | solution.py:614
  96.2 10.1 %collective-permute-start.24 = (bf16[256,256]{1,0:T(8,128)(2,1)S(1)}, bf16[256,256]{1,0:T(8,128)(2,1)S(1)}, u32[]{:S(2)}, u32[]{:S(2)}) collective-permute-start(bf16[256,256]{1,0:T(8,128)(2,1)S(1)} %bitcast.75), channel_id=1, source_target_pairs={{0,2},{1,3},{2,0},{3,1},{4,6},{5,7},{6,4},{7,5},{8,10},{9,11},{10,... | collective-permute-start | bytes 393224 | tf_op jit(solution)/shard_map/ppermute | solution.py:607
  97.4 5.3 %collective-permute-start.13 = (bf16[128,256]{1,0:T(8,128)(2,1)S(1)}, bf16[128,256]{1,0:T(8,128)(2,1)S(1)}, u32[]{:S(2)}, u32[]{:S(2)}) collective-permute-start(bf16[128,256]{1,0:T(8,128)(2,1)S(1)} %total.2.refs_0_), channel_id=1, source_target_pairs={{0,8},{1,9},{2,10},{3,11},{4,12},{5,13},{6,14},{7,15},{8,0},{9,1},... | collective-permute-start | bytes 196616 | tf_op jit(solution)/shard_map/ppermute | solution.py:607
  99.0 7.8 %collective-permute-start.25 = (bf16[256,256]{1,0:T(8,128)(2,1)S(1)}, bf16[256,256]{1,0:T(8,128)(2,1)S(1)}, u32[]{:S(2)}, u32[]{:S(2)}) collective-permute-start(bf16[256,256]{1,0:T(8,128)(2,1)S(1)} %bitcast.76), channel_id=1, source_target_pairs={{0,4},{1,5},{2,6},{3,7},{4,0},{5,1},{6,2},{7,3},{8,12},{9,13},{10,... | collective-permute-start | bytes 393224 | tf_op jit(solution)/shard_map/ppermute | solution.py:607
  101.3 7.6 %collective-permute-start.26 = (bf16[256,256]{1,0:T(8,128)(2,1)S(1)}, bf16[256,256]{1,0:T(8,128)(2,1)S(1)}, u32[]{:S(2)}, u32[]{:S(2)}) collective-permute-start(bf16[256,256]{1,0:T(8,128)(2,1)S(1)} %bitcast.77), channel_id=1, source_target_pairs={{0,6},{1,7},{2,4},{3,5},{4,2},{5,3},{6,0},{7,1},{8,14},{9,15},{10,... | collective-permute-start | bytes 393224 | tf_op jit(solution)/shard_map/ppermute | solution.py:607
  103.3 7.4 %collective-permute-start.14 = (bf16[256,256]{1,0:T(8,128)(2,1)S(1)}, bf16[256,256]{1,0:T(8,128)(2,1)S(1)}, u32[]{:S(2)}, u32[]{:S(2)}) collective-permute-start(bf16[256,256]{1,0:T(8,128)(2,1)S(1)} %bitcast.79), channel_id=1, source_target_pairs={{0,2},{1,3},{2,0},{3,1},{4,6},{5,7},{6,4},{7,5},{8,10},{9,11},{10,... | collective-permute-start | bytes 393224 | tf_op jit(solution)/shard_map/ppermute | solution.py:607
  104.3 6.3 %collective-permute-start.15 = (bf16[256,256]{1,0:T(8,128)(2,1)S(1)}, bf16[256,256]{1,0:T(8,128)(2,1)S(1)}, u32[]{:S(2)}, u32[]{:S(2)}) collective-permute-start(bf16[256,256]{1,0:T(8,128)(2,1)S(1)} %bitcast.80), channel_id=1, source_target_pairs={{0,4},{1,5},{2,6},{3,7},{4,0},{5,1},{6,2},{7,3},{8,12},{9,13},{10,... | collective-permute-start | bytes 393224 | tf_op jit(solution)/shard_map/ppermute | solution.py:607
  106.4 5.9 %collective-permute-start.16 = (bf16[256,256]{1,0:T(8,128)(2,1)S(1)}, bf16[256,256]{1,0:T(8,128)(2,1)S(1)}, u32[]{:S(2)}, u32[]{:S(2)}) collective-permute-start(bf16[256,256]{1,0:T(8,128)(2,1)S(1)} %bitcast.81), channel_id=1, source_target_pairs={{0,6},{1,7},{2,4},{3,5},{4,2},{5,3},{6,0},{7,1},{8,14},{9,15},{10,... | collective-permute-start | bytes 393224 | tf_op jit(solution)/shard_map/ppermute | solution.py:607
  109.4 30.9 %collective-permute-start.27 = (bf16[1024,256]{1,0:T(8,128)(2,1)S(1)}, bf16[1024,256]{1,0:T(8,128)(2,1)S(1)}, u32[]{:S(2)}, u32[]{:S(2)}) collective-permute-start(bf16[1024,256]{1,0:T(8,128)(2,1)S(1)} %bitcast.67), channel_id=1, source_target_pairs={{0,1},{1,0},{2,3},{3,2},{4,5},{5,4},{6,7},{7,6},{8,9},{9,8},{10,11... | collective-permute-start | bytes 1572872 | tf_op jit(solution)/shard_map/ppermute | solution.py:607
  112.8 27.5 %collective-permute-start.17 = (bf16[1024,256]{1,0:T(8,128)(2,1)S(1)}, bf16[1024,256]{1,0:T(8,128)(2,1)S(1)}, u32[]{:S(2)}, u32[]{:S(2)}) collective-permute-start(bf16[1024,256]{1,0:T(8,128)(2,1)S(1)} %bitcast.69), channel_id=1, source_target_pairs={{0,1},{1,0},{2,3},{3,2},{4,5},{5,4},{6,7},{7,6},{8,9},{9,8},{10,11... | collective-permute-start | bytes 1572872 | tf_op jit(solution)/shard_map/ppermute | solution.py:607
  120.8 1.4 %collective-permute-start.28 = (bf16[128,256]{1,0:T(8,128)(2,1)S(1)}, bf16[128,256]{1,0:T(8,128)(2,1)S(1)}, u32[]{:S(2)}, u32[]{:S(2)}) collective-permute-start(bf16[128,256]{1,0:T(8,128)(2,1)S(1)} %taps.1.refs_0_), channel_id=1, source_target_pairs={{0,1},{1,0},{2,3},{3,2},{4,5},{5,4},{6,7},{7,6},{8,9},{9,8},{10,11... | collective-permute-start | bytes 196616 | tf_op jit(solution)/shard_map/ppermute | solution.py:607
  122.3 4.4 %collective-permute-start.29 = (bf16[128,256]{1,0:T(8,128)(2,1)S(1)}, bf16[128,256]{1,0:T(8,128)(2,1)S(1)}, u32[]{:S(2)}, u32[]{:S(2)}) collective-permute-start(bf16[128,256]{1,0:T(8,128)(2,1)S(1)} %total_small.3.refs_0_), channel_id=1, source_target_pairs={{0,2},{1,3},{2,0},{3,1},{4,6},{5,7},{6,4},{7,5},{8,10},{9,11},{10,... | collective-permute-start | bytes 196616 | tf_op jit(solution)/shard_map/ppermute | solution.py:607
  122.8 6.0 %collective-permute-start.30 = (bf16[128,256]{1,0:T(8,128)(2,1)S(1)}, bf16[128,256]{1,0:T(8,128)(2,1)S(1)}, u32[]{:S(2)}, u32[]{:S(2)}) collective-permute-start(bf16[128,256]{1,0:T(8,128)(2,1)S(1)} %total_small.3.refs_0_), channel_id=1, source_target_pairs={{0,4},{1,5},{2,6},{3,7},{4,0},{5,1},{6,2},{7,3},{8,12},{9,13},{10,... | collective-permute-start | bytes 196616 | tf_op jit(solution)/shard_map/ppermute | solution.py:607
  124.4 15.0 %collective-permute-start.6 = (bf16[8,3,16,256]{3,2,1,0:T(8,128)(2,1)S(1)}, bf16[8,3,16,256]{3,2,1,0:T(8,128)(2,1)S(1)}, u32[]{:S(2)}, u32[]{:S(2)}) collective-permute-start(bf16[8,3,16,256]{3,2,1,0:T(8,128)(2,1)S(1)} %get-tuple-element.91), channel_id=1, source_target_pairs={{0,1},{1,2},{2,3},{3,4},{4,5},{5,6},{6,7},{7,8},{8,9},{9,10},{10,1... | collective-permute-start | bytes 589832 | tf_op jit(solution)/shard_map/ppermute | solution.py:601
  126.7 12.7 %collective-permute-start.7 = (bf16[8,3,16,256]{3,2,1,0:T(8,128)(2,1)S(1)}, bf16[8,3,16,256]{3,2,1,0:T(8,128)(2,1)S(1)}, u32[]{:S(2)}, u32[]{:S(2)}) collective-permute-start(bf16[8,3,16,256]{3,2,1,0:T(8,128)(2,1)S(1)} %get-tuple-element.92), channel_id=1, source_target_pairs={{0,15},{1,0},{2,1},{3,2},{4,3},{5,4},{6,5},{7,6},{8,7},{9,8},{10,9... | collective-permute-start | bytes 589832 | tf_op jit(solution)/shard_map/ppermute | solution.py:601
  128.8 5.2 %collective-permute-start.31 = (bf16[128,256]{1,0:T(8,128)(2,1)S(1)}, bf16[128,256]{1,0:T(8,128)(2,1)S(1)}, u32[]{:S(2)}, u32[]{:S(2)}) collective-permute-start(bf16[128,256]{1,0:T(8,128)(2,1)S(1)} %total_small.3.refs_0_), channel_id=1, source_target_pairs={{0,6},{1,7},{2,4},{3,5},{4,2},{5,3},{6,0},{7,1},{8,14},{9,15},{10,... | collective-permute-start | bytes 196616 | tf_op jit(solution)/shard_map/ppermute | solution.py:607
  134.1 5.2 %collective-permute-start.32 = (bf16[128,256]{1,0:T(8,128)(2,1)S(1)}, bf16[128,256]{1,0:T(8,128)(2,1)S(1)}, u32[]{:S(2)}, u32[]{:S(2)}) collective-permute-start(bf16[128,256]{1,0:T(8,128)(2,1)S(1)} %total_small.4.refs_0_), channel_id=1, source_target_pairs={{0,8},{1,9},{2,10},{3,11},{4,12},{5,13},{6,14},{7,15},{8,0},{9,1},... | collective-permute-start | bytes 196616 | tf_op jit(solution)/shard_map/ppermute | solution.py:607

commit v3 on v2

--- a/solution.py
+++ b/solution.py
@@ -85,6 +85,32 @@
     else:
         at = (last - x, r)
     return at[0] * PITCH + at[1]
+
+
+def read_plan(sz, table):
+    columns = lax.axis_size("tile")
+    device = lax.axis_index("tile")
+    below = lax.rem(device + columns - 1, columns)
+    plan = []
+    for q in range(sz.tiles):
+        for side in range(4):
+            source = table[side, 0, device * sz.tiles + q]
+            owner = lax.div(source, sz.tiles)
+            local = (source - owner * sz.tiles) * 4 + table[side, 1, device * sz.tiles + q]
+            shift = jnp.where(
+                owner == device, 0, jnp.where(owner == below, sz.pieces, 2 * sz.pieces)
+            )
+            plan.append(shift + local)
+    return plan
+
+
+def digit_of(level):
+    device = lax.axis_index("tile")
+    if level == 0:
+        return lax.rem(device, 2)
+    if level == 1:
+        return lax.rem(lax.div(device, 2), 4)
+    return lax.div(device, 8)
 
 
 def write_strips(sz, flat, strips_ref):
@@ -403,10 +429,11 @@
 
 
 def forward_kernel(
-    sz, layer, strip_at, corner_at, cur, own, below, above, kern, gain, lscale, up, down,
+    sz, layer, seams, corners, cur, own, below, above, kern, gain, lscale, up, down,
     out, strips, pad, normal, inverse, normed, slope, active, branch,
     pool, taps, conv, upward, flat,
 ):
+    strip_at, corner_at = read_plan(sz, seams), read_plan(sz, corners)
     surround(sz, strip_at, corner_at, cur, own, below, above, pool, pad)
     hold_taps(sz, kern, layer, taps)
     convolve(sz, pad, taps, conv)
@@ -419,11 +446,12 @@
 
 
 def turn_kernel(
-    sz, layer, strip_at, corner_at, cur, own, below, above, kern, gain, lscale, up, down, out_grad,
+    sz, layer, seams, corners, cur, own, below, above, kern, gain, lscale, up, down, out_grad,
     out_hbm, base, grad_own, grad_below, grad_above,
     pad, grad_conv, normed, active, down_in, up_in, gain_sums, scale_sums,
     pool, taps, conv, upward, out, normal, inverse, slope, branch, grad_pool, grad_pad, out_sem,
 ):
+    strip_at, corner_at = read_plan(sz, seams), read_plan(sz, corners)
     surround(sz, strip_at, corner_at, cur, own, below, above, pool, pad)
     hold_taps(sz, kern, layer, taps)
     convolve(sz, pad, taps, conv)
@@ -451,17 +479,17 @@
 
 
 def weights_kernel(
-    sz, place, pad, grad_conv, normed, active, down_in, up_in, gain_sums, scale_sums,
+    sz, pad, grad_conv, normed, active, down_in, up_in, gain_sums, scale_sums,
     keep, send, small, tap_sums, both,
 ):
     small[...] = jnp.zeros_like(small)
-    weight_gradients(sz, place[0], active, down_in, normed, up_in, both, keep, send)
+    weight_gradients(sz, digit_of(0), active, down_in, normed, up_in, both, keep, send)
     tap_gradients(sz, pad, grad_conv, tap_sums, small)
     fill_small(small, gain_sums, scale_sums)
 
 
 def backward_kernel(
-    sz, layer, place, base, own, first, second, lscale, down, normed, slope, active, branch,
+    sz, layer, base, own, first, second, lscale, down, normed, slope, active, branch,
     keep, send, flat, up_in, scale_sums,
     hidden, down_in, both,
 ):
@@ -471,14 +499,15 @@
     scale_rows(sz, flat_grad_row(sz, flat), branch, lscale, layer, down_in, scale_sums)
     hidden[...] = multiply(down_in[...], down[layer], 1, 1)
     slope_rows(sz, hidden, slope, up_in)
-    weight_gradients(sz, place[0], active, down_in, normed, up_in, both, keep, send)
+    weight_gradients(sz, digit_of(0), active, down_in, normed, up_in, both, keep, send)
 
 
 def spread_kernel(
-    sz, layer, strip_at, corner_at, kern, gain, up, flat, up_in, normal, inverse,
+    sz, layer, seams, corners, kern, gain, up, flat, up_in, normal, inverse,
     base, grad_own, grad_below, grad_above, grad_conv, gain_sums,
     taps, branch, grad_pool, grad_pad,
 ):
+    strip_at, corner_at = read_plan(sz, seams), read_plan(sz, corners)
     branch[...] = multiply(up_in[...], up[layer], 1, 1)
     norm_gradients(sz, branch, normal, inverse, gain, layer, grad_conv, gain_sums)
     hold_taps(sz, kern, layer, taps)
@@ -514,41 +543,60 @@
         out[rows] = sum(values[1:], values[0]).astype(BF16)
 
 
-def share_kernel(digit, *refs):
-    place, refs = refs[0], refs[1:]
-    count = refs[0].shape[0]
-    arrays, outs = refs[:-count], refs[-count:]
+def share_near_kernel(*refs):
+    arrays, outs = refs[:2], refs[2:]
     for k, out in enumerate(outs):
-        piece = place[digit] ^ k
+        piece = digit_of(1) ^ k
         add_rows(out, [lambda rows, array=array: array[piece, rows] for array in arrays])
 
 
+def share_far_kernel(*refs):
+    rest, share = refs[0].shape[:2]
+    arrays, outs = refs[:-rest], refs[-rest:]
+    for k, out in enumerate(outs):
+        piece = digit_of(2) ^ k
+        for layer in range(2):
+            parts = arrays[4 * layer : 4 * layer + 4]
+            add_rows(
+                out.at[layer],
+                [lambda rows, array=array: array[piece, rows] for array in parts],
+            )
+
+
 def total_kernel(*refs):
-    add_rows(refs[-1], [lambda rows, array=array: array[rows] for array in refs[:-1]])
-
-
-def order_kernel(digit, place, *refs):
+    out = refs[-1]
+    if len(out.shape) == 2:
+        add_rows(out, [lambda rows, array=array: array[rows] for array in refs[:-1]])
+        return
+    for layer in range(out.shape[0]):
+        add_rows(
+            out.at[layer],
+            [lambda rows, array=array: array[layer, rows] for array in refs[:-1]],
+        )
+
+
+def order_kernel(level, *refs):
     for k, piece in enumerate(refs[:-1]):
-        refs[-1][place[digit] ^ k] = piece[...]
+        refs[-1][digit_of(level) ^ k] = piece[...]
 
 
 def unpack_kernel(
-    sz, place, mine_zero, theirs_zero, mine_one, theirs_one, small,
-    up_hbm, down_hbm, kernel_out, gain_out, scale_out, up, down, sems,
+    sz, mine, theirs, small, up_hbm, down_hbm, kernel_out, gain_out, scale_out, up, down, sems,
 ):
-    even = place[0] == 0
+    even = digit_of(0) == 0
+    pieces, _, share, _ = mine.shape
     copies = []
-    step = 32
-    for layer, mine, theirs in ((1, mine_one, theirs_one), (0, mine_zero, theirs_zero)):
-        for start in range(0, sz.hidden, step):
-            rows = slice(start, start + step)
-            down[layer, rows] = jnp.where(even, mine[rows], theirs[rows]).astype(F32)
+    for layer in range(2):
+        for j in range(pieces):
+            start = j * share
+            down[layer, start : start + share] = jnp.where(
+                even, mine[j, layer], theirs[j, layer]
+            ).astype(F32)
         copies.append((down.at[layer], down_hbm.at[layer]))
-        for start in range(0, sz.hidden, step):
-            rows = slice(start, start + step)
-            k, c = divmod(start, sz.channels)
-            up[layer, c : c + step, k * sz.channels : (k + 1) * sz.channels] = jnp.where(
-                even, theirs[rows], mine[rows]
+        for j in range(pieces):
+            k, c = divmod(j * share, sz.channels)
+            up[layer, c : c + share, k * sz.channels : (k + 1) * sz.channels] = jnp.where(
+                even, theirs[j, layer], mine[j, layer]
             ).astype(F32)
         copies.append((up.at[layer], up_hbm.at[layer]))
         for k in range(len(copies) - 2, len(copies)):
@@ -573,10 +621,15 @@
 IN_HBM = pl.BlockSpec(memory_space=pltpu.HBM)
 
 
-def call(body, name, micros, ins, outs, scratch):
+def call(body, name, micros, ins, outs, scratch, after=()):
+    count = len(ins)
+
+    def run(*refs):
+        body(*refs[:count], *refs[count + len(after) :])
+
     return pl.pallas_call(
-        body,
-        in_specs=[spec for spec, _ in ins],
+        run,
+        in_specs=[spec for spec, _ in ins] + [pl.BlockSpec(memory_space=pl.ANY)] * len(after),
         out_specs=[spec for spec, _ in outs],
         out_shape=[out for _, out in outs],
         scratch_shapes=scratch,
@@ -585,7 +638,7 @@
             flops=0, bytes_accessed=int(micros * 3.5e6), transcendentals=0
         ),
         name=name,
-    )(*[array for _, array in ins])
+    )(*[array for _, array in ins], *after)
 
 
 def near(*arrays):
@@ -617,72 +670,64 @@
 
 
 class Reduction:
-    def __init__(self, place, devices):
-        self.place = [(IN_SMEM, place)]
+    def __init__(self, devices):
+        self.devices = devices
         self.rest = devices // 8
         self.near_masks = [2 * k for k in range(1, 4)]
         self.rest_masks = [8 * k for k in range(1, self.rest)]
 
-    def scatter(self, keep, send):
+    def start(self, keep, send):
         rows, channels = keep.shape
         (came,) = swap([send], [1])
         quarter = rows // 4
         parts = (4, quarter, channels)
         shape = jax.ShapeDtypeStruct((quarter, channels), BF16)
         pieces = call(
-            functools.partial(share_kernel, 1), "share_near", 0.7,
-            self.place + near(keep.reshape(parts), came.reshape(parts)), near(*[shape] * 4), [],
+            share_near_kernel, "share_near", 0.7,
+            near(keep.reshape(parts), came.reshape(parts)), near(*[shape] * 4), [],
         )
-        arrived = swap(pieces[1:], self.near_masks)
-        parts = (self.rest, quarter // self.rest, channels)
-        shape = jax.ShapeDtypeStruct(parts[1:], BF16)
-        arrays = [piece.reshape(parts) for piece in [pieces[0]] + arrived]
+        return [pieces[0]] + swap(pieces[1:], self.near_masks)
+
+    def finish(self, parts, after):
+        quarter, channels = parts[0][0].shape
+        dims = (self.rest, quarter // self.rest, channels)
+        arrays = [part.reshape(dims) for layer in parts for part in layer]
+        shape = jax.ShapeDtypeStruct((2,) + dims[1:], BF16)
         pieces = call(
-            functools.partial(share_kernel, 2), "share_far", 0.5,
-            self.place + near(*arrays), near(*[shape] * self.rest), [],
+            share_far_kernel, "share_far", 0.9,
+            near(*arrays), near(*[shape] * self.rest), [], after,
         )
         arrived = swap(pieces[1:], self.rest_masks)
         (total,) = call(
-            total_kernel, "total", 0.3, near(pieces[0], *arrived), near(shape), []
+            total_kernel, "total", 0.4, near(pieces[0], *arrived), near(shape), []
         )
-        return total
-
-    def gather(self, total):
-        rows, channels = total.shape
-        for digit, masks, name in ((2, self.rest_masks, "order_far"), (1, self.near_masks, "order_near")):
+        return pieces[0], total
+
+    def gather(self, total, after):
+        for level, masks, name in (
+            (2, self.rest_masks, "order_far"),
+            (1, self.near_masks, "order_near"),
+        ):
             pieces = [total] + partners(total, masks)
             shape = jax.ShapeDtypeStruct((len(pieces),) + total.shape, BF16)
             (total,) = call(
-                functools.partial(order_kernel, digit), name, 0.3,
-                self.place + near(*pieces), near(shape), [],
+                functools.partial(order_kernel, level), name, 0.5,
+                near(*pieces), near(shape), [], after,
             )
-            total = total.reshape((-1, channels))
+            after = ()
+        total = total.reshape((4 * self.rest,) + total.shape[2:])
         return total, partners(total, [1])[0]
 
     def whole(self, array):
-        for masks in ([1], self.near_masks, self.rest_masks):
+        mask = 1
+        while mask < self.devices:
             shape = jax.ShapeDtypeStruct(array.shape, BF16)
             (array,) = call(
                 total_kernel, "total_small", 0.3,
-                near(array, *partners(array, masks)), near(shape), [],
+                near(array, *partners(array, [mask])), near(shape), [],
             )
+            mask *= 2
         return array
-
-
-def margin_plan(table, tile_count, columns, device):
-    pieces = tile_count * 4
-    entries = lax.dynamic_slice_in_dim(table, device * tile_count, tile_count, 0).reshape(
-        (pieces, 2)
-    )
-    source = entries[:, 0]
-    source_device = source // tile_count
-    local_piece = (source - source_device * tile_count) * 4 + entries[:, 1]
-    below_device = (device + columns - 1) % columns
-    return jnp.where(
-        source_device == device,
-        local_piece,
-        jnp.where(source_device == below_device, pieces + local_piece, 2 * pieces + local_piece),
-    )
 
 
 def on_device(
@@ -700,15 +745,10 @@
     layers, _, hidden = up_weight.shape
     sz = Sizes(tiles, edge, channels, hidden)
     columns = lax.axis_size("tile")
-    device = lax.axis_index("tile")
-    strip_at = margin_plan(seam_table, tiles, columns, device)
-    corner_at = margin_plan(corner_table, tiles, columns, device)
-    plan = [(IN_SMEM, strip_at), (IN_SMEM, corner_at)]
-    kernel_turned = kernel.transpose((1, 2, 0, 3))
-
-    place = jnp.stack([device % 2, device // 2 % 4, device // 8]).astype(jnp.int32)
-    where = [(IN_SMEM, place)]
-    reduction = Reduction(place, columns)
+    plan = [(IN_SMEM, table.transpose((1, 2, 0))) for table in (seam_table, corner_table)]
+    kern = kernel.transpose((1, 2, 0, 3))
+    gain, lscale, up, down = norm_gain, layer_scale, up_weight, down_weight
+    reduction = Reduction(columns)
 
     shape = jax.ShapeDtypeStruct
     image = shape(inputs.shape, BF16)
@@ -745,13 +785,14 @@
         vmem(slabs),
     )
     below, above = pass_on(strips, 1), pass_on(strips, -1)
-    fetched = (inputs, out_grad, kernel_turned, norm_gain, layer_scale, up_weight, down_weight)
+    fetched = (inputs, out_grad, kern, gain, lscale, up, down)
     inputs, out_grad, kern, gain, lscale, up, down = call(
         fetch_kernel,
         "fetch", 2.0,
         far(*fetched),
         near(*[shape(one.shape, one.dtype) for one in fetched]),
         sems(len(fetched)),
+        (strips,),
     )
     middle, strips, pad_zero, normal, inverse, normed, slope, active, branch = call(
         functools.partial(forward_kernel, sz, 0),
@@ -782,29 +823,30 @@
     keep_one, send_one, small_one = call(
         functools.partial(weights_kernel, sz),
         "weights", 2.8,
-        where + near(*for_weights),
+        near(*for_weights),
         near(half, half, small),
         vmem(tap_sums, two_halves),
     )
-    sum_one = reduction.scatter(keep_one, send_one)
+    parts_one = reduction.start(keep_one, send_one)
     keep_zero, send_zero, flat, up_in, scale_sums = call(
         functools.partial(backward_kernel, sz, 0),
         "backward", 2.9,
-        where
-        + near(
+        near(
             base, grad_own, from_below, from_above, lscale, down, normed, slope, active, branch
         ),
         near(half, half, slabs, wide_short, sums),
         vmem(wide, narrow_short, two_halves),
     )
-    sum_zero = reduction.scatter(keep_zero, send_zero)
+    parts_zero = reduction.start(keep_zero, send_zero)
     base, grad_own, grad_below, grad_above, grad_conv, gain_sums = call(
         functools.partial(spread_kernel, sz, 0),
         "spread", 6.0,
         plan + near(kern, gain, up, flat, up_in, normal, inverse),
         near(slabs, own_shape, strips_shape, strips_shape, grad_slabs, sums),
         vmem(taps, narrow, grad_pool, padded),
-    )
+        (parts_zero[0],),
+    )
+    share, total = reduction.finish((parts_zero, parts_one), (gain_sums,))
     from_below, from_above = pass_on(grad_above, 1), pass_on(grad_below, -1)
     (small_both,) = call(
         functools.partial(taps_kernel, sz),
@@ -812,6 +854,7 @@
         near(pad_zero, grad_conv, gain_sums, scale_sums, small_one),
         near(shape((2 * SMALL_ROWS, channels), BF16)),
         vmem(tap_sums, small),
+        (share,),
     )
     (in_grad,) = call(
         functools.partial(last_kernel, sz),
@@ -823,13 +866,10 @@
     grad_up, grad_down, grad_kernel, grad_gain, grad_scale = call(
         functools.partial(unpack_kernel, sz),
         "unpack", 2.7,
-        where
-        + near(
-            *reduction.gather(sum_zero), *reduction.gather(sum_one), reduction.whole(small_both)
-        ),
+        near(*reduction.gather(total, (in_grad,)), reduction.whole(small_both)),
         far(shape(up_weight.shape, F32), shape(down_weight.shape, F32))
         + near(
-            shape(kernel_turned.shape, F32), shape(norm_gain.shape, F32),
+            shape(kern.shape, F32), shape(norm_gain.shape, F32),
             shape(norm_gain.shape, F32),
         ),
         vmem(shape(up_weight.shape, F32), shape(down_weight.shape, F32)) + sems(4),

time: 144 us -> 124 us (0.86)
  local copies, waits for them, and re-layouts: 20.2 us -> 7.55 us
  Pallas kernels: 48.5 us -> 42.3 us
  starting transfers between devices: 41.4 us -> 37.5 us
  waiting for transfers between devices: 32.4 us -> 35.2 us
    unnamed x58 -> x20, local copies, waits for them, and re-layouts: 19 us -> 7.55 us
    pallas_call x23 -> x20, Pallas kernels: 48.5 us -> 42.3 us  [call(): pl.pallas_call(run, in_specs=[spec for spec, _ in ins] + [pl.BlockSpec(me...]
    ppermute x15 -> x9, starting transfers between devices: 13.7 us -> 9.5 us  [partners(): lax.ppermute(array, 'tile', [(i, i ^ mask) for i in range(length)])]
    ppermute x15 -> x9, waiting for transfers between devices: 21.1 us -> 24.8 us  [partners(): lax.ppermute(array, 'tile', [(i, i ^ mask) for i in range(length)])]
    ppermute x10 -> x9, waiting for transfers between devices: 7.69 us -> 4.46 us  [swap(): lax.ppermute(array, 'tile', [(i, i ^ mask) for i in range(length)])]
    ppermute x8, waiting for transfers between devices: 3.58 us -> 5.9 us  [pass_on(): lax.ppermute(shard, 'tile', [(i, (i + by) % length) for i in range(length)])]
    ppermute x8, starting transfers between devices: 17 us -> 19.2 us  [pass_on(): lax.ppermute(shard, 'tile', [(i, (i + by) % length) for i in range(length)])]
    ppermute x10 -> x9, starting transfers between devices: 10.8 us -> 8.77 us  [swap(): lax.ppermute(array, 'tile', [(i, i ^ mask) for i in range(length)])]
  transfers between devices with their start and end apart: 33 -> 26, of which waited for: 13 -> 14; matrix products, arithmetic and copies ran while one was open for 1% -> 0% of each run, Pallas kernels for 14% -> 12%
where the time goes in v3:
time: 124 us
  Pallas kernels  42.3 us (34%)
  starting transfers between devices  37.5 us (30%)
  waiting for transfers between devices  35.2 us (28%)
  local copies, waits for them, and re-layouts  7.55 us (6%)
    pallas_call x20, Pallas kernels, call(): pl.pallas_call(run, in_specs=[spec for spec, _ in ins] + [pl.BlockSpec(me...  42.3 us
    ppermute x9, waiting for transfers between devices, partners(): lax.ppermute(array, 'tile', [(i, i ^ mask) for i in range(length)])  24.8 us
    ppermute x8, starting transfers between devices, pass_on(): lax.ppermute(shard, 'tile', [(i, (i + by) % length) for i in range(length)])  19.2 us
    ppermute x9, starting transfers between devices, partners(): lax.ppermute(array, 'tile', [(i, i ^ mask) for i in range(length)])  9.5 us
    ppermute x9, starting transfers between devices, swap(): lax.ppermute(array, 'tile', [(i, i ^ mask) for i in range(length)])  8.77 us
    unnamed x20, local copies, waits for them, and re-layouts  7.55 us
    ppermute x8, waiting for transfers between devices, pass_on(): lax.ppermute(shard, 'tile', [(i, (i + by) % length) for i in range(length)])  5.9 us
    ppermute x9, waiting for transfers between devices, swap(): lax.ppermute(array, 'tile', [(i, i ^ mask) for i in range(length)])  4.46 us
  transfers between devices with their start and end apart: 26, of which 14 were waited for; matrix products, arithmetic and copies ran while one was open for 0% of the time, Pallas kernels for 12%

profile of v3, /device:TPU:0, one launch (start us, length us, event | category | flops | bytes accessed | tf_op | source)
XLA Modules:
  0.0 123.6 jit_solution(4522396381475888175)
XLA Ops:
  0.6 0.9 copy-done.2
  1.6 0.1 strips.1.refs_7_.refs_3_
  1.7 0.5 collective-permute-start
  2.2 5.1 %collective-permute-start.1 = (bf16[8,3,16,256]{3,2,1,0:T(8,128)(2,1)S(1)}, bf16[8,3,16,256]{3,2,1,0:T(8,128)(2,1)S(1)}, u32[]{:S(2)}, u32[]{:S(2)}) collective-permute-start(bf16[8,3,16,256]{3,2,1,0:T(8,128)(2,1)S(1)} %strips.1.refs_7_.refs_3_), channel_id=1, source_target_pairs={{0,15},{1,0},{2,1},{3,2},{4,3},{5,4},{6,5},{7,6},{8,7},{9,8},{10,9... | collective-permute-start | bytes 589832 | tf_op jit(solution)/shard_map/ppermute | solution.py:654
  7.3 1.2 copy-done
  8.5 1.2 copy-done.1
  9.7 0.9 copy-done.4
  10.7 0.9 copy-done.5
  11.6 0.7 copy-done.8
  12.2 0.7 copy-done.9
  12.9 0.4 fetch.1
  13.3 0.0 collective-permute-done.refs_4_
  13.3 0.0 collective-permute-done.1.refs_5_
  13.3 8.7 %forward.1 = (bf16[2,16,16,256]{3,2,1,0:T(8,128)(2,1)S(1)}, bf16[8,3,16,256]{3,2,1,0:T(8,128)(2,1)S(1)}, f32[4,528,128]{2,1,0:T(8,128)S(1)}, f32[4,256,128]{2,1,...) custom-call(s32[4,2,32]{2,1,0:T(2,128)S(1)} %bitcast.32, ...), custom_call_target="tpu_custom_call" | custom-call | bytes 30450000 | tf_op jit(solution)/shard_map/forward/pallas_call | solution.py:630
  22.0 0.1 collective-permute-start.2
  22.1 4.4 %collective-permute-start.3 = (bf16[8,3,16,256]{3,2,1,0:T(8,128)(2,1)S(1)}, bf16[8,3,16,256]{3,2,1,0:T(8,128)(2,1)S(1)}, u32[]{:S(2)}, u32[]{:S(2)}) collective-permute-start(bf16[8,3,16,256]{3,2,1,0:T(8,128)(2,1)S(1)} %get-tuple-element.72.refs_3_), channel_id=1, source_target_pairs={{0,15},{1,0},{2,1},{3,2},{4,3},{5,4},{6,5},{7,6},{8,7},{9,8},{10,9... | collective-permute-start | bytes 589832 | tf_op jit(solution)/shard_map/ppermute | solution.py:654
  26.5 3.3 %collective-permute-done.2.refs_4_ = bf16[8,3,16,256]{3,2,1,0:T(8,128)(2,1)S(1)} collective-permute-done((bf16[8,3,16,256]{3,2,1,0:T(8,128)(2,1)S(1)}, bf16[8,3,16,256]{3,2,1,0:T(8,128)(2,1)S(1)}, u32[]{:S(2)}, u32[]{:S(2)}) %collective-permute-start.2) | collective-permute-done | bytes 196640 | tf_op jit(solution)/shard_map/ppermute | solution.py:654
  29.9 0.0 collective-permute-done.3.refs_5_
  29.9 15.5 %turn.1 = (bf16[2,16,16,256]{3,2,1,0:T(8,128)(2,1)}, f32[4,256,128]{2,1,0:T(8,128)S(1)}, f32[8,3,2,16,128]{4,3,2,1,0:T(8,128)S(1)}, bf16[8,3,16,256]{3,2,1,0:T(8...) custom-call(s32[4,2,32]{2,1,0:T(2,128)S(1)} %bitcast.33, ...), custom_call_target="tpu_custom_call" | custom-call | bytes 53900000 | tf_op jit(solution)/shard_map/turn/pallas_call | solution.py:630
  45.4 0.1 collective-permute-start.4
  45.4 4.7 %collective-permute-start.5 = (bf16[8,3,16,256]{3,2,1,0:T(8,128)(2,1)S(1)}, bf16[8,3,16,256]{3,2,1,0:T(8,128)(2,1)S(1)}, u32[]{:S(2)}, u32[]{:S(2)}) collective-permute-start(bf16[8,3,16,256]{3,2,1,0:T(8,128)(2,1)S(1)} %get-tuple-element.78), channel_id=1, source_target_pairs={{0,15},{1,0},{2,1},{3,2},{4,3},{5,4},{6,5},{7,6},{8,7},{9,8},{10,9... | collective-permute-start | bytes 589832 | tf_op jit(solution)/shard_map/ppermute | solution.py:654
  50.1 3.1 %weights.1 = (bf16[1024,256]{1,0:T(8,128)(2,1)S(1)}, bf16[1024,256]{1,0:T(8,128)(2,1)S(1)}, f32[64,256]{1,0:T(8,128)S(1)}) custom-call(f32[4,528,128]{2,1,0:T(8,128)S(1)} %get-tuple-element.97.refs_0_, f32[4,512,128]{2,1,0:T(8,128)S(1)} %get-tuple-element.98.refs_1_, bf16[512,256]{1,0:T(8,128)(2,1)S(1)} %get-tuple-element.99.refs_2_, ...), custom_call_target="tpu_custom_call" | custom-call | bytes 9800000 | tf_op jit(solution)/shard_map/weights/pallas_call | solution.py:630
  53.2 0.1 collective-permute-start.12
  53.3 0.0 collective-permute-done.5.refs_3_
  53.3 2.3 %backward.1 = (bf16[1024,256]{1,0:T(8,128)(2,1)S(1)}, bf16[1024,256]{1,0:T(8,128)(2,1)S(1)}, f32[4,256,128]{2,1,0:T(8,128)S(1)}, bf16[512,1024]{1,0:T(8,128)(2,1)S(1)}, f32[16,256]{1,0:T(8,128)S(1)}) custom-call(f32[4,256,128]{2,1,0:T(8,128)S(1)} %get-tuple-element.75.refs_0_, f32[8,3,2,16,128]{4,3,2,1,0:T(8,128)S(1)} %get-tuple-element.76.refs_1_, ...), custom_call_target="tpu_custom_call" | custom-call | bytes 10150000 | tf_op jit(solution)/shard_map/backward/pallas_call | solution.py:630
  55.6 0.5 collective-permute-start.6
  56.1 0.1 share_near.3
  56.3 0.1 collective-permute-start.13
  56.3 0.1 collective-permute-start.14
  56.4 3.4 %collective-permute-start.15 = (bf16[256,256]{1,0:T(8,128)(2,1)S(1)}, bf16[256,256]{1,0:T(8,128)(2,1)S(1)}, u32[]{:S(2)}, u32[]{:S(2)}) collective-permute-start(bf16[256,256]{1,0:T(8,128)(2,1)S(1)} %get-tuple-element.110), channel_id=1, source_target_pairs={{0,6},{1,7},{2,4},{3,5},{4,2},{5,3},{6,0},{7,1},{8,14},{9,15},{10,... | collective-permute-start | bytes 393224 | tf_op jit(solution)/shard_map/ppermute | solution.py:667
  59.8 0.1 share_near.2
  59.9 0.1 collective-permute-start.9
  60.1 0.5 collective-permute-start.10
  60.6 1.2 %collective-permute-done.13 = bf16[256,256]{1,0:T(8,128)(2,1)S(1)} collective-permute-done((bf16[256,256]{1,0:T(8,128)(2,1)S(1)}, bf16[256,256]{1,0:T(8,128)(2,1)S(1)}, u32[]{:S(2)}, u32[]{:S(2)}) %collective-permute-start.13) | collective-permute-done | bytes 131104 | tf_op jit(solution)/shard_map/ppermute | solution.py:667
  61.8 1.7 %collective-permute-start.11 = (bf16[256,256]{1,0:T(8,128)(2,1)S(1)}, bf16[256,256]{1,0:T(8,128)(2,1)S(1)}, u32[]{:S(2)}, u32[]{:S(2)}) collective-permute-start(bf16[256,256]{1,0:T(8,128)(2,1)S(1)} %get-tuple-element.96), channel_id=1, source_target_pairs={{0,6},{1,7},{2,4},{3,5},{4,2},{5,3},{6,0},{7,1},{8,14},{9,15},{10,... | collective-permute-start | bytes 393224 | tf_op jit(solution)/shard_map/ppermute | solution.py:667
  63.5 5.9 %spread.1 = (f32[4,256,128]{2,1,0:T(8,128)S(1)}, f32[8,3,2,16,128]{4,3,2,1,0:T(8,128)S(1)}, bf16[8,3,16,256]{3,2,1,0:T(8,128)(2,1)S(1)}, bf16[8,3,16,256]{3,2,1,...) custom-call(s32[4,2,32]{2,1,0:T(2,128)S(1)} %bitcast.34, s32[4,2,32]{2,1,0:T(2,128)S(1)} %bitcast.37, ...), custom_call_target="tpu_custom_call" | custom-call | bytes 21000000 | tf_op jit(solution)/shard_map/spread/pallas_call | solution.py:630
  69.5 1.9 %collective-permute-done.11 = bf16[256,256]{1,0:T(8,128)(2,1)S(1)} collective-permute-done((bf16[256,256]{1,0:T(8,128)(2,1)S(1)}, bf16[256,256]{1,0:T(8,128)(2,1)S(1)}, u32[]{:S(2)}, u32[]{:S(2)}) %collective-permute-start.11) | collective-permute-done | bytes 131104 | tf_op jit(solution)/shard_map/ppermute | solution.py:667
  71.4 0.1 share_far.1
  71.5 2.3 %collective-permute-start.16 = (bf16[2,128,256]{2,1,0:T(8,128)(2,1)S(1)}, bf16[2,128,256]{2,1,0:T(8,128)(2,1)S(1)}, u32[]{:S(2)}, u32[]{:S(2)}) collective-permute-start(bf16[2,128,256]{2,1,0:T(8,128)(2,1)S(1)} %get-tuple-element.113), channel_id=1, source_target_pairs={{0,8},{1,9},{2,10},{3,11},{4,12},{5,13},{6,14},{7,15},{8,0},{9,1},... | collective-permute-start | bytes 393224 | tf_op jit(solution)/shard_map/ppermute | solution.py:667
  73.8 4.4 %collective-permute-start.8 = (bf16[8,3,16,256]{3,2,1,0:T(8,128)(2,1)S(1)}, bf16[8,3,16,256]{3,2,1,0:T(8,128)(2,1)S(1)}, u32[]{:S(2)}, u32[]{:S(2)}) collective-permute-start(bf16[8,3,16,256]{3,2,1,0:T(8,128)(2,1)S(1)} %get-tuple-element.93), channel_id=1, source_target_pairs={{0,15},{1,0},{2,1},{3,2},{4,3},{5,4},{6,5},{7,6},{8,7},{9,8},{10,9... | collective-permute-start | bytes 589832 | tf_op jit(solution)/shard_map/ppermute | solution.py:654
  78.3 1.3 %collective-permute-done.16.refs_1_ = bf16[2,128,256]{2,1,0:T(8,128)(2,1)S(1)} collective-permute-done((bf16[2,128,256]{2,1,0:T(8,128)(2,1)S(1)}, bf16[2,128,256]{2,1,0:T(8,128)(2,1)S(1)}, u32[]{:S(2)}, u32[]{:S(2)}) %collective-permute-start.16) | collective-permute-done | bytes 131104 | tf_op jit(solution)/shard_map/ppermute | solution.py:667
  79.6 0.3 collective-permute-start.17
  79.9 1.9 %collective-permute-done.7.refs_2_ = bf16[8,3,16,256]{3,2,1,0:T(8,128)(2,1)S(1)} collective-permute-done((bf16[8,3,16,256]{3,2,1,0:T(8,128)(2,1)S(1)}, bf16[8,3,16,256]{3,2,1,0:T(8,128)(2,1)S(1)}, u32[]{:S(2)}, u32[]{:S(2)}) %collective-permute-start.7) | collective-permute-done | bytes 196640 | tf_op jit(solution)/shard_map/ppermute | solution.py:654
  81.8 0.7 collective-permute-done.8.refs_3_
  82.4 0.9 last.1.refs_2_
  83.4 4.2 %collective-permute-done.17.refs_1_ = bf16[2,128,256]{2,1,0:T(8,128)(2,1)S(1)} collective-permute-done((bf16[2,128,256]{2,1,0:T(8,128)(2,1)S(1)}, bf16[2,128,256]{2,1,0:T(8,128)(2,1)S(1)}, u32[]{:S(2)}, u32[]{:S(2)}) %collective-permute-start.17) | collective-permute-done | bytes 131104 | tf_op jit(solution)/shard_map/ppermute | solution.py:660
  87.6 0.9 copy-done.3
  88.6 2.0 %collective-permute-start.18 = (bf16[2,2,128,256]{3,2,1,0:T(8,128)(2,1)S(1)}, bf16[2,2,128,256]{3,2,1,0:T(8,128)(2,1)S(1)}, u32[]{:S(2)}, u32[]{:S(2)}) collective-permute-start(bf16[2,2,128,256]{3,2,1,0:T(8,128)(2,1)S(1)} %order_far.1.refs_0_), channel_id=1, source_target_pairs={{0,2},{1,3},{2,0},{3,1},{4,6},{5,7},{6,4},{7,5},{8,10},{9,11},{10,... | collective-permute-start | bytes 786440 | tf_op jit(solution)/shard_map/ppermute | solution.py:660
  90.6 1.5 %collective-permute-start.20 = (bf16[2,2,128,256]{3,2,1,0:T(8,128)(2,1)S(1)}, bf16[2,2,128,256]{3,2,1,0:T(8,128)(2,1)S(1)}, u32[]{:S(2)}, u32[]{:S(2)}) collective-permute-start(bf16[2,2,128,256]{3,2,1,0:T(8,128)(2,1)S(1)} %order_far.1.refs_0_), channel_id=1, source_target_pairs={{0,6},{1,7},{2,4},{3,5},{4,2},{5,3},{6,0},{7,1},{8,14},{9,15},{10,... | collective-permute-start | bytes 786440 | tf_op jit(solution)/shard_map/ppermute | solution.py:660
  92.2 5.2 %collective-permute-done.18.refs_1_ = bf16[2,2,128,256]{3,2,1,0:T(8,128)(2,1)S(1)} collective-permute-done((bf16[2,2,128,256]{3,2,1,0:T(8,128)(2,1)S(1)}, bf16[2,2,128,256]{3,2,1,0:T(8,128)(2,1)S(1)}, u32[]{:S(2)}, u32[]{:S(2)}) %collective-permute-start.18) | collective-permute-done | bytes 262176 | tf_op jit(solution)/shard_map/ppermute | solution.py:660
  97.4 1.6 %collective-permute-done.19.refs_2_ = bf16[2,2,128,256]{3,2,1,0:T(8,128)(2,1)S(1)} collective-permute-done((bf16[2,2,128,256]{3,2,1,0:T(8,128)(2,1)S(1)}, bf16[2,2,128,256]{3,2,1,0:T(8,128)(2,1)S(1)}, u32[]{:S(2)}, u32[]{:S(2)}) %collective-permute-start.19) | collective-permute-done | bytes 262176 | tf_op jit(solution)/shard_map/ppermute | solution.py:660
  98.9 3.9 %collective-permute-done.20.refs_3_ = bf16[2,2,128,256]{3,2,1,0:T(8,128)(2,1)S(1)} collective-permute-done((bf16[2,2,128,256]{3,2,1,0:T(8,128)(2,1)S(1)}, bf16[2,2,128,256]{3,2,1,0:T(8,128)(2,1)S(1)}, u32[]{:S(2)}, u32[]{:S(2)}) %collective-permute-start.20) | collective-permute-done | bytes 262176 | tf_op jit(solution)/shard_map/ppermute | solution.py:660
  102.8 0.1 order_near.1
  102.9 0.1 collective-permute-start.21
  103.0 2.1 %taps.1.refs_0_ = bf16[128,256]{1,0:T(8,128)(2,1)S(1)} custom-call(f32[4,528,128]{2,1,0:T(8,128)S(1)} %get-tuple-element.114.refs_0_, f32[4,512,128]{2,1,0:T(8,128)S(1)} %get-tuple-element.115.refs_1_, f32[16,256]{1,0:T(8,128)S(1)} %get-tuple-element.111.refs_8_.refs_2_, f32[16,256]{1,0:T(8,128)S(1)} %get-tuple-element.116.refs_3_, ...), custom_call_target="tpu_custom_call" | custom-call | bytes 7350000 | tf_op jit(solution)/shard_map/taps/pallas_call | solution.py:630
  105.0 0.6 collective-permute-start.22
  105.6 0.9 collective-permute-done.22.refs_1_
  106.5 0.5 collective-permute-start.23
  107.0 3.9 %collective-permute-done.23.refs_1_ = bf16[128,256]{1,0:T(8,128)(2,1)S(1)} collective-permute-done((bf16[128,256]{1,0:T(8,128)(2,1)S(1)}, bf16[128,256]{1,0:T(8,128)(2,1)S(1)}, u32[]{:S(2)}, u32[]{:S(2)}) %collective-permute-start.23) | collective-permute-done | bytes 65568 | tf_op jit(solution)/shard_map/ppermute | solution.py:660
  111.0 1.5 %collective-permute-start.24 = (bf16[128,256]{1,0:T(8,128)(2,1)S(1)}, bf16[128,256]{1,0:T(8,128)(2,1)S(1)}, u32[]{:S(2)}, u32[]{:S(2)}) collective-permute-start(bf16[128,256]{1,0:T(8,128)(2,1)S(1)} %total_small.5.refs_0_), channel_id=1, source_target_pairs={{0,4},{1,5},{2,6},{3,7},{4,0},{5,1},{6,2},{7,3},{8,12},{9,13},{10,... | collective-permute-start | bytes 196616 | tf_op jit(solution)/shard_map/ppermute | solution.py:660
  112.4 2.9 %collective-permute-done.24.refs_1_ = bf16[128,256]{1,0:T(8,128)(2,1)S(1)} collective-permute-done((bf16[128,256]{1,0:T(8,128)(2,1)S(1)}, bf16[128,256]{1,0:T(8,128)(2,1)S(1)}, u32[]{:S(2)}, u32[]{:S(2)}) %collective-permute-start.24) | collective-permute-done | bytes 65568 | tf_op jit(solution)/shard_map/ppermute | solution.py:660
  115.3 3.1 %collective-permute-start.25 = (bf16[128,256]{1,0:T(8,128)(2,1)S(1)}, bf16[128,256]{1,0:T(8,128)(2,1)S(1)}, u32[]{:S(2)}, u32[]{:S(2)}) collective-permute-start(bf16[128,256]{1,0:T(8,128)(2,1)S(1)} %total_small.6.refs_0_), channel_id=1, source_target_pairs={{0,8},{1,9},{2,10},{3,11},{4,12},{5,13},{6,14},{7,15},{8,0},{9,1},... | collective-permute-start | bytes 196616 | tf_op jit(solution)/shard_map/ppermute | solution.py:660
  118.4 2.2 %collective-permute-done.25.refs_1_ = bf16[128,256]{1,0:T(8,128)(2,1)S(1)} collective-permute-done((bf16[128,256]{1,0:T(8,128)(2,1)S(1)}, bf16[128,256]{1,0:T(8,128)(2,1)S(1)}, u32[]{:S(2)}, u32[]{:S(2)}) %collective-permute-start.25) | collective-permute-done | bytes 65568 | tf_op jit(solution)/shard_map/ppermute | solution.py:660
  120.7 2.8 %unpack.1 = (f32[2,256,1024]{2,1,0:T(8,128)}, f32[2,1024,256]{2,1,0:T(8,128)}, f32[7,7,2,256]{3,2,1,0:T(2,128)}, f32[2,256]{1,0:T(2,128)}, f32[2,256]{1,0:T(2,128)}) custom-call(bf16[8,2,128,256]{3,2,1,0:T(8,128)(2,1)S(1)} %bitcast.18, bf16[8,2,128,256]{3,2,1,0:T(8,128)(2,1)S(1)} %collective-permute-done.21.refs_1_, bf16[128,256]{1,0:T(8,128)(2,1)S(1)} %total_small.7.refs_2_), custom_call_target="tpu_custom_call" | custom-call | bytes 9450000 | tf_op jit(solution)/shard_map/unpack/pallas_call | solution.py:630
  (28 shorter events, 0.2 us)
Async XLA Ops:
  0.6 1.0 copy-start.2
  1.6 11.7 %copy-start.6 = (s32[32,4,2]{0,2,1:T(2,128)S(1)}, s32[32,4,2]{0,2,1:T(2,128)}, u32[]{:S(2)}) copy-start(s32[32,4,2]{0,2,1:T(2,128)} %param.16) | copy-start | bytes 3076
  1.6 11.7 %copy-start.7 = (s32[32,4,2]{0,2,1:T(2,128)S(1)}, s32[32,4,2]{0,2,1:T(2,128)}, u32[]{:S(2)}) copy-start(s32[32,4,2]{0,2,1:T(2,128)} %param.17) | copy-start | bytes 3076
  1.7 11.6 %collective-permute-start = (bf16[8,3,16,256]{3,2,1,0:T(8,128)(2,1)S(1)}, bf16[8,3,16,256]{3,2,1,0:T(8,128)(2,1)S(1)}, u32[]{:S(2)}, u32[]{:S(2)}) collective-permute-start(bf16[8,3,16,256]{3,2,1,0:T(8,128)(2,1)S(1)} %strips.1.refs_7_.refs_3_), channel_id=1, source_target_pairs={{0,1},{1,2},{2,3},{3,4},{4,5},{5,6},{6,7},{7,8},{8,9},{9,10},{10,1... | collective-permute-start | bytes 589832 | tf_op jit(solution)/shard_map/ppermute | solution.py:654
  2.2 11.1 %collective-permute-start.1 = (bf16[8,3,16,256]{3,2,1,0:T(8,128)(2,1)S(1)}, bf16[8,3,16,256]{3,2,1,0:T(8,128)(2,1)S(1)}, u32[]{:S(2)}, u32[]{:S(2)}) collective-permute-start(bf16[8,3,16,256]{3,2,1,0:T(8,128)(2,1)S(1)} %strips.1.refs_7_.refs_3_), channel_id=1, source_target_pairs={{0,15},{1,0},{2,1},{3,2},{4,3},{5,4},{6,5},{7,6},{8,7},{9,8},{10,9... | collective-permute-start | bytes 589832 | tf_op jit(solution)/shard_map/ppermute | solution.py:654
  7.3 1.2 copy-start
  8.5 1.2 copy-start.1
  9.7 0.9 copy-start.4
  10.7 0.9 copy-start.5
  11.5 0.7 copy-start.8
  12.2 0.7 copy-start.9
  22.0 7.8 %collective-permute-start.2 = (bf16[8,3,16,256]{3,2,1,0:T(8,128)(2,1)S(1)}, bf16[8,3,16,256]{3,2,1,0:T(8,128)(2,1)S(1)}, u32[]{:S(2)}, u32[]{:S(2)}) collective-permute-start(bf16[8,3,16,256]{3,2,1,0:T(8,128)(2,1)S(1)} %get-tuple-element.72.refs_3_), channel_id=1, source_target_pairs={{0,1},{1,2},{2,3},{3,4},{4,5},{5,6},{6,7},{7,8},{8,9},{9,10},{10,1... | collective-permute-start | bytes 589832 | tf_op jit(solution)/shard_map/ppermute | solution.py:654
  22.1 7.8 %collective-permute-start.3 = (bf16[8,3,16,256]{3,2,1,0:T(8,128)(2,1)S(1)}, bf16[8,3,16,256]{3,2,1,0:T(8,128)(2,1)S(1)}, u32[]{:S(2)}, u32[]{:S(2)}) collective-permute-start(bf16[8,3,16,256]{3,2,1,0:T(8,128)(2,1)S(1)} %get-tuple-element.72.refs_3_), channel_id=1, source_target_pairs={{0,15},{1,0},{2,1},{3,2},{4,3},{5,4},{6,5},{7,6},{8,7},{9,8},{10,9... | collective-permute-start | bytes 589832 | tf_op jit(solution)/shard_map/ppermute | solution.py:654
  45.4 7.9 %collective-permute-start.4 = (bf16[8,3,16,256]{3,2,1,0:T(8,128)(2,1)S(1)}, bf16[8,3,16,256]{3,2,1,0:T(8,128)(2,1)S(1)}, u32[]{:S(2)}, u32[]{:S(2)}) collective-permute-start(bf16[8,3,16,256]{3,2,1,0:T(8,128)(2,1)S(1)} %get-tuple-element.77), channel_id=1, source_target_pairs={{0,1},{1,2},{2,3},{3,4},{4,5},{5,6},{6,7},{7,8},{8,9},{9,10},{10,1... | collective-permute-start | bytes 589832 | tf_op jit(solution)/shard_map/ppermute | solution.py:654
  45.4 7.9 %collective-permute-start.5 = (bf16[8,3,16,256]{3,2,1,0:T(8,128)(2,1)S(1)}, bf16[8,3,16,256]{3,2,1,0:T(8,128)(2,1)S(1)}, u32[]{:S(2)}, u32[]{:S(2)}) collective-permute-start(bf16[8,3,16,256]{3,2,1,0:T(8,128)(2,1)S(1)} %get-tuple-element.78), channel_id=1, source_target_pairs={{0,15},{1,0},{2,1},{3,2},{4,3},{5,4},{6,5},{7,6},{8,7},{9,8},{10,9... | collective-permute-start | bytes 589832 | tf_op jit(solution)/shard_map/ppermute | solution.py:654
  53.2 2.9 %collective-permute-start.12 = (bf16[1024,256]{1,0:T(8,128)(2,1)S(1)}, bf16[1024,256]{1,0:T(8,128)(2,1)S(1)}, u32[]{:S(2)}, u32[]{:S(2)}) collective-permute-start(bf16[1024,256]{1,0:T(8,128)(2,1)S(1)} %get-tuple-element.106), channel_id=1, source_target_pairs={{0,1},{1,0},{2,3},{3,2},{4,5},{5,4},{6,7},{7,6},{8,9},{9,8},{10,11... | collective-permute-start | bytes 1572872 | tf_op jit(solution)/shard_map/ppermute | solution.py:667
  55.6 4.2 %collective-permute-start.6 = (bf16[1024,256]{1,0:T(8,128)(2,1)S(1)}, bf16[1024,256]{1,0:T(8,128)(2,1)S(1)}, u32[]{:S(2)}, u32[]{:S(2)}) collective-permute-start(bf16[1024,256]{1,0:T(8,128)(2,1)S(1)} %get-tuple-element.88), channel_id=1, source_target_pairs={{0,1},{1,0},{2,3},{3,2},{4,5},{5,4},{6,7},{7,6},{8,9},{9,8},{10,11... | collective-permute-start | bytes 1572872 | tf_op jit(solution)/shard_map/ppermute | solution.py:667
  56.3 5.6 %collective-permute-start.13 = (bf16[256,256]{1,0:T(8,128)(2,1)S(1)}, bf16[256,256]{1,0:T(8,128)(2,1)S(1)}, u32[]{:S(2)}, u32[]{:S(2)}) collective-permute-start(bf16[256,256]{1,0:T(8,128)(2,1)S(1)} %get-tuple-element.108), channel_id=1, source_target_pairs={{0,2},{1,3},{2,0},{3,1},{4,6},{5,7},{6,4},{7,5},{8,10},{9,11},{10,... | collective-permute-start | bytes 393224 | tf_op jit(solution)/shard_map/ppermute | solution.py:667
  56.3 13.1 %collective-permute-start.14 = (bf16[256,256]{1,0:T(8,128)(2,1)S(1)}, bf16[256,256]{1,0:T(8,128)(2,1)S(1)}, u32[]{:S(2)}, u32[]{:S(2)}) collective-permute-start(bf16[256,256]{1,0:T(8,128)(2,1)S(1)} %get-tuple-element.109), channel_id=1, source_target_pairs={{0,4},{1,5},{2,6},{3,7},{4,0},{5,1},{6,2},{7,3},{8,12},{9,13},{10,... | collective-permute-start | bytes 393224 | tf_op jit(solution)/shard_map/ppermute | solution.py:667
  56.4 13.0 %collective-permute-start.15 = (bf16[256,256]{1,0:T(8,128)(2,1)S(1)}, bf16[256,256]{1,0:T(8,128)(2,1)S(1)}, u32[]{:S(2)}, u32[]{:S(2)}) collective-permute-start(bf16[256,256]{1,0:T(8,128)(2,1)S(1)} %get-tuple-element.110), channel_id=1, source_target_pairs={{0,6},{1,7},{2,4},{3,5},{4,2},{5,3},{6,0},{7,1},{8,14},{9,15},{10,... | collective-permute-start | bytes 393224 | tf_op jit(solution)/shard_map/ppermute | solution.py:667
  59.9 9.5 %collective-permute-start.9 = (bf16[256,256]{1,0:T(8,128)(2,1)S(1)}, bf16[256,256]{1,0:T(8,128)(2,1)S(1)}, u32[]{:S(2)}, u32[]{:S(2)}) collective-permute-start(bf16[256,256]{1,0:T(8,128)(2,1)S(1)} %get-tuple-element.94), channel_id=1, source_target_pairs={{0,2},{1,3},{2,0},{3,1},{4,6},{5,7},{6,4},{7,5},{8,10},{9,11},{10,... | collective-permute-start | bytes 393224 | tf_op jit(solution)/shard_map/ppermute | solution.py:667
  60.1 9.4 %collective-permute-start.10 = (bf16[256,256]{1,0:T(8,128)(2,1)S(1)}, bf16[256,256]{1,0:T(8,128)(2,1)S(1)}, u32[]{:S(2)}, u32[]{:S(2)}) collective-permute-start(bf16[256,256]{1,0:T(8,128)(2,1)S(1)} %get-tuple-element.95), channel_id=1, source_target_pairs={{0,4},{1,5},{2,6},{3,7},{4,0},{5,1},{6,2},{7,3},{8,12},{9,13},{10,... | collective-permute-start | bytes 393224 | tf_op jit(solution)/shard_map/ppermute | solution.py:667
  61.8 9.6 %collective-permute-start.11 = (bf16[256,256]{1,0:T(8,128)(2,1)S(1)}, bf16[256,256]{1,0:T(8,128)(2,1)S(1)}, u32[]{:S(2)}, u32[]{:S(2)}) collective-permute-start(bf16[256,256]{1,0:T(8,128)(2,1)S(1)} %get-tuple-element.96), channel_id=1, source_target_pairs={{0,6},{1,7},{2,4},{3,5},{4,2},{5,3},{6,0},{7,1},{8,14},{9,15},{10,... | collective-permute-start | bytes 393224 | tf_op jit(solution)/shard_map/ppermute | solution.py:667
  71.5 8.1 %collective-permute-start.16 = (bf16[2,128,256]{2,1,0:T(8,128)(2,1)S(1)}, bf16[2,128,256]{2,1,0:T(8,128)(2,1)S(1)}, u32[]{:S(2)}, u32[]{:S(2)}) collective-permute-start(bf16[2,128,256]{2,1,0:T(8,128)(2,1)S(1)} %get-tuple-element.113), channel_id=1, source_target_pairs={{0,8},{1,9},{2,10},{3,11},{4,12},{5,13},{6,14},{7,15},{8,0},{9,1},... | collective-permute-start | bytes 393224 | tf_op jit(solution)/shard_map/ppermute | solution.py:667
  73.8 8.0 %collective-permute-start.7 = (bf16[8,3,16,256]{3,2,1,0:T(8,128)(2,1)S(1)}, bf16[8,3,16,256]{3,2,1,0:T(8,128)(2,1)S(1)}, u32[]{:S(2)}, u32[]{:S(2)}) collective-permute-start(bf16[8,3,16,256]{3,2,1,0:T(8,128)(2,1)S(1)} %get-tuple-element.92), channel_id=1, source_target_pairs={{0,1},{1,2},{2,3},{3,4},{4,5},{5,6},{6,7},{7,8},{8,9},{9,10},{10,1... | collective-permute-start | bytes 589832 | tf_op jit(solution)/shard_map/ppermute | solution.py:654
  73.8 8.6 %collective-permute-start.8 = (bf16[8,3,16,256]{3,2,1,0:T(8,128)(2,1)S(1)}, bf16[8,3,16,256]{3,2,1,0:T(8,128)(2,1)S(1)}, u32[]{:S(2)}, u32[]{:S(2)}) collective-permute-start(bf16[8,3,16,256]{3,2,1,0:T(8,128)(2,1)S(1)} %get-tuple-element.93), channel_id=1, source_target_pairs={{0,15},{1,0},{2,1},{3,2},{4,3},{5,4},{6,5},{7,6},{8,7},{9,8},{10,9... | collective-permute-start | bytes 589832 | tf_op jit(solution)/shard_map/ppermute | solution.py:654
  79.6 8.0 %collective-permute-start.17 = (bf16[2,128,256]{2,1,0:T(8,128)(2,1)S(1)}, bf16[2,128,256]{2,1,0:T(8,128)(2,1)S(1)}, u32[]{:S(2)}, u32[]{:S(2)}) collective-permute-start(bf16[2,128,256]{2,1,0:T(8,128)(2,1)S(1)} %total.1.refs_0_), channel_id=1, source_target_pairs={{0,8},{1,9},{2,10},{3,11},{4,12},{5,13},{6,14},{7,15},{8,0},{9,1},... | collective-permute-start | bytes 393224 | tf_op jit(solution)/shard_map/ppermute | solution.py:660
  87.6 1.0 copy-start.3
  88.6 8.8 %collective-permute-start.18 = (bf16[2,2,128,256]{3,2,1,0:T(8,128)(2,1)S(1)}, bf16[2,2,128,256]{3,2,1,0:T(8,128)(2,1)S(1)}, u32[]{:S(2)}, u32[]{:S(2)}) collective-permute-start(bf16[2,2,128,256]{3,2,1,0:T(8,128)(2,1)S(1)} %order_far.1.refs_0_), channel_id=1, source_target_pairs={{0,2},{1,3},{2,0},{3,1},{4,6},{5,7},{6,4},{7,5},{8,10},{9,11},{10,... | collective-permute-start | bytes 786440 | tf_op jit(solution)/shard_map/ppermute | solution.py:660
  90.6 8.3 %collective-permute-start.19 = (bf16[2,2,128,256]{3,2,1,0:T(8,128)(2,1)S(1)}, bf16[2,2,128,256]{3,2,1,0:T(8,128)(2,1)S(1)}, u32[]{:S(2)}, u32[]{:S(2)}) collective-permute-start(bf16[2,2,128,256]{3,2,1,0:T(8,128)(2,1)S(1)} %order_far.1.refs_0_), channel_id=1, source_target_pairs={{0,4},{1,5},{2,6},{3,7},{4,0},{5,1},{6,2},{7,3},{8,12},{9,13},{10,... | collective-permute-start | bytes 786440 | tf_op jit(solution)/shard_map/ppermute | solution.py:660
  90.6 12.2 %collective-permute-start.20 = (bf16[2,2,128,256]{3,2,1,0:T(8,128)(2,1)S(1)}, bf16[2,2,128,256]{3,2,1,0:T(8,128)(2,1)S(1)}, u32[]{:S(2)}, u32[]{:S(2)}) collective-permute-start(bf16[2,2,128,256]{3,2,1,0:T(8,128)(2,1)S(1)} %order_far.1.refs_0_), channel_id=1, source_target_pairs={{0,6},{1,7},{2,4},{3,5},{4,2},{5,3},{6,0},{7,1},{8,14},{9,15},{10,... | collective-permute-start | bytes 786440 | tf_op jit(solution)/shard_map/ppermute | solution.py:660
  102.9 17.8 %collective-permute-start.21 = (bf16[8,2,128,256]{3,2,1,0:T(8,128)(2,1)S(1)}, bf16[8,2,128,256]{3,2,1,0:T(8,128)(2,1)S(1)}, u32[]{:S(2)}, u32[]{:S(2)}) collective-permute-start(bf16[8,2,128,256]{3,2,1,0:T(8,128)(2,1)S(1)} %bitcast.17), channel_id=1, source_target_pairs={{0,1},{1,0},{2,3},{3,2},{4,5},{5,4},{6,7},{7,6},{8,9},{9,8},{10,11... | collective-permute-start | bytes 3145736 | tf_op jit(solution)/shard_map/ppermute | solution.py:660
  105.0 1.5 %collective-permute-start.22 = (bf16[128,256]{1,0:T(8,128)(2,1)S(1)}, bf16[128,256]{1,0:T(8,128)(2,1)S(1)}, u32[]{:S(2)}, u32[]{:S(2)}) collective-permute-start(bf16[128,256]{1,0:T(8,128)(2,1)S(1)} %taps.1.refs_0_), channel_id=1, source_target_pairs={{0,1},{1,0},{2,3},{3,2},{4,5},{5,4},{6,7},{7,6},{8,9},{9,8},{10,11... | collective-permute-start | bytes 196616 | tf_op jit(solution)/shard_map/ppermute | solution.py:660
  106.5 4.4 %collective-permute-start.23 = (bf16[128,256]{1,0:T(8,128)(2,1)S(1)}, bf16[128,256]{1,0:T(8,128)(2,1)S(1)}, u32[]{:S(2)}, u32[]{:S(2)}) collective-permute-start(bf16[128,256]{1,0:T(8,128)(2,1)S(1)} %total_small.4.refs_0_), channel_id=1, source_target_pairs={{0,2},{1,3},{2,0},{3,1},{4,6},{5,7},{6,4},{7,5},{8,10},{9,11},{10,... | collective-permute-start | bytes 196616 | tf_op jit(solution)/shard_map/ppermute | solution.py:660
  111.0 4.3 %collective-permute-start.24 = (bf16[128,256]{1,0:T(8,128)(2,1)S(1)}, bf16[128,256]{1,0:T(8,128)(2,1)S(1)}, u32[]{:S(2)}, u32[]{:S(2)}) collective-permute-start(bf16[128,256]{1,0:T(8,128)(2,1)S(1)} %total_small.5.refs_0_), channel_id=1, source_target_pairs={{0,4},{1,5},{2,6},{3,7},{4,0},{5,1},{6,2},{7,3},{8,12},{9,13},{10,... | collective-permute-start | bytes 196616 | tf_op jit(solution)/shard_map/ppermute | solution.py:660
  115.3 5.3 %collective-permute-start.25 = (bf16[128,256]{1,0:T(8,128)(2,1)S(1)}, bf16[128,256]{1,0:T(8,128)(2,1)S(1)}, u32[]{:S(2)}, u32[]{:S(2)}) collective-permute-start(bf16[128,256]{1,0:T(8,128)(2,1)S(1)} %total_small.6.refs_0_), channel_id=1, source_target_pairs={{0,8},{1,9},{2,10},{3,11},{4,12},{5,13},{6,14},{7,15},{8,0},{9,1},... | collective-permute-start | bytes 196616 | tf_op jit(solution)/shard_map/ppermute | solution.py:660

commit v4 on v3

--- a/solution.py
+++ b/solution.py
@@ -420,7 +420,8 @@
         copy.wait()
 
 
-def strips_kernel(sz, cur, strips, flat):
+def strips_kernel(sz, cur, strips, held, flat):
+    held[...] = cur[...]
     for q in range(sz.tiles):
         for i in range(sz.edge):
             for h, part in enumerate(halves(cur[q, i].astype(F32))):
@@ -525,7 +526,8 @@
     both[SMALL_ROWS : 2 * SMALL_ROWS] = other[...].astype(BF16)
 
 
-def last_kernel(sz, base, own, first, second, out_hbm, flat, out, sems):
+def last_kernel(sz, base, own, first, second, out_hbm, token, flat, out, sems):
+    token[...] = jnp.zeros_like(token)
     add_strips(sz, base, own, first, second, flat)
     row = flat_grad_row(sz, flat)
     for q in range(sz.tiles):
@@ -564,56 +566,85 @@
 
 
 def total_kernel(*refs):
-    out = refs[-1]
-    if len(out.shape) == 2:
-        add_rows(out, [lambda rows, array=array: array[rows] for array in refs[:-1]])
-        return
-    for layer in range(out.shape[0]):
+    out, small = refs[-1], refs[-2]
+    for layer in range(2):
         add_rows(
             out.at[layer],
-            [lambda rows, array=array: array[layer, rows] for array in refs[:-1]],
+            [lambda rows, array=array: array[layer, rows] for array in refs[:-2]],
         )
-
-
-def order_kernel(level, *refs):
-    for k, piece in enumerate(refs[:-1]):
-        refs[-1][digit_of(level) ^ k] = piece[...]
-
-
-def unpack_kernel(
-    sz, mine, theirs, small, up_hbm, down_hbm, kernel_out, gain_out, scale_out, up, down, sems,
-):
-    even = digit_of(0) == 0
-    pieces, _, share, _ = mine.shape
+    out[2:] = small[...]
+
+
+def order_kernel(level, small_units, *refs):
+    pieces, out = refs[:-1], refs[-1]
+    units = pieces[0].shape[0] - small_units
+    for k, piece in enumerate(pieces):
+        at = (digit_of(level) ^ k) * units
+        for j in range(units):
+            out[at + j] = piece[j]
+    for j in range(small_units):
+        add_rows(
+            out.at[len(pieces) * units + j],
+            [lambda rows, piece=piece: piece[units + j, rows] for piece in pieces],
+        )
+
+
+def unpack_half(sz, half, source, staged, up_hbm, down_hbm, sems):
+    share = source.shape[1]
+    target = (down_hbm, up_hbm)[half]
+    pieces = sz.hidden // share
     copies = []
     for layer in range(2):
         for j in range(pieces):
-            start = j * share
-            down[layer, start : start + share] = jnp.where(
-                even, mine[j, layer], theirs[j, layer]
-            ).astype(F32)
-        copies.append((down.at[layer], down_hbm.at[layer]))
-        for j in range(pieces):
-            k, c = divmod(j * share, sz.channels)
-            up[layer, c : c + share, k * sz.channels : (k + 1) * sz.channels] = jnp.where(
-                even, theirs[j, layer], mine[j, layer]
-            ).astype(F32)
-        copies.append((up.at[layer], up_hbm.at[layer]))
-        for k in range(len(copies) - 2, len(copies)):
-            copies[k] = pltpu.make_async_copy(*copies[k], sems.at[k])
-            copies[k].start()
+            value = source[2 * j + layer].astype(F32)
+            if half == 0:
+                staged[layer, j * share : (j + 1) * share] = value
+            else:
+                k, c = divmod(j * share, sz.channels)
+                staged[layer, k * sz.channels + c : k * sz.channels + c + share] = value
+        for k in range(sz.hidden // sz.channels):
+            rows = pl.ds(k * sz.channels, sz.channels)
+            place = target.at[layer, rows] if half == 0 else target.at[layer, :, rows]
+            copy = pltpu.make_async_copy(
+                staged.at[layer, rows], place, sems.at[half, len(copies)]
+            )
+            copy.start()
+            copies.append(copy)
+    for copy in copies:
+        copy.wait()
+
+
+def unpack_mine_kernel(sz, mine, up_hbm, down_hbm, staged, sems):
+    for half in range(2):
+
+        @pl.when(digit_of(0) == half)
+        def _(half=half):
+            unpack_half(sz, half, mine, staged, up_hbm, down_hbm, sems)
+
+
+def unpack_theirs_kernel(
+    sz, mine, theirs, _up, _down, up_hbm, down_hbm, kernel_out, gain_out, scale_out,
+    staged, small, sems,
+):
+    for half in range(2):
+
+        @pl.when(digit_of(0) == 1 - half)
+        def _(half=half):
+            unpack_half(sz, half, theirs, staged, up_hbm, down_hbm, sems)
+
+    share = mine.shape[1]
+    start = 2 * sz.hidden // share
+    for j in range(start, mine.shape[0]):
+        rows = pl.ds((j - start) * share, share)
+        small[rows, :] = mine[j].astype(F32) + theirs[j].astype(F32)
     for layer in range(2):
         at = layer * SMALL_ROWS
         for a in range(TAPS):
-            part = small[at + a * 8 - a % 2 * 8 : at + a * 8 - a % 2 * 8 + 16].astype(F32)
-            part = part[a % 2 * 8 : a % 2 * 8 + 8]
             for b in range(TAPS):
-                kernel_out[a, b, layer : layer + 1] = part[b : b + 1]
-        last = small[at + SMALL_ROWS - 16 : at + SMALL_ROWS].astype(F32)
-        gain_out[layer : layer + 1] = last[8:9]
-        scale_out[layer : layer + 1] = last[9:10]
-    for copy in copies:
-        copy.wait()
+                kernel_out[a, b, layer : layer + 1] = small[pl.ds(at + a * 8 + b, 1), :]
+        at = at + TAPS * 8
+        gain_out[layer : layer + 1] = small[pl.ds(at, 1), :]
+        scale_out[layer : layer + 1] = small[pl.ds(at + 1, 1), :]
 
 
 IN_VMEM = pl.BlockSpec(memory_space=pltpu.VMEM)
@@ -621,7 +652,7 @@
 IN_HBM = pl.BlockSpec(memory_space=pltpu.HBM)
 
 
-def call(body, name, micros, ins, outs, scratch, after=()):
+def call(body, name, micros, ins, outs, scratch, after=(), aliases={}):
     count = len(ins)
 
     def run(*refs):
@@ -637,6 +668,7 @@
         cost_estimate=pl.CostEstimate(
             flops=0, bytes_accessed=int(micros * 3.5e6), transcendentals=0
         ),
+        input_output_aliases=aliases,
         name=name,
     )(*[array for _, array in ins], *after)
 
@@ -688,7 +720,7 @@
         )
         return [pieces[0]] + swap(pieces[1:], self.near_masks)
 
-    def finish(self, parts, after):
+    def finish(self, parts, after, small):
         quarter, channels = parts[0][0].shape
         dims = (self.rest, quarter // self.rest, channels)
         arrays = [part.reshape(dims) for layer in parts for part in layer]
@@ -698,36 +730,27 @@
             near(*arrays), near(*[shape] * self.rest), [], after,
         )
         arrived = swap(pieces[1:], self.rest_masks)
+        small = small(pieces[0]).reshape((-1,) + dims[1:])
+        shape = jax.ShapeDtypeStruct((2 + small.shape[0],) + dims[1:], BF16)
         (total,) = call(
-            total_kernel, "total", 0.4, near(pieces[0], *arrived), near(shape), []
+            total_kernel, "total", 0.4, near(pieces[0], *arrived, small), near(shape), []
         )
-        return pieces[0], total
-
-    def gather(self, total, after):
+        return total, small.shape[0]
+
+    def gather(self, total, small_units, after):
         for level, masks, name in (
             (2, self.rest_masks, "order_far"),
             (1, self.near_masks, "order_near"),
         ):
             pieces = [total] + partners(total, masks)
-            shape = jax.ShapeDtypeStruct((len(pieces),) + total.shape, BF16)
+            units = (total.shape[0] - small_units) * len(pieces) + small_units
+            shape = jax.ShapeDtypeStruct((units,) + total.shape[1:], BF16)
             (total,) = call(
-                functools.partial(order_kernel, level), name, 0.5,
+                functools.partial(order_kernel, level, small_units), name, 0.5,
                 near(*pieces), near(shape), [], after,
             )
             after = ()
-        total = total.reshape((4 * self.rest,) + total.shape[2:])
         return total, partners(total, [1])[0]
-
-    def whole(self, array):
-        mask = 1
-        while mask < self.devices:
-            shape = jax.ShapeDtypeStruct(array.shape, BF16)
-            (array,) = call(
-                total_kernel, "total_small", 0.3,
-                near(array, *partners(array, [mask])), near(shape), [],
-            )
-            mask *= 2
-        return array
 
 
 def on_device(
@@ -777,16 +800,16 @@
     def sems(count):
         return [pltpu.SemaphoreType.DMA((count,))]
 
-    (strips,) = call(
+    strips, inputs = call(
         functools.partial(strips_kernel, sz),
         "strips", 0.3,
         near(inputs),
-        near(strips_shape),
+        near(strips_shape, image),
         vmem(slabs),
     )
     below, above = pass_on(strips, 1), pass_on(strips, -1)
-    fetched = (inputs, out_grad, kern, gain, lscale, up, down)
-    inputs, out_grad, kern, gain, lscale, up, down = call(
+    fetched = (kern, gain, lscale, up, down)
+    kern, gain, lscale, up, down = call(
         fetch_kernel,
         "fetch", 2.0,
         far(*fetched),
@@ -846,33 +869,52 @@
         vmem(taps, narrow, grad_pool, padded),
         (parts_zero[0],),
     )
-    share, total = reduction.finish((parts_zero, parts_one), (gain_sums,))
     from_below, from_above = pass_on(grad_above, 1), pass_on(grad_below, -1)
-    (small_both,) = call(
-        functools.partial(taps_kernel, sz),
-        "taps", 2.1,
-        near(pad_zero, grad_conv, gain_sums, scale_sums, small_one),
-        near(shape((2 * SMALL_ROWS, channels), BF16)),
-        vmem(tap_sums, small),
-        (share,),
-    )
-    (in_grad,) = call(
+
+    def small_gradients(share):
+        (both,) = call(
+            functools.partial(taps_kernel, sz),
+            "taps", 2.1,
+            near(pad_zero, grad_conv, gain_sums, scale_sums, small_one),
+            near(shape((2 * SMALL_ROWS, channels), BF16)),
+            vmem(tap_sums, small),
+            (share,),
+        )
+        return both
+
+    total, small_units = reduction.finish(
+        (parts_zero, parts_one), (gain_sums,), small_gradients
+    )
+    in_grad, token = call(
         functools.partial(last_kernel, sz),
         "last", 1.0,
         near(base, grad_own, from_below, from_above),
-        far(image),
+        far(image) + near(shape((8, LANES), F32)),
         vmem(slabs, image) + sems(1),
     )
+    mine, theirs = reduction.gather(total, small_units, (token,))
+    weight_shapes = [shape(up_weight.shape, F32), shape(down_weight.shape, F32)]
+    copies = layers * hidden // channels
+    scratch = vmem(shape(down_weight.shape, F32))
+    grad_up, grad_down = call(
+        functools.partial(unpack_mine_kernel, sz),
+        "unpack_mine", 1.5,
+        near(mine),
+        far(*weight_shapes),
+        scratch + [pltpu.SemaphoreType.DMA((2, copies))],
+    )
     grad_up, grad_down, grad_kernel, grad_gain, grad_scale = call(
-        functools.partial(unpack_kernel, sz),
-        "unpack", 2.7,
-        near(*reduction.gather(total, (in_grad,)), reduction.whole(small_both)),
-        far(shape(up_weight.shape, F32), shape(down_weight.shape, F32))
+        functools.partial(unpack_theirs_kernel, sz),
+        "unpack_theirs", 1.5,
+        near(mine, theirs) + far(grad_up, grad_down),
+        far(*weight_shapes)
         + near(
-            shape(kern.shape, F32), shape(norm_gain.shape, F32),
-            shape(norm_gain.shape, F32),
+            shape(kern.shape, F32), shape(norm_gain.shape, F32), shape(norm_gain.shape, F32)
         ),
-        vmem(shape(up_weight.shape, F32), shape(down_weight.shape, F32)) + sems(4),
+        scratch
+        + vmem(shape((2 * SMALL_ROWS, channels), F32))
+        + [pltpu.SemaphoreType.DMA((2, copies))],
+        aliases={2: 0, 3: 1},
     )
     return (
         result, in_grad, grad_kernel.transpose((2, 0, 1, 3)),

time: 124 us -> 112 us (0.903)
  starting transfers between devices: 37.5 us -> 31.7 us
  waiting for transfers between devices: 35.2 us -> 30.1 us
  local copies, waits for them, and re-layouts: 7.55 us -> 5.66 us
    ppermute x9 -> x5, starting transfers between devices: 9.5 us -> 3.7 us  [partners(): lax.ppermute(array, 'tile', [(i, i ^ mask) for i in range(length)])]
    ppermute x9 -> x5, waiting for transfers between devices: 24.8 us -> 20.9 us  [partners(): lax.ppermute(array, 'tile', [(i, i ^ mask) for i in range(length)])]
    unnamed x20 -> x18, local copies, waits for them, and re-layouts: 7.55 us -> 5.66 us
    ppermute x9, waiting for transfers between devices: 4.46 us -> 3.17 us  [swap(): lax.ppermute(array, 'tile', [(i, i ^ mask) for i in range(length)])]
    pallas_call x20 -> x17, Pallas kernels: 42.3 us -> 43.2 us  [call(): pl.pallas_call(run, in_specs=[spec for spec, _ in ins] + [pl.BlockSpec(me...]
  transfers between devices with their start and end apart: 26 -> 22, of which waited for: 14 -> 10; matrix products, arithmetic and copies ran while one was open for 0% -> 0% of each run, Pallas kernels for 12% -> 15%
where the time goes in v4:
time: 112 us
  Pallas kernels  43.2 us (39%)
  starting transfers between devices  31.7 us (28%)
  waiting for transfers between devices  30.1 us (27%)
  local copies, waits for them, and re-layouts  5.66 us (5%)
    pallas_call x17, Pallas kernels, call(): pl.pallas_call(run, in_specs=[spec for spec, _ in ins] + [pl.BlockSpec(me...  43.2 us
    ppermute x5, waiting for transfers between devices, partners(): lax.ppermute(array, 'tile', [(i, i ^ mask) for i in range(length)])  20.9 us
    ppermute x8, starting transfers between devices, pass_on(): lax.ppermute(shard, 'tile', [(i, (i + by) % length) for i in range(length)])  19.2 us
    ppermute x9, starting transfers between devices, swap(): lax.ppermute(array, 'tile', [(i, i ^ mask) for i in range(length)])  8.78 us
    ppermute x8, waiting for transfers between devices, pass_on(): lax.ppermute(shard, 'tile', [(i, (i + by) % length) for i in range(length)])  6.03 us
    unnamed x18, local copies, waits for them, and re-layouts  5.66 us
    ppermute x5, starting transfers between devices, partners(): lax.ppermute(array, 'tile', [(i, i ^ mask) for i in range(length)])  3.7 us
    ppermute x9, waiting for transfers between devices, swap(): lax.ppermute(array, 'tile', [(i, i ^ mask) for i in range(length)])  3.17 us
  transfers between devices with their start and end apart: 22, of which 10 were waited for; matrix products, arithmetic and copies ran while one was open for 0% of the time, Pallas kernels for 15%

profile of v4, /device:TPU:0, one launch (start us, length us, event | category | flops | bytes accessed | tf_op | source)
XLA Modules:
  0.0 111.7 jit_solution(15566286025888363532)
XLA Ops:
  0.6 0.9 copy-done.3
  1.6 0.1 strips.1
  1.7 0.5 collective-permute-start
  2.2 5.1 %collective-permute-start.1 = (bf16[8,3,16,256]{3,2,1,0:T(8,128)(2,1)S(1)}, bf16[8,3,16,256]{3,2,1,0:T(8,128)(2,1)S(1)}, u32[]{:S(2)}, u32[]{:S(2)}) collective-permute-start(bf16[8,3,16,256]{3,2,1,0:T(8,128)(2,1)S(1)} %get-tuple-element.70.refs_5_.refs_3_), channel_id=1, source_target_pairs={{0,15},{1,0},{2,1},{3,2},{4,3},{5,4},{6,5},{7,6},{8,7},{9,8},{10,9... | collective-permute-start | bytes 589832 | tf_op jit(solution)/shard_map/ppermute | solution.py:686
  7.3 1.2 %copy-done = bf16[2,256,1024]{2,1,0:T(8,128)(2,1)S(1)} copy-done((bf16[2,256,1024]{2,1,0:T(8,128)(2,1)S(1)}, bf16[2,256,1024]{2,1,0:T(8,128)(2,1)}, u32[]{:S(2)}) %copy-start) | copy-done | bytes 1048600
  8.5 1.2 %copy-done.1 = bf16[2,1024,256]{2,1,0:T(8,128)(2,1)S(1)} copy-done((bf16[2,1024,256]{2,1,0:T(8,128)(2,1)S(1)}, bf16[2,1024,256]{2,1,0:T(8,128)(2,1)}, u32[]{:S(2)}) %copy-start.1) | copy-done | bytes 1048600
  9.7 0.9 copy-done.4
  10.6 0.7 copy-done.7
  11.3 0.7 copy-done.8
  12.0 0.3 fetch.1
  12.3 0.0 copy-start.2
  12.3 0.0 collective-permute-done.refs_4_
  12.3 0.0 collective-permute-done.1.refs_5_
  12.3 8.7 %forward.1 = (bf16[2,16,16,256]{3,2,1,0:T(8,128)(2,1)S(1)}, bf16[8,3,16,256]{3,2,1,0:T(8,128)(2,1)S(1)}, f32[4,528,128]{2,1,0:T(8,128)S(1)}, f32[4,256,128]{2,1,...) custom-call(s32[4,2,32]{2,1,0:T(2,128)S(1)} %bitcast.31, ...), custom_call_target="tpu_custom_call" | custom-call | bytes 30450000 | tf_op jit(solution)/shard_map/forward/pallas_call | solution.py:661
  21.0 0.1 collective-permute-start.2
  21.1 4.4 %collective-permute-start.3 = (bf16[8,3,16,256]{3,2,1,0:T(8,128)(2,1)S(1)}, bf16[8,3,16,256]{3,2,1,0:T(8,128)(2,1)S(1)}, u32[]{:S(2)}, u32[]{:S(2)}) collective-permute-start(bf16[8,3,16,256]{3,2,1,0:T(8,128)(2,1)S(1)} %get-tuple-element.77.refs_3_), channel_id=1, source_target_pairs={{0,15},{1,0},{2,1},{3,2},{4,3},{5,4},{6,5},{7,6},{8,7},{9,8},{10,9... | collective-permute-start | bytes 589832 | tf_op jit(solution)/shard_map/ppermute | solution.py:686
  25.5 3.3 %collective-permute-done.2.refs_4_ = bf16[8,3,16,256]{3,2,1,0:T(8,128)(2,1)S(1)} collective-permute-done((bf16[8,3,16,256]{3,2,1,0:T(8,128)(2,1)S(1)}, bf16[8,3,16,256]{3,2,1,0:T(8,128)(2,1)S(1)}, u32[]{:S(2)}, u32[]{:S(2)}) %collective-permute-start.2) | collective-permute-done | bytes 196640 | tf_op jit(solution)/shard_map/ppermute | solution.py:686
  28.8 0.0 collective-permute-done.3.refs_5_
  28.9 15.5 %turn.1 = (bf16[2,16,16,256]{3,2,1,0:T(8,128)(2,1)}, f32[4,256,128]{2,1,0:T(8,128)S(1)}, f32[8,3,2,16,128]{4,3,2,1,0:T(8,128)S(1)}, bf16[8,3,16,256]{3,2,1,0:T(8...) custom-call(s32[4,2,32]{2,1,0:T(2,128)S(1)} %bitcast.32, ...), custom_call_target="tpu_custom_call" | custom-call | bytes 53900000 | tf_op jit(solution)/shard_map/turn/pallas_call | solution.py:661
  44.4 0.1 collective-permute-start.4
  44.4 4.7 %collective-permute-start.5 = (bf16[8,3,16,256]{3,2,1,0:T(8,128)(2,1)S(1)}, bf16[8,3,16,256]{3,2,1,0:T(8,128)(2,1)S(1)}, u32[]{:S(2)}, u32[]{:S(2)}) collective-permute-start(bf16[8,3,16,256]{3,2,1,0:T(8,128)(2,1)S(1)} %get-tuple-element.82), channel_id=1, source_target_pairs={{0,15},{1,0},{2,1},{3,2},{4,3},{5,4},{6,5},{7,6},{8,7},{9,8},{10,9... | collective-permute-start | bytes 589832 | tf_op jit(solution)/shard_map/ppermute | solution.py:686
  49.1 3.1 %weights.1 = (bf16[1024,256]{1,0:T(8,128)(2,1)S(1)}, bf16[1024,256]{1,0:T(8,128)(2,1)S(1)}, f32[64,256]{1,0:T(8,128)S(1)}) custom-call(f32[4,528,128]{2,1,0:T(8,128)S(1)} %get-tuple-element.102.refs_0_, f32[4,512,128]{2,1,0:T(8,128)S(1)} %get-tuple-element.103.refs_1_, bf16[512,256]{1,0:T(8,128)(2,1)S(1)} %get-tuple-element.104.refs_2_, ...), custom_call_target="tpu_custom_call" | custom-call | bytes 9800000 | tf_op jit(solution)/shard_map/weights/pallas_call | solution.py:661
  52.2 0.1 collective-permute-start.12
  52.3 0.0 collective-permute-done.4.refs_2_
  52.3 0.0 collective-permute-done.5.refs_3_
  52.3 2.2 %backward.1 = (bf16[1024,256]{1,0:T(8,128)(2,1)S(1)}, bf16[1024,256]{1,0:T(8,128)(2,1)S(1)}, f32[4,256,128]{2,1,0:T(8,128)S(1)}, bf16[512,1024]{1,0:T(8,128)(2,1)S(1)}, f32[16,256]{1,0:T(8,128)S(1)}) custom-call(f32[4,256,128]{2,1,0:T(8,128)S(1)} %get-tuple-element.79.refs_0_, f32[8,3,2,16,128]{4,3,2,1,0:T(8,128)S(1)} %get-tuple-element.80.refs_1_, ...), custom_call_target="tpu_custom_call" | custom-call | bytes 10150000 | tf_op jit(solution)/shard_map/backward/pallas_call | solution.py:661
  54.5 0.5 collective-permute-start.6
  55.1 0.0 collective-permute-done.12
  55.1 0.1 share_near.3
  55.2 0.1 collective-permute-start.13
  55.3 0.1 collective-permute-start.14
  55.4 3.4 %collective-permute-start.15 = (bf16[256,256]{1,0:T(8,128)(2,1)S(1)}, bf16[256,256]{1,0:T(8,128)(2,1)S(1)}, u32[]{:S(2)}, u32[]{:S(2)}) collective-permute-start(bf16[256,256]{1,0:T(8,128)(2,1)S(1)} %get-tuple-element.115), channel_id=1, source_target_pairs={{0,6},{1,7},{2,4},{3,5},{4,2},{5,3},{6,0},{7,1},{8,14},{9,15},{10,... | collective-permute-start | bytes 393224 | tf_op jit(solution)/shard_map/ppermute | solution.py:699
  58.8 0.1 share_near.2
  58.9 0.1 collective-permute-start.9
  59.0 0.5 collective-permute-start.10
  59.5 1.2 %collective-permute-done.13 = bf16[256,256]{1,0:T(8,128)(2,1)S(1)} collective-permute-done((bf16[256,256]{1,0:T(8,128)(2,1)S(1)}, bf16[256,256]{1,0:T(8,128)(2,1)S(1)}, u32[]{:S(2)}, u32[]{:S(2)}) %collective-permute-start.13) | collective-permute-done | bytes 131104 | tf_op jit(solution)/shard_map/ppermute | solution.py:699
  60.8 1.7 %collective-permute-start.11 = (bf16[256,256]{1,0:T(8,128)(2,1)S(1)}, bf16[256,256]{1,0:T(8,128)(2,1)S(1)}, u32[]{:S(2)}, u32[]{:S(2)}) collective-permute-start(bf16[256,256]{1,0:T(8,128)(2,1)S(1)} %get-tuple-element.101), channel_id=1, source_target_pairs={{0,6},{1,7},{2,4},{3,5},{4,2},{5,3},{6,0},{7,1},{8,14},{9,15},{10,... | collective-permute-start | bytes 393224 | tf_op jit(solution)/shard_map/ppermute | solution.py:699
  62.5 5.9 %spread.1 = (f32[4,256,128]{2,1,0:T(8,128)S(1)}, f32[8,3,2,16,128]{4,3,2,1,0:T(8,128)S(1)}, bf16[8,3,16,256]{3,2,1,0:T(8,128)(2,1)S(1)}, bf16[8,3,16,256]{3,2,1,...) custom-call(s32[4,2,32]{2,1,0:T(2,128)S(1)} %bitcast.33, s32[4,2,32]{2,1,0:T(2,128)S(1)} %bitcast.36, ...), custom_call_target="tpu_custom_call" | custom-call | bytes 21000000 | tf_op jit(solution)/shard_map/spread/pallas_call | solution.py:661
  68.4 0.0 collective-permute-done.14
  68.4 0.0 collective-permute-done.15
  68.4 0.0 collective-permute-done.10
  68.4 1.9 %collective-permute-done.11 = bf16[256,256]{1,0:T(8,128)(2,1)S(1)} collective-permute-done((bf16[256,256]{1,0:T(8,128)(2,1)S(1)}, bf16[256,256]{1,0:T(8,128)(2,1)S(1)}, u32[]{:S(2)}, u32[]{:S(2)}) %collective-permute-start.11) | collective-permute-done | bytes 131104 | tf_op jit(solution)/shard_map/ppermute | solution.py:699
  70.3 0.1 share_far.1
  70.5 2.3 %collective-permute-start.16 = (bf16[2,128,256]{2,1,0:T(8,128)(2,1)S(1)}, bf16[2,128,256]{2,1,0:T(8,128)(2,1)S(1)}, u32[]{:S(2)}, u32[]{:S(2)}) collective-permute-start(bf16[2,128,256]{2,1,0:T(8,128)(2,1)S(1)} %get-tuple-element.118), channel_id=1, source_target_pairs={{0,8},{1,9},{2,10},{3,11},{4,12},{5,13},{6,14},{7,15},{8,0},{9,1},... | collective-permute-start | bytes 393224 | tf_op jit(solution)/shard_map/ppermute | solution.py:699
  72.8 0.0 collective-permute-start.7
  72.8 4.4 %collective-permute-start.8 = (bf16[8,3,16,256]{3,2,1,0:T(8,128)(2,1)S(1)}, bf16[8,3,16,256]{3,2,1,0:T(8,128)(2,1)S(1)}, u32[]{:S(2)}, u32[]{:S(2)}) collective-permute-start(bf16[8,3,16,256]{3,2,1,0:T(8,128)(2,1)S(1)} %get-tuple-element.97), channel_id=1, source_target_pairs={{0,15},{1,0},{2,1},{3,2},{4,3},{5,4},{6,5},{7,6},{8,7},{9,8},{10,9... | collective-permute-start | bytes 589832 | tf_op jit(solution)/shard_map/ppermute | solution.py:686
  77.3 2.1 %taps.1 = bf16[128,256]{1,0:T(8,128)(2,1)S(1)} custom-call(f32[4,528,128]{2,1,0:T(8,128)S(1)} %get-tuple-element.119.refs_0_, f32[4,512,128]{2,1,0:T(8,128)S(1)} %get-tuple-element.120.refs_1_, f32[16,256]{1,0:T(8,128)S(1)} %get-tuple-element.116.refs_8_.refs_2_, f32[16,256]{1,0:T(8,128)S(1)} %get-tuple-element.121.refs_3_, ...), custom_call_target="tpu_custom_call" | custom-call | bytes 7350000 | tf_op jit(solution)/shard_map/taps/pallas_call | solution.py:661
  79.3 0.0 collective-permute-done.16.refs_1_
  79.4 0.1 collective-permute-start.17
  79.5 1.3 %collective-permute-done.7.refs_2_ = bf16[8,3,16,256]{3,2,1,0:T(8,128)(2,1)S(1)} collective-permute-done((bf16[8,3,16,256]{3,2,1,0:T(8,128)(2,1)S(1)}, bf16[8,3,16,256]{3,2,1,0:T(8,128)(2,1)S(1)}, u32[]{:S(2)}, u32[]{:S(2)}) %collective-permute-start.7) | collective-permute-done | bytes 196640 | tf_op jit(solution)/shard_map/ppermute | solution.py:686
  80.8 1.4 %collective-permute-done.8.refs_3_ = bf16[8,3,16,256]{3,2,1,0:T(8,128)(2,1)S(1)} collective-permute-done((bf16[8,3,16,256]{3,2,1,0:T(8,128)(2,1)S(1)}, bf16[8,3,16,256]{3,2,1,0:T(8,128)(2,1)S(1)}, u32[]{:S(2)}, u32[]{:S(2)}) %collective-permute-start.8) | collective-permute-done | bytes 196640 | tf_op jit(solution)/shard_map/ppermute | solution.py:686
  82.1 0.9 last.1
  83.1 6.3 %collective-permute-done.17.refs_1_ = bf16[3,128,256]{2,1,0:T(8,128)(2,1)S(1)} collective-permute-done((bf16[3,128,256]{2,1,0:T(8,128)(2,1)S(1)}, bf16[3,128,256]{2,1,0:T(8,128)(2,1)S(1)}, u32[]{:S(2)}, u32[]{:S(2)}) %collective-permute-start.17) | collective-permute-done | bytes 196640 | tf_op jit(solution)/shard_map/ppermute | solution.py:692
  89.4 2.0 %collective-permute-start.18 = (bf16[5,128,256]{2,1,0:T(8,128)(2,1)S(1)}, bf16[5,128,256]{2,1,0:T(8,128)(2,1)S(1)}, u32[]{:S(2)}, u32[]{:S(2)}) collective-permute-start(bf16[5,128,256]{2,1,0:T(8,128)(2,1)S(1)} %order_far.1.refs_0_), channel_id=1, source_target_pairs={{0,2},{1,3},{2,0},{3,1},{4,6},{5,7},{6,4},{7,5},{8,10},{9,11},{10,... | collective-permute-start | bytes 983048 | tf_op jit(solution)/shard_map/ppermute | solution.py:692
  91.4 0.0 collective-permute-start.19
  91.4 1.6 %collective-permute-start.20 = (bf16[5,128,256]{2,1,0:T(8,128)(2,1)S(1)}, bf16[5,128,256]{2,1,0:T(8,128)(2,1)S(1)}, u32[]{:S(2)}, u32[]{:S(2)}) collective-permute-start(bf16[5,128,256]{2,1,0:T(8,128)(2,1)S(1)} %order_far.1.refs_0_), channel_id=1, source_target_pairs={{0,6},{1,7},{2,4},{3,5},{4,2},{5,3},{6,0},{7,1},{8,14},{9,15},{10,... | collective-permute-start | bytes 983048 | tf_op jit(solution)/shard_map/ppermute | solution.py:692
  93.0 6.3 %collective-permute-done.18.refs_1_ = bf16[5,128,256]{2,1,0:T(8,128)(2,1)S(1)} collective-permute-done((bf16[5,128,256]{2,1,0:T(8,128)(2,1)S(1)}, bf16[5,128,256]{2,1,0:T(8,128)(2,1)S(1)}, u32[]{:S(2)}, u32[]{:S(2)}) %collective-permute-start.18) | collective-permute-done | bytes 327712 | tf_op jit(solution)/shard_map/ppermute | solution.py:692
  99.2 2.8 %collective-permute-done.19.refs_2_ = bf16[5,128,256]{2,1,0:T(8,128)(2,1)S(1)} collective-permute-done((bf16[5,128,256]{2,1,0:T(8,128)(2,1)S(1)}, bf16[5,128,256]{2,1,0:T(8,128)(2,1)S(1)}, u32[]{:S(2)}, u32[]{:S(2)}) %collective-permute-start.19) | collective-permute-done | bytes 327712 | tf_op jit(solution)/shard_map/ppermute | solution.py:692
  102.0 4.3 %collective-permute-done.20.refs_3_ = bf16[5,128,256]{2,1,0:T(8,128)(2,1)S(1)} collective-permute-done((bf16[5,128,256]{2,1,0:T(8,128)(2,1)S(1)}, bf16[5,128,256]{2,1,0:T(8,128)(2,1)S(1)}, u32[]{:S(2)}, u32[]{:S(2)}) %collective-permute-start.20) | collective-permute-done | bytes 327712 | tf_op jit(solution)/shard_map/ppermute | solution.py:692
  106.4 0.1 order_near.1.refs_0_
  106.5 0.1 collective-permute-start.21
  106.6 1.5 %unpack_mine.1 = (f32[2,256,1024]{2,1,0:T(8,128)}, f32[2,1024,256]{2,1,0:T(8,128)}) custom-call(bf16[17,128,256]{2,1,0:T(8,128)(2,1)S(1)} %order_near.1.refs_0_), custom_call_target="tpu_custom_call" | custom-call | bytes 5250000 | tf_op jit(solution)/shard_map/unpack_mine/pallas_call | solution.py:661
  108.1 1.2 %collective-permute-done.21.refs_1_ = bf16[17,128,256]{2,1,0:T(8,128)(2,1)S(1)} collective-permute-done((bf16[17,128,256]{2,1,0:T(8,128)(2,1)S(1)}, bf16[17,128,256]{2,1,0:T(8,128)(2,1)S(1)}, u32[]{:S(2)}, u32[]{:S(2)}) %collective-permute-start.21) | collective-permute-done | bytes 1114144 | tf_op jit(solution)/shard_map/ppermute | solution.py:692
  109.3 2.2 %unpack_theirs.1 = (f32[2,256,1024]{2,1,0:T(8,128)}, f32[2,1024,256]{2,1,0:T(8,128)}, f32[7,7,2,256]{3,2,1,0:T(2,128)}, f32[2,256]{1,0:T(2,128)}, f32[2,256]{1,0:T(2,128)}) custom-call(bf16[17,128,256]{2,1,0:T(8,128)(2,1)S(1)} %order_near.1.refs_0_, ...), custom_call_target="tpu_custom_call", output_to_operand_aliasing={{0}: (2, {}), {1}: (3, {})} | custom-call | bytes 5250000 | tf_op jit(solution)/shard_map/unpack_theirs/pallas_call | solution.py:661
  (15 shorter events, 0.1 us)
Async XLA Ops:
  0.6 1.0 copy-start.3
  1.6 10.7 %copy-start.5 = (s32[32,4,2]{0,2,1:T(2,128)S(1)}, s32[32,4,2]{0,2,1:T(2,128)}, u32[]{:S(2)}) copy-start(s32[32,4,2]{0,2,1:T(2,128)} %param.16) | copy-start | bytes 3076
  1.6 10.7 %copy-start.6 = (s32[32,4,2]{0,2,1:T(2,128)S(1)}, s32[32,4,2]{0,2,1:T(2,128)}, u32[]{:S(2)}) copy-start(s32[32,4,2]{0,2,1:T(2,128)} %param.17) | copy-start | bytes 3076
  1.7 10.6 %collective-permute-start = (bf16[8,3,16,256]{3,2,1,0:T(8,128)(2,1)S(1)}, bf16[8,3,16,256]{3,2,1,0:T(8,128)(2,1)S(1)}, u32[]{:S(2)}, u32[]{:S(2)}) collective-permute-start(bf16[8,3,16,256]{3,2,1,0:T(8,128)(2,1)S(1)} %get-tuple-element.70.refs_5_.refs_3_), channel_id=1, source_target_pairs={{0,1},{1,2},{2,3},{3,4},{4,5},{5,6},{6,7},{7,8},{8,9},{9,10},{10,1... | collective-permute-start | bytes 589832 | tf_op jit(solution)/shard_map/ppermute | solution.py:686
  2.2 10.1 %collective-permute-start.1 = (bf16[8,3,16,256]{3,2,1,0:T(8,128)(2,1)S(1)}, bf16[8,3,16,256]{3,2,1,0:T(8,128)(2,1)S(1)}, u32[]{:S(2)}, u32[]{:S(2)}) collective-permute-start(bf16[8,3,16,256]{3,2,1,0:T(8,128)(2,1)S(1)} %get-tuple-element.70.refs_5_.refs_3_), channel_id=1, source_target_pairs={{0,15},{1,0},{2,1},{3,2},{4,3},{5,4},{6,5},{7,6},{8,7},{9,8},{10,9... | collective-permute-start | bytes 589832 | tf_op jit(solution)/shard_map/ppermute | solution.py:686
  7.3 1.2 %copy-start = (bf16[2,256,1024]{2,1,0:T(8,128)(2,1)S(1)}, bf16[2,256,1024]{2,1,0:T(8,128)(2,1)}, u32[]{:S(2)}) copy-start(bf16[2,256,1024]{2,1,0:T(8,128)(2,1)} %refs_3_.1) | copy-start | bytes 3145732
  8.5 1.2 %copy-start.1 = (bf16[2,1024,256]{2,1,0:T(8,128)(2,1)S(1)}, bf16[2,1024,256]{2,1,0:T(8,128)(2,1)}, u32[]{:S(2)}) copy-start(bf16[2,1024,256]{2,1,0:T(8,128)(2,1)} %refs_4_.1) | copy-start | bytes 3145732
  9.7 0.9 copy-start.4
  10.6 0.7 copy-start.7
  11.3 0.7 copy-start.8
  12.3 16.6 %copy-start.2 = (bf16[2,16,16,256]{3,2,1,0:T(8,128)(2,1)S(1)}, bf16[2,16,16,256]{3,2,1,0:T(8,128)(2,1)}, u32[]{:S(2)}) copy-start(bf16[2,16,16,256]{3,2,1,0:T(8,128)(2,1)} %refs_11_.1) | copy-start | bytes 786436
  21.0 7.8 %collective-permute-start.2 = (bf16[8,3,16,256]{3,2,1,0:T(8,128)(2,1)S(1)}, bf16[8,3,16,256]{3,2,1,0:T(8,128)(2,1)S(1)}, u32[]{:S(2)}, u32[]{:S(2)}) collective-permute-start(bf16[8,3,16,256]{3,2,1,0:T(8,128)(2,1)S(1)} %get-tuple-element.77.refs_3_), channel_id=1, source_target_pairs={{0,1},{1,2},{2,3},{3,4},{4,5},{5,6},{6,7},{7,8},{8,9},{9,10},{10,1... | collective-permute-start | bytes 589832 | tf_op jit(solution)/shard_map/ppermute | solution.py:686
  21.1 7.8 %collective-permute-start.3 = (bf16[8,3,16,256]{3,2,1,0:T(8,128)(2,1)S(1)}, bf16[8,3,16,256]{3,2,1,0:T(8,128)(2,1)S(1)}, u32[]{:S(2)}, u32[]{:S(2)}) collective-permute-start(bf16[8,3,16,256]{3,2,1,0:T(8,128)(2,1)S(1)} %get-tuple-element.77.refs_3_), channel_id=1, source_target_pairs={{0,15},{1,0},{2,1},{3,2},{4,3},{5,4},{6,5},{7,6},{8,7},{9,8},{10,9... | collective-permute-start | bytes 589832 | tf_op jit(solution)/shard_map/ppermute | solution.py:686
  44.4 7.9 %collective-permute-start.4 = (bf16[8,3,16,256]{3,2,1,0:T(8,128)(2,1)S(1)}, bf16[8,3,16,256]{3,2,1,0:T(8,128)(2,1)S(1)}, u32[]{:S(2)}, u32[]{:S(2)}) collective-permute-start(bf16[8,3,16,256]{3,2,1,0:T(8,128)(2,1)S(1)} %get-tuple-element.81), channel_id=1, source_target_pairs={{0,1},{1,2},{2,3},{3,4},{4,5},{5,6},{6,7},{7,8},{8,9},{9,10},{10,1... | collective-permute-start | bytes 589832 | tf_op jit(solution)/shard_map/ppermute | solution.py:686
  44.4 7.9 %collective-permute-start.5 = (bf16[8,3,16,256]{3,2,1,0:T(8,128)(2,1)S(1)}, bf16[8,3,16,256]{3,2,1,0:T(8,128)(2,1)S(1)}, u32[]{:S(2)}, u32[]{:S(2)}) collective-permute-start(bf16[8,3,16,256]{3,2,1,0:T(8,128)(2,1)S(1)} %get-tuple-element.82), channel_id=1, source_target_pairs={{0,15},{1,0},{2,1},{3,2},{4,3},{5,4},{6,5},{7,6},{8,7},{9,8},{10,9... | collective-permute-start | bytes 589832 | tf_op jit(solution)/shard_map/ppermute | solution.py:686
  52.2 2.9 %collective-permute-start.12 = (bf16[1024,256]{1,0:T(8,128)(2,1)S(1)}, bf16[1024,256]{1,0:T(8,128)(2,1)S(1)}, u32[]{:S(2)}, u32[]{:S(2)}) collective-permute-start(bf16[1024,256]{1,0:T(8,128)(2,1)S(1)} %get-tuple-element.111), channel_id=1, source_target_pairs={{0,1},{1,0},{2,3},{3,2},{4,5},{5,4},{6,7},{7,6},{8,9},{9,8},{10,11... | collective-permute-start | bytes 1572872 | tf_op jit(solution)/shard_map/ppermute | solution.py:699
  54.5 4.2 %collective-permute-start.6 = (bf16[1024,256]{1,0:T(8,128)(2,1)S(1)}, bf16[1024,256]{1,0:T(8,128)(2,1)S(1)}, u32[]{:S(2)}, u32[]{:S(2)}) collective-permute-start(bf16[1024,256]{1,0:T(8,128)(2,1)S(1)} %get-tuple-element.92), channel_id=1, source_target_pairs={{0,1},{1,0},{2,3},{3,2},{4,5},{5,4},{6,7},{7,6},{8,9},{9,8},{10,11... | collective-permute-start | bytes 1572872 | tf_op jit(solution)/shard_map/ppermute | solution.py:699
  55.2 5.6 %collective-permute-start.13 = (bf16[256,256]{1,0:T(8,128)(2,1)S(1)}, bf16[256,256]{1,0:T(8,128)(2,1)S(1)}, u32[]{:S(2)}, u32[]{:S(2)}) collective-permute-start(bf16[256,256]{1,0:T(8,128)(2,1)S(1)} %get-tuple-element.113), channel_id=1, source_target_pairs={{0,2},{1,3},{2,0},{3,1},{4,6},{5,7},{6,4},{7,5},{8,10},{9,11},{10,... | collective-permute-start | bytes 393224 | tf_op jit(solution)/shard_map/ppermute | solution.py:699
  55.3 13.1 %collective-permute-start.14 = (bf16[256,256]{1,0:T(8,128)(2,1)S(1)}, bf16[256,256]{1,0:T(8,128)(2,1)S(1)}, u32[]{:S(2)}, u32[]{:S(2)}) collective-permute-start(bf16[256,256]{1,0:T(8,128)(2,1)S(1)} %get-tuple-element.114), channel_id=1, source_target_pairs={{0,4},{1,5},{2,6},{3,7},{4,0},{5,1},{6,2},{7,3},{8,12},{9,13},{10,... | collective-permute-start | bytes 393224 | tf_op jit(solution)/shard_map/ppermute | solution.py:699
  55.4 13.0 %collective-permute-start.15 = (bf16[256,256]{1,0:T(8,128)(2,1)S(1)}, bf16[256,256]{1,0:T(8,128)(2,1)S(1)}, u32[]{:S(2)}, u32[]{:S(2)}) collective-permute-start(bf16[256,256]{1,0:T(8,128)(2,1)S(1)} %get-tuple-element.115), channel_id=1, source_target_pairs={{0,6},{1,7},{2,4},{3,5},{4,2},{5,3},{6,0},{7,1},{8,14},{9,15},{10,... | collective-permute-start | bytes 393224 | tf_op jit(solution)/shard_map/ppermute | solution.py:699
  58.9 9.5 %collective-permute-start.9 = (bf16[256,256]{1,0:T(8,128)(2,1)S(1)}, bf16[256,256]{1,0:T(8,128)(2,1)S(1)}, u32[]{:S(2)}, u32[]{:S(2)}) collective-permute-start(bf16[256,256]{1,0:T(8,128)(2,1)S(1)} %get-tuple-element.99), channel_id=1, source_target_pairs={{0,2},{1,3},{2,0},{3,1},{4,6},{5,7},{6,4},{7,5},{8,10},{9,11},{10,... | collective-permute-start | bytes 393224 | tf_op jit(solution)/shard_map/ppermute | solution.py:699
  59.0 9.4 %collective-permute-start.10 = (bf16[256,256]{1,0:T(8,128)(2,1)S(1)}, bf16[256,256]{1,0:T(8,128)(2,1)S(1)}, u32[]{:S(2)}, u32[]{:S(2)}) collective-permute-start(bf16[256,256]{1,0:T(8,128)(2,1)S(1)} %get-tuple-element.100), channel_id=1, source_target_pairs={{0,4},{1,5},{2,6},{3,7},{4,0},{5,1},{6,2},{7,3},{8,12},{9,13},{10,... | collective-permute-start | bytes 393224 | tf_op jit(solution)/shard_map/ppermute | solution.py:699
  60.8 9.6 %collective-permute-start.11 = (bf16[256,256]{1,0:T(8,128)(2,1)S(1)}, bf16[256,256]{1,0:T(8,128)(2,1)S(1)}, u32[]{:S(2)}, u32[]{:S(2)}) collective-permute-start(bf16[256,256]{1,0:T(8,128)(2,1)S(1)} %get-tuple-element.101), channel_id=1, source_target_pairs={{0,6},{1,7},{2,4},{3,5},{4,2},{5,3},{6,0},{7,1},{8,14},{9,15},{10,... | collective-permute-start | bytes 393224 | tf_op jit(solution)/shard_map/ppermute | solution.py:699
  70.5 8.8 %collective-permute-start.16 = (bf16[2,128,256]{2,1,0:T(8,128)(2,1)S(1)}, bf16[2,128,256]{2,1,0:T(8,128)(2,1)S(1)}, u32[]{:S(2)}, u32[]{:S(2)}) collective-permute-start(bf16[2,128,256]{2,1,0:T(8,128)(2,1)S(1)} %get-tuple-element.118), channel_id=1, source_target_pairs={{0,8},{1,9},{2,10},{3,11},{4,12},{5,13},{6,14},{7,15},{8,0},{9,1},... | collective-permute-start | bytes 393224 | tf_op jit(solution)/shard_map/ppermute | solution.py:699
  72.8 8.0 %collective-permute-start.7 = (bf16[8,3,16,256]{3,2,1,0:T(8,128)(2,1)S(1)}, bf16[8,3,16,256]{3,2,1,0:T(8,128)(2,1)S(1)}, u32[]{:S(2)}, u32[]{:S(2)}) collective-permute-start(bf16[8,3,16,256]{3,2,1,0:T(8,128)(2,1)S(1)} %get-tuple-element.96), channel_id=1, source_target_pairs={{0,1},{1,2},{2,3},{3,4},{4,5},{5,6},{6,7},{7,8},{8,9},{9,10},{10,1... | collective-permute-start | bytes 589832 | tf_op jit(solution)/shard_map/ppermute | solution.py:686
  72.8 9.3 %collective-permute-start.8 = (bf16[8,3,16,256]{3,2,1,0:T(8,128)(2,1)S(1)}, bf16[8,3,16,256]{3,2,1,0:T(8,128)(2,1)S(1)}, u32[]{:S(2)}, u32[]{:S(2)}) collective-permute-start(bf16[8,3,16,256]{3,2,1,0:T(8,128)(2,1)S(1)} %get-tuple-element.97), channel_id=1, source_target_pairs={{0,15},{1,0},{2,1},{3,2},{4,3},{5,4},{6,5},{7,6},{8,7},{9,8},{10,9... | collective-permute-start | bytes 589832 | tf_op jit(solution)/shard_map/ppermute | solution.py:686
  79.4 10.0 %collective-permute-start.17 = (bf16[3,128,256]{2,1,0:T(8,128)(2,1)S(1)}, bf16[3,128,256]{2,1,0:T(8,128)(2,1)S(1)}, u32[]{:S(2)}, u32[]{:S(2)}) collective-permute-start(bf16[3,128,256]{2,1,0:T(8,128)(2,1)S(1)} %total.1.refs_0_), channel_id=1, source_target_pairs={{0,8},{1,9},{2,10},{3,11},{4,12},{5,13},{6,14},{7,15},{8,0},{9,1},... | collective-permute-start | bytes 589832 | tf_op jit(solution)/shard_map/ppermute | solution.py:692
  89.4 9.8 %collective-permute-start.18 = (bf16[5,128,256]{2,1,0:T(8,128)(2,1)S(1)}, bf16[5,128,256]{2,1,0:T(8,128)(2,1)S(1)}, u32[]{:S(2)}, u32[]{:S(2)}) collective-permute-start(bf16[5,128,256]{2,1,0:T(8,128)(2,1)S(1)} %order_far.1.refs_0_), channel_id=1, source_target_pairs={{0,2},{1,3},{2,0},{3,1},{4,6},{5,7},{6,4},{7,5},{8,10},{9,11},{10,... | collective-permute-start | bytes 983048 | tf_op jit(solution)/shard_map/ppermute | solution.py:692
  91.4 10.6 %collective-permute-start.19 = (bf16[5,128,256]{2,1,0:T(8,128)(2,1)S(1)}, bf16[5,128,256]{2,1,0:T(8,128)(2,1)S(1)}, u32[]{:S(2)}, u32[]{:S(2)}) collective-permute-start(bf16[5,128,256]{2,1,0:T(8,128)(2,1)S(1)} %order_far.1.refs_0_), channel_id=1, source_target_pairs={{0,4},{1,5},{2,6},{3,7},{4,0},{5,1},{6,2},{7,3},{8,12},{9,13},{10,... | collective-permute-start | bytes 983048 | tf_op jit(solution)/shard_map/ppermute | solution.py:692
  91.4 15.0 %collective-permute-start.20 = (bf16[5,128,256]{2,1,0:T(8,128)(2,1)S(1)}, bf16[5,128,256]{2,1,0:T(8,128)(2,1)S(1)}, u32[]{:S(2)}, u32[]{:S(2)}) collective-permute-start(bf16[5,128,256]{2,1,0:T(8,128)(2,1)S(1)} %order_far.1.refs_0_), channel_id=1, source_target_pairs={{0,6},{1,7},{2,4},{3,5},{4,2},{5,3},{6,0},{7,1},{8,14},{9,15},{10,... | collective-permute-start | bytes 983048 | tf_op jit(solution)/shard_map/ppermute | solution.py:692
  106.5 2.8 %collective-permute-start.21 = (bf16[17,128,256]{2,1,0:T(8,128)(2,1)S(1)}, bf16[17,128,256]{2,1,0:T(8,128)(2,1)S(1)}, u32[]{:S(2)}, u32[]{:S(2)}) collective-permute-start(bf16[17,128,256]{2,1,0:T(8,128)(2,1)S(1)} %order_near.1.refs_0_), channel_id=1, source_target_pairs={{0,1},{1,0},{2,3},{3,2},{4,5},{5,4},{6,7},{7,6},{8,9},{9,8},{10,11... | collective-permute-start | bytes 3342344 | tf_op jit(solution)/shard_map/ppermute | solution.py:692

commit v5 on v4

--- a/solution.py
+++ b/solution.py
@@ -546,22 +546,25 @@
 
 
 def share_near_kernel(*refs):
-    arrays, outs = refs[:2], refs[2:]
+    arrays, outs = refs[:4], refs[4:]
     for k, out in enumerate(outs):
         piece = digit_of(1) ^ k
-        add_rows(out, [lambda rows, array=array: array[piece, rows] for array in arrays])
+        for layer in range(2):
+            parts = arrays[2 * layer : 2 * layer + 2]
+            add_rows(
+                out.at[layer],
+                [lambda rows, array=array: array[piece, rows] for array in parts],
+            )
 
 
 def share_far_kernel(*refs):
-    rest, share = refs[0].shape[:2]
-    arrays, outs = refs[:-rest], refs[-rest:]
+    arrays, outs = refs[:4], refs[4:]
     for k, out in enumerate(outs):
         piece = digit_of(2) ^ k
         for layer in range(2):
-            parts = arrays[4 * layer : 4 * layer + 4]
             add_rows(
                 out.at[layer],
-                [lambda rows, array=array: array[piece, rows] for array in parts],
+                [lambda rows, array=array: array[layer, piece, rows] for array in arrays],
             )
 
 
@@ -575,17 +578,35 @@
     out[2:] = small[...]
 
 
+def quarter_kernel(*refs):
+    arrays, small, out = refs[:4], refs[4], refs[5]
+    rest = arrays[0].shape[1]
+    for piece in range(rest):
+        for layer in range(2):
+            add_rows(
+                out.at[2 * piece + layer],
+                [lambda rows, array=array: array[layer, piece, rows] for array in arrays],
+            )
+    out[2 * rest :] = small[...]
+
+
+def pair_kernel(first, second, out):
+    for j in range(out.shape[0]):
+        add_rows(out.at[j], [lambda rows: first[j, rows], lambda rows: second[j, rows]])
+
+
 def order_kernel(level, small_units, *refs):
-    pieces, out = refs[:-1], refs[-1]
+    pieces, out, held = refs[:-2], refs[-2], refs[-1]
     units = pieces[0].shape[0] - small_units
     for k, piece in enumerate(pieces):
-        at = (digit_of(level) ^ k) * units
+        place = digit_of(level) ^ k
         for j in range(units):
-            out[at + j] = piece[j]
+            out[place * units + j] = piece[j]
+        held[place] = piece[units:]
     for j in range(small_units):
         add_rows(
             out.at[len(pieces) * units + j],
-            [lambda rows, piece=piece: piece[units + j, rows] for piece in pieces],
+            [lambda rows, k=k: held[k, j, rows] for k in range(len(pieces))],
         )
 
 
@@ -708,48 +729,60 @@
         self.near_masks = [2 * k for k in range(1, 4)]
         self.rest_masks = [8 * k for k in range(1, self.rest)]
 
-    def start(self, keep, send):
-        rows, channels = keep.shape
-        (came,) = swap([send], [1])
-        quarter = rows // 4
-        parts = (4, quarter, channels)
-        shape = jax.ShapeDtypeStruct((quarter, channels), BF16)
+    def start(self, halves_of_layers):
+        arrays = []
+        for keep, send in halves_of_layers:
+            rows, channels = keep.shape
+            dims = (4, rows // 4, channels)
+            arrays += [keep.reshape(dims), swap([send], [1])[0].reshape(dims)]
+        shape = jax.ShapeDtypeStruct((2,) + dims[1:], BF16)
         pieces = call(
-            share_near_kernel, "share_near", 0.7,
-            near(keep.reshape(parts), came.reshape(parts)), near(*[shape] * 4), [],
+            share_near_kernel, "share_near", 1.2, near(*arrays), near(*[shape] * 4), [],
         )
         return [pieces[0]] + swap(pieces[1:], self.near_masks)
 
-    def finish(self, parts, after, small):
-        quarter, channels = parts[0][0].shape
-        dims = (self.rest, quarter // self.rest, channels)
-        arrays = [part.reshape(dims) for layer in parts for part in layer]
-        shape = jax.ShapeDtypeStruct((2,) + dims[1:], BF16)
+    def finish(self, parts, after, small, beside):
+        _, quarter, channels = parts[0].shape
+        dims = (2, self.rest, quarter // self.rest, channels)
+        arrays = [part.reshape(dims) for part in parts]
+        if self.rest == 2:
+            small = small(after).reshape((-1,) + dims[2:])
+            shape = jax.ShapeDtypeStruct((2 * self.rest + small.shape[0],) + dims[2:], BF16)
+            (total,) = call(
+                quarter_kernel, "quarter", 0.9, near(*arrays, small), near(shape), []
+            )
+            (total,) = call(
+                pair_kernel, "pair", 0.5, near(total, *partners(total, [8])), near(shape), [],
+                beside,
+            )
+            return total, small.shape[0]
+        shape = jax.ShapeDtypeStruct((2,) + dims[2:], BF16)
         pieces = call(
             share_far_kernel, "share_far", 0.9,
-            near(*arrays), near(*[shape] * self.rest), [], after,
+            near(*arrays), near(*[shape] * self.rest), [], (after,),
         )
         arrived = swap(pieces[1:], self.rest_masks)
-        small = small(pieces[0]).reshape((-1,) + dims[1:])
-        shape = jax.ShapeDtypeStruct((2 + small.shape[0],) + dims[1:], BF16)
+        small = small(pieces[0]).reshape((-1,) + dims[2:])
+        shape = jax.ShapeDtypeStruct((2 + small.shape[0],) + dims[2:], BF16)
         (total,) = call(
-            total_kernel, "total", 0.4, near(pieces[0], *arrived, small), near(shape), []
+            total_kernel, "total", 0.4, near(pieces[0], *arrived, small), near(shape), [],
+            beside,
         )
         return total, small.shape[0]
 
-    def gather(self, total, small_units, after):
-        for level, masks, name in (
-            (2, self.rest_masks, "order_far"),
-            (1, self.near_masks, "order_near"),
-        ):
+    def gather(self, total, small_units):
+        levels = [(1, self.near_masks, "order_near")]
+        if self.rest != 2:
+            levels = [(2, self.rest_masks, "order_far")] + levels
+        for level, masks, name in levels:
             pieces = [total] + partners(total, masks)
             units = (total.shape[0] - small_units) * len(pieces) + small_units
             shape = jax.ShapeDtypeStruct((units,) + total.shape[1:], BF16)
             (total,) = call(
                 functools.partial(order_kernel, level, small_units), name, 0.5,
-                near(*pieces), near(shape), [], after,
+                near(*pieces), near(shape),
+                [pltpu.VMEM((len(pieces), small_units) + total.shape[1:], BF16)],
             )
-            after = ()
         return total, partners(total, [1])[0]
 
 
@@ -850,7 +883,6 @@
         near(half, half, small),
         vmem(tap_sums, two_halves),
     )
-    parts_one = reduction.start(keep_one, send_one)
     keep_zero, send_zero, flat, up_in, scale_sums = call(
         functools.partial(backward_kernel, sz, 0),
         "backward", 2.9,
@@ -860,14 +892,14 @@
         near(half, half, slabs, wide_short, sums),
         vmem(wide, narrow_short, two_halves),
     )
-    parts_zero = reduction.start(keep_zero, send_zero)
+    parts = reduction.start(((keep_zero, send_zero), (keep_one, send_one)))
     base, grad_own, grad_below, grad_above, grad_conv, gain_sums = call(
         functools.partial(spread_kernel, sz, 0),
         "spread", 6.0,
         plan + near(kern, gain, up, flat, up_in, normal, inverse),
         near(slabs, own_shape, strips_shape, strips_shape, grad_slabs, sums),
         vmem(taps, narrow, grad_pool, padded),
-        (parts_zero[0],),
+        (parts[0],),
     )
     from_below, from_above = pass_on(grad_above, 1), pass_on(grad_below, -1)
 
@@ -882,9 +914,6 @@
         )
         return both
 
-    total, small_units = reduction.finish(
-        (parts_zero, parts_one), (gain_sums,), small_gradients
-    )
     in_grad, token = call(
         functools.partial(last_kernel, sz),
         "last", 1.0,
@@ -892,7 +921,10 @@
         far(image) + near(shape((8, LANES), F32)),
         vmem(slabs, image) + sems(1),
     )
-    mine, theirs = reduction.gather(total, small_units, (token,))
+    total, small_units = reduction.finish(
+        parts, gain_sums, small_gradients, (token,)
+    )
+    mine, theirs = reduction.gather(total, small_units)
     weight_shapes = [shape(up_weight.shape, F32), shape(down_weight.shape, F32)]
     copies = layers * hidden // channels
     scratch = vmem(shape(down_weight.shape, F32))

time: 112 us -> 115 us (1.027)
  waiting for transfers between devices: 30.1 us -> 33.6 us
    ppermute x9 -> x5, starting transfers between devices: 8.78 us -> 4.15 us  [swap(): lax.ppermute(array, 'tile', [(i, i ^ mask) for i in range(length)])]
    ppermute x5, starting transfers between devices: 3.7 us -> 7.62 us  [partners(): lax.ppermute(array, 'tile', [(i, i ^ mask) for i in range(length)])]
    ppermute x8, waiting for transfers between devices: 6.03 us -> 9.82 us  [pass_on(): lax.ppermute(shard, 'tile', [(i, (i + by) % length) for i in range(length)])]
    ppermute x5, waiting for transfers between devices: 20.9 us -> 19.5 us  [partners(): lax.ppermute(array, 'tile', [(i, i ^ mask) for i in range(length)])]
    ppermute x9 -> x5, waiting for transfers between devices: 3.17 us -> 4.3 us  [swap(): lax.ppermute(array, 'tile', [(i, i ^ mask) for i in range(length)])]
    pallas_call x17 -> x15, Pallas kernels: 43.2 us -> 43.2 us  [call(): pl.pallas_call(run, in_specs=[spec for spec, _ in ins] + [pl.BlockSpec(me...]
  transfers between devices with their start and end apart: 22 -> 18, of which waited for: 10 -> 9; matrix products, arithmetic and copies ran while one was open for 0% -> 0% of each run, Pallas kernels for 15% -> 14%
where the time goes in v5:
time: 115 us; the launch traced here: 114 us
  Pallas kernels  43.2 us (38%)
  waiting for transfers between devices  33.6 us (29%)
  starting transfers between devices  31 us (27%)
  local copies, waits for them, and re-layouts  5.66 us (5%)
    pallas_call x15, Pallas kernels, call(): pl.pallas_call(run, in_specs=[spec for spec, _ in ins] + [pl.BlockSpec(me...  43.2 us
    ppermute x5, waiting for transfers between devices, partners(): lax.ppermute(array, 'tile', [(i, i ^ mask) for i in range(length)])  19.5 us
    ppermute x8, starting transfers between devices, pass_on(): lax.ppermute(shard, 'tile', [(i, (i + by) % length) for i in range(length)])  19.2 us
    ppermute x8, waiting for transfers between devices, pass_on(): lax.ppermute(shard, 'tile', [(i, (i + by) % length) for i in range(length)])  9.82 us
    ppermute x5, starting transfers between devices, partners(): lax.ppermute(array, 'tile', [(i, i ^ mask) for i in range(length)])  7.62 us
    unnamed x18, local copies, waits for them, and re-layouts  5.66 us
    ppermute x5, waiting for transfers between devices, swap(): lax.ppermute(array, 'tile', [(i, i ^ mask) for i in range(length)])  4.3 us
    ppermute x5, starting transfers between devices, swap(): lax.ppermute(array, 'tile', [(i, i ^ mask) for i in range(length)])  4.15 us
  transfers between devices with their start and end apart: 18, of which 9 were waited for; matrix products, arithmetic and copies ran while one was open for 0% of the time, Pallas kernels for 14%

profile of v5, /device:TPU:0, one launch (start us, length us, event | category | flops | bytes accessed | tf_op | source)
XLA Modules:
  0.0 114.4 jit_solution(9203203505117813041)
XLA Ops:
  0.6 0.0 copy-start.3
  0.6 0.9 copy-done.3
  1.6 0.0 copy-start.5
  1.6 0.0 copy-start.6
  1.6 0.1 strips.1
  1.7 0.5 collective-permute-start
  2.2 5.1 %collective-permute-start.1 = (bf16[8,3,16,256]{3,2,1,0:T(8,128)(2,1)S(1)}, bf16[8,3,16,256]{3,2,1,0:T(8,128)(2,1)S(1)}, u32[]{:S(2)}, u32[]{:S(2)}) collective-permute-start(bf16[8,3,16,256]{3,2,1,0:T(8,128)(2,1)S(1)} %get-tuple-element.64.refs_5_.refs_3_), channel_id=1, source_target_pairs={{0,15},{1,0},{2,1},{3,2},{4,3},{5,4},{6,5},{7,6},{8,7},{9,8},{10,9... | collective-permute-start | bytes 589832 | tf_op jit(solution)/shard_map/ppermute | solution.py:707
  7.3 1.2 %copy-done = bf16[2,256,1024]{2,1,0:T(8,128)(2,1)S(1)} copy-done((bf16[2,256,1024]{2,1,0:T(8,128)(2,1)S(1)}, bf16[2,256,1024]{2,1,0:T(8,128)(2,1)}, u32[]{:S(2)}) %copy-start) | copy-done | bytes 1048600
  8.5 1.2 %copy-done.1 = bf16[2,1024,256]{2,1,0:T(8,128)(2,1)S(1)} copy-done((bf16[2,1024,256]{2,1,0:T(8,128)(2,1)S(1)}, bf16[2,1024,256]{2,1,0:T(8,128)(2,1)}, u32[]{:S(2)}) %copy-start.1) | copy-done | bytes 1048600
  9.7 0.9 copy-done.4
  10.6 0.7 copy-done.7
  11.3 0.7 copy-done.8
  12.0 0.3 fetch.1
  12.3 0.0 copy-start.2
  12.3 0.0 collective-permute-done.refs_4_
  12.3 0.0 collective-permute-done.1.refs_5_
  12.3 0.0 copy-done.5
  12.3 0.0 copy-done.6
  12.3 8.7 %forward.1 = (bf16[2,16,16,256]{3,2,1,0:T(8,128)(2,1)S(1)}, bf16[8,3,16,256]{3,2,1,0:T(8,128)(2,1)S(1)}, f32[4,528,128]{2,1,0:T(8,128)S(1)}, f32[4,256,128]{2,1,...) custom-call(s32[4,2,32]{2,1,0:T(2,128)S(1)} %bitcast.23, ...), custom_call_target="tpu_custom_call" | custom-call | bytes 30450000 | tf_op jit(solution)/shard_map/forward/pallas_call | solution.py:682
  21.0 0.1 collective-permute-start.2
  21.1 4.4 %collective-permute-start.3 = (bf16[8,3,16,256]{3,2,1,0:T(8,128)(2,1)S(1)}, bf16[8,3,16,256]{3,2,1,0:T(8,128)(2,1)S(1)}, u32[]{:S(2)}, u32[]{:S(2)}) collective-permute-start(bf16[8,3,16,256]{3,2,1,0:T(8,128)(2,1)S(1)} %get-tuple-element.71.refs_3_), channel_id=1, source_target_pairs={{0,15},{1,0},{2,1},{3,2},{4,3},{5,4},{6,5},{7,6},{8,7},{9,8},{10,9... | collective-permute-start | bytes 589832 | tf_op jit(solution)/shard_map/ppermute | solution.py:707
  25.5 3.3 %collective-permute-done.2.refs_4_ = bf16[8,3,16,256]{3,2,1,0:T(8,128)(2,1)S(1)} collective-permute-done((bf16[8,3,16,256]{3,2,1,0:T(8,128)(2,1)S(1)}, bf16[8,3,16,256]{3,2,1,0:T(8,128)(2,1)S(1)}, u32[]{:S(2)}, u32[]{:S(2)}) %collective-permute-start.2) | collective-permute-done | bytes 196640 | tf_op jit(solution)/shard_map/ppermute | solution.py:707
  28.8 0.0 collective-permute-done.3.refs_5_
  28.8 0.0 copy-done.2
  28.9 15.5 %turn.1 = (bf16[2,16,16,256]{3,2,1,0:T(8,128)(2,1)}, f32[4,256,128]{2,1,0:T(8,128)S(1)}, f32[8,3,2,16,128]{4,3,2,1,0:T(8,128)S(1)}, bf16[8,3,16,256]{3,2,1,0:T(8...) custom-call(s32[4,2,32]{2,1,0:T(2,128)S(1)} %bitcast.24, ...), custom_call_target="tpu_custom_call" | custom-call | bytes 53900000 | tf_op jit(solution)/shard_map/turn/pallas_call | solution.py:682
  44.4 0.1 collective-permute-start.4
  44.4 4.7 %collective-permute-start.5 = (bf16[8,3,16,256]{3,2,1,0:T(8,128)(2,1)S(1)}, bf16[8,3,16,256]{3,2,1,0:T(8,128)(2,1)S(1)}, u32[]{:S(2)}, u32[]{:S(2)}) collective-permute-start(bf16[8,3,16,256]{3,2,1,0:T(8,128)(2,1)S(1)} %get-tuple-element.76), channel_id=1, source_target_pairs={{0,15},{1,0},{2,1},{3,2},{4,3},{5,4},{6,5},{7,6},{8,7},{9,8},{10,9... | collective-permute-start | bytes 589832 | tf_op jit(solution)/shard_map/ppermute | solution.py:707
  49.1 3.1 %weights.1 = (bf16[1024,256]{1,0:T(8,128)(2,1)S(1)}, bf16[1024,256]{1,0:T(8,128)(2,1)S(1)}, f32[64,256]{1,0:T(8,128)S(1)}) custom-call(f32[4,528,128]{2,1,0:T(8,128)S(1)} %get-tuple-element.87.refs_0_, f32[4,512,128]{2,1,0:T(8,128)S(1)} %get-tuple-element.88.refs_1_, bf16[512,256]{1,0:T(8,128)(2,1)S(1)} %get-tuple-element.89.refs_2_, ...), custom_call_target="tpu_custom_call" | custom-call | bytes 9800000 | tf_op jit(solution)/shard_map/weights/pallas_call | solution.py:682
  52.2 0.1 collective-permute-start.7
  52.3 0.0 collective-permute-done.4.refs_2_
  52.3 0.0 collective-permute-done.5.refs_3_
  52.3 2.3 %backward.1 = (bf16[1024,256]{1,0:T(8,128)(2,1)S(1)}, bf16[1024,256]{1,0:T(8,128)(2,1)S(1)}, f32[4,256,128]{2,1,0:T(8,128)S(1)}, bf16[512,1024]{1,0:T(8,128)(2,1)S(1)}, f32[16,256]{1,0:T(8,128)S(1)}) custom-call(f32[4,256,128]{2,1,0:T(8,128)S(1)} %get-tuple-element.73.refs_0_, f32[8,3,2,16,128]{4,3,2,1,0:T(8,128)S(1)} %get-tuple-element.74.refs_1_, ...), custom_call_target="tpu_custom_call" | custom-call | bytes 10150000 | tf_op jit(solution)/shard_map/backward/pallas_call | solution.py:682
  54.6 0.5 collective-permute-start.6
  55.1 0.0 collective-permute-done.7
  55.1 1.5 %collective-permute-done.6 = bf16[1024,256]{1,0:T(8,128)(2,1)S(1)} collective-permute-done((bf16[1024,256]{1,0:T(8,128)(2,1)S(1)}, bf16[1024,256]{1,0:T(8,128)(2,1)S(1)}, u32[]{:S(2)}, u32[]{:S(2)}) %collective-permute-start.6) | collective-permute-done | bytes 524320 | tf_op jit(solution)/shard_map/ppermute | solution.py:720
  56.6 0.2 share_near.1
  56.9 0.1 collective-permute-start.12
  56.9 0.1 collective-permute-start.10
  57.0 3.4 %collective-permute-start.11 = (bf16[2,256,256]{2,1,0:T(8,128)(2,1)S(1)}, bf16[2,256,256]{2,1,0:T(8,128)(2,1)S(1)}, u32[]{:S(2)}, u32[]{:S(2)}) collective-permute-start(bf16[2,256,256]{2,1,0:T(8,128)(2,1)S(1)} %get-tuple-element.104), channel_id=1, source_target_pairs={{0,4},{1,5},{2,6},{3,7},{4,0},{5,1},{6,2},{7,3},{8,12},{9,13},{10,... | collective-permute-start | bytes 786440 | tf_op jit(solution)/shard_map/ppermute | solution.py:720
  60.4 5.9 %spread.1 = (f32[4,256,128]{2,1,0:T(8,128)S(1)}, f32[8,3,2,16,128]{4,3,2,1,0:T(8,128)S(1)}, bf16[8,3,16,256]{3,2,1,0:T(8,128)(2,1)S(1)}, bf16[8,3,16,256]{3,2,1,...) custom-call(s32[4,2,32]{2,1,0:T(2,128)S(1)} %bitcast.25, s32[4,2,32]{2,1,0:T(2,128)S(1)} %bitcast.28, ...), custom_call_target="tpu_custom_call" | custom-call | bytes 21000000 | tf_op jit(solution)/shard_map/spread/pallas_call | solution.py:682
  66.4 2.1 %taps.1 = bf16[128,256]{1,0:T(8,128)(2,1)S(1)} custom-call(f32[4,528,128]{2,1,0:T(8,128)S(1)} %get-tuple-element.106.refs_0_, f32[4,512,128]{2,1,0:T(8,128)S(1)} %get-tuple-element.107.refs_1_, f32[16,256]{1,0:T(8,128)S(1)} %get-tuple-element.108.refs_2_.refs_5_, f32[16,256]{1,0:T(8,128)S(1)} %get-tuple-element.109.refs_3_, ...), custom_call_target="tpu_custom_call" | custom-call | bytes 7350000 | tf_op jit(solution)/shard_map/taps/pallas_call | solution.py:682
  68.4 0.0 collective-permute-done.12
  68.4 2.8 %collective-permute-done.10 = bf16[2,256,256]{2,1,0:T(8,128)(2,1)S(1)} collective-permute-done((bf16[2,256,256]{2,1,0:T(8,128)(2,1)S(1)}, bf16[2,256,256]{2,1,0:T(8,128)(2,1)S(1)}, u32[]{:S(2)}, u32[]{:S(2)}) %collective-permute-start.10) | collective-permute-done | bytes 262176 | tf_op jit(solution)/shard_map/ppermute | solution.py:720
  71.2 0.0 collective-permute-done.11
  71.2 0.1 quarter.1.refs_0_
  71.4 3.3 %collective-permute-start.13 = (bf16[5,128,256]{2,1,0:T(8,128)(2,1)S(1)}, bf16[5,128,256]{2,1,0:T(8,128)(2,1)S(1)}, u32[]{:S(2)}, u32[]{:S(2)}) collective-permute-start(bf16[5,128,256]{2,1,0:T(8,128)(2,1)S(1)} %quarter.1.refs_0_), channel_id=1, source_target_pairs={{0,8},{1,9},{2,10},{3,11},{4,12},{5,13},{6,14},{7,15},{8,0},{9,1},... | collective-permute-start | bytes 983048 | tf_op jit(solution)/shard_map/ppermute | solution.py:713
  74.7 0.0 collective-permute-start.8
  74.7 4.4 %collective-permute-start.9 = (bf16[8,3,16,256]{3,2,1,0:T(8,128)(2,1)S(1)}, bf16[8,3,16,256]{3,2,1,0:T(8,128)(2,1)S(1)}, u32[]{:S(2)}, u32[]{:S(2)}) collective-permute-start(bf16[8,3,16,256]{3,2,1,0:T(8,128)(2,1)S(1)} %get-tuple-element.101), channel_id=1, source_target_pairs={{0,15},{1,0},{2,1},{3,2},{4,3},{5,4},{6,5},{7,6},{8,7},{9,8},{10,9... | collective-permute-start | bytes 589832 | tf_op jit(solution)/shard_map/ppermute | solution.py:707
  79.1 6.4 %collective-permute-done.8.refs_2_ = bf16[8,3,16,256]{3,2,1,0:T(8,128)(2,1)S(1)} collective-permute-done((bf16[8,3,16,256]{3,2,1,0:T(8,128)(2,1)S(1)}, bf16[8,3,16,256]{3,2,1,0:T(8,128)(2,1)S(1)}, u32[]{:S(2)}, u32[]{:S(2)}) %collective-permute-start.8) | collective-permute-done | bytes 196640 | tf_op jit(solution)/shard_map/ppermute | solution.py:707
  85.6 0.0 collective-permute-done.9.refs_3_
  85.6 0.9 last.1
  86.5 3.1 %collective-permute-done.13.refs_1_ = bf16[5,128,256]{2,1,0:T(8,128)(2,1)S(1)} collective-permute-done((bf16[5,128,256]{2,1,0:T(8,128)(2,1)S(1)}, bf16[5,128,256]{2,1,0:T(8,128)(2,1)S(1)}, u32[]{:S(2)}, u32[]{:S(2)}) %collective-permute-start.13) | collective-permute-done | bytes 327712 | tf_op jit(solution)/shard_map/ppermute | solution.py:713
  89.6 0.1 pair.1.refs_0_
  89.7 2.5 %collective-permute-start.14 = (bf16[5,128,256]{2,1,0:T(8,128)(2,1)S(1)}, bf16[5,128,256]{2,1,0:T(8,128)(2,1)S(1)}, u32[]{:S(2)}, u32[]{:S(2)}) collective-permute-start(bf16[5,128,256]{2,1,0:T(8,128)(2,1)S(1)} %pair.1.refs_0_), channel_id=1, source_target_pairs={{0,2},{1,3},{2,0},{3,1},{4,6},{5,7},{6,4},{7,5},{8,10},{9,11},{10,... | collective-permute-start | bytes 983048 | tf_op jit(solution)/shard_map/ppermute | solution.py:713
  92.2 0.3 collective-permute-start.15
  92.5 1.4 %collective-permute-start.16 = (bf16[5,128,256]{2,1,0:T(8,128)(2,1)S(1)}, bf16[5,128,256]{2,1,0:T(8,128)(2,1)S(1)}, u32[]{:S(2)}, u32[]{:S(2)}) collective-permute-start(bf16[5,128,256]{2,1,0:T(8,128)(2,1)S(1)} %pair.1.refs_0_), channel_id=1, source_target_pairs={{0,6},{1,7},{2,4},{3,5},{4,2},{5,3},{6,0},{7,1},{8,14},{9,15},{10,... | collective-permute-start | bytes 983048 | tf_op jit(solution)/shard_map/ppermute | solution.py:713
  93.9 5.2 %collective-permute-done.14.refs_1_ = bf16[5,128,256]{2,1,0:T(8,128)(2,1)S(1)} collective-permute-done((bf16[5,128,256]{2,1,0:T(8,128)(2,1)S(1)}, bf16[5,128,256]{2,1,0:T(8,128)(2,1)S(1)}, u32[]{:S(2)}, u32[]{:S(2)}) %collective-permute-start.14) | collective-permute-done | bytes 327712 | tf_op jit(solution)/shard_map/ppermute | solution.py:713
  99.1 3.7 %collective-permute-done.15.refs_2_ = bf16[5,128,256]{2,1,0:T(8,128)(2,1)S(1)} collective-permute-done((bf16[5,128,256]{2,1,0:T(8,128)(2,1)S(1)}, bf16[5,128,256]{2,1,0:T(8,128)(2,1)S(1)}, u32[]{:S(2)}, u32[]{:S(2)}) %collective-permute-start.15) | collective-permute-done | bytes 327712 | tf_op jit(solution)/shard_map/ppermute | solution.py:713
  102.8 6.3 %collective-permute-done.16.refs_3_ = bf16[5,128,256]{2,1,0:T(8,128)(2,1)S(1)} collective-permute-done((bf16[5,128,256]{2,1,0:T(8,128)(2,1)S(1)}, bf16[5,128,256]{2,1,0:T(8,128)(2,1)S(1)}, u32[]{:S(2)}, u32[]{:S(2)}) %collective-permute-start.16) | collective-permute-done | bytes 327712 | tf_op jit(solution)/shard_map/ppermute | solution.py:713
  109.1 0.1 order_near.1.refs_0_
  109.2 0.1 collective-permute-start.17
  109.3 1.5 %unpack_mine.1 = (f32[2,256,1024]{2,1,0:T(8,128)}, f32[2,1024,256]{2,1,0:T(8,128)}) custom-call(bf16[17,128,256]{2,1,0:T(8,128)(2,1)S(1)} %order_near.1.refs_0_), custom_call_target="tpu_custom_call" | custom-call | bytes 5250000 | tf_op jit(solution)/shard_map/unpack_mine/pallas_call | solution.py:682
  110.8 1.2 %collective-permute-done.17.refs_1_ = bf16[17,128,256]{2,1,0:T(8,128)(2,1)S(1)} collective-permute-done((bf16[17,128,256]{2,1,0:T(8,128)(2,1)S(1)}, bf16[17,128,256]{2,1,0:T(8,128)(2,1)S(1)}, u32[]{:S(2)}, u32[]{:S(2)}) %collective-permute-start.17) | collective-permute-done | bytes 1114144 | tf_op jit(solution)/shard_map/ppermute | solution.py:713
  112.1 2.2 %unpack_theirs.1 = (f32[2,256,1024]{2,1,0:T(8,128)}, f32[2,1024,256]{2,1,0:T(8,128)}, f32[7,7,2,256]{3,2,1,0:T(2,128)}, f32[2,256]{1,0:T(2,128)}, f32[2,256]{1,0:T(2,128)}) custom-call(bf16[17,128,256]{2,1,0:T(8,128)(2,1)S(1)} %order_near.1.refs_0_, ...), custom_call_target="tpu_custom_call", output_to_operand_aliasing={{0}: (2, {}), {1}: (3, {})} | custom-call | bytes 5250000 | tf_op jit(solution)/shard_map/unpack_theirs/pallas_call | solution.py:682
  (5 shorter events, 0.0 us)
Async XLA Ops:
  0.6 1.0 copy-start.3
  1.6 10.7 %copy-start.5 = (s32[32,4,2]{0,2,1:T(2,128)S(1)}, s32[32,4,2]{0,2,1:T(2,128)}, u32[]{:S(2)}) copy-start(s32[32,4,2]{0,2,1:T(2,128)} %param.16) | copy-start | bytes 3076
  1.6 10.7 %copy-start.6 = (s32[32,4,2]{0,2,1:T(2,128)S(1)}, s32[32,4,2]{0,2,1:T(2,128)}, u32[]{:S(2)}) copy-start(s32[32,4,2]{0,2,1:T(2,128)} %param.17) | copy-start | bytes 3076
  1.7 10.6 %collective-permute-start = (bf16[8,3,16,256]{3,2,1,0:T(8,128)(2,1)S(1)}, bf16[8,3,16,256]{3,2,1,0:T(8,128)(2,1)S(1)}, u32[]{:S(2)}, u32[]{:S(2)}) collective-permute-start(bf16[8,3,16,256]{3,2,1,0:T(8,128)(2,1)S(1)} %get-tuple-element.64.refs_5_.refs_3_), channel_id=1, source_target_pairs={{0,1},{1,2},{2,3},{3,4},{4,5},{5,6},{6,7},{7,8},{8,9},{9,10},{10,1... | collective-permute-start | bytes 589832 | tf_op jit(solution)/shard_map/ppermute | solution.py:707
  2.2 10.1 %collective-permute-start.1 = (bf16[8,3,16,256]{3,2,1,0:T(8,128)(2,1)S(1)}, bf16[8,3,16,256]{3,2,1,0:T(8,128)(2,1)S(1)}, u32[]{:S(2)}, u32[]{:S(2)}) collective-permute-start(bf16[8,3,16,256]{3,2,1,0:T(8,128)(2,1)S(1)} %get-tuple-element.64.refs_5_.refs_3_), channel_id=1, source_target_pairs={{0,15},{1,0},{2,1},{3,2},{4,3},{5,4},{6,5},{7,6},{8,7},{9,8},{10,9... | collective-permute-start | bytes 589832 | tf_op jit(solution)/shard_map/ppermute | solution.py:707
  7.3 1.2 %copy-start = (bf16[2,256,1024]{2,1,0:T(8,128)(2,1)S(1)}, bf16[2,256,1024]{2,1,0:T(8,128)(2,1)}, u32[]{:S(2)}) copy-start(bf16[2,256,1024]{2,1,0:T(8,128)(2,1)} %refs_3_.1) | copy-start | bytes 3145732
  8.5 1.2 %copy-start.1 = (bf16[2,1024,256]{2,1,0:T(8,128)(2,1)S(1)}, bf16[2,1024,256]{2,1,0:T(8,128)(2,1)}, u32[]{:S(2)}) copy-start(bf16[2,1024,256]{2,1,0:T(8,128)(2,1)} %refs_4_.1) | copy-start | bytes 3145732
  9.7 0.9 copy-start.4
  10.6 0.7 copy-start.7
  11.3 0.7 copy-start.8
  12.3 16.6 %copy-start.2 = (bf16[2,16,16,256]{3,2,1,0:T(8,128)(2,1)S(1)}, bf16[2,16,16,256]{3,2,1,0:T(8,128)(2,1)}, u32[]{:S(2)}) copy-start(bf16[2,16,16,256]{3,2,1,0:T(8,128)(2,1)} %refs_11_.1) | copy-start | bytes 786436
  21.0 7.8 %collective-permute-start.2 = (bf16[8,3,16,256]{3,2,1,0:T(8,128)(2,1)S(1)}, bf16[8,3,16,256]{3,2,1,0:T(8,128)(2,1)S(1)}, u32[]{:S(2)}, u32[]{:S(2)}) collective-permute-start(bf16[8,3,16,256]{3,2,1,0:T(8,128)(2,1)S(1)} %get-tuple-element.71.refs_3_), channel_id=1, source_target_pairs={{0,1},{1,2},{2,3},{3,4},{4,5},{5,6},{6,7},{7,8},{8,9},{9,10},{10,1... | collective-permute-start | bytes 589832 | tf_op jit(solution)/shard_map/ppermute | solution.py:707
  21.1 7.8 %collective-permute-start.3 = (bf16[8,3,16,256]{3,2,1,0:T(8,128)(2,1)S(1)}, bf16[8,3,16,256]{3,2,1,0:T(8,128)(2,1)S(1)}, u32[]{:S(2)}, u32[]{:S(2)}) collective-permute-start(bf16[8,3,16,256]{3,2,1,0:T(8,128)(2,1)S(1)} %get-tuple-element.71.refs_3_), channel_id=1, source_target_pairs={{0,15},{1,0},{2,1},{3,2},{4,3},{5,4},{6,5},{7,6},{8,7},{9,8},{10,9... | collective-permute-start | bytes 589832 | tf_op jit(solution)/shard_map/ppermute | solution.py:707
  44.4 7.9 %collective-permute-start.4 = (bf16[8,3,16,256]{3,2,1,0:T(8,128)(2,1)S(1)}, bf16[8,3,16,256]{3,2,1,0:T(8,128)(2,1)S(1)}, u32[]{:S(2)}, u32[]{:S(2)}) collective-permute-start(bf16[8,3,16,256]{3,2,1,0:T(8,128)(2,1)S(1)} %get-tuple-element.75), channel_id=1, source_target_pairs={{0,1},{1,2},{2,3},{3,4},{4,5},{5,6},{6,7},{7,8},{8,9},{9,10},{10,1... | collective-permute-start | bytes 589832 | tf_op jit(solution)/shard_map/ppermute | solution.py:707
  44.4 7.9 %collective-permute-start.5 = (bf16[8,3,16,256]{3,2,1,0:T(8,128)(2,1)S(1)}, bf16[8,3,16,256]{3,2,1,0:T(8,128)(2,1)S(1)}, u32[]{:S(2)}, u32[]{:S(2)}) collective-permute-start(bf16[8,3,16,256]{3,2,1,0:T(8,128)(2,1)S(1)} %get-tuple-element.76), channel_id=1, source_target_pairs={{0,15},{1,0},{2,1},{3,2},{4,3},{5,4},{6,5},{7,6},{8,7},{9,8},{10,9... | collective-permute-start | bytes 589832 | tf_op jit(solution)/shard_map/ppermute | solution.py:707
  52.2 2.9 %collective-permute-start.7 = (bf16[1024,256]{1,0:T(8,128)(2,1)S(1)}, bf16[1024,256]{1,0:T(8,128)(2,1)S(1)}, u32[]{:S(2)}, u32[]{:S(2)}) collective-permute-start(bf16[1024,256]{1,0:T(8,128)(2,1)S(1)} %get-tuple-element.96), channel_id=1, source_target_pairs={{0,1},{1,0},{2,3},{3,2},{4,5},{5,4},{6,7},{7,6},{8,9},{9,8},{10,11... | collective-permute-start | bytes 1572872 | tf_op jit(solution)/shard_map/ppermute | solution.py:720
  54.6 2.1 %collective-permute-start.6 = (bf16[1024,256]{1,0:T(8,128)(2,1)S(1)}, bf16[1024,256]{1,0:T(8,128)(2,1)S(1)}, u32[]{:S(2)}, u32[]{:S(2)}) collective-permute-start(bf16[1024,256]{1,0:T(8,128)(2,1)S(1)} %get-tuple-element.86), channel_id=1, source_target_pairs={{0,1},{1,0},{2,3},{3,2},{4,5},{5,4},{6,7},{7,6},{8,9},{9,8},{10,11... | collective-permute-start | bytes 1572872 | tf_op jit(solution)/shard_map/ppermute | solution.py:720
  56.9 11.6 %collective-permute-start.12 = (bf16[2,256,256]{2,1,0:T(8,128)(2,1)S(1)}, bf16[2,256,256]{2,1,0:T(8,128)(2,1)S(1)}, u32[]{:S(2)}, u32[]{:S(2)}) collective-permute-start(bf16[2,256,256]{2,1,0:T(8,128)(2,1)S(1)} %get-tuple-element.105), channel_id=1, source_target_pairs={{0,6},{1,7},{2,4},{3,5},{4,2},{5,3},{6,0},{7,1},{8,14},{9,15},{10,... | collective-permute-start | bytes 786440 | tf_op jit(solution)/shard_map/ppermute | solution.py:720
  56.9 14.3 %collective-permute-start.10 = (bf16[2,256,256]{2,1,0:T(8,128)(2,1)S(1)}, bf16[2,256,256]{2,1,0:T(8,128)(2,1)S(1)}, u32[]{:S(2)}, u32[]{:S(2)}) collective-permute-start(bf16[2,256,256]{2,1,0:T(8,128)(2,1)S(1)} %get-tuple-element.103), channel_id=1, source_target_pairs={{0,2},{1,3},{2,0},{3,1},{4,6},{5,7},{6,4},{7,5},{8,10},{9,11},{10,... | collective-permute-start | bytes 786440 | tf_op jit(solution)/shard_map/ppermute | solution.py:720
  57.0 14.2 %collective-permute-start.11 = (bf16[2,256,256]{2,1,0:T(8,128)(2,1)S(1)}, bf16[2,256,256]{2,1,0:T(8,128)(2,1)S(1)}, u32[]{:S(2)}, u32[]{:S(2)}) collective-permute-start(bf16[2,256,256]{2,1,0:T(8,128)(2,1)S(1)} %get-tuple-element.104), channel_id=1, source_target_pairs={{0,4},{1,5},{2,6},{3,7},{4,0},{5,1},{6,2},{7,3},{8,12},{9,13},{10,... | collective-permute-start | bytes 786440 | tf_op jit(solution)/shard_map/ppermute | solution.py:720
  71.4 18.3 %collective-permute-start.13 = (bf16[5,128,256]{2,1,0:T(8,128)(2,1)S(1)}, bf16[5,128,256]{2,1,0:T(8,128)(2,1)S(1)}, u32[]{:S(2)}, u32[]{:S(2)}) collective-permute-start(bf16[5,128,256]{2,1,0:T(8,128)(2,1)S(1)} %quarter.1.refs_0_), channel_id=1, source_target_pairs={{0,8},{1,9},{2,10},{3,11},{4,12},{5,13},{6,14},{7,15},{8,0},{9,1},... | collective-permute-start | bytes 983048 | tf_op jit(solution)/shard_map/ppermute | solution.py:713
  74.7 10.9 %collective-permute-start.8 = (bf16[8,3,16,256]{3,2,1,0:T(8,128)(2,1)S(1)}, bf16[8,3,16,256]{3,2,1,0:T(8,128)(2,1)S(1)}, u32[]{:S(2)}, u32[]{:S(2)}) collective-permute-start(bf16[8,3,16,256]{3,2,1,0:T(8,128)(2,1)S(1)} %get-tuple-element.100), channel_id=1, source_target_pairs={{0,1},{1,2},{2,3},{3,4},{4,5},{5,6},{6,7},{7,8},{8,9},{9,10},{10,1... | collective-permute-start | bytes 589832 | tf_op jit(solution)/shard_map/ppermute | solution.py:707
  74.7 10.9 %collective-permute-start.9 = (bf16[8,3,16,256]{3,2,1,0:T(8,128)(2,1)S(1)}, bf16[8,3,16,256]{3,2,1,0:T(8,128)(2,1)S(1)}, u32[]{:S(2)}, u32[]{:S(2)}) collective-permute-start(bf16[8,3,16,256]{3,2,1,0:T(8,128)(2,1)S(1)} %get-tuple-element.101), channel_id=1, source_target_pairs={{0,15},{1,0},{2,1},{3,2},{4,3},{5,4},{6,5},{7,6},{8,7},{9,8},{10,9... | collective-permute-start | bytes 589832 | tf_op jit(solution)/shard_map/ppermute | solution.py:707
  89.7 9.4 %collective-permute-start.14 = (bf16[5,128,256]{2,1,0:T(8,128)(2,1)S(1)}, bf16[5,128,256]{2,1,0:T(8,128)(2,1)S(1)}, u32[]{:S(2)}, u32[]{:S(2)}) collective-permute-start(bf16[5,128,256]{2,1,0:T(8,128)(2,1)S(1)} %pair.1.refs_0_), channel_id=1, source_target_pairs={{0,2},{1,3},{2,0},{3,1},{4,6},{5,7},{6,4},{7,5},{8,10},{9,11},{10,... | collective-permute-start | bytes 983048 | tf_op jit(solution)/shard_map/ppermute | solution.py:713
  92.2 10.5 %collective-permute-start.15 = (bf16[5,128,256]{2,1,0:T(8,128)(2,1)S(1)}, bf16[5,128,256]{2,1,0:T(8,128)(2,1)S(1)}, u32[]{:S(2)}, u32[]{:S(2)}) collective-permute-start(bf16[5,128,256]{2,1,0:T(8,128)(2,1)S(1)} %pair.1.refs_0_), channel_id=1, source_target_pairs={{0,4},{1,5},{2,6},{3,7},{4,0},{5,1},{6,2},{7,3},{8,12},{9,13},{10,... | collective-permute-start | bytes 983048 | tf_op jit(solution)/shard_map/ppermute | solution.py:713
  92.5 16.6 %collective-permute-start.16 = (bf16[5,128,256]{2,1,0:T(8,128)(2,1)S(1)}, bf16[5,128,256]{2,1,0:T(8,128)(2,1)S(1)}, u32[]{:S(2)}, u32[]{:S(2)}) collective-permute-start(bf16[5,128,256]{2,1,0:T(8,128)(2,1)S(1)} %pair.1.refs_0_), channel_id=1, source_target_pairs={{0,6},{1,7},{2,4},{3,5},{4,2},{5,3},{6,0},{7,1},{8,14},{9,15},{10,... | collective-permute-start | bytes 983048 | tf_op jit(solution)/shard_map/ppermute | solution.py:713
  109.2 2.8 %collective-permute-start.17 = (bf16[17,128,256]{2,1,0:T(8,128)(2,1)S(1)}, bf16[17,128,256]{2,1,0:T(8,128)(2,1)S(1)}, u32[]{:S(2)}, u32[]{:S(2)}) collective-permute-start(bf16[17,128,256]{2,1,0:T(8,128)(2,1)S(1)} %order_near.1.refs_0_), channel_id=1, source_target_pairs={{0,1},{1,0},{2,3},{3,2},{4,5},{5,4},{6,7},{7,6},{8,9},{9,8},{10,11... | collective-permute-start | bytes 3342344 | tf_op jit(solution)/shard_map/ppermute | solution.py:713

commit v6 on v4

--- a/solution.py
+++ b/solution.py
@@ -518,12 +518,16 @@
     gather_inner(sz, flat_grad_row(sz, flat), grad_pad, base)
 
 
-def taps_kernel(sz, pad, grad_conv, gain_sums, scale_sums, other, both, tap_sums, small):
+def taps_kernel(
+    sz, pad, grad_conv, gain_sums, scale_sums, other, keep, send, tap_sums, small, both
+):
     small[...] = jnp.zeros_like(small)
     tap_gradients(sz, pad, grad_conv, tap_sums, small)
     fill_small(small, gain_sums, scale_sums)
-    both[0:SMALL_ROWS] = small[...].astype(BF16)
-    both[SMALL_ROWS : 2 * SMALL_ROWS] = other[...].astype(BF16)
+    both[0] = small[...]
+    both[1] = other[...]
+    keep[...] = both[digit_of(0)].astype(BF16)
+    send[...] = both[1 - digit_of(0)].astype(BF16)
 
 
 def last_kernel(sz, base, own, first, second, out_hbm, token, flat, out, sems):
@@ -546,70 +550,70 @@
 
 
 def share_near_kernel(*refs):
-    arrays, outs = refs[:2], refs[2:]
+    arrays, outs = refs[:4], refs[4:]
     for k, out in enumerate(outs):
         piece = digit_of(1) ^ k
-        add_rows(out, [lambda rows, array=array: array[piece, rows] for array in arrays])
-
-
-def share_far_kernel(*refs):
-    rest, share = refs[0].shape[:2]
-    arrays, outs = refs[:-rest], refs[-rest:]
-    for k, out in enumerate(outs):
-        piece = digit_of(2) ^ k
         for layer in range(2):
-            parts = arrays[4 * layer : 4 * layer + 4]
+            parts = arrays[2 * layer : 2 * layer + 2]
             add_rows(
                 out.at[layer],
                 [lambda rows, array=array: array[piece, rows] for array in parts],
             )
 
 
-def total_kernel(*refs):
-    out, small = refs[-1], refs[-2]
+def quarter_kernel(*refs):
+    arrays, keep, came, out = refs[:4], refs[4], refs[5], refs[6]
+    quarter = arrays[0].shape[1]
     for layer in range(2):
         add_rows(
-            out.at[layer],
-            [lambda rows, array=array: array[layer, rows] for array in refs[:-2]],
+            out.at[layer * quarter : (layer + 1) * quarter],
+            [lambda rows, array=array: array[layer, rows] for array in arrays],
         )
-    out[2:] = small[...]
-
-
-def order_kernel(level, small_units, *refs):
-    pieces, out = refs[:-1], refs[-1]
-    units = pieces[0].shape[0] - small_units
+    add_rows(out.at[2 * quarter :], [lambda rows: keep[rows], lambda rows: came[rows]])
+
+
+def far_kernel(*refs):
+    pieces, out, held = refs[:-2], refs[-2], refs[-1]
+    if len(pieces) == 2:
+        add_rows(out, [lambda rows: pieces[0][rows], lambda rows: pieces[1][rows]])
+        return
     for k, piece in enumerate(pieces):
-        at = (digit_of(level) ^ k) * units
-        for j in range(units):
-            out[at + j] = piece[j]
-    for j in range(small_units):
-        add_rows(
-            out.at[len(pieces) * units + j],
-            [lambda rows, piece=piece: piece[units + j, rows] for piece in pieces],
-        )
+        held[digit_of(2) ^ k] = piece[...]
+    add_rows(out, [lambda rows, k=k: held[k, rows] for k in range(len(pieces))])
+
+
+def order_kernel(quarter, *refs):
+    pieces, out, held = refs[:4], refs[4], refs[5]
+    for k, piece in enumerate(pieces):
+        place = digit_of(1) ^ k
+        out[pl.ds(pl.multiple_of(place * quarter, quarter), quarter), :] = piece[0:quarter]
+        if quarter < piece.shape[0]:
+            held[place] = piece[quarter:]
+    if out.shape[0] > 4 * quarter:
+        add_rows(out.at[4 * quarter :], [lambda rows, k=k: held[k, rows] for k in range(4)])
 
 
 def unpack_half(sz, half, source, staged, up_hbm, down_hbm, sems):
-    share = source.shape[1]
-    target = (down_hbm, up_hbm)[half]
-    pieces = sz.hidden // share
     copies = []
+    size = sz.hidden // 4
     for layer in range(2):
-        for j in range(pieces):
-            value = source[2 * j + layer].astype(F32)
+        for k in range(4):
+            start = (2 * k + layer) * size
+            rows = slice(k * size, (k + 1) * size)
+            staged[layer, rows] = source[start : start + size].astype(F32)
             if half == 0:
-                staged[layer, j * share : (j + 1) * share] = value
+                pairs = [(rows, down_hbm.at[layer, rows])]
             else:
-                k, c = divmod(j * share, sz.channels)
-                staged[layer, k * sz.channels + c : k * sz.channels + c + share] = value
-        for k in range(sz.hidden // sz.channels):
-            rows = pl.ds(k * sz.channels, sz.channels)
-            place = target.at[layer, rows] if half == 0 else target.at[layer, :, rows]
-            copy = pltpu.make_async_copy(
-                staged.at[layer, rows], place, sems.at[half, len(copies)]
-            )
-            copy.start()
-            copies.append(copy)
+                pairs = []
+                for at in range(k * size, (k + 1) * size, sz.channels):
+                    columns = slice(at, at + sz.channels)
+                    pairs.append((columns, up_hbm.at[layer, :, columns]))
+            for part, place in pairs:
+                copy = pltpu.make_async_copy(
+                    staged.at[layer, part], place, sems.at[half, len(copies)]
+                )
+                copy.start()
+                copies.append(copy)
     for copy in copies:
         copy.wait()
 
@@ -626,25 +630,20 @@
     sz, mine, theirs, _up, _down, up_hbm, down_hbm, kernel_out, gain_out, scale_out,
     staged, small, sems,
 ):
+    start = 2 * sz.hidden
+    small[digit_of(0)] = mine[start:].astype(F32)
+    small[1 - digit_of(0)] = theirs[start:].astype(F32)
+    for layer in range(2):
+        for a in range(TAPS):
+            for b in range(TAPS):
+                kernel_out[a, b, layer : layer + 1] = small[layer, pl.ds(a * 8 + b, 1), :]
+        gain_out[layer : layer + 1] = small[layer, pl.ds(TAPS * 8, 1), :]
+        scale_out[layer : layer + 1] = small[layer, pl.ds(TAPS * 8 + 1, 1), :]
     for half in range(2):
 
         @pl.when(digit_of(0) == 1 - half)
         def _(half=half):
             unpack_half(sz, half, theirs, staged, up_hbm, down_hbm, sems)
-
-    share = mine.shape[1]
-    start = 2 * sz.hidden // share
-    for j in range(start, mine.shape[0]):
-        rows = pl.ds((j - start) * share, share)
-        small[rows, :] = mine[j].astype(F32) + theirs[j].astype(F32)
-    for layer in range(2):
-        at = layer * SMALL_ROWS
-        for a in range(TAPS):
-            for b in range(TAPS):
-                kernel_out[a, b, layer : layer + 1] = small[pl.ds(at + a * 8 + b, 1), :]
-        at = at + TAPS * 8
-        gain_out[layer : layer + 1] = small[pl.ds(at, 1), :]
-        scale_out[layer : layer + 1] = small[pl.ds(at + 1, 1), :]
 
 
 IN_VMEM = pl.BlockSpec(memory_space=pltpu.VMEM)
@@ -703,54 +702,48 @@
 
 class Reduction:
     def __init__(self, devices):
-        self.devices = devices
-        self.rest = devices // 8
         self.near_masks = [2 * k for k in range(1, 4)]
-        self.rest_masks = [8 * k for k in range(1, self.rest)]
-
-    def start(self, keep, send):
-        rows, channels = keep.shape
-        (came,) = swap([send], [1])
-        quarter = rows // 4
-        parts = (4, quarter, channels)
-        shape = jax.ShapeDtypeStruct((quarter, channels), BF16)
+        self.far_masks = [8 * k for k in range(1, devices // 8)]
+
+    def share(self, *halves_of_layers):
+        arrays = []
+        for keep, send in halves_of_layers:
+            rows, channels = keep.shape
+            dims = (4, rows // 4, channels)
+            arrays += [keep.reshape(dims), swap([send], [1])[0].reshape(dims)]
+        shape = jax.ShapeDtypeStruct((2,) + dims[1:], BF16)
         pieces = call(
-            share_near_kernel, "share_near", 0.7,
-            near(keep.reshape(parts), came.reshape(parts)), near(*[shape] * 4), [],
+            share_near_kernel, "share_near", 0.3, near(*arrays), near(*[shape] * 4), [],
         )
         return [pieces[0]] + swap(pieces[1:], self.near_masks)
 
-    def finish(self, parts, after, small):
-        quarter, channels = parts[0][0].shape
-        dims = (self.rest, quarter // self.rest, channels)
-        arrays = [part.reshape(dims) for layer in parts for part in layer]
-        shape = jax.ShapeDtypeStruct((2,) + dims[1:], BF16)
-        pieces = call(
-            share_far_kernel, "share_far", 0.9,
-            near(*arrays), near(*[shape] * self.rest), [], after,
+    def quarters(self, parts, keep, send):
+        _, rows, channels = parts[0].shape
+        shape = jax.ShapeDtypeStruct((2 * rows + keep.shape[0], channels), BF16)
+        (total,) = call(
+            quarter_kernel, "quarter", 0.4,
+            near(*parts, keep, *swap([send], [1])), near(shape), [],
         )
-        arrived = swap(pieces[1:], self.rest_masks)
-        small = small(pieces[0]).reshape((-1,) + dims[1:])
-        shape = jax.ShapeDtypeStruct((2 + small.shape[0],) + dims[1:], BF16)
+        return total
+
+    def exchange(self, total, after=()):
+        shape = jax.ShapeDtypeStruct(total.shape, BF16)
+        pieces = [total] + partners(total, self.far_masks)
+        held = (len(pieces),) + total.shape if len(pieces) > 2 else (1, 16, LANES)
         (total,) = call(
-            total_kernel, "total", 0.4, near(pieces[0], *arrived, small), near(shape), []
+            far_kernel, "far", 0.3, near(*pieces), near(shape), [pltpu.VMEM(held, BF16)], after
         )
-        return total, small.shape[0]
-
-    def gather(self, total, small_units, after):
-        for level, masks, name in (
-            (2, self.rest_masks, "order_far"),
-            (1, self.near_masks, "order_near"),
-        ):
-            pieces = [total] + partners(total, masks)
-            units = (total.shape[0] - small_units) * len(pieces) + small_units
-            shape = jax.ShapeDtypeStruct((units,) + total.shape[1:], BF16)
-            (total,) = call(
-                functools.partial(order_kernel, level, small_units), name, 0.5,
-                near(*pieces), near(shape), [], after,
-            )
-            after = ()
-        return total, partners(total, [1])[0]
+        return total
+
+    def gather(self, total, quarter, after=()):
+        rows, channels = total.shape
+        shape = jax.ShapeDtypeStruct((3 * quarter + rows, channels), BF16)
+        (whole,) = call(
+            functools.partial(order_kernel, quarter), "order", 0.4,
+            near(total, *partners(total, self.near_masks)), near(shape),
+            [pltpu.VMEM((4, max(rows - quarter, 16), channels), BF16)], after,
+        )
+        return whole
 
 
 def on_device(
@@ -850,7 +843,6 @@
         near(half, half, small),
         vmem(tap_sums, two_halves),
     )
-    parts_one = reduction.start(keep_one, send_one)
     keep_zero, send_zero, flat, up_in, scale_sums = call(
         functools.partial(backward_kernel, sz, 0),
         "backward", 2.9,
@@ -860,30 +852,22 @@
         near(half, half, slabs, wide_short, sums),
         vmem(wide, narrow_short, two_halves),
     )
-    parts_zero = reduction.start(keep_zero, send_zero)
+    parts = reduction.share((keep_zero, send_zero), (keep_one, send_one))
     base, grad_own, grad_below, grad_above, grad_conv, gain_sums = call(
         functools.partial(spread_kernel, sz, 0),
         "spread", 6.0,
         plan + near(kern, gain, up, flat, up_in, normal, inverse),
         near(slabs, own_shape, strips_shape, strips_shape, grad_slabs, sums),
         vmem(taps, narrow, grad_pool, padded),
-        (parts_zero[0],),
+        (parts[0],),
     )
     from_below, from_above = pass_on(grad_above, 1), pass_on(grad_below, -1)
-
-    def small_gradients(share):
-        (both,) = call(
-            functools.partial(taps_kernel, sz),
-            "taps", 2.1,
-            near(pad_zero, grad_conv, gain_sums, scale_sums, small_one),
-            near(shape((2 * SMALL_ROWS, channels), BF16)),
-            vmem(tap_sums, small),
-            (share,),
-        )
-        return both
-
-    total, small_units = reduction.finish(
-        (parts_zero, parts_one), (gain_sums,), small_gradients
+    small_keep, small_send = call(
+        functools.partial(taps_kernel, sz),
+        "taps", 2.1,
+        near(pad_zero, grad_conv, gain_sums, scale_sums, small_one),
+        near(*[shape(small.shape, BF16)] * 2),
+        vmem(tap_sums, small, shape((2,) + small.shape, F32)),
     )
     in_grad, token = call(
         functools.partial(last_kernel, sz),
@@ -892,28 +876,29 @@
         far(image) + near(shape((8, LANES), F32)),
         vmem(slabs, image) + sems(1),
     )
-    mine, theirs = reduction.gather(total, small_units, (token,))
+    total = reduction.quarters(parts, small_keep, small_send)
+    total = reduction.exchange(total, (token,))
+    mine = reduction.gather(total, hidden // 2)
+    theirs = partners(mine, [1])[0]
     weight_shapes = [shape(up_weight.shape, F32), shape(down_weight.shape, F32)]
-    copies = layers * hidden // channels
-    scratch = vmem(shape(down_weight.shape, F32))
+    staged = shape((layers, hidden, channels), F32)
+    copies = [pltpu.SemaphoreType.DMA((2, layers * hidden // channels))]
     grad_up, grad_down = call(
         functools.partial(unpack_mine_kernel, sz),
-        "unpack_mine", 1.5,
+        "unpack_mine", 1.0,
         near(mine),
         far(*weight_shapes),
-        scratch + [pltpu.SemaphoreType.DMA((2, copies))],
+        vmem(staged) + copies,
     )
     grad_up, grad_down, grad_kernel, grad_gain, grad_scale = call(
         functools.partial(unpack_theirs_kernel, sz),
-        "unpack_theirs", 1.5,
+        "unpack_theirs", 1.3,
         near(mine, theirs) + far(grad_up, grad_down),
         far(*weight_shapes)
         + near(
             shape(kern.shape, F32), shape(norm_gain.shape, F32), shape(norm_gain.shape, F32)
         ),
-        scratch
-        + vmem(shape((2 * SMALL_ROWS, channels), F32))
-        + [pltpu.SemaphoreType.DMA((2, copies))],
+        vmem(staged, shape((2,) + small.shape, F32)) + copies,
         aliases={2: 0, 3: 1},
     )
     return (

time: 112 us -> 112 us (level)
    ppermute x5, waiting for transfers between devices: 20.9 us -> 16 us  [partners(): lax.ppermute(array, 'tile', [(i, i ^ mask) for i in range(length)])]
    ppermute x9 -> x6, starting transfers between devices: 8.78 us -> 4.22 us  [swap(): lax.ppermute(array, 'tile', [(i, i ^ mask) for i in range(length)])]
    ppermute x8, waiting for transfers between devices: 6.03 us -> 9.82 us  [pass_on(): lax.ppermute(shard, 'tile', [(i, (i + by) % length) for i in range(length)])]
    ppermute x5, starting transfers between devices: 3.7 us -> 7.47 us  [partners(): lax.ppermute(array, 'tile', [(i, i ^ mask) for i in range(length)])]
    ppermute x9 -> x6, waiting for transfers between devices: 3.17 us -> 5.31 us  [swap(): lax.ppermute(array, 'tile', [(i, i ^ mask) for i in range(length)])]
    pallas_call x17 -> x15, Pallas kernels: 43.2 us -> 43.1 us  [call(): pl.pallas_call(run, in_specs=[spec for spec, _ in ins] + [pl.BlockSpec(me...]
  transfers between devices with their start and end apart: 22 -> 19, of which waited for: 10 -> 10; matrix products, arithmetic and copies ran while one was open for 0% -> 0% of each run, Pallas kernels for 15% -> 14%
where the time goes in v6:
time: 112 us
  Pallas kernels  43.1 us (38%)
  waiting for transfers between devices  31.1 us (28%)
  starting transfers between devices  30.9 us (28%)
  local copies, waits for them, and re-layouts  5.66 us (5%)
    pallas_call x15, Pallas kernels, call(): pl.pallas_call(run, in_specs=[spec for spec, _ in ins] + [pl.BlockSpec(me...  43.1 us
    ppermute x8, starting transfers between devices, pass_on(): lax.ppermute(shard, 'tile', [(i, (i + by) % length) for i in range(length)])  19.2 us
    ppermute x5, waiting for transfers between devices, partners(): lax.ppermute(array, 'tile', [(i, i ^ mask) for i in range(length)])  16 us
    ppermute x8, waiting for transfers between devices, pass_on(): lax.ppermute(shard, 'tile', [(i, (i + by) % length) for i in range(length)])  9.82 us
    ppermute x5, starting transfers between devices, partners(): lax.ppermute(array, 'tile', [(i, i ^ mask) for i in range(length)])  7.47 us
    unnamed x18, local copies, waits for them, and re-layouts  5.66 us
    ppermute x6, waiting for transfers between devices, swap(): lax.ppermute(array, 'tile', [(i, i ^ mask) for i in range(length)])  5.31 us
    ppermute x6, starting transfers between devices, swap(): lax.ppermute(array, 'tile', [(i, i ^ mask) for i in range(length)])  4.22 us
  transfers between devices with their start and end apart: 19, of which 10 were waited for; matrix products, arithmetic and copies ran while one was open for 0% of the time, Pallas kernels for 14%

profile of v6, /device:TPU:0, one launch (start us, length us, event | category | flops | bytes accessed | tf_op | source)
XLA Modules:
  0.0 111.8 jit_solution(1010311602103141217)
XLA Ops:
  0.6 0.0 copy-start.3
  0.6 0.9 copy-done.3
  1.6 0.1 strips.1
  1.7 0.5 collective-permute-start
  2.2 5.1 %collective-permute-start.1 = (bf16[8,3,16,256]{3,2,1,0:T(8,128)(2,1)S(1)}, bf16[8,3,16,256]{3,2,1,0:T(8,128)(2,1)S(1)}, u32[]{:S(2)}, u32[]{:S(2)}) collective-permute-start(bf16[8,3,16,256]{3,2,1,0:T(8,128)(2,1)S(1)} %get-tuple-element.66.refs_5_.refs_3_), channel_id=1, source_target_pairs={{0,15},{1,0},{2,1},{3,2},{4,3},{5,4},{6,5},{7,6},{8,7},{9,8},{10,9... | collective-permute-start | bytes 589832 | tf_op jit(solution)/shard_map/ppermute | solution.py:685
  7.3 1.2 %copy-done = bf16[2,256,1024]{2,1,0:T(8,128)(2,1)S(1)} copy-done((bf16[2,256,1024]{2,1,0:T(8,128)(2,1)S(1)}, bf16[2,256,1024]{2,1,0:T(8,128)(2,1)}, u32[]{:S(2)}) %copy-start) | copy-done | bytes 1048600
  8.5 1.2 %copy-done.1 = bf16[2,1024,256]{2,1,0:T(8,128)(2,1)S(1)} copy-done((bf16[2,1024,256]{2,1,0:T(8,128)(2,1)S(1)}, bf16[2,1024,256]{2,1,0:T(8,128)(2,1)}, u32[]{:S(2)}) %copy-start.1) | copy-done | bytes 1048600
  9.7 0.9 copy-done.4
  10.6 0.7 copy-done.7
  11.3 0.7 copy-done.8
  12.0 0.3 fetch.1
  12.3 0.0 copy-start.2
  12.3 0.0 collective-permute-done.refs_4_
  12.3 0.0 collective-permute-done.1.refs_5_
  12.3 0.0 copy-done.5
  12.3 0.0 copy-done.6
  12.3 8.7 %forward.1 = (bf16[2,16,16,256]{3,2,1,0:T(8,128)(2,1)S(1)}, bf16[8,3,16,256]{3,2,1,0:T(8,128)(2,1)S(1)}, f32[4,528,128]{2,1,0:T(8,128)S(1)}, f32[4,256,128]{2,1,...) custom-call(s32[4,2,32]{2,1,0:T(2,128)S(1)} %bitcast.13, ...), custom_call_target="tpu_custom_call" | custom-call | bytes 30450000 | tf_op jit(solution)/shard_map/forward/pallas_call | solution.py:660
  21.0 0.1 collective-permute-start.2
  21.1 4.4 %collective-permute-start.3 = (bf16[8,3,16,256]{3,2,1,0:T(8,128)(2,1)S(1)}, bf16[8,3,16,256]{3,2,1,0:T(8,128)(2,1)S(1)}, u32[]{:S(2)}, u32[]{:S(2)}) collective-permute-start(bf16[8,3,16,256]{3,2,1,0:T(8,128)(2,1)S(1)} %get-tuple-element.73.refs_3_), channel_id=1, source_target_pairs={{0,15},{1,0},{2,1},{3,2},{4,3},{5,4},{6,5},{7,6},{8,7},{9,8},{10,9... | collective-permute-start | bytes 589832 | tf_op jit(solution)/shard_map/ppermute | solution.py:685
  25.5 3.3 %collective-permute-done.2.refs_4_ = bf16[8,3,16,256]{3,2,1,0:T(8,128)(2,1)S(1)} collective-permute-done((bf16[8,3,16,256]{3,2,1,0:T(8,128)(2,1)S(1)}, bf16[8,3,16,256]{3,2,1,0:T(8,128)(2,1)S(1)}, u32[]{:S(2)}, u32[]{:S(2)}) %collective-permute-start.2) | collective-permute-done | bytes 196640 | tf_op jit(solution)/shard_map/ppermute | solution.py:685
  28.8 0.0 collective-permute-done.3.refs_5_
  28.8 0.0 copy-done.2
  28.9 15.5 %turn.1 = (bf16[2,16,16,256]{3,2,1,0:T(8,128)(2,1)}, f32[4,256,128]{2,1,0:T(8,128)S(1)}, f32[8,3,2,16,128]{4,3,2,1,0:T(8,128)S(1)}, bf16[8,3,16,256]{3,2,1,0:T(8...) custom-call(s32[4,2,32]{2,1,0:T(2,128)S(1)} %bitcast.14, ...), custom_call_target="tpu_custom_call" | custom-call | bytes 53900000 | tf_op jit(solution)/shard_map/turn/pallas_call | solution.py:660
  44.4 0.1 collective-permute-start.4
  44.4 4.7 %collective-permute-start.5 = (bf16[8,3,16,256]{3,2,1,0:T(8,128)(2,1)S(1)}, bf16[8,3,16,256]{3,2,1,0:T(8,128)(2,1)S(1)}, u32[]{:S(2)}, u32[]{:S(2)}) collective-permute-start(bf16[8,3,16,256]{3,2,1,0:T(8,128)(2,1)S(1)} %get-tuple-element.78), channel_id=1, source_target_pairs={{0,15},{1,0},{2,1},{3,2},{4,3},{5,4},{6,5},{7,6},{8,7},{9,8},{10,9... | collective-permute-start | bytes 589832 | tf_op jit(solution)/shard_map/ppermute | solution.py:685
  49.1 3.1 %weights.1 = (bf16[1024,256]{1,0:T(8,128)(2,1)S(1)}, bf16[1024,256]{1,0:T(8,128)(2,1)S(1)}, f32[64,256]{1,0:T(8,128)S(1)}) custom-call(f32[4,528,128]{2,1,0:T(8,128)S(1)} %get-tuple-element.89.refs_0_, f32[4,512,128]{2,1,0:T(8,128)S(1)} %get-tuple-element.90.refs_1_, bf16[512,256]{1,0:T(8,128)(2,1)S(1)} %get-tuple-element.91.refs_2_, ...), custom_call_target="tpu_custom_call" | custom-call | bytes 9800000 | tf_op jit(solution)/shard_map/weights/pallas_call | solution.py:660
  52.2 0.1 collective-permute-start.7
  52.3 0.0 collective-permute-done.4.refs_2_
  52.3 0.0 collective-permute-done.5.refs_3_
  52.3 2.3 %backward.1 = (bf16[1024,256]{1,0:T(8,128)(2,1)S(1)}, bf16[1024,256]{1,0:T(8,128)(2,1)S(1)}, f32[4,256,128]{2,1,0:T(8,128)S(1)}, bf16[512,1024]{1,0:T(8,128)(2,1)S(1)}, f32[16,256]{1,0:T(8,128)S(1)}) custom-call(f32[4,256,128]{2,1,0:T(8,128)S(1)} %get-tuple-element.75.refs_0_, f32[8,3,2,16,128]{4,3,2,1,0:T(8,128)S(1)} %get-tuple-element.76.refs_1_, ...), custom_call_target="tpu_custom_call" | custom-call | bytes 10150000 | tf_op jit(solution)/shard_map/backward/pallas_call | solution.py:660
  54.6 0.5 collective-permute-start.6
  55.1 0.0 collective-permute-done.7
  55.1 1.5 %collective-permute-done.6 = bf16[1024,256]{1,0:T(8,128)(2,1)S(1)} collective-permute-done((bf16[1024,256]{1,0:T(8,128)(2,1)S(1)}, bf16[1024,256]{1,0:T(8,128)(2,1)S(1)}, u32[]{:S(2)}, u32[]{:S(2)}) %collective-permute-start.6) | collective-permute-done | bytes 524320 | tf_op jit(solution)/shard_map/ppermute | solution.py:698
  56.6 0.2 share_near.1
  56.9 0.1 collective-permute-start.10
  57.0 0.1 collective-permute-start.11
  57.0 3.4 %collective-permute-start.12 = (bf16[2,256,256]{2,1,0:T(8,128)(2,1)S(1)}, bf16[2,256,256]{2,1,0:T(8,128)(2,1)S(1)}, u32[]{:S(2)}, u32[]{:S(2)}) collective-permute-start(bf16[2,256,256]{2,1,0:T(8,128)(2,1)S(1)} %get-tuple-element.107), channel_id=1, source_target_pairs={{0,6},{1,7},{2,4},{3,5},{4,2},{5,3},{6,0},{7,1},{8,14},{9,15},{10,... | collective-permute-start | bytes 786440 | tf_op jit(solution)/shard_map/ppermute | solution.py:698
  60.5 5.9 %spread.1 = (f32[4,256,128]{2,1,0:T(8,128)S(1)}, f32[8,3,2,16,128]{4,3,2,1,0:T(8,128)S(1)}, bf16[8,3,16,256]{3,2,1,0:T(8,128)(2,1)S(1)}, bf16[8,3,16,256]{3,2,1,...) custom-call(s32[4,2,32]{2,1,0:T(2,128)S(1)} %bitcast.15, s32[4,2,32]{2,1,0:T(2,128)S(1)} %bitcast.18, ...), custom_call_target="tpu_custom_call" | custom-call | bytes 21000000 | tf_op jit(solution)/shard_map/spread/pallas_call | solution.py:660
  66.4 2.1 %taps.1 = (bf16[64,256]{1,0:T(8,128)(2,1)S(1)}, bf16[64,256]{1,0:T(8,128)(2,1)S(1)}) custom-call(f32[4,528,128]{2,1,0:T(8,128)S(1)} %get-tuple-element.108.refs_0_, f32[4,512,128]{2,1,0:T(8,128)S(1)} %get-tuple-element.109.refs_1_, f32[16,256]{1,0:T(8,128)S(1)} %get-tuple-element.110.refs_2_, f32[16,256]{1,0:T(8,128)S(1)} %get-tuple-element.111.refs_3_, ...), custom_call_target="tpu_custom_call" | custom-call | bytes 7350000 | tf_op jit(solution)/shard_map/taps/pallas_call | solution.py:660
  68.5 0.1 collective-permute-start.13
  68.6 1.2 %collective-permute-done.13.refs_5_ = bf16[64,256]{1,0:T(8,128)(2,1)S(1)} collective-permute-done((bf16[64,256]{1,0:T(8,128)(2,1)S(1)}, bf16[64,256]{1,0:T(8,128)(2,1)S(1)}, u32[]{:S(2)}, u32[]{:S(2)}) %collective-permute-start.13) | collective-permute-done | bytes 32800 | tf_op jit(solution)/shard_map/ppermute | solution.py:698
  69.8 0.0 collective-permute-done.10.refs_1_
  69.8 0.0 collective-permute-done.11.refs_2_
  69.8 2.6 %collective-permute-done.12.refs_3_ = bf16[2,256,256]{2,1,0:T(8,128)(2,1)S(1)} collective-permute-done((bf16[2,256,256]{2,1,0:T(8,128)(2,1)S(1)}, bf16[2,256,256]{2,1,0:T(8,128)(2,1)S(1)}, u32[]{:S(2)}, u32[]{:S(2)}) %collective-permute-start.12) | collective-permute-done | bytes 262176 | tf_op jit(solution)/shard_map/ppermute | solution.py:698
  72.3 0.1 quarter.1.refs_0_
  72.5 2.3 %collective-permute-start.14 = (bf16[576,256]{1,0:T(8,128)(2,1)S(1)}, bf16[576,256]{1,0:T(8,128)(2,1)S(1)}, u32[]{:S(2)}, u32[]{:S(2)}) collective-permute-start(bf16[576,256]{1,0:T(8,128)(2,1)S(1)} %quarter.1.refs_0_), channel_id=1, source_target_pairs={{0,8},{1,9},{2,10},{3,11},{4,12},{5,13},{6,14},{7,15},{8,0},{9,1},... | collective-permute-start | bytes 884744 | tf_op jit(solution)/shard_map/ppermute | solution.py:691
  74.8 0.0 collective-permute-start.8
  74.8 4.4 %collective-permute-start.9 = (bf16[8,3,16,256]{3,2,1,0:T(8,128)(2,1)S(1)}, bf16[8,3,16,256]{3,2,1,0:T(8,128)(2,1)S(1)}, u32[]{:S(2)}, u32[]{:S(2)}) collective-permute-start(bf16[8,3,16,256]{3,2,1,0:T(8,128)(2,1)S(1)} %get-tuple-element.103), channel_id=1, source_target_pairs={{0,15},{1,0},{2,1},{3,2},{4,3},{5,4},{6,5},{7,6},{8,7},{9,8},{10,9... | collective-permute-start | bytes 589832 | tf_op jit(solution)/shard_map/ppermute | solution.py:685
  79.2 6.5 %collective-permute-done.8.refs_2_ = bf16[8,3,16,256]{3,2,1,0:T(8,128)(2,1)S(1)} collective-permute-done((bf16[8,3,16,256]{3,2,1,0:T(8,128)(2,1)S(1)}, bf16[8,3,16,256]{3,2,1,0:T(8,128)(2,1)S(1)}, u32[]{:S(2)}, u32[]{:S(2)}) %collective-permute-start.8) | collective-permute-done | bytes 196640 | tf_op jit(solution)/shard_map/ppermute | solution.py:685
  85.7 0.0 collective-permute-done.9.refs_3_
  85.7 0.9 last.1
  86.6 1.5 %collective-permute-done.14.refs_1_ = bf16[576,256]{1,0:T(8,128)(2,1)S(1)} collective-permute-done((bf16[576,256]{1,0:T(8,128)(2,1)S(1)}, bf16[576,256]{1,0:T(8,128)(2,1)S(1)}, u32[]{:S(2)}, u32[]{:S(2)}) %collective-permute-start.14) | collective-permute-done | bytes 294944 | tf_op jit(solution)/shard_map/ppermute | solution.py:691
  88.1 0.1 far.1.refs_0_
  88.2 3.6 %collective-permute-start.15 = (bf16[576,256]{1,0:T(8,128)(2,1)S(1)}, bf16[576,256]{1,0:T(8,128)(2,1)S(1)}, u32[]{:S(2)}, u32[]{:S(2)}) collective-permute-start(bf16[576,256]{1,0:T(8,128)(2,1)S(1)} %far.1.refs_0_), channel_id=1, source_target_pairs={{0,2},{1,3},{2,0},{3,1},{4,6},{5,7},{6,4},{7,5},{8,10},{9,11},{10,... | collective-permute-start | bytes 884744 | tf_op jit(solution)/shard_map/ppermute | solution.py:691
  91.7 0.0 collective-permute-start.16
  91.7 1.5 %collective-permute-start.17 = (bf16[576,256]{1,0:T(8,128)(2,1)S(1)}, bf16[576,256]{1,0:T(8,128)(2,1)S(1)}, u32[]{:S(2)}, u32[]{:S(2)}) collective-permute-start(bf16[576,256]{1,0:T(8,128)(2,1)S(1)} %far.1.refs_0_), channel_id=1, source_target_pairs={{0,6},{1,7},{2,4},{3,5},{4,2},{5,3},{6,0},{7,1},{8,14},{9,15},{10,... | collective-permute-start | bytes 884744 | tf_op jit(solution)/shard_map/ppermute | solution.py:691
  93.3 4.8 %collective-permute-done.15.refs_1_ = bf16[576,256]{1,0:T(8,128)(2,1)S(1)} collective-permute-done((bf16[576,256]{1,0:T(8,128)(2,1)S(1)}, bf16[576,256]{1,0:T(8,128)(2,1)S(1)}, u32[]{:S(2)}, u32[]{:S(2)}) %collective-permute-start.15) | collective-permute-done | bytes 294944 | tf_op jit(solution)/shard_map/ppermute | solution.py:691
  98.0 3.6 %collective-permute-done.16.refs_2_ = bf16[576,256]{1,0:T(8,128)(2,1)S(1)} collective-permute-done((bf16[576,256]{1,0:T(8,128)(2,1)S(1)}, bf16[576,256]{1,0:T(8,128)(2,1)S(1)}, u32[]{:S(2)}, u32[]{:S(2)}) %collective-permute-start.16) | collective-permute-done | bytes 294944 | tf_op jit(solution)/shard_map/ppermute | solution.py:691
  101.6 4.9 %collective-permute-done.17.refs_3_ = bf16[576,256]{1,0:T(8,128)(2,1)S(1)} collective-permute-done((bf16[576,256]{1,0:T(8,128)(2,1)S(1)}, bf16[576,256]{1,0:T(8,128)(2,1)S(1)}, u32[]{:S(2)}, u32[]{:S(2)}) %collective-permute-start.17) | collective-permute-done | bytes 294944 | tf_op jit(solution)/shard_map/ppermute | solution.py:691
  106.6 0.1 order.1.refs_0_
  106.7 0.1 collective-permute-start.18
  106.7 1.5 %unpack_mine.1 = (f32[2,256,1024]{2,1,0:T(8,128)}, f32[2,1024,256]{2,1,0:T(8,128)}) custom-call(bf16[2112,256]{1,0:T(8,128)(2,1)S(1)} %order.1.refs_0_), custom_call_target="tpu_custom_call" | custom-call | bytes 3500000 | tf_op jit(solution)/shard_map/unpack_mine/pallas_call | solution.py:660
  108.2 1.2 %collective-permute-done.18.refs_1_ = bf16[2112,256]{1,0:T(8,128)(2,1)S(1)} collective-permute-done((bf16[2112,256]{1,0:T(8,128)(2,1)S(1)}, bf16[2112,256]{1,0:T(8,128)(2,1)S(1)}, u32[]{:S(2)}, u32[]{:S(2)}) %collective-permute-start.18) | collective-permute-done | bytes 1081376 | tf_op jit(solution)/shard_map/ppermute | solution.py:691
  109.4 2.2 %unpack_theirs.1 = (f32[2,256,1024]{2,1,0:T(8,128)}, f32[2,1024,256]{2,1,0:T(8,128)}, f32[7,7,2,256]{3,2,1,0:T(2,128)}, f32[2,256]{1,0:T(2,128)}, f32[2,256]{1,0:T(2,128)}) custom-call(bf16[2112,256]{1,0:T(8,128)(2,1)S(1)} %order.1.refs_0_, bf16[2112,256]{1,0:T(8,128)(2,1)S(1)} %collective-permute-done.18.refs_1_, ...), custom_call_target="tpu_custom_call", output_to_operand_aliasing={{0}: (2, {}), {1}: (3, {})} | custom-call | bytes 4550000 | tf_op jit(solution)/shard_map/unpack_theirs/pallas_call | solution.py:660
  (7 shorter events, 0.0 us)
Async XLA Ops:
  0.6 1.0 copy-start.3
  1.6 10.7 %copy-start.5 = (s32[32,4,2]{0,2,1:T(2,128)S(1)}, s32[32,4,2]{0,2,1:T(2,128)}, u32[]{:S(2)}) copy-start(s32[32,4,2]{0,2,1:T(2,128)} %param.16) | copy-start | bytes 3076
  1.6 10.7 %copy-start.6 = (s32[32,4,2]{0,2,1:T(2,128)S(1)}, s32[32,4,2]{0,2,1:T(2,128)}, u32[]{:S(2)}) copy-start(s32[32,4,2]{0,2,1:T(2,128)} %param.17) | copy-start | bytes 3076
  1.7 10.6 %collective-permute-start = (bf16[8,3,16,256]{3,2,1,0:T(8,128)(2,1)S(1)}, bf16[8,3,16,256]{3,2,1,0:T(8,128)(2,1)S(1)}, u32[]{:S(2)}, u32[]{:S(2)}) collective-permute-start(bf16[8,3,16,256]{3,2,1,0:T(8,128)(2,1)S(1)} %get-tuple-element.66.refs_5_.refs_3_), channel_id=1, source_target_pairs={{0,1},{1,2},{2,3},{3,4},{4,5},{5,6},{6,7},{7,8},{8,9},{9,10},{10,1... | collective-permute-start | bytes 589832 | tf_op jit(solution)/shard_map/ppermute | solution.py:685
  2.2 10.1 %collective-permute-start.1 = (bf16[8,3,16,256]{3,2,1,0:T(8,128)(2,1)S(1)}, bf16[8,3,16,256]{3,2,1,0:T(8,128)(2,1)S(1)}, u32[]{:S(2)}, u32[]{:S(2)}) collective-permute-start(bf16[8,3,16,256]{3,2,1,0:T(8,128)(2,1)S(1)} %get-tuple-element.66.refs_5_.refs_3_), channel_id=1, source_target_pairs={{0,15},{1,0},{2,1},{3,2},{4,3},{5,4},{6,5},{7,6},{8,7},{9,8},{10,9... | collective-permute-start | bytes 589832 | tf_op jit(solution)/shard_map/ppermute | solution.py:685
  7.3 1.2 %copy-start = (bf16[2,256,1024]{2,1,0:T(8,128)(2,1)S(1)}, bf16[2,256,1024]{2,1,0:T(8,128)(2,1)}, u32[]{:S(2)}) copy-start(bf16[2,256,1024]{2,1,0:T(8,128)(2,1)} %refs_3_.1) | copy-start | bytes 3145732
  8.5 1.2 %copy-start.1 = (bf16[2,1024,256]{2,1,0:T(8,128)(2,1)S(1)}, bf16[2,1024,256]{2,1,0:T(8,128)(2,1)}, u32[]{:S(2)}) copy-start(bf16[2,1024,256]{2,1,0:T(8,128)(2,1)} %refs_4_.1) | copy-start | bytes 3145732
  9.7 0.9 copy-start.4
  10.6 0.7 copy-start.7
  11.3 0.7 copy-start.8
  12.3 16.6 %copy-start.2 = (bf16[2,16,16,256]{3,2,1,0:T(8,128)(2,1)S(1)}, bf16[2,16,16,256]{3,2,1,0:T(8,128)(2,1)}, u32[]{:S(2)}) copy-start(bf16[2,16,16,256]{3,2,1,0:T(8,128)(2,1)} %refs_11_.1) | copy-start | bytes 786436
  21.0 7.8 %collective-permute-start.2 = (bf16[8,3,16,256]{3,2,1,0:T(8,128)(2,1)S(1)}, bf16[8,3,16,256]{3,2,1,0:T(8,128)(2,1)S(1)}, u32[]{:S(2)}, u32[]{:S(2)}) collective-permute-start(bf16[8,3,16,256]{3,2,1,0:T(8,128)(2,1)S(1)} %get-tuple-element.73.refs_3_), channel_id=1, source_target_pairs={{0,1},{1,2},{2,3},{3,4},{4,5},{5,6},{6,7},{7,8},{8,9},{9,10},{10,1... | collective-permute-start | bytes 589832 | tf_op jit(solution)/shard_map/ppermute | solution.py:685
  21.1 7.8 %collective-permute-start.3 = (bf16[8,3,16,256]{3,2,1,0:T(8,128)(2,1)S(1)}, bf16[8,3,16,256]{3,2,1,0:T(8,128)(2,1)S(1)}, u32[]{:S(2)}, u32[]{:S(2)}) collective-permute-start(bf16[8,3,16,256]{3,2,1,0:T(8,128)(2,1)S(1)} %get-tuple-element.73.refs_3_), channel_id=1, source_target_pairs={{0,15},{1,0},{2,1},{3,2},{4,3},{5,4},{6,5},{7,6},{8,7},{9,8},{10,9... | collective-permute-start | bytes 589832 | tf_op jit(solution)/shard_map/ppermute | solution.py:685
  44.4 7.9 %collective-permute-start.4 = (bf16[8,3,16,256]{3,2,1,0:T(8,128)(2,1)S(1)}, bf16[8,3,16,256]{3,2,1,0:T(8,128)(2,1)S(1)}, u32[]{:S(2)}, u32[]{:S(2)}) collective-permute-start(bf16[8,3,16,256]{3,2,1,0:T(8,128)(2,1)S(1)} %get-tuple-element.77), channel_id=1, source_target_pairs={{0,1},{1,2},{2,3},{3,4},{4,5},{5,6},{6,7},{7,8},{8,9},{9,10},{10,1... | collective-permute-start | bytes 589832 | tf_op jit(solution)/shard_map/ppermute | solution.py:685
  44.4 7.9 %collective-permute-start.5 = (bf16[8,3,16,256]{3,2,1,0:T(8,128)(2,1)S(1)}, bf16[8,3,16,256]{3,2,1,0:T(8,128)(2,1)S(1)}, u32[]{:S(2)}, u32[]{:S(2)}) collective-permute-start(bf16[8,3,16,256]{3,2,1,0:T(8,128)(2,1)S(1)} %get-tuple-element.78), channel_id=1, source_target_pairs={{0,15},{1,0},{2,1},{3,2},{4,3},{5,4},{6,5},{7,6},{8,7},{9,8},{10,9... | collective-permute-start | bytes 589832 | tf_op jit(solution)/shard_map/ppermute | solution.py:685
  52.2 2.9 %collective-permute-start.7 = (bf16[1024,256]{1,0:T(8,128)(2,1)S(1)}, bf16[1024,256]{1,0:T(8,128)(2,1)S(1)}, u32[]{:S(2)}, u32[]{:S(2)}) collective-permute-start(bf16[1024,256]{1,0:T(8,128)(2,1)S(1)} %get-tuple-element.98), channel_id=1, source_target_pairs={{0,1},{1,0},{2,3},{3,2},{4,5},{5,4},{6,7},{7,6},{8,9},{9,8},{10,11... | collective-permute-start | bytes 1572872 | tf_op jit(solution)/shard_map/ppermute | solution.py:698
  54.6 2.1 %collective-permute-start.6 = (bf16[1024,256]{1,0:T(8,128)(2,1)S(1)}, bf16[1024,256]{1,0:T(8,128)(2,1)S(1)}, u32[]{:S(2)}, u32[]{:S(2)}) collective-permute-start(bf16[1024,256]{1,0:T(8,128)(2,1)S(1)} %get-tuple-element.88), channel_id=1, source_target_pairs={{0,1},{1,0},{2,3},{3,2},{4,5},{5,4},{6,7},{7,6},{8,9},{9,8},{10,11... | collective-permute-start | bytes 1572872 | tf_op jit(solution)/shard_map/ppermute | solution.py:698
  56.9 12.9 %collective-permute-start.10 = (bf16[2,256,256]{2,1,0:T(8,128)(2,1)S(1)}, bf16[2,256,256]{2,1,0:T(8,128)(2,1)S(1)}, u32[]{:S(2)}, u32[]{:S(2)}) collective-permute-start(bf16[2,256,256]{2,1,0:T(8,128)(2,1)S(1)} %get-tuple-element.105), channel_id=1, source_target_pairs={{0,2},{1,3},{2,0},{3,1},{4,6},{5,7},{6,4},{7,5},{8,10},{9,11},{10,... | collective-permute-start | bytes 786440 | tf_op jit(solution)/shard_map/ppermute | solution.py:698
  57.0 12.8 %collective-permute-start.11 = (bf16[2,256,256]{2,1,0:T(8,128)(2,1)S(1)}, bf16[2,256,256]{2,1,0:T(8,128)(2,1)S(1)}, u32[]{:S(2)}, u32[]{:S(2)}) collective-permute-start(bf16[2,256,256]{2,1,0:T(8,128)(2,1)S(1)} %get-tuple-element.106), channel_id=1, source_target_pairs={{0,4},{1,5},{2,6},{3,7},{4,0},{5,1},{6,2},{7,3},{8,12},{9,13},{10,... | collective-permute-start | bytes 786440 | tf_op jit(solution)/shard_map/ppermute | solution.py:698
  57.0 15.3 %collective-permute-start.12 = (bf16[2,256,256]{2,1,0:T(8,128)(2,1)S(1)}, bf16[2,256,256]{2,1,0:T(8,128)(2,1)S(1)}, u32[]{:S(2)}, u32[]{:S(2)}) collective-permute-start(bf16[2,256,256]{2,1,0:T(8,128)(2,1)S(1)} %get-tuple-element.107), channel_id=1, source_target_pairs={{0,6},{1,7},{2,4},{3,5},{4,2},{5,3},{6,0},{7,1},{8,14},{9,15},{10,... | collective-permute-start | bytes 786440 | tf_op jit(solution)/shard_map/ppermute | solution.py:698
  68.5 1.3 %collective-permute-start.13 = (bf16[64,256]{1,0:T(8,128)(2,1)S(1)}, bf16[64,256]{1,0:T(8,128)(2,1)S(1)}, u32[]{:S(2)}, u32[]{:S(2)}) collective-permute-start(bf16[64,256]{1,0:T(8,128)(2,1)S(1)} %get-tuple-element.114), channel_id=1, source_target_pairs={{0,1},{1,0},{2,3},{3,2},{4,5},{5,4},{6,7},{7,6},{8,9},{9,8},{10,11... | collective-permute-start | bytes 98312 | tf_op jit(solution)/shard_map/ppermute | solution.py:698
  72.5 15.6 %collective-permute-start.14 = (bf16[576,256]{1,0:T(8,128)(2,1)S(1)}, bf16[576,256]{1,0:T(8,128)(2,1)S(1)}, u32[]{:S(2)}, u32[]{:S(2)}) collective-permute-start(bf16[576,256]{1,0:T(8,128)(2,1)S(1)} %quarter.1.refs_0_), channel_id=1, source_target_pairs={{0,8},{1,9},{2,10},{3,11},{4,12},{5,13},{6,14},{7,15},{8,0},{9,1},... | collective-permute-start | bytes 884744 | tf_op jit(solution)/shard_map/ppermute | solution.py:691
  74.8 10.9 %collective-permute-start.8 = (bf16[8,3,16,256]{3,2,1,0:T(8,128)(2,1)S(1)}, bf16[8,3,16,256]{3,2,1,0:T(8,128)(2,1)S(1)}, u32[]{:S(2)}, u32[]{:S(2)}) collective-permute-start(bf16[8,3,16,256]{3,2,1,0:T(8,128)(2,1)S(1)} %get-tuple-element.102), channel_id=1, source_target_pairs={{0,1},{1,2},{2,3},{3,4},{4,5},{5,6},{6,7},{7,8},{8,9},{9,10},{10,1... | collective-permute-start | bytes 589832 | tf_op jit(solution)/shard_map/ppermute | solution.py:685
  74.8 10.9 %collective-permute-start.9 = (bf16[8,3,16,256]{3,2,1,0:T(8,128)(2,1)S(1)}, bf16[8,3,16,256]{3,2,1,0:T(8,128)(2,1)S(1)}, u32[]{:S(2)}, u32[]{:S(2)}) collective-permute-start(bf16[8,3,16,256]{3,2,1,0:T(8,128)(2,1)S(1)} %get-tuple-element.103), channel_id=1, source_target_pairs={{0,15},{1,0},{2,1},{3,2},{4,3},{5,4},{6,5},{7,6},{8,7},{9,8},{10,9... | collective-permute-start | bytes 589832 | tf_op jit(solution)/shard_map/ppermute | solution.py:685
  88.2 9.9 %collective-permute-start.15 = (bf16[576,256]{1,0:T(8,128)(2,1)S(1)}, bf16[576,256]{1,0:T(8,128)(2,1)S(1)}, u32[]{:S(2)}, u32[]{:S(2)}) collective-permute-start(bf16[576,256]{1,0:T(8,128)(2,1)S(1)} %far.1.refs_0_), channel_id=1, source_target_pairs={{0,2},{1,3},{2,0},{3,1},{4,6},{5,7},{6,4},{7,5},{8,10},{9,11},{10,... | collective-permute-start | bytes 884744 | tf_op jit(solution)/shard_map/ppermute | solution.py:691
  91.7 9.9 %collective-permute-start.16 = (bf16[576,256]{1,0:T(8,128)(2,1)S(1)}, bf16[576,256]{1,0:T(8,128)(2,1)S(1)}, u32[]{:S(2)}, u32[]{:S(2)}) collective-permute-start(bf16[576,256]{1,0:T(8,128)(2,1)S(1)} %far.1.refs_0_), channel_id=1, source_target_pairs={{0,4},{1,5},{2,6},{3,7},{4,0},{5,1},{6,2},{7,3},{8,12},{9,13},{10,... | collective-permute-start | bytes 884744 | tf_op jit(solution)/shard_map/ppermute | solution.py:691
  91.7 14.8 %collective-permute-start.17 = (bf16[576,256]{1,0:T(8,128)(2,1)S(1)}, bf16[576,256]{1,0:T(8,128)(2,1)S(1)}, u32[]{:S(2)}, u32[]{:S(2)}) collective-permute-start(bf16[576,256]{1,0:T(8,128)(2,1)S(1)} %far.1.refs_0_), channel_id=1, source_target_pairs={{0,6},{1,7},{2,4},{3,5},{4,2},{5,3},{6,0},{7,1},{8,14},{9,15},{10,... | collective-permute-start | bytes 884744 | tf_op jit(solution)/shard_map/ppermute | solution.py:691
  106.7 2.8 %collective-permute-start.18 = (bf16[2112,256]{1,0:T(8,128)(2,1)S(1)}, bf16[2112,256]{1,0:T(8,128)(2,1)S(1)}, u32[]{:S(2)}, u32[]{:S(2)}) collective-permute-start(bf16[2112,256]{1,0:T(8,128)(2,1)S(1)} %order.1.refs_0_), channel_id=1, source_target_pairs={{0,1},{1,0},{2,3},{3,2},{4,5},{5,4},{6,7},{7,6},{8,9},{9,8},{10,11... | collective-permute-start | bytes 3244040 | tf_op jit(solution)/shard_map/ppermute | solution.py:691

commit v7 on v6

--- a/solution.py
+++ b/solution.py
@@ -549,27 +549,14 @@
         out[rows] = sum(values[1:], values[0]).astype(BF16)
 
 
-def share_near_kernel(*refs):
-    arrays, outs = refs[:4], refs[4:]
+def share_near_kernel(keep, came, *outs):
     for k, out in enumerate(outs):
         piece = digit_of(1) ^ k
-        for layer in range(2):
-            parts = arrays[2 * layer : 2 * layer + 2]
-            add_rows(
-                out.at[layer],
-                [lambda rows, array=array: array[piece, rows] for array in parts],
-            )
+        add_rows(out, [lambda rows: keep[piece, rows], lambda rows: came[piece, rows]])
 
 
 def quarter_kernel(*refs):
-    arrays, keep, came, out = refs[:4], refs[4], refs[5], refs[6]
-    quarter = arrays[0].shape[1]
-    for layer in range(2):
-        add_rows(
-            out.at[layer * quarter : (layer + 1) * quarter],
-            [lambda rows, array=array: array[layer, rows] for array in arrays],
-        )
-    add_rows(out.at[2 * quarter :], [lambda rows: keep[rows], lambda rows: came[rows]])
+    add_rows(refs[4], [lambda rows, array=array: array[rows] for array in refs[:4]])
 
 
 def far_kernel(*refs):
@@ -580,6 +567,17 @@
     for k, piece in enumerate(pieces):
         held[digit_of(2) ^ k] = piece[...]
     add_rows(out, [lambda rows, k=k: held[k, rows] for k in range(len(pieces))])
+
+
+def middle_kernel(*refs):
+    total, payload, held = refs[-3:]
+    pieces, (parts, small) = refs[:-9], (refs[-9:-5], refs[-5:-3])
+    far_kernel(*pieces, total, held)
+    quarter = parts[0].shape[0]
+    add_rows(
+        payload.at[0:quarter], [lambda rows, array=array: array[rows] for array in parts]
+    )
+    add_rows(payload.at[quarter:], [lambda rows, array=array: array[rows] for array in small])
 
 
 def order_kernel(quarter, *refs):
@@ -593,57 +591,58 @@
         add_rows(out.at[4 * quarter :], [lambda rows, k=k: held[k, rows] for k in range(4)])
 
 
-def unpack_half(sz, half, source, staged, up_hbm, down_hbm, sems):
+def unpack_half(sz, half, layer, source, staged, up_hbm, down_hbm, sems):
     copies = []
-    size = sz.hidden // 4
-    for layer in range(2):
-        for k in range(4):
-            start = (2 * k + layer) * size
-            rows = slice(k * size, (k + 1) * size)
-            staged[layer, rows] = source[start : start + size].astype(F32)
-            if half == 0:
-                pairs = [(rows, down_hbm.at[layer, rows])]
-            else:
-                pairs = []
-                for at in range(k * size, (k + 1) * size, sz.channels):
-                    columns = slice(at, at + sz.channels)
-                    pairs.append((columns, up_hbm.at[layer, :, columns]))
-            for part, place in pairs:
-                copy = pltpu.make_async_copy(
-                    staged.at[layer, part], place, sems.at[half, len(copies)]
-                )
-                copy.start()
-                copies.append(copy)
-    for copy in copies:
-        copy.wait()
-
-
-def unpack_mine_kernel(sz, mine, up_hbm, down_hbm, staged, sems):
+    for k in range(sz.hidden // sz.channels):
+        rows = slice(k * sz.channels, (k + 1) * sz.channels)
+        staged[rows, :] = source[rows, :].astype(F32)
+        place = down_hbm.at[layer, rows] if half == 0 else up_hbm.at[layer, :, rows]
+        copy = pltpu.make_async_copy(staged.at[rows], place, sems.at[half, k])
+        copy.start()
+        copies.append(copy)
+    return copies
+
+
+def unpack_layer_kernel(sz, layer, mine, theirs, up_hbm, down_hbm, token, first, second, sems):
+    token[...] = jnp.zeros_like(token)
     for half in range(2):
 
         @pl.when(digit_of(0) == half)
         def _(half=half):
-            unpack_half(sz, half, mine, staged, up_hbm, down_hbm, sems)
+            copies = unpack_half(sz, half, layer, mine, first, up_hbm, down_hbm, sems)
+            copies += unpack_half(sz, 1 - half, layer, theirs, second, up_hbm, down_hbm, sems)
+            for copy in copies:
+                copy.wait()
+
+
+def unpack_mine_kernel(sz, layer, mine, _up, _down, up_hbm, down_hbm, staged, sems):
+    for half in range(2):
+
+        @pl.when(digit_of(0) == half)
+        def _(half=half):
+            for copy in unpack_half(sz, half, layer, mine, staged, up_hbm, down_hbm, sems):
+                copy.wait()
 
 
 def unpack_theirs_kernel(
-    sz, mine, theirs, _up, _down, up_hbm, down_hbm, kernel_out, gain_out, scale_out,
+    sz, layer, mine, theirs, _up, _down, up_hbm, down_hbm, kernel_out, gain_out, scale_out,
     staged, small, sems,
 ):
-    start = 2 * sz.hidden
-    small[digit_of(0)] = mine[start:].astype(F32)
-    small[1 - digit_of(0)] = theirs[start:].astype(F32)
+    for half in range(2):
+
+        @pl.when(digit_of(0) == 1 - half)
+        def _(half=half):
+            for copy in unpack_half(sz, half, layer, theirs, staged, up_hbm, down_hbm, sems):
+                copy.wait()
+
+    small[digit_of(0)] = mine[sz.hidden :].astype(F32)
+    small[1 - digit_of(0)] = theirs[sz.hidden :].astype(F32)
     for layer in range(2):
         for a in range(TAPS):
             for b in range(TAPS):
                 kernel_out[a, b, layer : layer + 1] = small[layer, pl.ds(a * 8 + b, 1), :]
         gain_out[layer : layer + 1] = small[layer, pl.ds(TAPS * 8, 1), :]
         scale_out[layer : layer + 1] = small[layer, pl.ds(TAPS * 8 + 1, 1), :]
-    for half in range(2):
-
-        @pl.when(digit_of(0) == 1 - half)
-        def _(half=half):
-            unpack_half(sz, half, theirs, staged, up_hbm, down_hbm, sems)
 
 
 IN_VMEM = pl.BlockSpec(memory_space=pltpu.VMEM)
@@ -705,34 +704,42 @@
         self.near_masks = [2 * k for k in range(1, 4)]
         self.far_masks = [8 * k for k in range(1, devices // 8)]
 
-    def share(self, *halves_of_layers):
-        arrays = []
-        for keep, send in halves_of_layers:
-            rows, channels = keep.shape
-            dims = (4, rows // 4, channels)
-            arrays += [keep.reshape(dims), swap([send], [1])[0].reshape(dims)]
-        shape = jax.ShapeDtypeStruct((2,) + dims[1:], BF16)
+    def share(self, keep, send, after=()):
+        rows, channels = keep.shape
+        dims = (4, rows // 4, channels)
+        shape = jax.ShapeDtypeStruct(dims[1:], BF16)
         pieces = call(
-            share_near_kernel, "share_near", 0.3, near(*arrays), near(*[shape] * 4), [],
+            share_near_kernel, "share_near", 0.3,
+            near(keep.reshape(dims), swap([send], [1])[0].reshape(dims)),
+            near(*[shape] * 4), [], after,
         )
         return [pieces[0]] + swap(pieces[1:], self.near_masks)
 
-    def quarters(self, parts, keep, send):
-        _, rows, channels = parts[0].shape
-        shape = jax.ShapeDtypeStruct((2 * rows + keep.shape[0], channels), BF16)
-        (total,) = call(
-            quarter_kernel, "quarter", 0.4,
-            near(*parts, keep, *swap([send], [1])), near(shape), [],
-        )
+    def quarter(self, parts):
+        shape = jax.ShapeDtypeStruct(parts[0].shape, BF16)
+        (total,) = call(quarter_kernel, "quarter", 0.3, near(*parts), near(shape), [])
         return total
 
-    def exchange(self, total, after=()):
-        shape = jax.ShapeDtypeStruct(total.shape, BF16)
+    def far(self, total):
         pieces = [total] + partners(total, self.far_masks)
         held = (len(pieces),) + total.shape if len(pieces) > 2 else (1, 16, LANES)
-        (total,) = call(
-            far_kernel, "far", 0.3, near(*pieces), near(shape), [pltpu.VMEM(held, BF16)], after
+        return pieces, [pltpu.VMEM(held, BF16)]
+
+    def middle(self, quarter, parts, keep, send):
+        pieces, scratch = self.far(quarter)
+        rows, channels = quarter.shape
+        shapes = [
+            jax.ShapeDtypeStruct((rows + more, channels), BF16) for more in (0, keep.shape[0])
+        ]
+        return call(
+            middle_kernel, "middle", 0.5,
+            near(*pieces, *parts, keep, *swap([send], [1])), near(*shapes), scratch,
         )
+
+    def exchange(self, total, after=()):
+        pieces, scratch = self.far(total)
+        shape = jax.ShapeDtypeStruct(total.shape, BF16)
+        (total,) = call(far_kernel, "far", 0.3, near(*pieces), near(shape), scratch, after)
         return total
 
     def gather(self, total, quarter, after=()):
@@ -852,14 +859,16 @@
         near(half, half, slabs, wide_short, sums),
         vmem(wide, narrow_short, two_halves),
     )
-    parts = reduction.share((keep_zero, send_zero), (keep_one, send_one))
+    parts_one = reduction.share(keep_one, send_one, (scale_sums,))
+    quarter_one = reduction.quarter(parts_one)
+    parts_zero = reduction.share(keep_zero, send_zero)
     base, grad_own, grad_below, grad_above, grad_conv, gain_sums = call(
         functools.partial(spread_kernel, sz, 0),
         "spread", 6.0,
         plan + near(kern, gain, up, flat, up_in, normal, inverse),
         near(slabs, own_shape, strips_shape, strips_shape, grad_slabs, sums),
         vmem(taps, narrow, grad_pool, padded),
-        (parts[0],),
+        (parts_zero[0], quarter_one),
     )
     from_below, from_above = pass_on(grad_above, 1), pass_on(grad_below, -1)
     small_keep, small_send = call(
@@ -876,22 +885,33 @@
         far(image) + near(shape((8, LANES), F32)),
         vmem(slabs, image) + sems(1),
     )
-    total = reduction.quarters(parts, small_keep, small_send)
-    total = reduction.exchange(total, (token,))
-    mine = reduction.gather(total, hidden // 2)
+    rows = hidden // 4
+    total_one, total_zero = reduction.middle(quarter_one, parts_zero, small_keep, small_send)
+    total_zero = reduction.exchange(total_zero, (token,))
+    mine_one = reduction.gather(total_one, rows, (total_zero,))
+    theirs_one = partners(mine_one, [1])[0]
+    weight_shapes = [shape(up_weight.shape, F32), shape(down_weight.shape, F32)]
+    staged = shape((hidden, channels), F32)
+    copies = [pltpu.SemaphoreType.DMA((2, hidden // channels))]
+    grad_up, grad_down, token = call(
+        functools.partial(unpack_layer_kernel, sz, 1),
+        "unpack_one", 1.8,
+        near(mine_one, theirs_one),
+        far(*weight_shapes) + near(shape((8, LANES), F32)),
+        vmem(staged, staged) + copies,
+    )
+    mine = reduction.gather(total_zero, rows, (token,))
     theirs = partners(mine, [1])[0]
-    weight_shapes = [shape(up_weight.shape, F32), shape(down_weight.shape, F32)]
-    staged = shape((layers, hidden, channels), F32)
-    copies = [pltpu.SemaphoreType.DMA((2, layers * hidden // channels))]
     grad_up, grad_down = call(
-        functools.partial(unpack_mine_kernel, sz),
+        functools.partial(unpack_mine_kernel, sz, 0),
         "unpack_mine", 1.0,
-        near(mine),
+        near(mine) + far(grad_up, grad_down),
         far(*weight_shapes),
         vmem(staged) + copies,
+        aliases={1: 0, 2: 1},
     )
     grad_up, grad_down, grad_kernel, grad_gain, grad_scale = call(
-        functools.partial(unpack_theirs_kernel, sz),
+        functools.partial(unpack_theirs_kernel, sz, 0),
         "unpack_theirs", 1.3,
         near(mine, theirs) + far(grad_up, grad_down),
         far(*weight_shapes)

time: 112 us -> 116 us (1.036)
  starting transfers between devices: 30.9 us -> 37.5 us
  waiting for transfers between devices: 31.1 us -> 27.7 us
    ppermute x8, waiting for transfers between devices: 9.82 us -> 3.37 us  [pass_on(): lax.ppermute(shard, 'tile', [(i, (i + by) % length) for i in range(length)])]
    ppermute x6 -> x9, waiting for transfers between devices: 5.31 us -> 10.9 us  [swap(): lax.ppermute(array, 'tile', [(i, i ^ mask) for i in range(length)])]
    ppermute x5 -> x10, starting transfers between devices: 7.47 us -> 11.4 us  [partners(): lax.ppermute(array, 'tile', [(i, i ^ mask) for i in range(length)])]
    ppermute x6 -> x9, starting transfers between devices: 4.22 us -> 7.69 us  [swap(): lax.ppermute(array, 'tile', [(i, i ^ mask) for i in range(length)])]
    ppermute x5 -> x10, waiting for transfers between devices: 16 us -> 13.4 us  [partners(): lax.ppermute(array, 'tile', [(i, i ^ mask) for i in range(length)])]
    pallas_call x15 -> x19, Pallas kernels: 43.1 us -> 43.7 us  [call(): pl.pallas_call(run, in_specs=[spec for spec, _ in ins] + [pl.BlockSpec(me...]
  transfers between devices with their start and end apart: 19 -> 27, of which waited for: 10 -> 11; matrix products, arithmetic and copies ran while one was open for 0% -> 0% of each run, Pallas kernels for 14% -> 15%
where the time goes in v7:
time: 116 us
  Pallas kernels  43.7 us (38%)
  starting transfers between devices  37.5 us (32%)
  waiting for transfers between devices  27.7 us (24%)
  local copies, waits for them, and re-layouts  5.66 us (5%)
    pallas_call x19, Pallas kernels, call(): pl.pallas_call(run, in_specs=[spec for spec, _ in ins] + [pl.BlockSpec(me...  43.7 us
    ppermute x8, starting transfers between devices, pass_on(): lax.ppermute(shard, 'tile', [(i, (i + by) % length) for i in range(length)])  18.4 us
    ppermute x10, waiting for transfers between devices, partners(): lax.ppermute(array, 'tile', [(i, i ^ mask) for i in range(length)])  13.4 us
    ppermute x10, starting transfers between devices, partners(): lax.ppermute(array, 'tile', [(i, i ^ mask) for i in range(length)])  11.4 us
    ppermute x9, waiting for transfers between devices, swap(): lax.ppermute(array, 'tile', [(i, i ^ mask) for i in range(length)])  10.9 us
    ppermute x9, starting transfers between devices, swap(): lax.ppermute(array, 'tile', [(i, i ^ mask) for i in range(length)])  7.69 us
    unnamed x18, local copies, waits for them, and re-layouts  5.66 us
    ppermute x8, waiting for transfers between devices, pass_on(): lax.ppermute(shard, 'tile', [(i, (i + by) % length) for i in range(length)])  3.37 us
  transfers between devices with their start and end apart: 27, of which 11 were waited for; matrix products, arithmetic and copies ran while one was open for 0% of the time, Pallas kernels for 15%

profile of v7, /device:TPU:0, one launch (start us, length us, event | category | flops | bytes accessed | tf_op | source)
XLA Modules:
  0.0 115.7 jit_solution(5976945460387462619)
XLA Ops:
  0.6 0.9 copy-done.3
  1.6 0.1 strips.1
  1.7 0.5 collective-permute-start
  2.2 5.1 %collective-permute-start.1 = (bf16[8,3,16,256]{3,2,1,0:T(8,128)(2,1)S(1)}, bf16[8,3,16,256]{3,2,1,0:T(8,128)(2,1)S(1)}, u32[]{:S(2)}, u32[]{:S(2)}) collective-permute-start(bf16[8,3,16,256]{3,2,1,0:T(8,128)(2,1)S(1)} %get-tuple-element.75.refs_5_.refs_3_), channel_id=1, source_target_pairs={{0,15},{1,0},{2,1},{3,2},{4,3},{5,4},{6,5},{7,6},{8,7},{9,8},{10,9... | collective-permute-start | bytes 589832 | tf_op jit(solution)/shard_map/ppermute | solution.py:684
  7.3 1.2 %copy-done = bf16[2,256,1024]{2,1,0:T(8,128)(2,1)S(1)} copy-done((bf16[2,256,1024]{2,1,0:T(8,128)(2,1)S(1)}, bf16[2,256,1024]{2,1,0:T(8,128)(2,1)}, u32[]{:S(2)}) %copy-start) | copy-done | bytes 1048600
  8.5 1.2 %copy-done.1 = bf16[2,1024,256]{2,1,0:T(8,128)(2,1)S(1)} copy-done((bf16[2,1024,256]{2,1,0:T(8,128)(2,1)S(1)}, bf16[2,1024,256]{2,1,0:T(8,128)(2,1)}, u32[]{:S(2)}) %copy-start.1) | copy-done | bytes 1048600
  9.7 0.9 copy-done.4
  10.6 0.7 copy-done.7
  11.3 0.7 copy-done.8
  12.0 0.3 fetch.1
  12.3 0.0 copy-start.2
  12.3 0.0 collective-permute-done.refs_4_
  12.3 8.7 %forward.1 = (bf16[2,16,16,256]{3,2,1,0:T(8,128)(2,1)S(1)}, bf16[8,3,16,256]{3,2,1,0:T(8,128)(2,1)S(1)}, f32[4,528,128]{2,1,0:T(8,128)S(1)}, f32[4,256,128]{2,1,...) custom-call(s32[4,2,32]{2,1,0:T(2,128)S(1)} %bitcast.13, ...), custom_call_target="tpu_custom_call" | custom-call | bytes 30450000 | tf_op jit(solution)/shard_map/forward/pallas_call | solution.py:659
  21.0 0.1 collective-permute-start.2
  21.1 4.4 %collective-permute-start.3 = (bf16[8,3,16,256]{3,2,1,0:T(8,128)(2,1)S(1)}, bf16[8,3,16,256]{3,2,1,0:T(8,128)(2,1)S(1)}, u32[]{:S(2)}, u32[]{:S(2)}) collective-permute-start(bf16[8,3,16,256]{3,2,1,0:T(8,128)(2,1)S(1)} %get-tuple-element.82.refs_3_), channel_id=1, source_target_pairs={{0,15},{1,0},{2,1},{3,2},{4,3},{5,4},{6,5},{7,6},{8,7},{9,8},{10,9... | collective-permute-start | bytes 589832 | tf_op jit(solution)/shard_map/ppermute | solution.py:684
  25.5 3.3 %collective-permute-done.2.refs_4_ = bf16[8,3,16,256]{3,2,1,0:T(8,128)(2,1)S(1)} collective-permute-done((bf16[8,3,16,256]{3,2,1,0:T(8,128)(2,1)S(1)}, bf16[8,3,16,256]{3,2,1,0:T(8,128)(2,1)S(1)}, u32[]{:S(2)}, u32[]{:S(2)}) %collective-permute-start.2) | collective-permute-done | bytes 196640 | tf_op jit(solution)/shard_map/ppermute | solution.py:684
  28.9 15.5 %turn.1 = (bf16[2,16,16,256]{3,2,1,0:T(8,128)(2,1)}, f32[4,256,128]{2,1,0:T(8,128)S(1)}, f32[8,3,2,16,128]{4,3,2,1,0:T(8,128)S(1)}, bf16[8,3,16,256]{3,2,1,0:T(8...) custom-call(s32[4,2,32]{2,1,0:T(2,128)S(1)} %bitcast.14, ...), custom_call_target="tpu_custom_call" | custom-call | bytes 53900000 | tf_op jit(solution)/shard_map/turn/pallas_call | solution.py:659
  44.4 0.1 collective-permute-start.4
  44.4 4.7 %collective-permute-start.5 = (bf16[8,3,16,256]{3,2,1,0:T(8,128)(2,1)S(1)}, bf16[8,3,16,256]{3,2,1,0:T(8,128)(2,1)S(1)}, u32[]{:S(2)}, u32[]{:S(2)}) collective-permute-start(bf16[8,3,16,256]{3,2,1,0:T(8,128)(2,1)S(1)} %get-tuple-element.87), channel_id=1, source_target_pairs={{0,15},{1,0},{2,1},{3,2},{4,3},{5,4},{6,5},{7,6},{8,7},{9,8},{10,9... | collective-permute-start | bytes 589832 | tf_op jit(solution)/shard_map/ppermute | solution.py:684
  49.1 3.1 %weights.1 = (bf16[1024,256]{1,0:T(8,128)(2,1)S(1)}, bf16[1024,256]{1,0:T(8,128)(2,1)S(1)}, f32[64,256]{1,0:T(8,128)S(1)}) custom-call(f32[4,528,128]{2,1,0:T(8,128)S(1)} %get-tuple-element.99.refs_0_, f32[4,512,128]{2,1,0:T(8,128)S(1)} %get-tuple-element.100.refs_1_, bf16[512,256]{1,0:T(8,128)(2,1)S(1)} %get-tuple-element.101.refs_2_, ...), custom_call_target="tpu_custom_call" | custom-call | bytes 9800000 | tf_op jit(solution)/shard_map/weights/pallas_call | solution.py:659
  52.2 0.1 collective-permute-start.7
  52.3 2.2 %backward.1 = (bf16[1024,256]{1,0:T(8,128)(2,1)S(1)}, bf16[1024,256]{1,0:T(8,128)(2,1)S(1)}, f32[4,256,128]{2,1,0:T(8,128)S(1)}, bf16[512,1024]{1,0:T(8,128)(2,1)S(1)}, f32[16,256]{1,0:T(8,128)S(1)}) custom-call(f32[4,256,128]{2,1,0:T(8,128)S(1)} %get-tuple-element.84.refs_0_, f32[8,3,2,16,128]{4,3,2,1,0:T(8,128)S(1)} %get-tuple-element.85.refs_1_, ...), custom_call_target="tpu_custom_call" | custom-call | bytes 10150000 | tf_op jit(solution)/shard_map/backward/pallas_call | solution.py:659
  54.6 0.5 collective-permute-start.6
  55.1 0.1 share_near.3
  55.2 0.1 collective-permute-start.10
  55.3 0.1 collective-permute-start.8
  55.4 3.4 %collective-permute-start.9 = (bf16[256,256]{1,0:T(8,128)(2,1)S(1)}, bf16[256,256]{1,0:T(8,128)(2,1)S(1)}, u32[]{:S(2)}, u32[]{:S(2)}) collective-permute-start(bf16[256,256]{1,0:T(8,128)(2,1)S(1)} %get-tuple-element.112), channel_id=1, source_target_pairs={{0,4},{1,5},{2,6},{3,7},{4,0},{5,1},{6,2},{7,3},{8,12},{9,13},{10,... | collective-permute-start | bytes 393224 | tf_op jit(solution)/shard_map/ppermute | solution.py:697
  58.8 3.8 %collective-permute-done.10.refs_3_ = bf16[256,256]{1,0:T(8,128)(2,1)S(1)} collective-permute-done((bf16[256,256]{1,0:T(8,128)(2,1)S(1)}, bf16[256,256]{1,0:T(8,128)(2,1)S(1)}, u32[]{:S(2)}, u32[]{:S(2)}) %collective-permute-start.10) | collective-permute-done | bytes 131104 | tf_op jit(solution)/shard_map/ppermute | solution.py:697
  62.6 1.0 collective-permute-done.8.refs_1_
  63.6 0.1 quarter.1.refs_10_.refs_0_
  63.7 3.3 %collective-permute-start.13 = (bf16[256,256]{1,0:T(8,128)(2,1)S(1)}, bf16[256,256]{1,0:T(8,128)(2,1)S(1)}, u32[]{:S(2)}, u32[]{:S(2)}) collective-permute-start(bf16[256,256]{1,0:T(8,128)(2,1)S(1)} %quarter.1.refs_10_.refs_0_), channel_id=1, source_target_pairs={{0,8},{1,9},{2,10},{3,11},{4,12},{5,13},{6,14},{7,15},{8,0},{9,1},... | collective-permute-start | bytes 393224 | tf_op jit(solution)/shard_map/ppermute | solution.py:690
  67.0 0.1 share_near.2
  67.1 5.9 %spread.1 = (f32[4,256,128]{2,1,0:T(8,128)S(1)}, f32[8,3,2,16,128]{4,3,2,1,0:T(8,128)S(1)}, bf16[8,3,16,256]{3,2,1,0:T(8,128)(2,1)S(1)}, bf16[8,3,16,256]{3,2,1,...) custom-call(s32[4,2,32]{2,1,0:T(2,128)S(1)} %bitcast.15, s32[4,2,32]{2,1,0:T(2,128)S(1)} %bitcast.18, ...), custom_call_target="tpu_custom_call" | custom-call | bytes 21000000 | tf_op jit(solution)/shard_map/spread/pallas_call | solution.py:659
  73.1 2.1 %taps.1 = (bf16[64,256]{1,0:T(8,128)(2,1)S(1)}, bf16[64,256]{1,0:T(8,128)(2,1)S(1)}) custom-call(f32[4,528,128]{2,1,0:T(8,128)S(1)} %get-tuple-element.122.refs_0_, f32[4,512,128]{2,1,0:T(8,128)S(1)} %get-tuple-element.123.refs_1_, f32[16,256]{1,0:T(8,128)S(1)} %get-tuple-element.124.refs_2_, f32[16,256]{1,0:T(8,128)S(1)} %get-tuple-element.109.refs_2_.refs_3_, ...), custom_call_target="tpu_custom_call" | custom-call | bytes 7350000 | tf_op jit(solution)/shard_map/taps/pallas_call | solution.py:659
  75.2 0.1 collective-permute-start.17
  75.2 0.5 collective-permute-start.11
  75.7 0.6 collective-permute-start.14
  76.3 1.8 %collective-permute-start.15 = (bf16[256,256]{1,0:T(8,128)(2,1)S(1)}, bf16[256,256]{1,0:T(8,128)(2,1)S(1)}, u32[]{:S(2)}, u32[]{:S(2)}) collective-permute-start(bf16[256,256]{1,0:T(8,128)(2,1)S(1)} %get-tuple-element.120), channel_id=1, source_target_pairs={{0,4},{1,5},{2,6},{3,7},{4,0},{5,1},{6,2},{7,3},{8,12},{9,13},{10,... | collective-permute-start | bytes 393224 | tf_op jit(solution)/shard_map/ppermute | solution.py:697
  78.1 1.1 collective-permute-start.16
  79.2 3.2 %collective-permute-start.12 = (bf16[8,3,16,256]{3,2,1,0:T(8,128)(2,1)S(1)}, bf16[8,3,16,256]{3,2,1,0:T(8,128)(2,1)S(1)}, u32[]{:S(2)}, u32[]{:S(2)}) collective-permute-start(bf16[8,3,16,256]{3,2,1,0:T(8,128)(2,1)S(1)} %get-tuple-element.117), channel_id=1, source_target_pairs={{0,15},{1,0},{2,1},{3,2},{4,3},{5,4},{6,5},{7,6},{8,7},{9,8},{10,9... | collective-permute-start | bytes 589832 | tf_op jit(solution)/shard_map/ppermute | solution.py:684
  82.4 0.5 collective-permute-done.14.refs_3_
  82.9 5.6 %collective-permute-done.16.refs_5_ = bf16[256,256]{1,0:T(8,128)(2,1)S(1)} collective-permute-done((bf16[256,256]{1,0:T(8,128)(2,1)S(1)}, bf16[256,256]{1,0:T(8,128)(2,1)S(1)}, u32[]{:S(2)}, u32[]{:S(2)}) %collective-permute-start.16) | collective-permute-done | bytes 131104 | tf_op jit(solution)/shard_map/ppermute | solution.py:697
  88.5 0.1 middle.1
  88.6 0.1 collective-permute-start.18
  88.7 0.1 collective-permute-start.22
  88.7 2.0 %collective-permute-start.23 = (bf16[256,256]{1,0:T(8,128)(2,1)S(1)}, bf16[256,256]{1,0:T(8,128)(2,1)S(1)}, u32[]{:S(2)}, u32[]{:S(2)}) collective-permute-start(bf16[256,256]{1,0:T(8,128)(2,1)S(1)} %get-tuple-element.130.refs_0_), channel_id=1, source_target_pairs={{0,4},{1,5},{2,6},{3,7},{4,0},{5,1},{6,2},{7,3},{8,12},{9,13},{10,... | collective-permute-start | bytes 393224 | tf_op jit(solution)/shard_map/ppermute | solution.py:690
  90.7 1.5 %collective-permute-start.24 = (bf16[256,256]{1,0:T(8,128)(2,1)S(1)}, bf16[256,256]{1,0:T(8,128)(2,1)S(1)}, u32[]{:S(2)}, u32[]{:S(2)}) collective-permute-start(bf16[256,256]{1,0:T(8,128)(2,1)S(1)} %get-tuple-element.130.refs_0_), channel_id=1, source_target_pairs={{0,6},{1,7},{2,4},{3,5},{4,2},{5,3},{6,0},{7,1},{8,14},{9,15},{10,... | collective-permute-start | bytes 393224 | tf_op jit(solution)/shard_map/ppermute | solution.py:690
  92.2 1.0 last.1
  93.2 5.7 %collective-permute-done.18.refs_1_ = bf16[320,256]{1,0:T(8,128)(2,1)S(1)} collective-permute-done((bf16[320,256]{1,0:T(8,128)(2,1)S(1)}, bf16[320,256]{1,0:T(8,128)(2,1)S(1)}, u32[]{:S(2)}, u32[]{:S(2)}) %collective-permute-start.18) | collective-permute-done | bytes 163872 | tf_op jit(solution)/shard_map/ppermute | solution.py:690
  99.0 0.3 collective-permute-done.24.refs_3_
  99.2 0.1 order.2.refs_0_
  99.3 0.1 collective-permute-start.25
  99.4 2.8 %collective-permute-start.19 = (bf16[320,256]{1,0:T(8,128)(2,1)S(1)}, bf16[320,256]{1,0:T(8,128)(2,1)S(1)}, u32[]{:S(2)}, u32[]{:S(2)}) collective-permute-start(bf16[320,256]{1,0:T(8,128)(2,1)S(1)} %far.1.refs_4_.refs_0_), channel_id=1, source_target_pairs={{0,2},{1,3},{2,0},{3,1},{4,6},{5,7},{6,4},{7,5},{8,10},{9,11},{10,... | collective-permute-start | bytes 491528 | tf_op jit(solution)/shard_map/ppermute | solution.py:690
  102.2 0.2 collective-permute-start.20
  102.3 1.4 %collective-permute-start.21 = (bf16[320,256]{1,0:T(8,128)(2,1)S(1)}, bf16[320,256]{1,0:T(8,128)(2,1)S(1)}, u32[]{:S(2)}, u32[]{:S(2)}) collective-permute-start(bf16[320,256]{1,0:T(8,128)(2,1)S(1)} %far.1.refs_4_.refs_0_), channel_id=1, source_target_pairs={{0,6},{1,7},{2,4},{3,5},{4,2},{5,3},{6,0},{7,1},{8,14},{9,15},{10,... | collective-permute-start | bytes 491528 | tf_op jit(solution)/shard_map/ppermute | solution.py:690
  103.7 1.4 %unpack_one.1 = (f32[2,256,1024]{2,1,0:T(8,128)}, f32[2,1024,256]{2,1,0:T(8,128)}, f32[8,128]{1,0:T(8,128)S(1)}) custom-call(bf16[1024,256]{1,0:T(8,128)(2,1)S(1)} %order.2.refs_0_, bf16[1024,256]{1,0:T(8,128)(2,1)S(1)} %collective-permute-done.25.refs_1_), custom_call_target="tpu_custom_call" | custom-call | bytes 6300000 | tf_op jit(solution)/shard_map/unpack_one/pallas_call | solution.py:659
  105.1 1.8 %collective-permute-done.19.refs_1_ = bf16[320,256]{1,0:T(8,128)(2,1)S(1)} collective-permute-done((bf16[320,256]{1,0:T(8,128)(2,1)S(1)}, bf16[320,256]{1,0:T(8,128)(2,1)S(1)}, u32[]{:S(2)}, u32[]{:S(2)}) %collective-permute-start.19) | collective-permute-done | bytes 163872 | tf_op jit(solution)/shard_map/ppermute | solution.py:690
  107.0 2.3 %collective-permute-done.20.refs_2_ = bf16[320,256]{1,0:T(8,128)(2,1)S(1)} collective-permute-done((bf16[320,256]{1,0:T(8,128)(2,1)S(1)}, bf16[320,256]{1,0:T(8,128)(2,1)S(1)}, u32[]{:S(2)}, u32[]{:S(2)}) %collective-permute-start.20) | collective-permute-done | bytes 163872 | tf_op jit(solution)/shard_map/ppermute | solution.py:690
  109.2 2.4 %collective-permute-done.21.refs_3_ = bf16[320,256]{1,0:T(8,128)(2,1)S(1)} collective-permute-done((bf16[320,256]{1,0:T(8,128)(2,1)S(1)}, bf16[320,256]{1,0:T(8,128)(2,1)S(1)}, u32[]{:S(2)}, u32[]{:S(2)}) %collective-permute-start.21) | collective-permute-done | bytes 163872 | tf_op jit(solution)/shard_map/ppermute | solution.py:690
  111.6 0.1 order.3.refs_0_
  111.7 0.1 collective-permute-start.26
  111.8 1.1 unpack_mine.1
  112.9 0.9 collective-permute-done.26.refs_1_
  113.8 1.8 %unpack_theirs.1 = (f32[2,256,1024]{2,1,0:T(8,128)}, f32[2,1024,256]{2,1,0:T(8,128)}, f32[7,7,2,256]{3,2,1,0:T(2,128)}, f32[2,256]{1,0:T(2,128)}, f32[2,256]{1,0:T(2,128)}) custom-call(bf16[1088,256]{1,0:T(8,128)(2,1)S(1)} %order.3.refs_0_, bf16[1088,256]{1,0:T(8,128)(2,1)S(1)} %collective-permute-done.26.refs_1_, ...), custom_call_target="tpu_custom_call", output_to_operand_aliasing={{0}: (2, {}), {1}: (3, {})} | custom-call | bytes 4550000 | tf_op jit(solution)/shard_map/unpack_theirs/pallas_call | solution.py:659
  (27 shorter events, 0.1 us)
Async XLA Ops:
  0.6 1.0 copy-start.3
  1.6 10.7 %copy-start.5 = (s32[32,4,2]{0,2,1:T(2,128)S(1)}, s32[32,4,2]{0,2,1:T(2,128)}, u32[]{:S(2)}) copy-start(s32[32,4,2]{0,2,1:T(2,128)} %param.16) | copy-start | bytes 3076
  1.6 10.7 %copy-start.6 = (s32[32,4,2]{0,2,1:T(2,128)S(1)}, s32[32,4,2]{0,2,1:T(2,128)}, u32[]{:S(2)}) copy-start(s32[32,4,2]{0,2,1:T(2,128)} %param.17) | copy-start | bytes 3076
  1.7 10.6 %collective-permute-start = (bf16[8,3,16,256]{3,2,1,0:T(8,128)(2,1)S(1)}, bf16[8,3,16,256]{3,2,1,0:T(8,128)(2,1)S(1)}, u32[]{:S(2)}, u32[]{:S(2)}) collective-permute-start(bf16[8,3,16,256]{3,2,1,0:T(8,128)(2,1)S(1)} %get-tuple-element.75.refs_5_.refs_3_), channel_id=1, source_target_pairs={{0,1},{1,2},{2,3},{3,4},{4,5},{5,6},{6,7},{7,8},{8,9},{9,10},{10,1... | collective-permute-start | bytes 589832 | tf_op jit(solution)/shard_map/ppermute | solution.py:684
  2.2 10.1 %collective-permute-start.1 = (bf16[8,3,16,256]{3,2,1,0:T(8,128)(2,1)S(1)}, bf16[8,3,16,256]{3,2,1,0:T(8,128)(2,1)S(1)}, u32[]{:S(2)}, u32[]{:S(2)}) collective-permute-start(bf16[8,3,16,256]{3,2,1,0:T(8,128)(2,1)S(1)} %get-tuple-element.75.refs_5_.refs_3_), channel_id=1, source_target_pairs={{0,15},{1,0},{2,1},{3,2},{4,3},{5,4},{6,5},{7,6},{8,7},{9,8},{10,9... | collective-permute-start | bytes 589832 | tf_op jit(solution)/shard_map/ppermute | solution.py:684
  7.3 1.2 %copy-start = (bf16[2,256,1024]{2,1,0:T(8,128)(2,1)S(1)}, bf16[2,256,1024]{2,1,0:T(8,128)(2,1)}, u32[]{:S(2)}) copy-start(bf16[2,256,1024]{2,1,0:T(8,128)(2,1)} %refs_3_.1) | copy-start | bytes 3145732
  8.5 1.2 %copy-start.1 = (bf16[2,1024,256]{2,1,0:T(8,128)(2,1)S(1)}, bf16[2,1024,256]{2,1,0:T(8,128)(2,1)}, u32[]{:S(2)}) copy-start(bf16[2,1024,256]{2,1,0:T(8,128)(2,1)} %refs_4_.1) | copy-start | bytes 3145732
  9.7 0.9 copy-start.4
  10.6 0.7 copy-start.7
  11.3 0.7 copy-start.8
  12.3 16.6 %copy-start.2 = (bf16[2,16,16,256]{3,2,1,0:T(8,128)(2,1)S(1)}, bf16[2,16,16,256]{3,2,1,0:T(8,128)(2,1)}, u32[]{:S(2)}) copy-start(bf16[2,16,16,256]{3,2,1,0:T(8,128)(2,1)} %refs_11_.1) | copy-start | bytes 786436
  21.0 7.8 %collective-permute-start.2 = (bf16[8,3,16,256]{3,2,1,0:T(8,128)(2,1)S(1)}, bf16[8,3,16,256]{3,2,1,0:T(8,128)(2,1)S(1)}, u32[]{:S(2)}, u32[]{:S(2)}) collective-permute-start(bf16[8,3,16,256]{3,2,1,0:T(8,128)(2,1)S(1)} %get-tuple-element.82.refs_3_), channel_id=1, source_target_pairs={{0,1},{1,2},{2,3},{3,4},{4,5},{5,6},{6,7},{7,8},{8,9},{9,10},{10,1... | collective-permute-start | bytes 589832 | tf_op jit(solution)/shard_map/ppermute | solution.py:684
  21.1 7.8 %collective-permute-start.3 = (bf16[8,3,16,256]{3,2,1,0:T(8,128)(2,1)S(1)}, bf16[8,3,16,256]{3,2,1,0:T(8,128)(2,1)S(1)}, u32[]{:S(2)}, u32[]{:S(2)}) collective-permute-start(bf16[8,3,16,256]{3,2,1,0:T(8,128)(2,1)S(1)} %get-tuple-element.82.refs_3_), channel_id=1, source_target_pairs={{0,15},{1,0},{2,1},{3,2},{4,3},{5,4},{6,5},{7,6},{8,7},{9,8},{10,9... | collective-permute-start | bytes 589832 | tf_op jit(solution)/shard_map/ppermute | solution.py:684
  44.4 7.9 %collective-permute-start.4 = (bf16[8,3,16,256]{3,2,1,0:T(8,128)(2,1)S(1)}, bf16[8,3,16,256]{3,2,1,0:T(8,128)(2,1)S(1)}, u32[]{:S(2)}, u32[]{:S(2)}) collective-permute-start(bf16[8,3,16,256]{3,2,1,0:T(8,128)(2,1)S(1)} %get-tuple-element.86), channel_id=1, source_target_pairs={{0,1},{1,2},{2,3},{3,4},{4,5},{5,6},{6,7},{7,8},{8,9},{9,10},{10,1... | collective-permute-start | bytes 589832 | tf_op jit(solution)/shard_map/ppermute | solution.py:684
  44.4 7.9 %collective-permute-start.5 = (bf16[8,3,16,256]{3,2,1,0:T(8,128)(2,1)S(1)}, bf16[8,3,16,256]{3,2,1,0:T(8,128)(2,1)S(1)}, u32[]{:S(2)}, u32[]{:S(2)}) collective-permute-start(bf16[8,3,16,256]{3,2,1,0:T(8,128)(2,1)S(1)} %get-tuple-element.87), channel_id=1, source_target_pairs={{0,15},{1,0},{2,1},{3,2},{4,3},{5,4},{6,5},{7,6},{8,7},{9,8},{10,9... | collective-permute-start | bytes 589832 | tf_op jit(solution)/shard_map/ppermute | solution.py:684
  52.2 2.9 %collective-permute-start.7 = (bf16[1024,256]{1,0:T(8,128)(2,1)S(1)}, bf16[1024,256]{1,0:T(8,128)(2,1)S(1)}, u32[]{:S(2)}, u32[]{:S(2)}) collective-permute-start(bf16[1024,256]{1,0:T(8,128)(2,1)S(1)} %get-tuple-element.108), channel_id=1, source_target_pairs={{0,1},{1,0},{2,3},{3,2},{4,5},{5,4},{6,7},{7,6},{8,9},{9,8},{10,11... | collective-permute-start | bytes 1572872 | tf_op jit(solution)/shard_map/ppermute | solution.py:697
  54.6 12.4 %collective-permute-start.6 = (bf16[1024,256]{1,0:T(8,128)(2,1)S(1)}, bf16[1024,256]{1,0:T(8,128)(2,1)S(1)}, u32[]{:S(2)}, u32[]{:S(2)}) collective-permute-start(bf16[1024,256]{1,0:T(8,128)(2,1)S(1)} %get-tuple-element.97), channel_id=1, source_target_pairs={{0,1},{1,0},{2,3},{3,2},{4,5},{5,4},{6,7},{7,6},{8,9},{9,8},{10,11... | collective-permute-start | bytes 1572872 | tf_op jit(solution)/shard_map/ppermute | solution.py:697
  55.2 7.4 %collective-permute-start.10 = (bf16[256,256]{1,0:T(8,128)(2,1)S(1)}, bf16[256,256]{1,0:T(8,128)(2,1)S(1)}, u32[]{:S(2)}, u32[]{:S(2)}) collective-permute-start(bf16[256,256]{1,0:T(8,128)(2,1)S(1)} %get-tuple-element.113), channel_id=1, source_target_pairs={{0,6},{1,7},{2,4},{3,5},{4,2},{5,3},{6,0},{7,1},{8,14},{9,15},{10,... | collective-permute-start | bytes 393224 | tf_op jit(solution)/shard_map/ppermute | solution.py:697
  55.3 8.3 %collective-permute-start.8 = (bf16[256,256]{1,0:T(8,128)(2,1)S(1)}, bf16[256,256]{1,0:T(8,128)(2,1)S(1)}, u32[]{:S(2)}, u32[]{:S(2)}) collective-permute-start(bf16[256,256]{1,0:T(8,128)(2,1)S(1)} %get-tuple-element.111), channel_id=1, source_target_pairs={{0,2},{1,3},{2,0},{3,1},{4,6},{5,7},{6,4},{7,5},{8,10},{9,11},{10,... | collective-permute-start | bytes 393224 | tf_op jit(solution)/shard_map/ppermute | solution.py:697
  55.4 8.2 %collective-permute-start.9 = (bf16[256,256]{1,0:T(8,128)(2,1)S(1)}, bf16[256,256]{1,0:T(8,128)(2,1)S(1)}, u32[]{:S(2)}, u32[]{:S(2)}) collective-permute-start(bf16[256,256]{1,0:T(8,128)(2,1)S(1)} %get-tuple-element.112), channel_id=1, source_target_pairs={{0,4},{1,5},{2,6},{3,7},{4,0},{5,1},{6,2},{7,3},{8,12},{9,13},{10,... | collective-permute-start | bytes 393224 | tf_op jit(solution)/shard_map/ppermute | solution.py:697
  63.7 15.5 %collective-permute-start.13 = (bf16[256,256]{1,0:T(8,128)(2,1)S(1)}, bf16[256,256]{1,0:T(8,128)(2,1)S(1)}, u32[]{:S(2)}, u32[]{:S(2)}) collective-permute-start(bf16[256,256]{1,0:T(8,128)(2,1)S(1)} %quarter.1.refs_10_.refs_0_), channel_id=1, source_target_pairs={{0,8},{1,9},{2,10},{3,11},{4,12},{5,13},{6,14},{7,15},{8,0},{9,1},... | collective-permute-start | bytes 393224 | tf_op jit(solution)/shard_map/ppermute | solution.py:690
  75.2 3.0 %collective-permute-start.17 = (bf16[64,256]{1,0:T(8,128)(2,1)S(1)}, bf16[64,256]{1,0:T(8,128)(2,1)S(1)}, u32[]{:S(2)}, u32[]{:S(2)}) collective-permute-start(bf16[64,256]{1,0:T(8,128)(2,1)S(1)} %get-tuple-element.127), channel_id=1, source_target_pairs={{0,1},{1,0},{2,3},{3,2},{4,5},{5,4},{6,7},{7,6},{8,9},{9,8},{10,11... | collective-permute-start | bytes 98312 | tf_op jit(solution)/shard_map/ppermute | solution.py:697
  75.2 15.5 %collective-permute-start.11 = (bf16[8,3,16,256]{3,2,1,0:T(8,128)(2,1)S(1)}, bf16[8,3,16,256]{3,2,1,0:T(8,128)(2,1)S(1)}, u32[]{:S(2)}, u32[]{:S(2)}) collective-permute-start(bf16[8,3,16,256]{3,2,1,0:T(8,128)(2,1)S(1)} %get-tuple-element.116), channel_id=1, source_target_pairs={{0,1},{1,2},{2,3},{3,4},{4,5},{5,6},{6,7},{7,8},{8,9},{9,10},{10,1... | collective-permute-start | bytes 589832 | tf_op jit(solution)/shard_map/ppermute | solution.py:684
  75.7 7.1 %collective-permute-start.14 = (bf16[256,256]{1,0:T(8,128)(2,1)S(1)}, bf16[256,256]{1,0:T(8,128)(2,1)S(1)}, u32[]{:S(2)}, u32[]{:S(2)}) collective-permute-start(bf16[256,256]{1,0:T(8,128)(2,1)S(1)} %get-tuple-element.119), channel_id=1, source_target_pairs={{0,2},{1,3},{2,0},{3,1},{4,6},{5,7},{6,4},{7,5},{8,10},{9,11},{10,... | collective-permute-start | bytes 393224 | tf_op jit(solution)/shard_map/ppermute | solution.py:697
  76.3 6.6 %collective-permute-start.15 = (bf16[256,256]{1,0:T(8,128)(2,1)S(1)}, bf16[256,256]{1,0:T(8,128)(2,1)S(1)}, u32[]{:S(2)}, u32[]{:S(2)}) collective-permute-start(bf16[256,256]{1,0:T(8,128)(2,1)S(1)} %get-tuple-element.120), channel_id=1, source_target_pairs={{0,4},{1,5},{2,6},{3,7},{4,0},{5,1},{6,2},{7,3},{8,12},{9,13},{10,... | collective-permute-start | bytes 393224 | tf_op jit(solution)/shard_map/ppermute | solution.py:697
  78.1 10.3 %collective-permute-start.16 = (bf16[256,256]{1,0:T(8,128)(2,1)S(1)}, bf16[256,256]{1,0:T(8,128)(2,1)S(1)}, u32[]{:S(2)}, u32[]{:S(2)}) collective-permute-start(bf16[256,256]{1,0:T(8,128)(2,1)S(1)} %get-tuple-element.121), channel_id=1, source_target_pairs={{0,6},{1,7},{2,4},{3,5},{4,2},{5,3},{6,0},{7,1},{8,14},{9,15},{10,... | collective-permute-start | bytes 393224 | tf_op jit(solution)/shard_map/ppermute | solution.py:697
  79.2 13.0 %collective-permute-start.12 = (bf16[8,3,16,256]{3,2,1,0:T(8,128)(2,1)S(1)}, bf16[8,3,16,256]{3,2,1,0:T(8,128)(2,1)S(1)}, u32[]{:S(2)}, u32[]{:S(2)}) collective-permute-start(bf16[8,3,16,256]{3,2,1,0:T(8,128)(2,1)S(1)} %get-tuple-element.117), channel_id=1, source_target_pairs={{0,15},{1,0},{2,1},{3,2},{4,3},{5,4},{6,5},{7,6},{8,7},{9,8},{10,9... | collective-permute-start | bytes 589832 | tf_op jit(solution)/shard_map/ppermute | solution.py:684
  88.6 10.3 %collective-permute-start.18 = (bf16[320,256]{1,0:T(8,128)(2,1)S(1)}, bf16[320,256]{1,0:T(8,128)(2,1)S(1)}, u32[]{:S(2)}, u32[]{:S(2)}) collective-permute-start(bf16[320,256]{1,0:T(8,128)(2,1)S(1)} %get-tuple-element.128.refs_0_), channel_id=1, source_target_pairs={{0,8},{1,9},{2,10},{3,11},{4,12},{5,13},{6,14},{7,15},{8,0},{9,1},... | collective-permute-start | bytes 491528 | tf_op jit(solution)/shard_map/ppermute | solution.py:690
  88.7 10.3 %collective-permute-start.22 = (bf16[256,256]{1,0:T(8,128)(2,1)S(1)}, bf16[256,256]{1,0:T(8,128)(2,1)S(1)}, u32[]{:S(2)}, u32[]{:S(2)}) collective-permute-start(bf16[256,256]{1,0:T(8,128)(2,1)S(1)} %get-tuple-element.130.refs_0_), channel_id=1, source_target_pairs={{0,2},{1,3},{2,0},{3,1},{4,6},{5,7},{6,4},{7,5},{8,10},{9,11},{10,... | collective-permute-start | bytes 393224 | tf_op jit(solution)/shard_map/ppermute | solution.py:690
  88.7 10.2 %collective-permute-start.23 = (bf16[256,256]{1,0:T(8,128)(2,1)S(1)}, bf16[256,256]{1,0:T(8,128)(2,1)S(1)}, u32[]{:S(2)}, u32[]{:S(2)}) collective-permute-start(bf16[256,256]{1,0:T(8,128)(2,1)S(1)} %get-tuple-element.130.refs_0_), channel_id=1, source_target_pairs={{0,4},{1,5},{2,6},{3,7},{4,0},{5,1},{6,2},{7,3},{8,12},{9,13},{10,... | collective-permute-start | bytes 393224 | tf_op jit(solution)/shard_map/ppermute | solution.py:690
  90.7 8.5 %collective-permute-start.24 = (bf16[256,256]{1,0:T(8,128)(2,1)S(1)}, bf16[256,256]{1,0:T(8,128)(2,1)S(1)}, u32[]{:S(2)}, u32[]{:S(2)}) collective-permute-start(bf16[256,256]{1,0:T(8,128)(2,1)S(1)} %get-tuple-element.130.refs_0_), channel_id=1, source_target_pairs={{0,6},{1,7},{2,4},{3,5},{4,2},{5,3},{6,0},{7,1},{8,14},{9,15},{10,... | collective-permute-start | bytes 393224 | tf_op jit(solution)/shard_map/ppermute | solution.py:690
  99.3 4.4 %collective-permute-start.25 = (bf16[1024,256]{1,0:T(8,128)(2,1)S(1)}, bf16[1024,256]{1,0:T(8,128)(2,1)S(1)}, u32[]{:S(2)}, u32[]{:S(2)}) collective-permute-start(bf16[1024,256]{1,0:T(8,128)(2,1)S(1)} %order.2.refs_0_), channel_id=1, source_target_pairs={{0,1},{1,0},{2,3},{3,2},{4,5},{5,4},{6,7},{7,6},{8,9},{9,8},{10,11... | collective-permute-start | bytes 1572872 | tf_op jit(solution)/shard_map/ppermute | solution.py:690
  99.4 7.6 %collective-permute-start.19 = (bf16[320,256]{1,0:T(8,128)(2,1)S(1)}, bf16[320,256]{1,0:T(8,128)(2,1)S(1)}, u32[]{:S(2)}, u32[]{:S(2)}) collective-permute-start(bf16[320,256]{1,0:T(8,128)(2,1)S(1)} %far.1.refs_4_.refs_0_), channel_id=1, source_target_pairs={{0,2},{1,3},{2,0},{3,1},{4,6},{5,7},{6,4},{7,5},{8,10},{9,11},{10,... | collective-permute-start | bytes 491528 | tf_op jit(solution)/shard_map/ppermute | solution.py:690
  102.2 7.0 %collective-permute-start.20 = (bf16[320,256]{1,0:T(8,128)(2,1)S(1)}, bf16[320,256]{1,0:T(8,128)(2,1)S(1)}, u32[]{:S(2)}, u32[]{:S(2)}) collective-permute-start(bf16[320,256]{1,0:T(8,128)(2,1)S(1)} %far.1.refs_4_.refs_0_), channel_id=1, source_target_pairs={{0,4},{1,5},{2,6},{3,7},{4,0},{5,1},{6,2},{7,3},{8,12},{9,13},{10,... | collective-permute-start | bytes 491528 | tf_op jit(solution)/shard_map/ppermute | solution.py:690
  102.3 9.3 %collective-permute-start.21 = (bf16[320,256]{1,0:T(8,128)(2,1)S(1)}, bf16[320,256]{1,0:T(8,128)(2,1)S(1)}, u32[]{:S(2)}, u32[]{:S(2)}) collective-permute-start(bf16[320,256]{1,0:T(8,128)(2,1)S(1)} %far.1.refs_4_.refs_0_), channel_id=1, source_target_pairs={{0,6},{1,7},{2,4},{3,5},{4,2},{5,3},{6,0},{7,1},{8,14},{9,15},{10,... | collective-permute-start | bytes 491528 | tf_op jit(solution)/shard_map/ppermute | solution.py:690
  111.7 2.0 %collective-permute-start.26 = (bf16[1088,256]{1,0:T(8,128)(2,1)S(1)}, bf16[1088,256]{1,0:T(8,128)(2,1)S(1)}, u32[]{:S(2)}, u32[]{:S(2)}) collective-permute-start(bf16[1088,256]{1,0:T(8,128)(2,1)S(1)} %order.3.refs_0_), channel_id=1, source_target_pairs={{0,1},{1,0},{2,3},{3,2},{4,5},{5,4},{6,7},{7,6},{8,9},{9,8},{10,11... | collective-permute-start | bytes 1671176 | tf_op jit(solution)/shard_map/ppermute | solution.py:690

commit v8 on v7

--- a/solution.py
+++ b/solution.py
@@ -571,13 +571,11 @@
 
 def middle_kernel(*refs):
     total, payload, held = refs[-3:]
-    pieces, (parts, small) = refs[:-9], (refs[-9:-5], refs[-5:-3])
+    pieces, quarter, small = refs[:-6], refs[-6], refs[-5:-3]
     far_kernel(*pieces, total, held)
-    quarter = parts[0].shape[0]
-    add_rows(
-        payload.at[0:quarter], [lambda rows, array=array: array[rows] for array in parts]
-    )
-    add_rows(payload.at[quarter:], [lambda rows, array=array: array[rows] for array in small])
+    rows = quarter.shape[0]
+    payload[0:rows] = quarter[...]
+    add_rows(payload.at[rows:], [lambda rows, array=array: array[rows] for array in small])
 
 
 def order_kernel(quarter, *refs):
@@ -715,9 +713,9 @@
         )
         return [pieces[0]] + swap(pieces[1:], self.near_masks)
 
-    def quarter(self, parts):
+    def quarter(self, parts, after):
         shape = jax.ShapeDtypeStruct(parts[0].shape, BF16)
-        (total,) = call(quarter_kernel, "quarter", 0.3, near(*parts), near(shape), [])
+        (total,) = call(quarter_kernel, "quarter", 0.3, near(*parts), near(shape), [], after)
         return total
 
     def far(self, total):
@@ -725,7 +723,7 @@
         held = (len(pieces),) + total.shape if len(pieces) > 2 else (1, 16, LANES)
         return pieces, [pltpu.VMEM(held, BF16)]
 
-    def middle(self, quarter, parts, keep, send):
+    def middle(self, quarter, other, keep, send):
         pieces, scratch = self.far(quarter)
         rows, channels = quarter.shape
         shapes = [
@@ -733,7 +731,7 @@
         ]
         return call(
             middle_kernel, "middle", 0.5,
-            near(*pieces, *parts, keep, *swap([send], [1])), near(*shapes), scratch,
+            near(*pieces, other, keep, *swap([send], [1])), near(*shapes), scratch,
         )
 
     def exchange(self, total, after=()):
@@ -860,7 +858,6 @@
         vmem(wide, narrow_short, two_halves),
     )
     parts_one = reduction.share(keep_one, send_one, (scale_sums,))
-    quarter_one = reduction.quarter(parts_one)
     parts_zero = reduction.share(keep_zero, send_zero)
     base, grad_own, grad_below, grad_above, grad_conv, gain_sums = call(
         functools.partial(spread_kernel, sz, 0),
@@ -868,8 +865,10 @@
         plan + near(kern, gain, up, flat, up_in, normal, inverse),
         near(slabs, own_shape, strips_shape, strips_shape, grad_slabs, sums),
         vmem(taps, narrow, grad_pool, padded),
-        (parts_zero[0], quarter_one),
-    )
+        (parts_zero[0], parts_one[0]),
+    )
+    quarter_one = reduction.quarter(parts_one, (gain_sums,))
+    quarter_zero = reduction.quarter(parts_zero, (quarter_one,))
     from_below, from_above = pass_on(grad_above, 1), pass_on(grad_below, -1)
     small_keep, small_send = call(
         functools.partial(taps_kernel, sz),
@@ -877,6 +876,7 @@
         near(pad_zero, grad_conv, gain_sums, scale_sums, small_one),
         near(*[shape(small.shape, BF16)] * 2),
         vmem(tap_sums, small, shape((2,) + small.shape, F32)),
+        (quarter_zero,),
     )
     in_grad, token = call(
         functools.partial(last_kernel, sz),
@@ -886,7 +886,7 @@
         vmem(slabs, image) + sems(1),
     )
     rows = hidden // 4
-    total_one, total_zero = reduction.middle(quarter_one, parts_zero, small_keep, small_send)
+    total_one, total_zero = reduction.middle(quarter_one, quarter_zero, small_keep, small_send)
     total_zero = reduction.exchange(total_zero, (token,))
     mine_one = reduction.gather(total_one, rows, (total_zero,))
     theirs_one = partners(mine_one, [1])[0]

time: 116 us -> 111 us (0.957)
  waiting for transfers between devices: 27.7 us -> 21.2 us
  starting transfers between devices: 37.5 us -> 39.2 us
    ppermute x9, waiting for transfers between devices: 10.9 us -> 1.26 us  [swap(): lax.ppermute(array, 'tile', [(i, i ^ mask) for i in range(length)])]
    ppermute x10, starting transfers between devices: 11.4 us -> 14.6 us  [partners(): lax.ppermute(array, 'tile', [(i, i ^ mask) for i in range(length)])]
    ppermute x10, waiting for transfers between devices: 13.4 us -> 16.6 us  [partners(): lax.ppermute(array, 'tile', [(i, i ^ mask) for i in range(length)])]
    ppermute x9, starting transfers between devices: 7.69 us -> 6.52 us  [swap(): lax.ppermute(array, 'tile', [(i, i ^ mask) for i in range(length)])]
    pallas_call x19 -> x20, Pallas kernels: 43.7 us -> 43.7 us  [call(): pl.pallas_call(run, in_specs=[spec for spec, _ in ins] + [pl.BlockSpec(me...]
  transfers between devices with their start and end apart: 27 -> 27, of which waited for: 11 -> 9; matrix products, arithmetic and copies ran while one was open for 0% -> 0% of each run, Pallas kernels for 15% -> 16%
where the time goes in v8:
time: 111 us
  Pallas kernels  43.7 us (39%)
  starting transfers between devices  39.2 us (35%)
  waiting for transfers between devices  21.2 us (19%)
  local copies, waits for them, and re-layouts  5.66 us (5%)
    pallas_call x20, Pallas kernels, call(): pl.pallas_call(run, in_specs=[spec for spec, _ in ins] + [pl.BlockSpec(me...  43.7 us
    ppermute x8, starting transfers between devices, pass_on(): lax.ppermute(shard, 'tile', [(i, (i + by) % length) for i in range(length)])  18.1 us
    ppermute x10, waiting for transfers between devices, partners(): lax.ppermute(array, 'tile', [(i, i ^ mask) for i in range(length)])  16.6 us
    ppermute x10, starting transfers between devices, partners(): lax.ppermute(array, 'tile', [(i, i ^ mask) for i in range(length)])  14.6 us
    ppermute x9, starting transfers between devices, swap(): lax.ppermute(array, 'tile', [(i, i ^ mask) for i in range(length)])  6.52 us
    unnamed x18, local copies, waits for them, and re-layouts  5.66 us
    ppermute x8, waiting for transfers between devices, pass_on(): lax.ppermute(shard, 'tile', [(i, (i + by) % length) for i in range(length)])  3.37 us
  transfers between devices with their start and end apart: 27, of which 9 were waited for; matrix products, arithmetic and copies ran while one was open for 0% of the time, Pallas kernels for 16%

profile of v8, /device:TPU:0, one launch (start us, length us, event | category | flops | bytes accessed | tf_op | source)
XLA Modules:
  0.0 110.8 jit_solution(13796336270262778941)
XLA Ops:
  0.6 0.9 copy-done.3
  1.6 0.1 strips.1
  1.7 0.5 collective-permute-start
  2.2 5.1 %collective-permute-start.1 = (bf16[8,3,16,256]{3,2,1,0:T(8,128)(2,1)S(1)}, bf16[8,3,16,256]{3,2,1,0:T(8,128)(2,1)S(1)}, u32[]{:S(2)}, u32[]{:S(2)}) collective-permute-start(bf16[8,3,16,256]{3,2,1,0:T(8,128)(2,1)S(1)} %get-tuple-element.75.refs_5_.refs_3_), channel_id=1, source_target_pairs={{0,15},{1,0},{2,1},{3,2},{4,3},{5,4},{6,5},{7,6},{8,7},{9,8},{10,9... | collective-permute-start | bytes 589832 | tf_op jit(solution)/shard_map/ppermute | solution.py:682
  7.3 1.2 %copy-done = bf16[2,256,1024]{2,1,0:T(8,128)(2,1)S(1)} copy-done((bf16[2,256,1024]{2,1,0:T(8,128)(2,1)S(1)}, bf16[2,256,1024]{2,1,0:T(8,128)(2,1)}, u32[]{:S(2)}) %copy-start) | copy-done | bytes 1048600
  8.5 1.2 %copy-done.1 = bf16[2,1024,256]{2,1,0:T(8,128)(2,1)S(1)} copy-done((bf16[2,1024,256]{2,1,0:T(8,128)(2,1)S(1)}, bf16[2,1024,256]{2,1,0:T(8,128)(2,1)}, u32[]{:S(2)}) %copy-start.1) | copy-done | bytes 1048600
  9.7 0.9 copy-done.4
  10.6 0.7 copy-done.7
  11.3 0.7 copy-done.8
  12.0 0.3 fetch.1
  12.3 0.0 copy-start.2
  12.3 0.0 collective-permute-done.1.refs_5_
  12.3 8.7 %forward.1 = (bf16[2,16,16,256]{3,2,1,0:T(8,128)(2,1)S(1)}, bf16[8,3,16,256]{3,2,1,0:T(8,128)(2,1)S(1)}, f32[4,528,128]{2,1,0:T(8,128)S(1)}, f32[4,256,128]{2,1,...) custom-call(s32[4,2,32]{2,1,0:T(2,128)S(1)} %bitcast.13, ...), custom_call_target="tpu_custom_call" | custom-call | bytes 30450000 | tf_op jit(solution)/shard_map/forward/pallas_call | solution.py:657
  21.0 0.1 collective-permute-start.2
  21.1 4.4 %collective-permute-start.3 = (bf16[8,3,16,256]{3,2,1,0:T(8,128)(2,1)S(1)}, bf16[8,3,16,256]{3,2,1,0:T(8,128)(2,1)S(1)}, u32[]{:S(2)}, u32[]{:S(2)}) collective-permute-start(bf16[8,3,16,256]{3,2,1,0:T(8,128)(2,1)S(1)} %get-tuple-element.82.refs_3_), channel_id=1, source_target_pairs={{0,15},{1,0},{2,1},{3,2},{4,3},{5,4},{6,5},{7,6},{8,7},{9,8},{10,9... | collective-permute-start | bytes 589832 | tf_op jit(solution)/shard_map/ppermute | solution.py:682
  25.5 3.3 %collective-permute-done.2.refs_4_ = bf16[8,3,16,256]{3,2,1,0:T(8,128)(2,1)S(1)} collective-permute-done((bf16[8,3,16,256]{3,2,1,0:T(8,128)(2,1)S(1)}, bf16[8,3,16,256]{3,2,1,0:T(8,128)(2,1)S(1)}, u32[]{:S(2)}, u32[]{:S(2)}) %collective-permute-start.2) | collective-permute-done | bytes 196640 | tf_op jit(solution)/shard_map/ppermute | solution.py:682
  28.8 0.0 collective-permute-done.3.refs_5_
  28.9 15.5 %turn.1 = (bf16[2,16,16,256]{3,2,1,0:T(8,128)(2,1)}, f32[4,256,128]{2,1,0:T(8,128)S(1)}, f32[8,3,2,16,128]{4,3,2,1,0:T(8,128)S(1)}, bf16[8,3,16,256]{3,2,1,0:T(8...) custom-call(s32[4,2,32]{2,1,0:T(2,128)S(1)} %bitcast.14, ...), custom_call_target="tpu_custom_call" | custom-call | bytes 53900000 | tf_op jit(solution)/shard_map/turn/pallas_call | solution.py:657
  44.4 0.1 collective-permute-start.4
  44.4 4.7 %collective-permute-start.5 = (bf16[8,3,16,256]{3,2,1,0:T(8,128)(2,1)S(1)}, bf16[8,3,16,256]{3,2,1,0:T(8,128)(2,1)S(1)}, u32[]{:S(2)}, u32[]{:S(2)}) collective-permute-start(bf16[8,3,16,256]{3,2,1,0:T(8,128)(2,1)S(1)} %get-tuple-element.87), channel_id=1, source_target_pairs={{0,15},{1,0},{2,1},{3,2},{4,3},{5,4},{6,5},{7,6},{8,7},{9,8},{10,9... | collective-permute-start | bytes 589832 | tf_op jit(solution)/shard_map/ppermute | solution.py:682
  49.1 3.1 %weights.1 = (bf16[1024,256]{1,0:T(8,128)(2,1)S(1)}, bf16[1024,256]{1,0:T(8,128)(2,1)S(1)}, f32[64,256]{1,0:T(8,128)S(1)}) custom-call(f32[4,528,128]{2,1,0:T(8,128)S(1)} %get-tuple-element.99.refs_0_, f32[4,512,128]{2,1,0:T(8,128)S(1)} %get-tuple-element.100.refs_1_, bf16[512,256]{1,0:T(8,128)(2,1)S(1)} %get-tuple-element.101.refs_2_, ...), custom_call_target="tpu_custom_call" | custom-call | bytes 9800000 | tf_op jit(solution)/shard_map/weights/pallas_call | solution.py:657
  52.2 0.1 collective-permute-start.7
  52.3 0.0 collective-permute-done.4.refs_2_
  52.3 0.0 collective-permute-done.5.refs_3_
  52.3 2.3 %backward.1 = (bf16[1024,256]{1,0:T(8,128)(2,1)S(1)}, bf16[1024,256]{1,0:T(8,128)(2,1)S(1)}, f32[4,256,128]{2,1,0:T(8,128)S(1)}, bf16[512,1024]{1,0:T(8,128)(2,1)S(1)}, f32[16,256]{1,0:T(8,128)S(1)}) custom-call(f32[4,256,128]{2,1,0:T(8,128)S(1)} %get-tuple-element.84.refs_0_, f32[8,3,2,16,128]{4,3,2,1,0:T(8,128)S(1)} %get-tuple-element.85.refs_1_, ...), custom_call_target="tpu_custom_call" | custom-call | bytes 10150000 | tf_op jit(solution)/shard_map/backward/pallas_call | solution.py:657
  54.6 0.5 collective-permute-start.6
  55.1 0.1 share_near.3
  55.2 0.1 collective-permute-start.10
  55.3 0.1 collective-permute-start.11
  55.4 3.4 %collective-permute-start.12 = (bf16[256,256]{1,0:T(8,128)(2,1)S(1)}, bf16[256,256]{1,0:T(8,128)(2,1)S(1)}, u32[]{:S(2)}, u32[]{:S(2)}) collective-permute-start(bf16[256,256]{1,0:T(8,128)(2,1)S(1)} %get-tuple-element.118), channel_id=1, source_target_pairs={{0,6},{1,7},{2,4},{3,5},{4,2},{5,3},{6,0},{7,1},{8,14},{9,15},{10,... | collective-permute-start | bytes 393224 | tf_op jit(solution)/shard_map/ppermute | solution.py:695
  58.8 0.1 share_near.2
  58.9 0.1 collective-permute-start.14
  59.0 0.5 collective-permute-start.15
  59.5 1.2 %collective-permute-done.10.refs_1_ = bf16[256,256]{1,0:T(8,128)(2,1)S(1)} collective-permute-done((bf16[256,256]{1,0:T(8,128)(2,1)S(1)}, bf16[256,256]{1,0:T(8,128)(2,1)S(1)}, u32[]{:S(2)}, u32[]{:S(2)}) %collective-permute-start.10) | collective-permute-done | bytes 131104 | tf_op jit(solution)/shard_map/ppermute | solution.py:695
  60.8 1.7 %collective-permute-start.16 = (bf16[256,256]{1,0:T(8,128)(2,1)S(1)}, bf16[256,256]{1,0:T(8,128)(2,1)S(1)}, u32[]{:S(2)}, u32[]{:S(2)}) collective-permute-start(bf16[256,256]{1,0:T(8,128)(2,1)S(1)} %get-tuple-element.122), channel_id=1, source_target_pairs={{0,6},{1,7},{2,4},{3,5},{4,2},{5,3},{6,0},{7,1},{8,14},{9,15},{10,... | collective-permute-start | bytes 393224 | tf_op jit(solution)/shard_map/ppermute | solution.py:695
  62.5 5.9 %spread.1 = (f32[4,256,128]{2,1,0:T(8,128)S(1)}, f32[8,3,2,16,128]{4,3,2,1,0:T(8,128)S(1)}, bf16[8,3,16,256]{3,2,1,0:T(8,128)(2,1)S(1)}, bf16[8,3,16,256]{3,2,1,...) custom-call(s32[4,2,32]{2,1,0:T(2,128)S(1)} %bitcast.15, s32[4,2,32]{2,1,0:T(2,128)S(1)} %bitcast.18, ...), custom_call_target="tpu_custom_call" | custom-call | bytes 21000000 | tf_op jit(solution)/shard_map/spread/pallas_call | solution.py:657
  68.4 0.1 collective-permute-start.8
  68.5 0.1 quarter.2.refs_4_.refs_0_
  68.6 3.5 %collective-permute-start.13 = (bf16[256,256]{1,0:T(8,128)(2,1)S(1)}, bf16[256,256]{1,0:T(8,128)(2,1)S(1)}, u32[]{:S(2)}, u32[]{:S(2)}) collective-permute-start(bf16[256,256]{1,0:T(8,128)(2,1)S(1)} %quarter.2.refs_4_.refs_0_), channel_id=1, source_target_pairs={{0,8},{1,9},{2,10},{3,11},{4,12},{5,13},{6,14},{7,15},{8,0},{9,1},... | collective-permute-start | bytes 393224 | tf_op jit(solution)/shard_map/ppermute | solution.py:688
  72.0 3.2 %collective-permute-start.9 = (bf16[8,3,16,256]{3,2,1,0:T(8,128)(2,1)S(1)}, bf16[8,3,16,256]{3,2,1,0:T(8,128)(2,1)S(1)}, u32[]{:S(2)}, u32[]{:S(2)}) collective-permute-start(bf16[8,3,16,256]{3,2,1,0:T(8,128)(2,1)S(1)} %get-tuple-element.114), channel_id=1, source_target_pairs={{0,15},{1,0},{2,1},{3,2},{4,3},{5,4},{6,5},{7,6},{8,7},{9,8},{10,9... | collective-permute-start | bytes 589832 | tf_op jit(solution)/shard_map/ppermute | solution.py:682
  75.3 0.1 quarter.3.refs_5_.refs_2_
  75.4 2.1 %taps.1 = (bf16[64,256]{1,0:T(8,128)(2,1)S(1)}, bf16[64,256]{1,0:T(8,128)(2,1)S(1)}) custom-call(f32[4,528,128]{2,1,0:T(8,128)S(1)} %get-tuple-element.123.refs_0_, f32[4,512,128]{2,1,0:T(8,128)S(1)} %get-tuple-element.124.refs_1_, f32[16,256]{1,0:T(8,128)S(1)} %get-tuple-element.119.refs_4_.refs_2_, f32[16,256]{1,0:T(8,128)S(1)} %get-tuple-element.109.refs_2_.refs_3_, ...), custom_call_target="tpu_custom_call" | custom-call | bytes 7350000 | tf_op jit(solution)/shard_map/taps/pallas_call | solution.py:657
  77.4 0.1 collective-permute-start.17
  77.5 1.4 %collective-permute-done.13.refs_1_ = bf16[256,256]{1,0:T(8,128)(2,1)S(1)} collective-permute-done((bf16[256,256]{1,0:T(8,128)(2,1)S(1)}, bf16[256,256]{1,0:T(8,128)(2,1)S(1)}, u32[]{:S(2)}, u32[]{:S(2)}) %collective-permute-start.13) | collective-permute-done | bytes 131104 | tf_op jit(solution)/shard_map/ppermute | solution.py:688
  79.0 0.1 collective-permute-start.18
  79.1 1.8 %collective-permute-start.22 = (bf16[256,256]{1,0:T(8,128)(2,1)S(1)}, bf16[256,256]{1,0:T(8,128)(2,1)S(1)}, u32[]{:S(2)}, u32[]{:S(2)}) collective-permute-start(bf16[256,256]{1,0:T(8,128)(2,1)S(1)} %get-tuple-element.130.refs_0_), channel_id=1, source_target_pairs={{0,2},{1,3},{2,0},{3,1},{4,6},{5,7},{6,4},{7,5},{8,10},{9,11},{10,... | collective-permute-start | bytes 393224 | tf_op jit(solution)/shard_map/ppermute | solution.py:688
  80.8 3.2 %collective-permute-start.23 = (bf16[256,256]{1,0:T(8,128)(2,1)S(1)}, bf16[256,256]{1,0:T(8,128)(2,1)S(1)}, u32[]{:S(2)}, u32[]{:S(2)}) collective-permute-start(bf16[256,256]{1,0:T(8,128)(2,1)S(1)} %get-tuple-element.130.refs_0_), channel_id=1, source_target_pairs={{0,4},{1,5},{2,6},{3,7},{4,0},{5,1},{6,2},{7,3},{8,12},{9,13},{10,... | collective-permute-start | bytes 393224 | tf_op jit(solution)/shard_map/ppermute | solution.py:688
  84.0 1.4 %collective-permute-start.24 = (bf16[256,256]{1,0:T(8,128)(2,1)S(1)}, bf16[256,256]{1,0:T(8,128)(2,1)S(1)}, u32[]{:S(2)}, u32[]{:S(2)}) collective-permute-start(bf16[256,256]{1,0:T(8,128)(2,1)S(1)} %get-tuple-element.130.refs_0_), channel_id=1, source_target_pairs={{0,6},{1,7},{2,4},{3,5},{4,2},{5,3},{6,0},{7,1},{8,14},{9,15},{10,... | collective-permute-start | bytes 393224 | tf_op jit(solution)/shard_map/ppermute | solution.py:688
  85.5 0.9 last.1
  86.4 1.5 %collective-permute-done.18.refs_1_ = bf16[320,256]{1,0:T(8,128)(2,1)S(1)} collective-permute-done((bf16[320,256]{1,0:T(8,128)(2,1)S(1)}, bf16[320,256]{1,0:T(8,128)(2,1)S(1)}, u32[]{:S(2)}, u32[]{:S(2)}) %collective-permute-start.18) | collective-permute-done | bytes 163872 | tf_op jit(solution)/shard_map/ppermute | solution.py:688
  87.9 6.9 %collective-permute-done.24.refs_3_ = bf16[256,256]{1,0:T(8,128)(2,1)S(1)} collective-permute-done((bf16[256,256]{1,0:T(8,128)(2,1)S(1)}, bf16[256,256]{1,0:T(8,128)(2,1)S(1)}, u32[]{:S(2)}, u32[]{:S(2)}) %collective-permute-start.24) | collective-permute-done | bytes 131104 | tf_op jit(solution)/shard_map/ppermute | solution.py:688
  94.8 0.1 order.2.refs_0_
  94.8 1.1 collective-permute-start.25
  95.9 0.4 collective-permute-start.20
  96.3 3.1 %collective-permute-start.21 = (bf16[320,256]{1,0:T(8,128)(2,1)S(1)}, bf16[320,256]{1,0:T(8,128)(2,1)S(1)}, u32[]{:S(2)}, u32[]{:S(2)}) collective-permute-start(bf16[320,256]{1,0:T(8,128)(2,1)S(1)} %far.1.refs_4_.refs_0_), channel_id=1, source_target_pairs={{0,6},{1,7},{2,4},{3,5},{4,2},{5,3},{6,0},{7,1},{8,14},{9,15},{10,... | collective-permute-start | bytes 491528 | tf_op jit(solution)/shard_map/ppermute | solution.py:688
  99.4 1.4 %unpack_one.1 = (f32[2,256,1024]{2,1,0:T(8,128)}, f32[2,1024,256]{2,1,0:T(8,128)}, f32[8,128]{1,0:T(8,128)S(1)}) custom-call(bf16[1024,256]{1,0:T(8,128)(2,1)S(1)} %order.2.refs_0_, bf16[1024,256]{1,0:T(8,128)(2,1)S(1)} %collective-permute-done.25.refs_1_), custom_call_target="tpu_custom_call" | custom-call | bytes 6300000 | tf_op jit(solution)/shard_map/unpack_one/pallas_call | solution.py:657
  100.8 1.3 %collective-permute-done.19.refs_1_ = bf16[320,256]{1,0:T(8,128)(2,1)S(1)} collective-permute-done((bf16[320,256]{1,0:T(8,128)(2,1)S(1)}, bf16[320,256]{1,0:T(8,128)(2,1)S(1)}, u32[]{:S(2)}, u32[]{:S(2)}) %collective-permute-start.19) | collective-permute-done | bytes 163872 | tf_op jit(solution)/shard_map/ppermute | solution.py:688
  102.1 0.9 collective-permute-done.20.refs_2_
  103.0 3.8 %collective-permute-done.21.refs_3_ = bf16[320,256]{1,0:T(8,128)(2,1)S(1)} collective-permute-done((bf16[320,256]{1,0:T(8,128)(2,1)S(1)}, bf16[320,256]{1,0:T(8,128)(2,1)S(1)}, u32[]{:S(2)}, u32[]{:S(2)}) %collective-permute-start.21) | collective-permute-done | bytes 163872 | tf_op jit(solution)/shard_map/ppermute | solution.py:688
  106.8 0.1 order.3.refs_0_
  106.9 0.1 collective-permute-start.26
  107.0 1.1 unpack_mine.1
  108.0 0.9 collective-permute-done.26.refs_1_
  108.9 1.8 %unpack_theirs.1 = (f32[2,256,1024]{2,1,0:T(8,128)}, f32[2,1024,256]{2,1,0:T(8,128)}, f32[7,7,2,256]{3,2,1,0:T(2,128)}, f32[2,256]{1,0:T(2,128)}, f32[2,256]{1,0:T(2,128)}) custom-call(bf16[1088,256]{1,0:T(8,128)(2,1)S(1)} %order.3.refs_0_, bf16[1088,256]{1,0:T(8,128)(2,1)S(1)} %collective-permute-done.26.refs_1_, ...), custom_call_target="tpu_custom_call", output_to_operand_aliasing={{0}: (2, {}), {1}: (3, {})} | custom-call | bytes 4550000 | tf_op jit(solution)/shard_map/unpack_theirs/pallas_call | solution.py:657
  (28 shorter events, 0.1 us)
Async XLA Ops:
  0.6 1.0 copy-start.3
  1.6 10.7 %copy-start.5 = (s32[32,4,2]{0,2,1:T(2,128)S(1)}, s32[32,4,2]{0,2,1:T(2,128)}, u32[]{:S(2)}) copy-start(s32[32,4,2]{0,2,1:T(2,128)} %param.16) | copy-start | bytes 3076
  1.6 10.7 %copy-start.6 = (s32[32,4,2]{0,2,1:T(2,128)S(1)}, s32[32,4,2]{0,2,1:T(2,128)}, u32[]{:S(2)}) copy-start(s32[32,4,2]{0,2,1:T(2,128)} %param.17) | copy-start | bytes 3076
  1.7 10.6 %collective-permute-start = (bf16[8,3,16,256]{3,2,1,0:T(8,128)(2,1)S(1)}, bf16[8,3,16,256]{3,2,1,0:T(8,128)(2,1)S(1)}, u32[]{:S(2)}, u32[]{:S(2)}) collective-permute-start(bf16[8,3,16,256]{3,2,1,0:T(8,128)(2,1)S(1)} %get-tuple-element.75.refs_5_.refs_3_), channel_id=1, source_target_pairs={{0,1},{1,2},{2,3},{3,4},{4,5},{5,6},{6,7},{7,8},{8,9},{9,10},{10,1... | collective-permute-start | bytes 589832 | tf_op jit(solution)/shard_map/ppermute | solution.py:682
  2.2 10.1 %collective-permute-start.1 = (bf16[8,3,16,256]{3,2,1,0:T(8,128)(2,1)S(1)}, bf16[8,3,16,256]{3,2,1,0:T(8,128)(2,1)S(1)}, u32[]{:S(2)}, u32[]{:S(2)}) collective-permute-start(bf16[8,3,16,256]{3,2,1,0:T(8,128)(2,1)S(1)} %get-tuple-element.75.refs_5_.refs_3_), channel_id=1, source_target_pairs={{0,15},{1,0},{2,1},{3,2},{4,3},{5,4},{6,5},{7,6},{8,7},{9,8},{10,9... | collective-permute-start | bytes 589832 | tf_op jit(solution)/shard_map/ppermute | solution.py:682
  7.3 1.2 %copy-start = (bf16[2,256,1024]{2,1,0:T(8,128)(2,1)S(1)}, bf16[2,256,1024]{2,1,0:T(8,128)(2,1)}, u32[]{:S(2)}) copy-start(bf16[2,256,1024]{2,1,0:T(8,128)(2,1)} %refs_3_.1) | copy-start | bytes 3145732
  8.5 1.2 %copy-start.1 = (bf16[2,1024,256]{2,1,0:T(8,128)(2,1)S(1)}, bf16[2,1024,256]{2,1,0:T(8,128)(2,1)}, u32[]{:S(2)}) copy-start(bf16[2,1024,256]{2,1,0:T(8,128)(2,1)} %refs_4_.1) | copy-start | bytes 3145732
  9.7 0.9 copy-start.4
  10.6 0.7 copy-start.7
  11.3 0.7 copy-start.8
  12.3 16.6 %copy-start.2 = (bf16[2,16,16,256]{3,2,1,0:T(8,128)(2,1)S(1)}, bf16[2,16,16,256]{3,2,1,0:T(8,128)(2,1)}, u32[]{:S(2)}) copy-start(bf16[2,16,16,256]{3,2,1,0:T(8,128)(2,1)} %refs_11_.1) | copy-start | bytes 786436
  21.0 7.8 %collective-permute-start.2 = (bf16[8,3,16,256]{3,2,1,0:T(8,128)(2,1)S(1)}, bf16[8,3,16,256]{3,2,1,0:T(8,128)(2,1)S(1)}, u32[]{:S(2)}, u32[]{:S(2)}) collective-permute-start(bf16[8,3,16,256]{3,2,1,0:T(8,128)(2,1)S(1)} %get-tuple-element.82.refs_3_), channel_id=1, source_target_pairs={{0,1},{1,2},{2,3},{3,4},{4,5},{5,6},{6,7},{7,8},{8,9},{9,10},{10,1... | collective-permute-start | bytes 589832 | tf_op jit(solution)/shard_map/ppermute | solution.py:682
  21.1 7.8 %collective-permute-start.3 = (bf16[8,3,16,256]{3,2,1,0:T(8,128)(2,1)S(1)}, bf16[8,3,16,256]{3,2,1,0:T(8,128)(2,1)S(1)}, u32[]{:S(2)}, u32[]{:S(2)}) collective-permute-start(bf16[8,3,16,256]{3,2,1,0:T(8,128)(2,1)S(1)} %get-tuple-element.82.refs_3_), channel_id=1, source_target_pairs={{0,15},{1,0},{2,1},{3,2},{4,3},{5,4},{6,5},{7,6},{8,7},{9,8},{10,9... | collective-permute-start | bytes 589832 | tf_op jit(solution)/shard_map/ppermute | solution.py:682
  44.4 7.9 %collective-permute-start.4 = (bf16[8,3,16,256]{3,2,1,0:T(8,128)(2,1)S(1)}, bf16[8,3,16,256]{3,2,1,0:T(8,128)(2,1)S(1)}, u32[]{:S(2)}, u32[]{:S(2)}) collective-permute-start(bf16[8,3,16,256]{3,2,1,0:T(8,128)(2,1)S(1)} %get-tuple-element.86), channel_id=1, source_target_pairs={{0,1},{1,2},{2,3},{3,4},{4,5},{5,6},{6,7},{7,8},{8,9},{9,10},{10,1... | collective-permute-start | bytes 589832 | tf_op jit(solution)/shard_map/ppermute | solution.py:682
  44.4 7.9 %collective-permute-start.5 = (bf16[8,3,16,256]{3,2,1,0:T(8,128)(2,1)S(1)}, bf16[8,3,16,256]{3,2,1,0:T(8,128)(2,1)S(1)}, u32[]{:S(2)}, u32[]{:S(2)}) collective-permute-start(bf16[8,3,16,256]{3,2,1,0:T(8,128)(2,1)S(1)} %get-tuple-element.87), channel_id=1, source_target_pairs={{0,15},{1,0},{2,1},{3,2},{4,3},{5,4},{6,5},{7,6},{8,7},{9,8},{10,9... | collective-permute-start | bytes 589832 | tf_op jit(solution)/shard_map/ppermute | solution.py:682
  52.2 2.9 %collective-permute-start.7 = (bf16[1024,256]{1,0:T(8,128)(2,1)S(1)}, bf16[1024,256]{1,0:T(8,128)(2,1)S(1)}, u32[]{:S(2)}, u32[]{:S(2)}) collective-permute-start(bf16[1024,256]{1,0:T(8,128)(2,1)S(1)} %get-tuple-element.108), channel_id=1, source_target_pairs={{0,1},{1,0},{2,3},{3,2},{4,5},{5,4},{6,7},{7,6},{8,9},{9,8},{10,11... | collective-permute-start | bytes 1572872 | tf_op jit(solution)/shard_map/ppermute | solution.py:695
  54.6 4.2 %collective-permute-start.6 = (bf16[1024,256]{1,0:T(8,128)(2,1)S(1)}, bf16[1024,256]{1,0:T(8,128)(2,1)S(1)}, u32[]{:S(2)}, u32[]{:S(2)}) collective-permute-start(bf16[1024,256]{1,0:T(8,128)(2,1)S(1)} %get-tuple-element.97), channel_id=1, source_target_pairs={{0,1},{1,0},{2,3},{3,2},{4,5},{5,4},{6,7},{7,6},{8,9},{9,8},{10,11... | collective-permute-start | bytes 1572872 | tf_op jit(solution)/shard_map/ppermute | solution.py:695
  55.2 5.6 %collective-permute-start.10 = (bf16[256,256]{1,0:T(8,128)(2,1)S(1)}, bf16[256,256]{1,0:T(8,128)(2,1)S(1)}, u32[]{:S(2)}, u32[]{:S(2)}) collective-permute-start(bf16[256,256]{1,0:T(8,128)(2,1)S(1)} %get-tuple-element.116), channel_id=1, source_target_pairs={{0,2},{1,3},{2,0},{3,1},{4,6},{5,7},{6,4},{7,5},{8,10},{9,11},{10,... | collective-permute-start | bytes 393224 | tf_op jit(solution)/shard_map/ppermute | solution.py:695
  55.3 13.1 %collective-permute-start.11 = (bf16[256,256]{1,0:T(8,128)(2,1)S(1)}, bf16[256,256]{1,0:T(8,128)(2,1)S(1)}, u32[]{:S(2)}, u32[]{:S(2)}) collective-permute-start(bf16[256,256]{1,0:T(8,128)(2,1)S(1)} %get-tuple-element.117), channel_id=1, source_target_pairs={{0,4},{1,5},{2,6},{3,7},{4,0},{5,1},{6,2},{7,3},{8,12},{9,13},{10,... | collective-permute-start | bytes 393224 | tf_op jit(solution)/shard_map/ppermute | solution.py:695
  55.4 13.1 %collective-permute-start.12 = (bf16[256,256]{1,0:T(8,128)(2,1)S(1)}, bf16[256,256]{1,0:T(8,128)(2,1)S(1)}, u32[]{:S(2)}, u32[]{:S(2)}) collective-permute-start(bf16[256,256]{1,0:T(8,128)(2,1)S(1)} %get-tuple-element.118), channel_id=1, source_target_pairs={{0,6},{1,7},{2,4},{3,5},{4,2},{5,3},{6,0},{7,1},{8,14},{9,15},{10,... | collective-permute-start | bytes 393224 | tf_op jit(solution)/shard_map/ppermute | solution.py:695
  58.9 13.1 %collective-permute-start.14 = (bf16[256,256]{1,0:T(8,128)(2,1)S(1)}, bf16[256,256]{1,0:T(8,128)(2,1)S(1)}, u32[]{:S(2)}, u32[]{:S(2)}) collective-permute-start(bf16[256,256]{1,0:T(8,128)(2,1)S(1)} %get-tuple-element.120), channel_id=1, source_target_pairs={{0,2},{1,3},{2,0},{3,1},{4,6},{5,7},{6,4},{7,5},{8,10},{9,11},{10,... | collective-permute-start | bytes 393224 | tf_op jit(solution)/shard_map/ppermute | solution.py:695
  59.0 16.2 %collective-permute-start.15 = (bf16[256,256]{1,0:T(8,128)(2,1)S(1)}, bf16[256,256]{1,0:T(8,128)(2,1)S(1)}, u32[]{:S(2)}, u32[]{:S(2)}) collective-permute-start(bf16[256,256]{1,0:T(8,128)(2,1)S(1)} %get-tuple-element.121), channel_id=1, source_target_pairs={{0,4},{1,5},{2,6},{3,7},{4,0},{5,1},{6,2},{7,3},{8,12},{9,13},{10,... | collective-permute-start | bytes 393224 | tf_op jit(solution)/shard_map/ppermute | solution.py:695
  60.8 14.5 %collective-permute-start.16 = (bf16[256,256]{1,0:T(8,128)(2,1)S(1)}, bf16[256,256]{1,0:T(8,128)(2,1)S(1)}, u32[]{:S(2)}, u32[]{:S(2)}) collective-permute-start(bf16[256,256]{1,0:T(8,128)(2,1)S(1)} %get-tuple-element.122), channel_id=1, source_target_pairs={{0,6},{1,7},{2,4},{3,5},{4,2},{5,3},{6,0},{7,1},{8,14},{9,15},{10,... | collective-permute-start | bytes 393224 | tf_op jit(solution)/shard_map/ppermute | solution.py:695
  68.4 15.6 %collective-permute-start.8 = (bf16[8,3,16,256]{3,2,1,0:T(8,128)(2,1)S(1)}, bf16[8,3,16,256]{3,2,1,0:T(8,128)(2,1)S(1)}, u32[]{:S(2)}, u32[]{:S(2)}) collective-permute-start(bf16[8,3,16,256]{3,2,1,0:T(8,128)(2,1)S(1)} %get-tuple-element.113), channel_id=1, source_target_pairs={{0,1},{1,2},{2,3},{3,4},{4,5},{5,6},{6,7},{7,8},{8,9},{9,10},{10,1... | collective-permute-start | bytes 589832 | tf_op jit(solution)/shard_map/ppermute | solution.py:682
  68.6 10.4 %collective-permute-start.13 = (bf16[256,256]{1,0:T(8,128)(2,1)S(1)}, bf16[256,256]{1,0:T(8,128)(2,1)S(1)}, u32[]{:S(2)}, u32[]{:S(2)}) collective-permute-start(bf16[256,256]{1,0:T(8,128)(2,1)S(1)} %quarter.2.refs_4_.refs_0_), channel_id=1, source_target_pairs={{0,8},{1,9},{2,10},{3,11},{4,12},{5,13},{6,14},{7,15},{8,0},{9,1},... | collective-permute-start | bytes 393224 | tf_op jit(solution)/shard_map/ppermute | solution.py:688
  72.0 13.4 %collective-permute-start.9 = (bf16[8,3,16,256]{3,2,1,0:T(8,128)(2,1)S(1)}, bf16[8,3,16,256]{3,2,1,0:T(8,128)(2,1)S(1)}, u32[]{:S(2)}, u32[]{:S(2)}) collective-permute-start(bf16[8,3,16,256]{3,2,1,0:T(8,128)(2,1)S(1)} %get-tuple-element.114), channel_id=1, source_target_pairs={{0,15},{1,0},{2,1},{3,2},{4,3},{5,4},{6,5},{7,6},{8,7},{9,8},{10,9... | collective-permute-start | bytes 589832 | tf_op jit(solution)/shard_map/ppermute | solution.py:682
  77.4 1.5 %collective-permute-start.17 = (bf16[64,256]{1,0:T(8,128)(2,1)S(1)}, bf16[64,256]{1,0:T(8,128)(2,1)S(1)}, u32[]{:S(2)}, u32[]{:S(2)}) collective-permute-start(bf16[64,256]{1,0:T(8,128)(2,1)S(1)} %get-tuple-element.127), channel_id=1, source_target_pairs={{0,1},{1,0},{2,3},{3,2},{4,5},{5,4},{6,7},{7,6},{8,9},{9,8},{10,11... | collective-permute-start | bytes 98312 | tf_op jit(solution)/shard_map/ppermute | solution.py:695
  79.0 8.9 %collective-permute-start.18 = (bf16[320,256]{1,0:T(8,128)(2,1)S(1)}, bf16[320,256]{1,0:T(8,128)(2,1)S(1)}, u32[]{:S(2)}, u32[]{:S(2)}) collective-permute-start(bf16[320,256]{1,0:T(8,128)(2,1)S(1)} %get-tuple-element.128.refs_0_), channel_id=1, source_target_pairs={{0,8},{1,9},{2,10},{3,11},{4,12},{5,13},{6,14},{7,15},{8,0},{9,1},... | collective-permute-start | bytes 491528 | tf_op jit(solution)/shard_map/ppermute | solution.py:688
  79.1 8.8 %collective-permute-start.22 = (bf16[256,256]{1,0:T(8,128)(2,1)S(1)}, bf16[256,256]{1,0:T(8,128)(2,1)S(1)}, u32[]{:S(2)}, u32[]{:S(2)}) collective-permute-start(bf16[256,256]{1,0:T(8,128)(2,1)S(1)} %get-tuple-element.130.refs_0_), channel_id=1, source_target_pairs={{0,2},{1,3},{2,0},{3,1},{4,6},{5,7},{6,4},{7,5},{8,10},{9,11},{10,... | collective-permute-start | bytes 393224 | tf_op jit(solution)/shard_map/ppermute | solution.py:688
  80.8 7.1 %collective-permute-start.23 = (bf16[256,256]{1,0:T(8,128)(2,1)S(1)}, bf16[256,256]{1,0:T(8,128)(2,1)S(1)}, u32[]{:S(2)}, u32[]{:S(2)}) collective-permute-start(bf16[256,256]{1,0:T(8,128)(2,1)S(1)} %get-tuple-element.130.refs_0_), channel_id=1, source_target_pairs={{0,4},{1,5},{2,6},{3,7},{4,0},{5,1},{6,2},{7,3},{8,12},{9,13},{10,... | collective-permute-start | bytes 393224 | tf_op jit(solution)/shard_map/ppermute | solution.py:688
  84.0 10.8 %collective-permute-start.24 = (bf16[256,256]{1,0:T(8,128)(2,1)S(1)}, bf16[256,256]{1,0:T(8,128)(2,1)S(1)}, u32[]{:S(2)}, u32[]{:S(2)}) collective-permute-start(bf16[256,256]{1,0:T(8,128)(2,1)S(1)} %get-tuple-element.130.refs_0_), channel_id=1, source_target_pairs={{0,6},{1,7},{2,4},{3,5},{4,2},{5,3},{6,0},{7,1},{8,14},{9,15},{10,... | collective-permute-start | bytes 393224 | tf_op jit(solution)/shard_map/ppermute | solution.py:688
  94.8 4.6 %collective-permute-start.25 = (bf16[1024,256]{1,0:T(8,128)(2,1)S(1)}, bf16[1024,256]{1,0:T(8,128)(2,1)S(1)}, u32[]{:S(2)}, u32[]{:S(2)}) collective-permute-start(bf16[1024,256]{1,0:T(8,128)(2,1)S(1)} %order.2.refs_0_), channel_id=1, source_target_pairs={{0,1},{1,0},{2,3},{3,2},{4,5},{5,4},{6,7},{7,6},{8,9},{9,8},{10,11... | collective-permute-start | bytes 1572872 | tf_op jit(solution)/shard_map/ppermute | solution.py:688
  95.9 6.2 %collective-permute-start.19 = (bf16[320,256]{1,0:T(8,128)(2,1)S(1)}, bf16[320,256]{1,0:T(8,128)(2,1)S(1)}, u32[]{:S(2)}, u32[]{:S(2)}) collective-permute-start(bf16[320,256]{1,0:T(8,128)(2,1)S(1)} %far.1.refs_4_.refs_0_), channel_id=1, source_target_pairs={{0,2},{1,3},{2,0},{3,1},{4,6},{5,7},{6,4},{7,5},{8,10},{9,11},{10,... | collective-permute-start | bytes 491528 | tf_op jit(solution)/shard_map/ppermute | solution.py:688
  95.9 7.0 %collective-permute-start.20 = (bf16[320,256]{1,0:T(8,128)(2,1)S(1)}, bf16[320,256]{1,0:T(8,128)(2,1)S(1)}, u32[]{:S(2)}, u32[]{:S(2)}) collective-permute-start(bf16[320,256]{1,0:T(8,128)(2,1)S(1)} %far.1.refs_4_.refs_0_), channel_id=1, source_target_pairs={{0,4},{1,5},{2,6},{3,7},{4,0},{5,1},{6,2},{7,3},{8,12},{9,13},{10,... | collective-permute-start | bytes 491528 | tf_op jit(solution)/shard_map/ppermute | solution.py:688
  96.3 10.5 %collective-permute-start.21 = (bf16[320,256]{1,0:T(8,128)(2,1)S(1)}, bf16[320,256]{1,0:T(8,128)(2,1)S(1)}, u32[]{:S(2)}, u32[]{:S(2)}) collective-permute-start(bf16[320,256]{1,0:T(8,128)(2,1)S(1)} %far.1.refs_4_.refs_0_), channel_id=1, source_target_pairs={{0,6},{1,7},{2,4},{3,5},{4,2},{5,3},{6,0},{7,1},{8,14},{9,15},{10,... | collective-permute-start | bytes 491528 | tf_op jit(solution)/shard_map/ppermute | solution.py:688
  106.9 2.0 %collective-permute-start.26 = (bf16[1088,256]{1,0:T(8,128)(2,1)S(1)}, bf16[1088,256]{1,0:T(8,128)(2,1)S(1)}, u32[]{:S(2)}, u32[]{:S(2)}) collective-permute-start(bf16[1088,256]{1,0:T(8,128)(2,1)S(1)} %order.3.refs_0_), channel_id=1, source_target_pairs={{0,1},{1,0},{2,3},{3,2},{4,5},{5,4},{6,7},{7,6},{8,9},{9,8},{10,11... | collective-permute-start | bytes 1671176 | tf_op jit(solution)/shard_map/ppermute | solution.py:688

commit v9 on v8

--- a/solution.py
+++ b/solution.py
@@ -202,7 +202,7 @@
 def activate(sz, upward, active, slope):
     width = 512
 
-    @pl.loop(0, sz.rows // 16)
+    @pl.loop(0, sz.rows // 16, unroll=2)
     def _(t):
         at = pl.ds(pl.multiple_of(t * 16, 16), 16)
         for start in range(0, sz.hidden, width):

time: 111 us -> 111 us (level)
  no operation moved by 1% of the time
where the time goes in v9:
time: 111 us; the launch traced here: 110 us
  Pallas kernels  43.3 us (39%)
  starting transfers between devices  39.2 us (35%)
  waiting for transfers between devices  21.2 us (19%)
  local copies, waits for them, and re-layouts  5.66 us (5%)
    pallas_call x20, Pallas kernels, call(): pl.pallas_call(run, in_specs=[spec for spec, _ in ins] + [pl.BlockSpec(me...  43.3 us
    ppermute x8, starting transfers between devices, pass_on(): lax.ppermute(shard, 'tile', [(i, (i + by) % length) for i in range(length)])  18.1 us
    ppermute x10, waiting for transfers between devices, partners(): lax.ppermute(array, 'tile', [(i, i ^ mask) for i in range(length)])  16.6 us
    ppermute x10, starting transfers between devices, partners(): lax.ppermute(array, 'tile', [(i, i ^ mask) for i in range(length)])  14.6 us
    ppermute x9, starting transfers between devices, swap(): lax.ppermute(array, 'tile', [(i, i ^ mask) for i in range(length)])  6.52 us
    unnamed x18, local copies, waits for them, and re-layouts  5.66 us
    ppermute x8, waiting for transfers between devices, pass_on(): lax.ppermute(shard, 'tile', [(i, (i + by) % length) for i in range(length)])  3.37 us
  transfers between devices with their start and end apart: 27, of which 9 were waited for; matrix products, arithmetic and copies ran while one was open for 0% of the time, Pallas kernels for 16%

profile of v9, /device:TPU:0, one launch (start us, length us, event | category | flops | bytes accessed | tf_op | source)
XLA Modules:
  0.0 110.4 jit_solution(15797470284550222395)
XLA Ops:
  0.6 0.9 copy-done.3
  1.6 0.1 strips.1
  1.7 0.5 collective-permute-start
  2.2 5.1 %collective-permute-start.1 = (bf16[8,3,16,256]{3,2,1,0:T(8,128)(2,1)S(1)}, bf16[8,3,16,256]{3,2,1,0:T(8,128)(2,1)S(1)}, u32[]{:S(2)}, u32[]{:S(2)}) collective-permute-start(bf16[8,3,16,256]{3,2,1,0:T(8,128)(2,1)S(1)} %get-tuple-element.75.refs_5_.refs_3_), channel_id=1, source_target_pairs={{0,15},{1,0},{2,1},{3,2},{4,3},{5,4},{6,5},{7,6},{8,7},{9,8},{10,9... | collective-permute-start | bytes 589832 | tf_op jit(solution)/shard_map/ppermute | solution.py:682
  7.3 1.2 %copy-done = bf16[2,256,1024]{2,1,0:T(8,128)(2,1)S(1)} copy-done((bf16[2,256,1024]{2,1,0:T(8,128)(2,1)S(1)}, bf16[2,256,1024]{2,1,0:T(8,128)(2,1)}, u32[]{:S(2)}) %copy-start) | copy-done | bytes 1048600
  8.5 1.2 %copy-done.1 = bf16[2,1024,256]{2,1,0:T(8,128)(2,1)S(1)} copy-done((bf16[2,1024,256]{2,1,0:T(8,128)(2,1)S(1)}, bf16[2,1024,256]{2,1,0:T(8,128)(2,1)}, u32[]{:S(2)}) %copy-start.1) | copy-done | bytes 1048600
  9.7 0.9 copy-done.4
  10.6 0.7 copy-done.7
  11.3 0.7 copy-done.8
  12.0 0.3 fetch.1
  12.3 0.0 copy-start.2
  12.3 0.0 collective-permute-done.1.refs_5_
  12.3 8.5 %forward.1 = (bf16[2,16,16,256]{3,2,1,0:T(8,128)(2,1)S(1)}, bf16[8,3,16,256]{3,2,1,0:T(8,128)(2,1)S(1)}, f32[4,528,128]{2,1,0:T(8,128)S(1)}, f32[4,256,128]{2,1,...) custom-call(s32[4,2,32]{2,1,0:T(2,128)S(1)} %bitcast.13, ...), custom_call_target="tpu_custom_call" | custom-call | bytes 30450000 | tf_op jit(solution)/shard_map/forward/pallas_call | solution.py:657
  20.8 0.1 collective-permute-start.2
  20.9 4.4 %collective-permute-start.3 = (bf16[8,3,16,256]{3,2,1,0:T(8,128)(2,1)S(1)}, bf16[8,3,16,256]{3,2,1,0:T(8,128)(2,1)S(1)}, u32[]{:S(2)}, u32[]{:S(2)}) collective-permute-start(bf16[8,3,16,256]{3,2,1,0:T(8,128)(2,1)S(1)} %get-tuple-element.82.refs_3_), channel_id=1, source_target_pairs={{0,15},{1,0},{2,1},{3,2},{4,3},{5,4},{6,5},{7,6},{8,7},{9,8},{10,9... | collective-permute-start | bytes 589832 | tf_op jit(solution)/shard_map/ppermute | solution.py:682
  25.3 3.3 %collective-permute-done.2.refs_4_ = bf16[8,3,16,256]{3,2,1,0:T(8,128)(2,1)S(1)} collective-permute-done((bf16[8,3,16,256]{3,2,1,0:T(8,128)(2,1)S(1)}, bf16[8,3,16,256]{3,2,1,0:T(8,128)(2,1)S(1)}, u32[]{:S(2)}, u32[]{:S(2)}) %collective-permute-start.2) | collective-permute-done | bytes 196640 | tf_op jit(solution)/shard_map/ppermute | solution.py:682
  28.7 0.0 collective-permute-done.3.refs_5_
  28.7 15.3 %turn.1 = (bf16[2,16,16,256]{3,2,1,0:T(8,128)(2,1)}, f32[4,256,128]{2,1,0:T(8,128)S(1)}, f32[8,3,2,16,128]{4,3,2,1,0:T(8,128)S(1)}, bf16[8,3,16,256]{3,2,1,0:T(8...) custom-call(s32[4,2,32]{2,1,0:T(2,128)S(1)} %bitcast.14, ...), custom_call_target="tpu_custom_call" | custom-call | bytes 53900000 | tf_op jit(solution)/shard_map/turn/pallas_call | solution.py:657
  44.0 0.1 collective-permute-start.4
  44.1 4.7 %collective-permute-start.5 = (bf16[8,3,16,256]{3,2,1,0:T(8,128)(2,1)S(1)}, bf16[8,3,16,256]{3,2,1,0:T(8,128)(2,1)S(1)}, u32[]{:S(2)}, u32[]{:S(2)}) collective-permute-start(bf16[8,3,16,256]{3,2,1,0:T(8,128)(2,1)S(1)} %get-tuple-element.87), channel_id=1, source_target_pairs={{0,15},{1,0},{2,1},{3,2},{4,3},{5,4},{6,5},{7,6},{8,7},{9,8},{10,9... | collective-permute-start | bytes 589832 | tf_op jit(solution)/shard_map/ppermute | solution.py:682
  48.7 3.1 %weights.1 = (bf16[1024,256]{1,0:T(8,128)(2,1)S(1)}, bf16[1024,256]{1,0:T(8,128)(2,1)S(1)}, f32[64,256]{1,0:T(8,128)S(1)}) custom-call(f32[4,528,128]{2,1,0:T(8,128)S(1)} %get-tuple-element.99.refs_0_, f32[4,512,128]{2,1,0:T(8,128)S(1)} %get-tuple-element.100.refs_1_, bf16[512,256]{1,0:T(8,128)(2,1)S(1)} %get-tuple-element.101.refs_2_, ...), custom_call_target="tpu_custom_call" | custom-call | bytes 9800000 | tf_op jit(solution)/shard_map/weights/pallas_call | solution.py:657
  51.8 0.1 collective-permute-start.7
  51.9 0.0 collective-permute-done.5.refs_3_
  51.9 2.3 %backward.1 = (bf16[1024,256]{1,0:T(8,128)(2,1)S(1)}, bf16[1024,256]{1,0:T(8,128)(2,1)S(1)}, f32[4,256,128]{2,1,0:T(8,128)S(1)}, bf16[512,1024]{1,0:T(8,128)(2,1)S(1)}, f32[16,256]{1,0:T(8,128)S(1)}) custom-call(f32[4,256,128]{2,1,0:T(8,128)S(1)} %get-tuple-element.84.refs_0_, f32[8,3,2,16,128]{4,3,2,1,0:T(8,128)S(1)} %get-tuple-element.85.refs_1_, ...), custom_call_target="tpu_custom_call" | custom-call | bytes 10150000 | tf_op jit(solution)/shard_map/backward/pallas_call | solution.py:657
  54.2 0.5 collective-permute-start.6
  54.7 0.0 collective-permute-done.7
  54.7 0.1 share_near.3
  54.8 0.1 collective-permute-start.10
  54.9 0.1 collective-permute-start.11
  55.0 3.4 %collective-permute-start.12 = (bf16[256,256]{1,0:T(8,128)(2,1)S(1)}, bf16[256,256]{1,0:T(8,128)(2,1)S(1)}, u32[]{:S(2)}, u32[]{:S(2)}) collective-permute-start(bf16[256,256]{1,0:T(8,128)(2,1)S(1)} %get-tuple-element.118), channel_id=1, source_target_pairs={{0,6},{1,7},{2,4},{3,5},{4,2},{5,3},{6,0},{7,1},{8,14},{9,15},{10,... | collective-permute-start | bytes 393224 | tf_op jit(solution)/shard_map/ppermute | solution.py:695
  58.4 0.1 share_near.2
  58.5 0.1 collective-permute-start.14
  58.7 0.5 collective-permute-start.15
  59.1 1.2 %collective-permute-done.10.refs_1_ = bf16[256,256]{1,0:T(8,128)(2,1)S(1)} collective-permute-done((bf16[256,256]{1,0:T(8,128)(2,1)S(1)}, bf16[256,256]{1,0:T(8,128)(2,1)S(1)}, u32[]{:S(2)}, u32[]{:S(2)}) %collective-permute-start.10) | collective-permute-done | bytes 131104 | tf_op jit(solution)/shard_map/ppermute | solution.py:695
  60.4 1.7 %collective-permute-start.16 = (bf16[256,256]{1,0:T(8,128)(2,1)S(1)}, bf16[256,256]{1,0:T(8,128)(2,1)S(1)}, u32[]{:S(2)}, u32[]{:S(2)}) collective-permute-start(bf16[256,256]{1,0:T(8,128)(2,1)S(1)} %get-tuple-element.122), channel_id=1, source_target_pairs={{0,6},{1,7},{2,4},{3,5},{4,2},{5,3},{6,0},{7,1},{8,14},{9,15},{10,... | collective-permute-start | bytes 393224 | tf_op jit(solution)/shard_map/ppermute | solution.py:695
  62.1 5.9 %spread.1 = (f32[4,256,128]{2,1,0:T(8,128)S(1)}, f32[8,3,2,16,128]{4,3,2,1,0:T(8,128)S(1)}, bf16[8,3,16,256]{3,2,1,0:T(8,128)(2,1)S(1)}, bf16[8,3,16,256]{3,2,1,...) custom-call(s32[4,2,32]{2,1,0:T(2,128)S(1)} %bitcast.15, s32[4,2,32]{2,1,0:T(2,128)S(1)} %bitcast.18, ...), custom_call_target="tpu_custom_call" | custom-call | bytes 21000000 | tf_op jit(solution)/shard_map/spread/pallas_call | solution.py:657
  68.0 0.1 collective-permute-start.8
  68.1 0.1 quarter.2.refs_4_.refs_0_
  68.2 3.5 %collective-permute-start.13 = (bf16[256,256]{1,0:T(8,128)(2,1)S(1)}, bf16[256,256]{1,0:T(8,128)(2,1)S(1)}, u32[]{:S(2)}, u32[]{:S(2)}) collective-permute-start(bf16[256,256]{1,0:T(8,128)(2,1)S(1)} %quarter.2.refs_4_.refs_0_), channel_id=1, source_target_pairs={{0,8},{1,9},{2,10},{3,11},{4,12},{5,13},{6,14},{7,15},{8,0},{9,1},... | collective-permute-start | bytes 393224 | tf_op jit(solution)/shard_map/ppermute | solution.py:688
  71.6 3.2 %collective-permute-start.9 = (bf16[8,3,16,256]{3,2,1,0:T(8,128)(2,1)S(1)}, bf16[8,3,16,256]{3,2,1,0:T(8,128)(2,1)S(1)}, u32[]{:S(2)}, u32[]{:S(2)}) collective-permute-start(bf16[8,3,16,256]{3,2,1,0:T(8,128)(2,1)S(1)} %get-tuple-element.114), channel_id=1, source_target_pairs={{0,15},{1,0},{2,1},{3,2},{4,3},{5,4},{6,5},{7,6},{8,7},{9,8},{10,9... | collective-permute-start | bytes 589832 | tf_op jit(solution)/shard_map/ppermute | solution.py:682
  74.9 0.1 quarter.3.refs_5_.refs_2_
  75.0 2.1 %taps.1 = (bf16[64,256]{1,0:T(8,128)(2,1)S(1)}, bf16[64,256]{1,0:T(8,128)(2,1)S(1)}) custom-call(f32[4,528,128]{2,1,0:T(8,128)S(1)} %get-tuple-element.123.refs_0_, f32[4,512,128]{2,1,0:T(8,128)S(1)} %get-tuple-element.124.refs_1_, f32[16,256]{1,0:T(8,128)S(1)} %get-tuple-element.119.refs_4_.refs_2_, f32[16,256]{1,0:T(8,128)S(1)} %get-tuple-element.109.refs_2_.refs_3_, ...), custom_call_target="tpu_custom_call" | custom-call | bytes 7350000 | tf_op jit(solution)/shard_map/taps/pallas_call | solution.py:657
  77.1 0.1 collective-permute-start.17
  77.1 1.4 %collective-permute-done.13.refs_1_ = bf16[256,256]{1,0:T(8,128)(2,1)S(1)} collective-permute-done((bf16[256,256]{1,0:T(8,128)(2,1)S(1)}, bf16[256,256]{1,0:T(8,128)(2,1)S(1)}, u32[]{:S(2)}, u32[]{:S(2)}) %collective-permute-start.13) | collective-permute-done | bytes 131104 | tf_op jit(solution)/shard_map/ppermute | solution.py:688
  78.6 0.1 collective-permute-start.18
  78.7 1.8 %collective-permute-start.22 = (bf16[256,256]{1,0:T(8,128)(2,1)S(1)}, bf16[256,256]{1,0:T(8,128)(2,1)S(1)}, u32[]{:S(2)}, u32[]{:S(2)}) collective-permute-start(bf16[256,256]{1,0:T(8,128)(2,1)S(1)} %get-tuple-element.130.refs_0_), channel_id=1, source_target_pairs={{0,2},{1,3},{2,0},{3,1},{4,6},{5,7},{6,4},{7,5},{8,10},{9,11},{10,... | collective-permute-start | bytes 393224 | tf_op jit(solution)/shard_map/ppermute | solution.py:688
  80.4 3.2 %collective-permute-start.23 = (bf16[256,256]{1,0:T(8,128)(2,1)S(1)}, bf16[256,256]{1,0:T(8,128)(2,1)S(1)}, u32[]{:S(2)}, u32[]{:S(2)}) collective-permute-start(bf16[256,256]{1,0:T(8,128)(2,1)S(1)} %get-tuple-element.130.refs_0_), channel_id=1, source_target_pairs={{0,4},{1,5},{2,6},{3,7},{4,0},{5,1},{6,2},{7,3},{8,12},{9,13},{10,... | collective-permute-start | bytes 393224 | tf_op jit(solution)/shard_map/ppermute | solution.py:688
  83.6 1.4 %collective-permute-start.24 = (bf16[256,256]{1,0:T(8,128)(2,1)S(1)}, bf16[256,256]{1,0:T(8,128)(2,1)S(1)}, u32[]{:S(2)}, u32[]{:S(2)}) collective-permute-start(bf16[256,256]{1,0:T(8,128)(2,1)S(1)} %get-tuple-element.130.refs_0_), channel_id=1, source_target_pairs={{0,6},{1,7},{2,4},{3,5},{4,2},{5,3},{6,0},{7,1},{8,14},{9,15},{10,... | collective-permute-start | bytes 393224 | tf_op jit(solution)/shard_map/ppermute | solution.py:688
  85.1 0.9 last.1
  86.0 1.5 %collective-permute-done.18.refs_1_ = bf16[320,256]{1,0:T(8,128)(2,1)S(1)} collective-permute-done((bf16[320,256]{1,0:T(8,128)(2,1)S(1)}, bf16[320,256]{1,0:T(8,128)(2,1)S(1)}, u32[]{:S(2)}, u32[]{:S(2)}) %collective-permute-start.18) | collective-permute-done | bytes 163872 | tf_op jit(solution)/shard_map/ppermute | solution.py:688
  87.5 6.9 %collective-permute-done.24.refs_3_ = bf16[256,256]{1,0:T(8,128)(2,1)S(1)} collective-permute-done((bf16[256,256]{1,0:T(8,128)(2,1)S(1)}, bf16[256,256]{1,0:T(8,128)(2,1)S(1)}, u32[]{:S(2)}, u32[]{:S(2)}) %collective-permute-start.24) | collective-permute-done | bytes 131104 | tf_op jit(solution)/shard_map/ppermute | solution.py:688
  94.4 0.1 order.2.refs_0_
  94.4 1.1 collective-permute-start.25
  95.5 0.4 collective-permute-start.20
  96.0 3.1 %collective-permute-start.21 = (bf16[320,256]{1,0:T(8,128)(2,1)S(1)}, bf16[320,256]{1,0:T(8,128)(2,1)S(1)}, u32[]{:S(2)}, u32[]{:S(2)}) collective-permute-start(bf16[320,256]{1,0:T(8,128)(2,1)S(1)} %far.1.refs_4_.refs_0_), channel_id=1, source_target_pairs={{0,6},{1,7},{2,4},{3,5},{4,2},{5,3},{6,0},{7,1},{8,14},{9,15},{10,... | collective-permute-start | bytes 491528 | tf_op jit(solution)/shard_map/ppermute | solution.py:688
  99.0 1.4 %unpack_one.1 = (f32[2,256,1024]{2,1,0:T(8,128)}, f32[2,1024,256]{2,1,0:T(8,128)}, f32[8,128]{1,0:T(8,128)S(1)}) custom-call(bf16[1024,256]{1,0:T(8,128)(2,1)S(1)} %order.2.refs_0_, bf16[1024,256]{1,0:T(8,128)(2,1)S(1)} %collective-permute-done.25.refs_1_), custom_call_target="tpu_custom_call" | custom-call | bytes 6300000 | tf_op jit(solution)/shard_map/unpack_one/pallas_call | solution.py:657
  100.4 1.3 %collective-permute-done.19.refs_1_ = bf16[320,256]{1,0:T(8,128)(2,1)S(1)} collective-permute-done((bf16[320,256]{1,0:T(8,128)(2,1)S(1)}, bf16[320,256]{1,0:T(8,128)(2,1)S(1)}, u32[]{:S(2)}, u32[]{:S(2)}) %collective-permute-start.19) | collective-permute-done | bytes 163872 | tf_op jit(solution)/shard_map/ppermute | solution.py:688
  101.7 0.9 collective-permute-done.20.refs_2_
  102.6 3.8 %collective-permute-done.21.refs_3_ = bf16[320,256]{1,0:T(8,128)(2,1)S(1)} collective-permute-done((bf16[320,256]{1,0:T(8,128)(2,1)S(1)}, bf16[320,256]{1,0:T(8,128)(2,1)S(1)}, u32[]{:S(2)}, u32[]{:S(2)}) %collective-permute-start.21) | collective-permute-done | bytes 163872 | tf_op jit(solution)/shard_map/ppermute | solution.py:688
  106.4 0.1 order.3.refs_0_
  106.5 0.1 collective-permute-start.26
  106.6 1.1 unpack_mine.1
  107.7 0.9 collective-permute-done.26.refs_1_
  108.5 1.8 %unpack_theirs.1 = (f32[2,256,1024]{2,1,0:T(8,128)}, f32[2,1024,256]{2,1,0:T(8,128)}, f32[7,7,2,256]{3,2,1,0:T(2,128)}, f32[2,256]{1,0:T(2,128)}, f32[2,256]{1,0:T(2,128)}) custom-call(bf16[1088,256]{1,0:T(8,128)(2,1)S(1)} %order.3.refs_0_, bf16[1088,256]{1,0:T(8,128)(2,1)S(1)} %collective-permute-done.26.refs_1_, ...), custom_call_target="tpu_custom_call", output_to_operand_aliasing={{0}: (2, {}), {1}: (3, {})} | custom-call | bytes 4550000 | tf_op jit(solution)/shard_map/unpack_theirs/pallas_call | solution.py:657
  (28 shorter events, 0.1 us)
Async XLA Ops:
  0.6 1.0 copy-start.3
  1.6 10.7 %copy-start.5 = (s32[32,4,2]{0,2,1:T(2,128)S(1)}, s32[32,4,2]{0,2,1:T(2,128)}, u32[]{:S(2)}) copy-start(s32[32,4,2]{0,2,1:T(2,128)} %param.16) | copy-start | bytes 3076
  1.6 10.7 %copy-start.6 = (s32[32,4,2]{0,2,1:T(2,128)S(1)}, s32[32,4,2]{0,2,1:T(2,128)}, u32[]{:S(2)}) copy-start(s32[32,4,2]{0,2,1:T(2,128)} %param.17) | copy-start | bytes 3076
  1.7 10.6 %collective-permute-start = (bf16[8,3,16,256]{3,2,1,0:T(8,128)(2,1)S(1)}, bf16[8,3,16,256]{3,2,1,0:T(8,128)(2,1)S(1)}, u32[]{:S(2)}, u32[]{:S(2)}) collective-permute-start(bf16[8,3,16,256]{3,2,1,0:T(8,128)(2,1)S(1)} %get-tuple-element.75.refs_5_.refs_3_), channel_id=1, source_target_pairs={{0,1},{1,2},{2,3},{3,4},{4,5},{5,6},{6,7},{7,8},{8,9},{9,10},{10,1... | collective-permute-start | bytes 589832 | tf_op jit(solution)/shard_map/ppermute | solution.py:682
  2.2 10.1 %collective-permute-start.1 = (bf16[8,3,16,256]{3,2,1,0:T(8,128)(2,1)S(1)}, bf16[8,3,16,256]{3,2,1,0:T(8,128)(2,1)S(1)}, u32[]{:S(2)}, u32[]{:S(2)}) collective-permute-start(bf16[8,3,16,256]{3,2,1,0:T(8,128)(2,1)S(1)} %get-tuple-element.75.refs_5_.refs_3_), channel_id=1, source_target_pairs={{0,15},{1,0},{2,1},{3,2},{4,3},{5,4},{6,5},{7,6},{8,7},{9,8},{10,9... | collective-permute-start | bytes 589832 | tf_op jit(solution)/shard_map/ppermute | solution.py:682
  7.3 1.2 %copy-start = (bf16[2,256,1024]{2,1,0:T(8,128)(2,1)S(1)}, bf16[2,256,1024]{2,1,0:T(8,128)(2,1)}, u32[]{:S(2)}) copy-start(bf16[2,256,1024]{2,1,0:T(8,128)(2,1)} %refs_3_.1) | copy-start | bytes 3145732
  8.5 1.2 %copy-start.1 = (bf16[2,1024,256]{2,1,0:T(8,128)(2,1)S(1)}, bf16[2,1024,256]{2,1,0:T(8,128)(2,1)}, u32[]{:S(2)}) copy-start(bf16[2,1024,256]{2,1,0:T(8,128)(2,1)} %refs_4_.1) | copy-start | bytes 3145732
  9.7 0.9 copy-start.4
  10.6 0.7 copy-start.7
  11.3 0.7 copy-start.8
  12.3 16.4 %copy-start.2 = (bf16[2,16,16,256]{3,2,1,0:T(8,128)(2,1)S(1)}, bf16[2,16,16,256]{3,2,1,0:T(8,128)(2,1)}, u32[]{:S(2)}) copy-start(bf16[2,16,16,256]{3,2,1,0:T(8,128)(2,1)} %refs_11_.1) | copy-start | bytes 786436
  20.8 7.8 %collective-permute-start.2 = (bf16[8,3,16,256]{3,2,1,0:T(8,128)(2,1)S(1)}, bf16[8,3,16,256]{3,2,1,0:T(8,128)(2,1)S(1)}, u32[]{:S(2)}, u32[]{:S(2)}) collective-permute-start(bf16[8,3,16,256]{3,2,1,0:T(8,128)(2,1)S(1)} %get-tuple-element.82.refs_3_), channel_id=1, source_target_pairs={{0,1},{1,2},{2,3},{3,4},{4,5},{5,6},{6,7},{7,8},{8,9},{9,10},{10,1... | collective-permute-start | bytes 589832 | tf_op jit(solution)/shard_map/ppermute | solution.py:682
  20.9 7.8 %collective-permute-start.3 = (bf16[8,3,16,256]{3,2,1,0:T(8,128)(2,1)S(1)}, bf16[8,3,16,256]{3,2,1,0:T(8,128)(2,1)S(1)}, u32[]{:S(2)}, u32[]{:S(2)}) collective-permute-start(bf16[8,3,16,256]{3,2,1,0:T(8,128)(2,1)S(1)} %get-tuple-element.82.refs_3_), channel_id=1, source_target_pairs={{0,15},{1,0},{2,1},{3,2},{4,3},{5,4},{6,5},{7,6},{8,7},{9,8},{10,9... | collective-permute-start | bytes 589832 | tf_op jit(solution)/shard_map/ppermute | solution.py:682
  44.0 7.9 %collective-permute-start.4 = (bf16[8,3,16,256]{3,2,1,0:T(8,128)(2,1)S(1)}, bf16[8,3,16,256]{3,2,1,0:T(8,128)(2,1)S(1)}, u32[]{:S(2)}, u32[]{:S(2)}) collective-permute-start(bf16[8,3,16,256]{3,2,1,0:T(8,128)(2,1)S(1)} %get-tuple-element.86), channel_id=1, source_target_pairs={{0,1},{1,2},{2,3},{3,4},{4,5},{5,6},{6,7},{7,8},{8,9},{9,10},{10,1... | collective-permute-start | bytes 589832 | tf_op jit(solution)/shard_map/ppermute | solution.py:682
  44.1 7.9 %collective-permute-start.5 = (bf16[8,3,16,256]{3,2,1,0:T(8,128)(2,1)S(1)}, bf16[8,3,16,256]{3,2,1,0:T(8,128)(2,1)S(1)}, u32[]{:S(2)}, u32[]{:S(2)}) collective-permute-start(bf16[8,3,16,256]{3,2,1,0:T(8,128)(2,1)S(1)} %get-tuple-element.87), channel_id=1, source_target_pairs={{0,15},{1,0},{2,1},{3,2},{4,3},{5,4},{6,5},{7,6},{8,7},{9,8},{10,9... | collective-permute-start | bytes 589832 | tf_op jit(solution)/shard_map/ppermute | solution.py:682
  51.8 2.9 %collective-permute-start.7 = (bf16[1024,256]{1,0:T(8,128)(2,1)S(1)}, bf16[1024,256]{1,0:T(8,128)(2,1)S(1)}, u32[]{:S(2)}, u32[]{:S(2)}) collective-permute-start(bf16[1024,256]{1,0:T(8,128)(2,1)S(1)} %get-tuple-element.108), channel_id=1, source_target_pairs={{0,1},{1,0},{2,3},{3,2},{4,5},{5,4},{6,7},{7,6},{8,9},{9,8},{10,11... | collective-permute-start | bytes 1572872 | tf_op jit(solution)/shard_map/ppermute | solution.py:695
  54.2 4.2 %collective-permute-start.6 = (bf16[1024,256]{1,0:T(8,128)(2,1)S(1)}, bf16[1024,256]{1,0:T(8,128)(2,1)S(1)}, u32[]{:S(2)}, u32[]{:S(2)}) collective-permute-start(bf16[1024,256]{1,0:T(8,128)(2,1)S(1)} %get-tuple-element.97), channel_id=1, source_target_pairs={{0,1},{1,0},{2,3},{3,2},{4,5},{5,4},{6,7},{7,6},{8,9},{9,8},{10,11... | collective-permute-start | bytes 1572872 | tf_op jit(solution)/shard_map/ppermute | solution.py:695
  54.8 5.6 %collective-permute-start.10 = (bf16[256,256]{1,0:T(8,128)(2,1)S(1)}, bf16[256,256]{1,0:T(8,128)(2,1)S(1)}, u32[]{:S(2)}, u32[]{:S(2)}) collective-permute-start(bf16[256,256]{1,0:T(8,128)(2,1)S(1)} %get-tuple-element.116), channel_id=1, source_target_pairs={{0,2},{1,3},{2,0},{3,1},{4,6},{5,7},{6,4},{7,5},{8,10},{9,11},{10,... | collective-permute-start | bytes 393224 | tf_op jit(solution)/shard_map/ppermute | solution.py:695
  54.9 13.1 %collective-permute-start.11 = (bf16[256,256]{1,0:T(8,128)(2,1)S(1)}, bf16[256,256]{1,0:T(8,128)(2,1)S(1)}, u32[]{:S(2)}, u32[]{:S(2)}) collective-permute-start(bf16[256,256]{1,0:T(8,128)(2,1)S(1)} %get-tuple-element.117), channel_id=1, source_target_pairs={{0,4},{1,5},{2,6},{3,7},{4,0},{5,1},{6,2},{7,3},{8,12},{9,13},{10,... | collective-permute-start | bytes 393224 | tf_op jit(solution)/shard_map/ppermute | solution.py:695
  55.0 13.1 %collective-permute-start.12 = (bf16[256,256]{1,0:T(8,128)(2,1)S(1)}, bf16[256,256]{1,0:T(8,128)(2,1)S(1)}, u32[]{:S(2)}, u32[]{:S(2)}) collective-permute-start(bf16[256,256]{1,0:T(8,128)(2,1)S(1)} %get-tuple-element.118), channel_id=1, source_target_pairs={{0,6},{1,7},{2,4},{3,5},{4,2},{5,3},{6,0},{7,1},{8,14},{9,15},{10,... | collective-permute-start | bytes 393224 | tf_op jit(solution)/shard_map/ppermute | solution.py:695
  58.5 13.1 %collective-permute-start.14 = (bf16[256,256]{1,0:T(8,128)(2,1)S(1)}, bf16[256,256]{1,0:T(8,128)(2,1)S(1)}, u32[]{:S(2)}, u32[]{:S(2)}) collective-permute-start(bf16[256,256]{1,0:T(8,128)(2,1)S(1)} %get-tuple-element.120), channel_id=1, source_target_pairs={{0,2},{1,3},{2,0},{3,1},{4,6},{5,7},{6,4},{7,5},{8,10},{9,11},{10,... | collective-permute-start | bytes 393224 | tf_op jit(solution)/shard_map/ppermute | solution.py:695
  58.7 16.2 %collective-permute-start.15 = (bf16[256,256]{1,0:T(8,128)(2,1)S(1)}, bf16[256,256]{1,0:T(8,128)(2,1)S(1)}, u32[]{:S(2)}, u32[]{:S(2)}) collective-permute-start(bf16[256,256]{1,0:T(8,128)(2,1)S(1)} %get-tuple-element.121), channel_id=1, source_target_pairs={{0,4},{1,5},{2,6},{3,7},{4,0},{5,1},{6,2},{7,3},{8,12},{9,13},{10,... | collective-permute-start | bytes 393224 | tf_op jit(solution)/shard_map/ppermute | solution.py:695
  60.4 14.5 %collective-permute-start.16 = (bf16[256,256]{1,0:T(8,128)(2,1)S(1)}, bf16[256,256]{1,0:T(8,128)(2,1)S(1)}, u32[]{:S(2)}, u32[]{:S(2)}) collective-permute-start(bf16[256,256]{1,0:T(8,128)(2,1)S(1)} %get-tuple-element.122), channel_id=1, source_target_pairs={{0,6},{1,7},{2,4},{3,5},{4,2},{5,3},{6,0},{7,1},{8,14},{9,15},{10,... | collective-permute-start | bytes 393224 | tf_op jit(solution)/shard_map/ppermute | solution.py:695
  68.0 15.6 %collective-permute-start.8 = (bf16[8,3,16,256]{3,2,1,0:T(8,128)(2,1)S(1)}, bf16[8,3,16,256]{3,2,1,0:T(8,128)(2,1)S(1)}, u32[]{:S(2)}, u32[]{:S(2)}) collective-permute-start(bf16[8,3,16,256]{3,2,1,0:T(8,128)(2,1)S(1)} %get-tuple-element.113), channel_id=1, source_target_pairs={{0,1},{1,2},{2,3},{3,4},{4,5},{5,6},{6,7},{7,8},{8,9},{9,10},{10,1... | collective-permute-start | bytes 589832 | tf_op jit(solution)/shard_map/ppermute | solution.py:682
  68.2 10.4 %collective-permute-start.13 = (bf16[256,256]{1,0:T(8,128)(2,1)S(1)}, bf16[256,256]{1,0:T(8,128)(2,1)S(1)}, u32[]{:S(2)}, u32[]{:S(2)}) collective-permute-start(bf16[256,256]{1,0:T(8,128)(2,1)S(1)} %quarter.2.refs_4_.refs_0_), channel_id=1, source_target_pairs={{0,8},{1,9},{2,10},{3,11},{4,12},{5,13},{6,14},{7,15},{8,0},{9,1},... | collective-permute-start | bytes 393224 | tf_op jit(solution)/shard_map/ppermute | solution.py:688
  71.6 13.4 %collective-permute-start.9 = (bf16[8,3,16,256]{3,2,1,0:T(8,128)(2,1)S(1)}, bf16[8,3,16,256]{3,2,1,0:T(8,128)(2,1)S(1)}, u32[]{:S(2)}, u32[]{:S(2)}) collective-permute-start(bf16[8,3,16,256]{3,2,1,0:T(8,128)(2,1)S(1)} %get-tuple-element.114), channel_id=1, source_target_pairs={{0,15},{1,0},{2,1},{3,2},{4,3},{5,4},{6,5},{7,6},{8,7},{9,8},{10,9... | collective-permute-start | bytes 589832 | tf_op jit(solution)/shard_map/ppermute | solution.py:682
  77.1 1.5 %collective-permute-start.17 = (bf16[64,256]{1,0:T(8,128)(2,1)S(1)}, bf16[64,256]{1,0:T(8,128)(2,1)S(1)}, u32[]{:S(2)}, u32[]{:S(2)}) collective-permute-start(bf16[64,256]{1,0:T(8,128)(2,1)S(1)} %get-tuple-element.127), channel_id=1, source_target_pairs={{0,1},{1,0},{2,3},{3,2},{4,5},{5,4},{6,7},{7,6},{8,9},{9,8},{10,11... | collective-permute-start | bytes 98312 | tf_op jit(solution)/shard_map/ppermute | solution.py:695
  78.6 8.9 %collective-permute-start.18 = (bf16[320,256]{1,0:T(8,128)(2,1)S(1)}, bf16[320,256]{1,0:T(8,128)(2,1)S(1)}, u32[]{:S(2)}, u32[]{:S(2)}) collective-permute-start(bf16[320,256]{1,0:T(8,128)(2,1)S(1)} %get-tuple-element.128.refs_0_), channel_id=1, source_target_pairs={{0,8},{1,9},{2,10},{3,11},{4,12},{5,13},{6,14},{7,15},{8,0},{9,1},... | collective-permute-start | bytes 491528 | tf_op jit(solution)/shard_map/ppermute | solution.py:688
  78.7 8.8 %collective-permute-start.22 = (bf16[256,256]{1,0:T(8,128)(2,1)S(1)}, bf16[256,256]{1,0:T(8,128)(2,1)S(1)}, u32[]{:S(2)}, u32[]{:S(2)}) collective-permute-start(bf16[256,256]{1,0:T(8,128)(2,1)S(1)} %get-tuple-element.130.refs_0_), channel_id=1, source_target_pairs={{0,2},{1,3},{2,0},{3,1},{4,6},{5,7},{6,4},{7,5},{8,10},{9,11},{10,... | collective-permute-start | bytes 393224 | tf_op jit(solution)/shard_map/ppermute | solution.py:688
  80.4 7.1 %collective-permute-start.23 = (bf16[256,256]{1,0:T(8,128)(2,1)S(1)}, bf16[256,256]{1,0:T(8,128)(2,1)S(1)}, u32[]{:S(2)}, u32[]{:S(2)}) collective-permute-start(bf16[256,256]{1,0:T(8,128)(2,1)S(1)} %get-tuple-element.130.refs_0_), channel_id=1, source_target_pairs={{0,4},{1,5},{2,6},{3,7},{4,0},{5,1},{6,2},{7,3},{8,12},{9,13},{10,... | collective-permute-start | bytes 393224 | tf_op jit(solution)/shard_map/ppermute | solution.py:688
  83.6 10.8 %collective-permute-start.24 = (bf16[256,256]{1,0:T(8,128)(2,1)S(1)}, bf16[256,256]{1,0:T(8,128)(2,1)S(1)}, u32[]{:S(2)}, u32[]{:S(2)}) collective-permute-start(bf16[256,256]{1,0:T(8,128)(2,1)S(1)} %get-tuple-element.130.refs_0_), channel_id=1, source_target_pairs={{0,6},{1,7},{2,4},{3,5},{4,2},{5,3},{6,0},{7,1},{8,14},{9,15},{10,... | collective-permute-start | bytes 393224 | tf_op jit(solution)/shard_map/ppermute | solution.py:688
  94.4 4.6 %collective-permute-start.25 = (bf16[1024,256]{1,0:T(8,128)(2,1)S(1)}, bf16[1024,256]{1,0:T(8,128)(2,1)S(1)}, u32[]{:S(2)}, u32[]{:S(2)}) collective-permute-start(bf16[1024,256]{1,0:T(8,128)(2,1)S(1)} %order.2.refs_0_), channel_id=1, source_target_pairs={{0,1},{1,0},{2,3},{3,2},{4,5},{5,4},{6,7},{7,6},{8,9},{9,8},{10,11... | collective-permute-start | bytes 1572872 | tf_op jit(solution)/shard_map/ppermute | solution.py:688
  95.5 6.2 %collective-permute-start.19 = (bf16[320,256]{1,0:T(8,128)(2,1)S(1)}, bf16[320,256]{1,0:T(8,128)(2,1)S(1)}, u32[]{:S(2)}, u32[]{:S(2)}) collective-permute-start(bf16[320,256]{1,0:T(8,128)(2,1)S(1)} %far.1.refs_4_.refs_0_), channel_id=1, source_target_pairs={{0,2},{1,3},{2,0},{3,1},{4,6},{5,7},{6,4},{7,5},{8,10},{9,11},{10,... | collective-permute-start | bytes 491528 | tf_op jit(solution)/shard_map/ppermute | solution.py:688
  95.5 7.0 %collective-permute-start.20 = (bf16[320,256]{1,0:T(8,128)(2,1)S(1)}, bf16[320,256]{1,0:T(8,128)(2,1)S(1)}, u32[]{:S(2)}, u32[]{:S(2)}) collective-permute-start(bf16[320,256]{1,0:T(8,128)(2,1)S(1)} %far.1.refs_4_.refs_0_), channel_id=1, source_target_pairs={{0,4},{1,5},{2,6},{3,7},{4,0},{5,1},{6,2},{7,3},{8,12},{9,13},{10,... | collective-permute-start | bytes 491528 | tf_op jit(solution)/shard_map/ppermute | solution.py:688
  96.0 10.5 %collective-permute-start.21 = (bf16[320,256]{1,0:T(8,128)(2,1)S(1)}, bf16[320,256]{1,0:T(8,128)(2,1)S(1)}, u32[]{:S(2)}, u32[]{:S(2)}) collective-permute-start(bf16[320,256]{1,0:T(8,128)(2,1)S(1)} %far.1.refs_4_.refs_0_), channel_id=1, source_target_pairs={{0,6},{1,7},{2,4},{3,5},{4,2},{5,3},{6,0},{7,1},{8,14},{9,15},{10,... | collective-permute-start | bytes 491528 | tf_op jit(solution)/shard_map/ppermute | solution.py:688
  106.5 2.0 %collective-permute-start.26 = (bf16[1088,256]{1,0:T(8,128)(2,1)S(1)}, bf16[1088,256]{1,0:T(8,128)(2,1)S(1)}, u32[]{:S(2)}, u32[]{:S(2)}) collective-permute-start(bf16[1088,256]{1,0:T(8,128)(2,1)S(1)} %order.3.refs_0_), channel_id=1, source_target_pairs={{0,1},{1,0},{2,3},{3,2},{4,5},{5,4},{6,7},{7,6},{8,9},{9,8},{10,11... | collective-permute-start | bytes 1671176 | tf_op jit(solution)/shard_map/ppermute | solution.py:688

commit v10 on v9

--- a/solution.py
+++ b/solution.py
@@ -181,7 +181,7 @@
     scale = 1.0 / sz.channels
     for q in range(sz.tiles):
 
-        @pl.loop(0, sz.edge, unroll=2)
+        @pl.loop(0, sz.edge, unroll=4)
         def _(i):
             at = pl.ds(pl.multiple_of(i * sz.edge, sz.edge), sz.edge)
             parts = [conv[q * sz.lanes + h, at, :] for h in range(sz.lanes)]
@@ -221,7 +221,7 @@
 def finish_forward(sz, cur, branch, lscale, layer, out, flat):
     for q in range(sz.tiles):
 
-        @pl.loop(0, sz.edge, unroll=2)
+        @pl.loop(0, sz.edge, unroll=4)
         def _(i):
             at = pl.ds(pl.multiple_of(q * sz.cells + i * sz.edge, sz.edge), sz.edge)
             value = cur[q, i].astype(F32) + branch[at, :] * lscale[layer : layer + 1, :]
@@ -237,7 +237,7 @@
     sums[...] = jnp.zeros_like(sums)
     for q in range(sz.tiles):
 
-        @pl.loop(0, sz.edge, unroll=2)
+        @pl.loop(0, sz.edge, unroll=4)
         def _(i):
             at = pl.ds(pl.multiple_of(q * sz.cells + i * sz.edge, sz.edge), sz.edge)
             g = grad_row(q, i)
@@ -267,7 +267,7 @@
     blank = jnp.zeros((8, LANES), F32)
     for q in range(sz.tiles):
 
-        @pl.loop(0, sz.edge, unroll=2)
+        @pl.loop(0, sz.edge, unroll=4)
         def _(i):
             at = pl.ds(pl.multiple_of(q * sz.cells + i * sz.edge, sz.edge), sz.edge)
             local = pl.ds(pl.multiple_of(i * sz.edge, sz.edge), sz.edge)

time: 111 us -> 106 us (0.955)
  Pallas kernels: 43.3 us -> 39 us
    pallas_call x20, Pallas kernels: 43.3 us -> 39 us  [call(): pl.pallas_call(run, in_specs=[spec for spec, _ in ins] + [pl.BlockSpec(me...]
where the time goes in v10:
time: 106 us
  starting transfers between devices  39.2 us (37%)
  Pallas kernels  39 us (37%)
  waiting for transfers between devices  21.2 us (20%)
  local copies, waits for them, and re-layouts  5.66 us (5%)
  between operations  1.07 us (1%)
    pallas_call x20, Pallas kernels, call(): pl.pallas_call(run, in_specs=[spec for spec, _ in ins] + [pl.BlockSpec(me...  39 us
    ppermute x8, starting transfers between devices, pass_on(): lax.ppermute(shard, 'tile', [(i, (i + by) % length) for i in range(length)])  18.1 us
    ppermute x10, waiting for transfers between devices, partners(): lax.ppermute(array, 'tile', [(i, i ^ mask) for i in range(length)])  16.6 us
    ppermute x10, starting transfers between devices, partners(): lax.ppermute(array, 'tile', [(i, i ^ mask) for i in range(length)])  14.6 us
    ppermute x9, starting transfers between devices, swap(): lax.ppermute(array, 'tile', [(i, i ^ mask) for i in range(length)])  6.53 us
    unnamed x18, local copies, waits for them, and re-layouts  5.66 us
    ppermute x8, waiting for transfers between devices, pass_on(): lax.ppermute(shard, 'tile', [(i, (i + by) % length) for i in range(length)])  3.37 us
  transfers between devices with their start and end apart: 27, of which 9 were waited for; matrix products, arithmetic and copies ran while one was open for 0% of the time, Pallas kernels for 16%

profile of v10, /device:TPU:0, one launch (start us, length us, event | category | flops | bytes accessed | tf_op | source)
XLA Modules:
  0.0 106.2 jit_solution(8885910167339852527)
XLA Ops:
  0.6 0.9 copy-done.3
  1.6 0.1 strips.1
  1.7 0.5 collective-permute-start
  2.2 5.1 %collective-permute-start.1 = (bf16[8,3,16,256]{3,2,1,0:T(8,128)(2,1)S(1)}, bf16[8,3,16,256]{3,2,1,0:T(8,128)(2,1)S(1)}, u32[]{:S(2)}, u32[]{:S(2)}) collective-permute-start(bf16[8,3,16,256]{3,2,1,0:T(8,128)(2,1)S(1)} %get-tuple-element.75.refs_5_.refs_3_), channel_id=1, source_target_pairs={{0,15},{1,0},{2,1},{3,2},{4,3},{5,4},{6,5},{7,6},{8,7},{9,8},{10,9... | collective-permute-start | bytes 589832 | tf_op jit(solution)/shard_map/ppermute | solution.py:682
  7.3 1.2 %copy-done = bf16[2,256,1024]{2,1,0:T(8,128)(2,1)S(1)} copy-done((bf16[2,256,1024]{2,1,0:T(8,128)(2,1)S(1)}, bf16[2,256,1024]{2,1,0:T(8,128)(2,1)}, u32[]{:S(2)}) %copy-start) | copy-done | bytes 1048600
  8.5 1.2 %copy-done.1 = bf16[2,1024,256]{2,1,0:T(8,128)(2,1)S(1)} copy-done((bf16[2,1024,256]{2,1,0:T(8,128)(2,1)S(1)}, bf16[2,1024,256]{2,1,0:T(8,128)(2,1)}, u32[]{:S(2)}) %copy-start.1) | copy-done | bytes 1048600
  9.7 0.9 copy-done.4
  10.6 0.7 copy-done.7
  11.3 0.7 copy-done.8
  12.0 0.3 fetch.1
  12.3 0.0 copy-start.2
  12.3 0.0 collective-permute-done.1.refs_5_
  12.3 7.1 %forward.1 = (bf16[2,16,16,256]{3,2,1,0:T(8,128)(2,1)S(1)}, bf16[8,3,16,256]{3,2,1,0:T(8,128)(2,1)S(1)}, f32[4,528,128]{2,1,0:T(8,128)S(1)}, f32[4,256,128]{2,1,...) custom-call(s32[4,2,32]{2,1,0:T(2,128)S(1)} %bitcast.13, ...), custom_call_target="tpu_custom_call" | custom-call | bytes 30450000 | tf_op jit(solution)/shard_map/forward/pallas_call | solution.py:657
  19.4 0.1 collective-permute-start.2
  19.5 4.4 %collective-permute-start.3 = (bf16[8,3,16,256]{3,2,1,0:T(8,128)(2,1)S(1)}, bf16[8,3,16,256]{3,2,1,0:T(8,128)(2,1)S(1)}, u32[]{:S(2)}, u32[]{:S(2)}) collective-permute-start(bf16[8,3,16,256]{3,2,1,0:T(8,128)(2,1)S(1)} %get-tuple-element.82.refs_3_), channel_id=1, source_target_pairs={{0,15},{1,0},{2,1},{3,2},{4,3},{5,4},{6,5},{7,6},{8,7},{9,8},{10,9... | collective-permute-start | bytes 589832 | tf_op jit(solution)/shard_map/ppermute | solution.py:682
  23.9 3.3 %collective-permute-done.2.refs_4_ = bf16[8,3,16,256]{3,2,1,0:T(8,128)(2,1)S(1)} collective-permute-done((bf16[8,3,16,256]{3,2,1,0:T(8,128)(2,1)S(1)}, bf16[8,3,16,256]{3,2,1,0:T(8,128)(2,1)S(1)}, u32[]{:S(2)}, u32[]{:S(2)}) %collective-permute-start.2) | collective-permute-done | bytes 196640 | tf_op jit(solution)/shard_map/ppermute | solution.py:682
  27.3 0.0 collective-permute-done.3.refs_5_
  27.3 13.2 %turn.1 = (bf16[2,16,16,256]{3,2,1,0:T(8,128)(2,1)}, f32[4,256,128]{2,1,0:T(8,128)S(1)}, f32[8,3,2,16,128]{4,3,2,1,0:T(8,128)S(1)}, bf16[8,3,16,256]{3,2,1,0:T(8...) custom-call(s32[4,2,32]{2,1,0:T(2,128)S(1)} %bitcast.14, ...), custom_call_target="tpu_custom_call" | custom-call | bytes 53900000 | tf_op jit(solution)/shard_map/turn/pallas_call | solution.py:657
  40.5 0.1 collective-permute-start.4
  40.5 4.7 %collective-permute-start.5 = (bf16[8,3,16,256]{3,2,1,0:T(8,128)(2,1)S(1)}, bf16[8,3,16,256]{3,2,1,0:T(8,128)(2,1)S(1)}, u32[]{:S(2)}, u32[]{:S(2)}) collective-permute-start(bf16[8,3,16,256]{3,2,1,0:T(8,128)(2,1)S(1)} %get-tuple-element.87), channel_id=1, source_target_pairs={{0,15},{1,0},{2,1},{3,2},{4,3},{5,4},{6,5},{7,6},{8,7},{9,8},{10,9... | collective-permute-start | bytes 589832 | tf_op jit(solution)/shard_map/ppermute | solution.py:682
  45.2 3.1 %weights.1 = (bf16[1024,256]{1,0:T(8,128)(2,1)S(1)}, bf16[1024,256]{1,0:T(8,128)(2,1)S(1)}, f32[64,256]{1,0:T(8,128)S(1)}) custom-call(f32[4,528,128]{2,1,0:T(8,128)S(1)} %get-tuple-element.99.refs_0_, f32[4,512,128]{2,1,0:T(8,128)S(1)} %get-tuple-element.100.refs_1_, bf16[512,256]{1,0:T(8,128)(2,1)S(1)} %get-tuple-element.101.refs_2_, ...), custom_call_target="tpu_custom_call" | custom-call | bytes 9800000 | tf_op jit(solution)/shard_map/weights/pallas_call | solution.py:657
  48.3 0.1 collective-permute-start.7
  48.4 0.0 collective-permute-done.5.refs_3_
  48.4 2.2 %backward.1 = (bf16[1024,256]{1,0:T(8,128)(2,1)S(1)}, bf16[1024,256]{1,0:T(8,128)(2,1)S(1)}, f32[4,256,128]{2,1,0:T(8,128)S(1)}, bf16[512,1024]{1,0:T(8,128)(2,1)S(1)}, f32[16,256]{1,0:T(8,128)S(1)}) custom-call(f32[4,256,128]{2,1,0:T(8,128)S(1)} %get-tuple-element.84.refs_0_, f32[8,3,2,16,128]{4,3,2,1,0:T(8,128)S(1)} %get-tuple-element.85.refs_1_, ...), custom_call_target="tpu_custom_call" | custom-call | bytes 10150000 | tf_op jit(solution)/shard_map/backward/pallas_call | solution.py:657
  50.6 0.5 collective-permute-start.6
  51.1 0.0 collective-permute-done.7
  51.1 0.1 share_near.3
  51.2 0.1 collective-permute-start.10
  51.3 0.1 collective-permute-start.11
  51.4 3.4 %collective-permute-start.12 = (bf16[256,256]{1,0:T(8,128)(2,1)S(1)}, bf16[256,256]{1,0:T(8,128)(2,1)S(1)}, u32[]{:S(2)}, u32[]{:S(2)}) collective-permute-start(bf16[256,256]{1,0:T(8,128)(2,1)S(1)} %get-tuple-element.118), channel_id=1, source_target_pairs={{0,6},{1,7},{2,4},{3,5},{4,2},{5,3},{6,0},{7,1},{8,14},{9,15},{10,... | collective-permute-start | bytes 393224 | tf_op jit(solution)/shard_map/ppermute | solution.py:695
  54.8 0.1 share_near.2
  54.9 0.1 collective-permute-start.14
  55.1 0.5 collective-permute-start.15
  55.6 1.2 %collective-permute-done.10.refs_1_ = bf16[256,256]{1,0:T(8,128)(2,1)S(1)} collective-permute-done((bf16[256,256]{1,0:T(8,128)(2,1)S(1)}, bf16[256,256]{1,0:T(8,128)(2,1)S(1)}, u32[]{:S(2)}, u32[]{:S(2)}) %collective-permute-start.10) | collective-permute-done | bytes 131104 | tf_op jit(solution)/shard_map/ppermute | solution.py:695
  56.8 1.7 %collective-permute-start.16 = (bf16[256,256]{1,0:T(8,128)(2,1)S(1)}, bf16[256,256]{1,0:T(8,128)(2,1)S(1)}, u32[]{:S(2)}, u32[]{:S(2)}) collective-permute-start(bf16[256,256]{1,0:T(8,128)(2,1)S(1)} %get-tuple-element.122), channel_id=1, source_target_pairs={{0,6},{1,7},{2,4},{3,5},{4,2},{5,3},{6,0},{7,1},{8,14},{9,15},{10,... | collective-permute-start | bytes 393224 | tf_op jit(solution)/shard_map/ppermute | solution.py:695
  58.5 5.3 %spread.1 = (f32[4,256,128]{2,1,0:T(8,128)S(1)}, f32[8,3,2,16,128]{4,3,2,1,0:T(8,128)S(1)}, bf16[8,3,16,256]{3,2,1,0:T(8,128)(2,1)S(1)}, bf16[8,3,16,256]{3,2,1,...) custom-call(s32[4,2,32]{2,1,0:T(2,128)S(1)} %bitcast.15, s32[4,2,32]{2,1,0:T(2,128)S(1)} %bitcast.18, ...), custom_call_target="tpu_custom_call" | custom-call | bytes 21000000 | tf_op jit(solution)/shard_map/spread/pallas_call | solution.py:657
  63.8 0.1 collective-permute-start.8
  63.8 0.1 quarter.2.refs_4_.refs_0_
  63.9 3.5 %collective-permute-start.13 = (bf16[256,256]{1,0:T(8,128)(2,1)S(1)}, bf16[256,256]{1,0:T(8,128)(2,1)S(1)}, u32[]{:S(2)}, u32[]{:S(2)}) collective-permute-start(bf16[256,256]{1,0:T(8,128)(2,1)S(1)} %quarter.2.refs_4_.refs_0_), channel_id=1, source_target_pairs={{0,8},{1,9},{2,10},{3,11},{4,12},{5,13},{6,14},{7,15},{8,0},{9,1},... | collective-permute-start | bytes 393224 | tf_op jit(solution)/shard_map/ppermute | solution.py:688
  67.4 3.2 %collective-permute-start.9 = (bf16[8,3,16,256]{3,2,1,0:T(8,128)(2,1)S(1)}, bf16[8,3,16,256]{3,2,1,0:T(8,128)(2,1)S(1)}, u32[]{:S(2)}, u32[]{:S(2)}) collective-permute-start(bf16[8,3,16,256]{3,2,1,0:T(8,128)(2,1)S(1)} %get-tuple-element.114), channel_id=1, source_target_pairs={{0,15},{1,0},{2,1},{3,2},{4,3},{5,4},{6,5},{7,6},{8,7},{9,8},{10,9... | collective-permute-start | bytes 589832 | tf_op jit(solution)/shard_map/ppermute | solution.py:682
  70.6 0.1 quarter.3.refs_5_.refs_2_
  70.7 2.1 %taps.1 = (bf16[64,256]{1,0:T(8,128)(2,1)S(1)}, bf16[64,256]{1,0:T(8,128)(2,1)S(1)}) custom-call(f32[4,528,128]{2,1,0:T(8,128)S(1)} %get-tuple-element.123.refs_0_, f32[4,512,128]{2,1,0:T(8,128)S(1)} %get-tuple-element.124.refs_1_, f32[16,256]{1,0:T(8,128)S(1)} %get-tuple-element.119.refs_4_.refs_2_, f32[16,256]{1,0:T(8,128)S(1)} %get-tuple-element.109.refs_2_.refs_3_, ...), custom_call_target="tpu_custom_call" | custom-call | bytes 7350000 | tf_op jit(solution)/shard_map/taps/pallas_call | solution.py:657
  72.8 0.1 collective-permute-start.17
  72.9 1.4 %collective-permute-done.13.refs_1_ = bf16[256,256]{1,0:T(8,128)(2,1)S(1)} collective-permute-done((bf16[256,256]{1,0:T(8,128)(2,1)S(1)}, bf16[256,256]{1,0:T(8,128)(2,1)S(1)}, u32[]{:S(2)}, u32[]{:S(2)}) %collective-permute-start.13) | collective-permute-done | bytes 131104 | tf_op jit(solution)/shard_map/ppermute | solution.py:688
  74.3 0.1 collective-permute-start.18
  74.4 1.8 %collective-permute-start.22 = (bf16[256,256]{1,0:T(8,128)(2,1)S(1)}, bf16[256,256]{1,0:T(8,128)(2,1)S(1)}, u32[]{:S(2)}, u32[]{:S(2)}) collective-permute-start(bf16[256,256]{1,0:T(8,128)(2,1)S(1)} %get-tuple-element.130.refs_0_), channel_id=1, source_target_pairs={{0,2},{1,3},{2,0},{3,1},{4,6},{5,7},{6,4},{7,5},{8,10},{9,11},{10,... | collective-permute-start | bytes 393224 | tf_op jit(solution)/shard_map/ppermute | solution.py:688
  76.2 3.2 %collective-permute-start.23 = (bf16[256,256]{1,0:T(8,128)(2,1)S(1)}, bf16[256,256]{1,0:T(8,128)(2,1)S(1)}, u32[]{:S(2)}, u32[]{:S(2)}) collective-permute-start(bf16[256,256]{1,0:T(8,128)(2,1)S(1)} %get-tuple-element.130.refs_0_), channel_id=1, source_target_pairs={{0,4},{1,5},{2,6},{3,7},{4,0},{5,1},{6,2},{7,3},{8,12},{9,13},{10,... | collective-permute-start | bytes 393224 | tf_op jit(solution)/shard_map/ppermute | solution.py:688
  79.4 1.5 %collective-permute-start.24 = (bf16[256,256]{1,0:T(8,128)(2,1)S(1)}, bf16[256,256]{1,0:T(8,128)(2,1)S(1)}, u32[]{:S(2)}, u32[]{:S(2)}) collective-permute-start(bf16[256,256]{1,0:T(8,128)(2,1)S(1)} %get-tuple-element.130.refs_0_), channel_id=1, source_target_pairs={{0,6},{1,7},{2,4},{3,5},{4,2},{5,3},{6,0},{7,1},{8,14},{9,15},{10,... | collective-permute-start | bytes 393224 | tf_op jit(solution)/shard_map/ppermute | solution.py:688
  80.8 0.9 last.1
  81.8 1.4 %collective-permute-done.18.refs_1_ = bf16[320,256]{1,0:T(8,128)(2,1)S(1)} collective-permute-done((bf16[320,256]{1,0:T(8,128)(2,1)S(1)}, bf16[320,256]{1,0:T(8,128)(2,1)S(1)}, u32[]{:S(2)}, u32[]{:S(2)}) %collective-permute-start.18) | collective-permute-done | bytes 163872 | tf_op jit(solution)/shard_map/ppermute | solution.py:688
  83.3 6.9 %collective-permute-done.24.refs_3_ = bf16[256,256]{1,0:T(8,128)(2,1)S(1)} collective-permute-done((bf16[256,256]{1,0:T(8,128)(2,1)S(1)}, bf16[256,256]{1,0:T(8,128)(2,1)S(1)}, u32[]{:S(2)}, u32[]{:S(2)}) %collective-permute-start.24) | collective-permute-done | bytes 131104 | tf_op jit(solution)/shard_map/ppermute | solution.py:688
  90.1 0.1 order.2.refs_0_
  90.2 1.1 %collective-permute-start.25 = (bf16[1024,256]{1,0:T(8,128)(2,1)S(1)}, bf16[1024,256]{1,0:T(8,128)(2,1)S(1)}, u32[]{:S(2)}, u32[]{:S(2)}) collective-permute-start(bf16[1024,256]{1,0:T(8,128)(2,1)S(1)} %order.2.refs_0_), channel_id=1, source_target_pairs={{0,1},{1,0},{2,3},{3,2},{4,5},{5,4},{6,7},{7,6},{8,9},{9,8},{10,11... | collective-permute-start | bytes 1572872 | tf_op jit(solution)/shard_map/ppermute | solution.py:688
  91.3 0.4 collective-permute-start.20
  91.7 3.1 %collective-permute-start.21 = (bf16[320,256]{1,0:T(8,128)(2,1)S(1)}, bf16[320,256]{1,0:T(8,128)(2,1)S(1)}, u32[]{:S(2)}, u32[]{:S(2)}) collective-permute-start(bf16[320,256]{1,0:T(8,128)(2,1)S(1)} %far.1.refs_4_.refs_0_), channel_id=1, source_target_pairs={{0,6},{1,7},{2,4},{3,5},{4,2},{5,3},{6,0},{7,1},{8,14},{9,15},{10,... | collective-permute-start | bytes 491528 | tf_op jit(solution)/shard_map/ppermute | solution.py:688
  94.8 1.4 %unpack_one.1 = (f32[2,256,1024]{2,1,0:T(8,128)}, f32[2,1024,256]{2,1,0:T(8,128)}, f32[8,128]{1,0:T(8,128)S(1)}) custom-call(bf16[1024,256]{1,0:T(8,128)(2,1)S(1)} %order.2.refs_0_, bf16[1024,256]{1,0:T(8,128)(2,1)S(1)} %collective-permute-done.25.refs_1_), custom_call_target="tpu_custom_call" | custom-call | bytes 6300000 | tf_op jit(solution)/shard_map/unpack_one/pallas_call | solution.py:657
  96.2 1.3 %collective-permute-done.19.refs_1_ = bf16[320,256]{1,0:T(8,128)(2,1)S(1)} collective-permute-done((bf16[320,256]{1,0:T(8,128)(2,1)S(1)}, bf16[320,256]{1,0:T(8,128)(2,1)S(1)}, u32[]{:S(2)}, u32[]{:S(2)}) %collective-permute-start.19) | collective-permute-done | bytes 163872 | tf_op jit(solution)/shard_map/ppermute | solution.py:688
  97.5 0.9 collective-permute-done.20.refs_2_
  98.3 3.8 %collective-permute-done.21.refs_3_ = bf16[320,256]{1,0:T(8,128)(2,1)S(1)} collective-permute-done((bf16[320,256]{1,0:T(8,128)(2,1)S(1)}, bf16[320,256]{1,0:T(8,128)(2,1)S(1)}, u32[]{:S(2)}, u32[]{:S(2)}) %collective-permute-start.21) | collective-permute-done | bytes 163872 | tf_op jit(solution)/shard_map/ppermute | solution.py:688
  102.2 0.1 order.3.refs_0_
  102.2 0.1 collective-permute-start.26
  102.3 1.1 %unpack_mine.1 = (f32[2,256,1024]{2,1,0:T(8,128)}, f32[2,1024,256]{2,1,0:T(8,128)}) custom-call(bf16[1088,256]{1,0:T(8,128)(2,1)S(1)} %order.3.refs_0_, f32[2,256,1024]{2,1,0:T(8,128)} %get-tuple-element.132.refs_1_, f32[2,1024,256]{2,1,0:T(8,128)} %get-tuple-element.133.refs_2_), custom_call_target="tpu_custom_call", output_to_operand_aliasing={{0}: (1, {}), {1}: (2, {})} | custom-call | bytes 3500000 | tf_op jit(solution)/shard_map/unpack_mine/pallas_call | solution.py:657
  103.4 0.9 collective-permute-done.26.refs_1_
  104.3 1.8 %unpack_theirs.1 = (f32[2,256,1024]{2,1,0:T(8,128)}, f32[2,1024,256]{2,1,0:T(8,128)}, f32[7,7,2,256]{3,2,1,0:T(2,128)}, f32[2,256]{1,0:T(2,128)}, f32[2,256]{1,0:T(2,128)}) custom-call(bf16[1088,256]{1,0:T(8,128)(2,1)S(1)} %order.3.refs_0_, bf16[1088,256]{1,0:T(8,128)(2,1)S(1)} %collective-permute-done.26.refs_1_, ...), custom_call_target="tpu_custom_call", output_to_operand_aliasing={{0}: (2, {}), {1}: (3, {})} | custom-call | bytes 4550000 | tf_op jit(solution)/shard_map/unpack_theirs/pallas_call | solution.py:657
  (28 shorter events, 0.1 us)
Async XLA Ops:
  0.6 1.0 copy-start.3
  1.6 10.7 %copy-start.5 = (s32[32,4,2]{0,2,1:T(2,128)S(1)}, s32[32,4,2]{0,2,1:T(2,128)}, u32[]{:S(2)}) copy-start(s32[32,4,2]{0,2,1:T(2,128)} %param.16) | copy-start | bytes 3076
  1.6 10.7 %copy-start.6 = (s32[32,4,2]{0,2,1:T(2,128)S(1)}, s32[32,4,2]{0,2,1:T(2,128)}, u32[]{:S(2)}) copy-start(s32[32,4,2]{0,2,1:T(2,128)} %param.17) | copy-start | bytes 3076
  1.7 10.6 %collective-permute-start = (bf16[8,3,16,256]{3,2,1,0:T(8,128)(2,1)S(1)}, bf16[8,3,16,256]{3,2,1,0:T(8,128)(2,1)S(1)}, u32[]{:S(2)}, u32[]{:S(2)}) collective-permute-start(bf16[8,3,16,256]{3,2,1,0:T(8,128)(2,1)S(1)} %get-tuple-element.75.refs_5_.refs_3_), channel_id=1, source_target_pairs={{0,1},{1,2},{2,3},{3,4},{4,5},{5,6},{6,7},{7,8},{8,9},{9,10},{10,1... | collective-permute-start | bytes 589832 | tf_op jit(solution)/shard_map/ppermute | solution.py:682
  2.2 10.1 %collective-permute-start.1 = (bf16[8,3,16,256]{3,2,1,0:T(8,128)(2,1)S(1)}, bf16[8,3,16,256]{3,2,1,0:T(8,128)(2,1)S(1)}, u32[]{:S(2)}, u32[]{:S(2)}) collective-permute-start(bf16[8,3,16,256]{3,2,1,0:T(8,128)(2,1)S(1)} %get-tuple-element.75.refs_5_.refs_3_), channel_id=1, source_target_pairs={{0,15},{1,0},{2,1},{3,2},{4,3},{5,4},{6,5},{7,6},{8,7},{9,8},{10,9... | collective-permute-start | bytes 589832 | tf_op jit(solution)/shard_map/ppermute | solution.py:682
  7.3 1.2 %copy-start = (bf16[2,256,1024]{2,1,0:T(8,128)(2,1)S(1)}, bf16[2,256,1024]{2,1,0:T(8,128)(2,1)}, u32[]{:S(2)}) copy-start(bf16[2,256,1024]{2,1,0:T(8,128)(2,1)} %refs_3_.1) | copy-start | bytes 3145732
  8.5 1.2 %copy-start.1 = (bf16[2,1024,256]{2,1,0:T(8,128)(2,1)S(1)}, bf16[2,1024,256]{2,1,0:T(8,128)(2,1)}, u32[]{:S(2)}) copy-start(bf16[2,1024,256]{2,1,0:T(8,128)(2,1)} %refs_4_.1) | copy-start | bytes 3145732
  9.7 0.9 copy-start.4
  10.6 0.7 copy-start.7
  11.3 0.7 copy-start.8
  12.3 15.0 %copy-start.2 = (bf16[2,16,16,256]{3,2,1,0:T(8,128)(2,1)S(1)}, bf16[2,16,16,256]{3,2,1,0:T(8,128)(2,1)}, u32[]{:S(2)}) copy-start(bf16[2,16,16,256]{3,2,1,0:T(8,128)(2,1)} %refs_11_.1) | copy-start | bytes 786436
  19.4 7.8 %collective-permute-start.2 = (bf16[8,3,16,256]{3,2,1,0:T(8,128)(2,1)S(1)}, bf16[8,3,16,256]{3,2,1,0:T(8,128)(2,1)S(1)}, u32[]{:S(2)}, u32[]{:S(2)}) collective-permute-start(bf16[8,3,16,256]{3,2,1,0:T(8,128)(2,1)S(1)} %get-tuple-element.82.refs_3_), channel_id=1, source_target_pairs={{0,1},{1,2},{2,3},{3,4},{4,5},{5,6},{6,7},{7,8},{8,9},{9,10},{10,1... | collective-permute-start | bytes 589832 | tf_op jit(solution)/shard_map/ppermute | solution.py:682
  19.5 7.8 %collective-permute-start.3 = (bf16[8,3,16,256]{3,2,1,0:T(8,128)(2,1)S(1)}, bf16[8,3,16,256]{3,2,1,0:T(8,128)(2,1)S(1)}, u32[]{:S(2)}, u32[]{:S(2)}) collective-permute-start(bf16[8,3,16,256]{3,2,1,0:T(8,128)(2,1)S(1)} %get-tuple-element.82.refs_3_), channel_id=1, source_target_pairs={{0,15},{1,0},{2,1},{3,2},{4,3},{5,4},{6,5},{7,6},{8,7},{9,8},{10,9... | collective-permute-start | bytes 589832 | tf_op jit(solution)/shard_map/ppermute | solution.py:682
  40.5 7.9 %collective-permute-start.4 = (bf16[8,3,16,256]{3,2,1,0:T(8,128)(2,1)S(1)}, bf16[8,3,16,256]{3,2,1,0:T(8,128)(2,1)S(1)}, u32[]{:S(2)}, u32[]{:S(2)}) collective-permute-start(bf16[8,3,16,256]{3,2,1,0:T(8,128)(2,1)S(1)} %get-tuple-element.86), channel_id=1, source_target_pairs={{0,1},{1,2},{2,3},{3,4},{4,5},{5,6},{6,7},{7,8},{8,9},{9,10},{10,1... | collective-permute-start | bytes 589832 | tf_op jit(solution)/shard_map/ppermute | solution.py:682
  40.5 7.9 %collective-permute-start.5 = (bf16[8,3,16,256]{3,2,1,0:T(8,128)(2,1)S(1)}, bf16[8,3,16,256]{3,2,1,0:T(8,128)(2,1)S(1)}, u32[]{:S(2)}, u32[]{:S(2)}) collective-permute-start(bf16[8,3,16,256]{3,2,1,0:T(8,128)(2,1)S(1)} %get-tuple-element.87), channel_id=1, source_target_pairs={{0,15},{1,0},{2,1},{3,2},{4,3},{5,4},{6,5},{7,6},{8,7},{9,8},{10,9... | collective-permute-start | bytes 589832 | tf_op jit(solution)/shard_map/ppermute | solution.py:682
  48.3 2.8 %collective-permute-start.7 = (bf16[1024,256]{1,0:T(8,128)(2,1)S(1)}, bf16[1024,256]{1,0:T(8,128)(2,1)S(1)}, u32[]{:S(2)}, u32[]{:S(2)}) collective-permute-start(bf16[1024,256]{1,0:T(8,128)(2,1)S(1)} %get-tuple-element.108), channel_id=1, source_target_pairs={{0,1},{1,0},{2,3},{3,2},{4,5},{5,4},{6,7},{7,6},{8,9},{9,8},{10,11... | collective-permute-start | bytes 1572872 | tf_op jit(solution)/shard_map/ppermute | solution.py:695
  50.6 4.2 %collective-permute-start.6 = (bf16[1024,256]{1,0:T(8,128)(2,1)S(1)}, bf16[1024,256]{1,0:T(8,128)(2,1)S(1)}, u32[]{:S(2)}, u32[]{:S(2)}) collective-permute-start(bf16[1024,256]{1,0:T(8,128)(2,1)S(1)} %get-tuple-element.97), channel_id=1, source_target_pairs={{0,1},{1,0},{2,3},{3,2},{4,5},{5,4},{6,7},{7,6},{8,9},{9,8},{10,11... | collective-permute-start | bytes 1572872 | tf_op jit(solution)/shard_map/ppermute | solution.py:695
  51.2 5.6 %collective-permute-start.10 = (bf16[256,256]{1,0:T(8,128)(2,1)S(1)}, bf16[256,256]{1,0:T(8,128)(2,1)S(1)}, u32[]{:S(2)}, u32[]{:S(2)}) collective-permute-start(bf16[256,256]{1,0:T(8,128)(2,1)S(1)} %get-tuple-element.116), channel_id=1, source_target_pairs={{0,2},{1,3},{2,0},{3,1},{4,6},{5,7},{6,4},{7,5},{8,10},{9,11},{10,... | collective-permute-start | bytes 393224 | tf_op jit(solution)/shard_map/ppermute | solution.py:695
  51.3 12.4 %collective-permute-start.11 = (bf16[256,256]{1,0:T(8,128)(2,1)S(1)}, bf16[256,256]{1,0:T(8,128)(2,1)S(1)}, u32[]{:S(2)}, u32[]{:S(2)}) collective-permute-start(bf16[256,256]{1,0:T(8,128)(2,1)S(1)} %get-tuple-element.117), channel_id=1, source_target_pairs={{0,4},{1,5},{2,6},{3,7},{4,0},{5,1},{6,2},{7,3},{8,12},{9,13},{10,... | collective-permute-start | bytes 393224 | tf_op jit(solution)/shard_map/ppermute | solution.py:695
  51.4 12.4 %collective-permute-start.12 = (bf16[256,256]{1,0:T(8,128)(2,1)S(1)}, bf16[256,256]{1,0:T(8,128)(2,1)S(1)}, u32[]{:S(2)}, u32[]{:S(2)}) collective-permute-start(bf16[256,256]{1,0:T(8,128)(2,1)S(1)} %get-tuple-element.118), channel_id=1, source_target_pairs={{0,6},{1,7},{2,4},{3,5},{4,2},{5,3},{6,0},{7,1},{8,14},{9,15},{10,... | collective-permute-start | bytes 393224 | tf_op jit(solution)/shard_map/ppermute | solution.py:695
  54.9 12.5 %collective-permute-start.14 = (bf16[256,256]{1,0:T(8,128)(2,1)S(1)}, bf16[256,256]{1,0:T(8,128)(2,1)S(1)}, u32[]{:S(2)}, u32[]{:S(2)}) collective-permute-start(bf16[256,256]{1,0:T(8,128)(2,1)S(1)} %get-tuple-element.120), channel_id=1, source_target_pairs={{0,2},{1,3},{2,0},{3,1},{4,6},{5,7},{6,4},{7,5},{8,10},{9,11},{10,... | collective-permute-start | bytes 393224 | tf_op jit(solution)/shard_map/ppermute | solution.py:695
  55.1 15.6 %collective-permute-start.15 = (bf16[256,256]{1,0:T(8,128)(2,1)S(1)}, bf16[256,256]{1,0:T(8,128)(2,1)S(1)}, u32[]{:S(2)}, u32[]{:S(2)}) collective-permute-start(bf16[256,256]{1,0:T(8,128)(2,1)S(1)} %get-tuple-element.121), channel_id=1, source_target_pairs={{0,4},{1,5},{2,6},{3,7},{4,0},{5,1},{6,2},{7,3},{8,12},{9,13},{10,... | collective-permute-start | bytes 393224 | tf_op jit(solution)/shard_map/ppermute | solution.py:695
  56.8 13.8 %collective-permute-start.16 = (bf16[256,256]{1,0:T(8,128)(2,1)S(1)}, bf16[256,256]{1,0:T(8,128)(2,1)S(1)}, u32[]{:S(2)}, u32[]{:S(2)}) collective-permute-start(bf16[256,256]{1,0:T(8,128)(2,1)S(1)} %get-tuple-element.122), channel_id=1, source_target_pairs={{0,6},{1,7},{2,4},{3,5},{4,2},{5,3},{6,0},{7,1},{8,14},{9,15},{10,... | collective-permute-start | bytes 393224 | tf_op jit(solution)/shard_map/ppermute | solution.py:695
  63.8 15.6 %collective-permute-start.8 = (bf16[8,3,16,256]{3,2,1,0:T(8,128)(2,1)S(1)}, bf16[8,3,16,256]{3,2,1,0:T(8,128)(2,1)S(1)}, u32[]{:S(2)}, u32[]{:S(2)}) collective-permute-start(bf16[8,3,16,256]{3,2,1,0:T(8,128)(2,1)S(1)} %get-tuple-element.113), channel_id=1, source_target_pairs={{0,1},{1,2},{2,3},{3,4},{4,5},{5,6},{6,7},{7,8},{8,9},{9,10},{10,1... | collective-permute-start | bytes 589832 | tf_op jit(solution)/shard_map/ppermute | solution.py:682
  63.9 10.4 %collective-permute-start.13 = (bf16[256,256]{1,0:T(8,128)(2,1)S(1)}, bf16[256,256]{1,0:T(8,128)(2,1)S(1)}, u32[]{:S(2)}, u32[]{:S(2)}) collective-permute-start(bf16[256,256]{1,0:T(8,128)(2,1)S(1)} %quarter.2.refs_4_.refs_0_), channel_id=1, source_target_pairs={{0,8},{1,9},{2,10},{3,11},{4,12},{5,13},{6,14},{7,15},{8,0},{9,1},... | collective-permute-start | bytes 393224 | tf_op jit(solution)/shard_map/ppermute | solution.py:688
  67.4 13.4 %collective-permute-start.9 = (bf16[8,3,16,256]{3,2,1,0:T(8,128)(2,1)S(1)}, bf16[8,3,16,256]{3,2,1,0:T(8,128)(2,1)S(1)}, u32[]{:S(2)}, u32[]{:S(2)}) collective-permute-start(bf16[8,3,16,256]{3,2,1,0:T(8,128)(2,1)S(1)} %get-tuple-element.114), channel_id=1, source_target_pairs={{0,15},{1,0},{2,1},{3,2},{4,3},{5,4},{6,5},{7,6},{8,7},{9,8},{10,9... | collective-permute-start | bytes 589832 | tf_op jit(solution)/shard_map/ppermute | solution.py:682
  72.8 1.5 %collective-permute-start.17 = (bf16[64,256]{1,0:T(8,128)(2,1)S(1)}, bf16[64,256]{1,0:T(8,128)(2,1)S(1)}, u32[]{:S(2)}, u32[]{:S(2)}) collective-permute-start(bf16[64,256]{1,0:T(8,128)(2,1)S(1)} %get-tuple-element.127), channel_id=1, source_target_pairs={{0,1},{1,0},{2,3},{3,2},{4,5},{5,4},{6,7},{7,6},{8,9},{9,8},{10,11... | collective-permute-start | bytes 98312 | tf_op jit(solution)/shard_map/ppermute | solution.py:695
  74.3 8.9 %collective-permute-start.18 = (bf16[320,256]{1,0:T(8,128)(2,1)S(1)}, bf16[320,256]{1,0:T(8,128)(2,1)S(1)}, u32[]{:S(2)}, u32[]{:S(2)}) collective-permute-start(bf16[320,256]{1,0:T(8,128)(2,1)S(1)} %get-tuple-element.128.refs_0_), channel_id=1, source_target_pairs={{0,8},{1,9},{2,10},{3,11},{4,12},{5,13},{6,14},{7,15},{8,0},{9,1},... | collective-permute-start | bytes 491528 | tf_op jit(solution)/shard_map/ppermute | solution.py:688
  74.4 8.8 %collective-permute-start.22 = (bf16[256,256]{1,0:T(8,128)(2,1)S(1)}, bf16[256,256]{1,0:T(8,128)(2,1)S(1)}, u32[]{:S(2)}, u32[]{:S(2)}) collective-permute-start(bf16[256,256]{1,0:T(8,128)(2,1)S(1)} %get-tuple-element.130.refs_0_), channel_id=1, source_target_pairs={{0,2},{1,3},{2,0},{3,1},{4,6},{5,7},{6,4},{7,5},{8,10},{9,11},{10,... | collective-permute-start | bytes 393224 | tf_op jit(solution)/shard_map/ppermute | solution.py:688
  76.2 7.1 %collective-permute-start.23 = (bf16[256,256]{1,0:T(8,128)(2,1)S(1)}, bf16[256,256]{1,0:T(8,128)(2,1)S(1)}, u32[]{:S(2)}, u32[]{:S(2)}) collective-permute-start(bf16[256,256]{1,0:T(8,128)(2,1)S(1)} %get-tuple-element.130.refs_0_), channel_id=1, source_target_pairs={{0,4},{1,5},{2,6},{3,7},{4,0},{5,1},{6,2},{7,3},{8,12},{9,13},{10,... | collective-permute-start | bytes 393224 | tf_op jit(solution)/shard_map/ppermute | solution.py:688
  79.4 10.8 %collective-permute-start.24 = (bf16[256,256]{1,0:T(8,128)(2,1)S(1)}, bf16[256,256]{1,0:T(8,128)(2,1)S(1)}, u32[]{:S(2)}, u32[]{:S(2)}) collective-permute-start(bf16[256,256]{1,0:T(8,128)(2,1)S(1)} %get-tuple-element.130.refs_0_), channel_id=1, source_target_pairs={{0,6},{1,7},{2,4},{3,5},{4,2},{5,3},{6,0},{7,1},{8,14},{9,15},{10,... | collective-permute-start | bytes 393224 | tf_op jit(solution)/shard_map/ppermute | solution.py:688
  90.2 4.6 %collective-permute-start.25 = (bf16[1024,256]{1,0:T(8,128)(2,1)S(1)}, bf16[1024,256]{1,0:T(8,128)(2,1)S(1)}, u32[]{:S(2)}, u32[]{:S(2)}) collective-permute-start(bf16[1024,256]{1,0:T(8,128)(2,1)S(1)} %order.2.refs_0_), channel_id=1, source_target_pairs={{0,1},{1,0},{2,3},{3,2},{4,5},{5,4},{6,7},{7,6},{8,9},{9,8},{10,11... | collective-permute-start | bytes 1572872 | tf_op jit(solution)/shard_map/ppermute | solution.py:688
  91.3 6.2 %collective-permute-start.19 = (bf16[320,256]{1,0:T(8,128)(2,1)S(1)}, bf16[320,256]{1,0:T(8,128)(2,1)S(1)}, u32[]{:S(2)}, u32[]{:S(2)}) collective-permute-start(bf16[320,256]{1,0:T(8,128)(2,1)S(1)} %far.1.refs_4_.refs_0_), channel_id=1, source_target_pairs={{0,2},{1,3},{2,0},{3,1},{4,6},{5,7},{6,4},{7,5},{8,10},{9,11},{10,... | collective-permute-start | bytes 491528 | tf_op jit(solution)/shard_map/ppermute | solution.py:688
  91.3 7.0 %collective-permute-start.20 = (bf16[320,256]{1,0:T(8,128)(2,1)S(1)}, bf16[320,256]{1,0:T(8,128)(2,1)S(1)}, u32[]{:S(2)}, u32[]{:S(2)}) collective-permute-start(bf16[320,256]{1,0:T(8,128)(2,1)S(1)} %far.1.refs_4_.refs_0_), channel_id=1, source_target_pairs={{0,4},{1,5},{2,6},{3,7},{4,0},{5,1},{6,2},{7,3},{8,12},{9,13},{10,... | collective-permute-start | bytes 491528 | tf_op jit(solution)/shard_map/ppermute | solution.py:688
  91.7 10.5 %collective-permute-start.21 = (bf16[320,256]{1,0:T(8,128)(2,1)S(1)}, bf16[320,256]{1,0:T(8,128)(2,1)S(1)}, u32[]{:S(2)}, u32[]{:S(2)}) collective-permute-start(bf16[320,256]{1,0:T(8,128)(2,1)S(1)} %far.1.refs_4_.refs_0_), channel_id=1, source_target_pairs={{0,6},{1,7},{2,4},{3,5},{4,2},{5,3},{6,0},{7,1},{8,14},{9,15},{10,... | collective-permute-start | bytes 491528 | tf_op jit(solution)/shard_map/ppermute | solution.py:688
  102.2 2.0 %collective-permute-start.26 = (bf16[1088,256]{1,0:T(8,128)(2,1)S(1)}, bf16[1088,256]{1,0:T(8,128)(2,1)S(1)}, u32[]{:S(2)}, u32[]{:S(2)}) collective-permute-start(bf16[1088,256]{1,0:T(8,128)(2,1)S(1)} %order.3.refs_0_), channel_id=1, source_target_pairs={{0,1},{1,0},{2,3},{3,2},{4,5},{5,4},{6,7},{7,6},{8,9},{9,8},{10,11... | collective-permute-start | bytes 1671176 | tf_op jit(solution)/shard_map/ppermute | solution.py:688
